TPU v7x, 128 devices: a whole 4x4x4 slice. The times are simulated.
128 devices in a mesh: sx: 8 (over y, z_hi), sy: 16 (over z_lo, x, core).
Axes of the slice: x: 4, y: 4, z: 4 (z_hi: 2, z_lo: 2; z = z_hi * 2 + z_lo), core: 2. Of those that a mesh axis runs over, the one named last changes fastest.
Arguments:
- tokens: bfloat16 [16384, 5120], P(('sx', 'sy')), may hold values from -5 to 5
- mod_shift: float32 [5120], replicated, may hold values from -3 to 3
- mod_scale: float32 [5120], replicated, may hold values from -2.5 to 2.5
- w_query: bfloat16 [5120, 4096], P(None, 'sy'), may hold values from -2.5 to 2.5
- w_key: bfloat16 [5120, 4096], P(None, 'sy'), may hold values from -2.5 to 2.5
- w_value: bfloat16 [5120, 4096], P(None, 'sy'), may hold values from -0.078125 to 0.078125
- query_gain: float32 [4096], replicated, may hold values from 0.1 to 1.9
- key_gain: float32 [4096], replicated, may hold values from 0.1 to 1.9
Outputs:
- attended: bfloat16 [16384, 4096], P(('sx', 'sy'))
- row_max: float32 [32, 16384], P(None, ('sx', 'sy'))
- row_sum: float32 [32, 16384], P(None, ('sx', 'sy'))
All inputs are finite; a program needn't handle non-finite values.
Results may differ from a plain program's by a relative error of at most 0.0061.
Values may be sent and summed in bfloat16 or wider, within the bound.
No kernel may reach another device: no remote copies, remote signals or barrier semaphores. Data moves between devices by JAX's collectives and lax.ppermute only.
A program may use at most 128 MiB of HBM per device.

v0:
```python
import jax
import jax.numpy as jnp
import numpy as np
from jax import lax
from jax.experimental import pallas as pl
from jax.experimental.pallas import tpu as pltpu
from jax.sharding import PartitionSpec as P

H = 32
HD = 128
ROUNDS = 4
GRID_W = 80
GRID_H = 45
BLK = 128
HALO = ROUNDS * BLK
EXTRA = 16
NSY = 16
SCALE = np.float32(1.0) / np.sqrt(np.float32(HD))
LOG2E = np.float32(1.4426950408889634)


def layer_norm(values, mod_shift, mod_scale):
    wide = values.astype(jnp.float32)
    center = jnp.mean(wide, axis=-1, keepdims=True)
    spread = jnp.mean((wide - center) ** 2, axis=-1, keepdims=True)
    scaled = (wide - center) * lax.rsqrt(spread + 1e-06)
    return (scaled * (1.0 + mod_scale) + mod_shift).astype(jnp.bfloat16)


def rope_tables(positions):
    small_pairs = HD // 6
    time_pairs = (HD - 4 * small_pairs) // 2
    frame = (positions // (GRID_H * GRID_W)).astype(jnp.float32)
    row_pos = (positions // GRID_W % GRID_H).astype(jnp.float32)
    col_pos = (positions % GRID_W).astype(jnp.float32)
    time_freq = 10000.0 ** (-jnp.arange(time_pairs, dtype=jnp.float32) / time_pairs)
    space_freq = 10000.0 ** (-jnp.arange(small_pairs, dtype=jnp.float32) / small_pairs)
    freq = jnp.repeat(jnp.concatenate([time_freq, space_freq, space_freq]), 2)
    pair = jnp.arange(HD, dtype=jnp.int32) // 2
    where = jnp.where(
        pair < time_pairs,
        frame[:, None],
        jnp.where(pair < time_pairs + small_pairs, row_pos[:, None], col_pos[:, None]),
    )
    angles = where * freq
    sign = jnp.where(jnp.arange(HD) % 2 == 0, -1.0, 1.0).astype(jnp.float32)
    return jnp.cos(angles), jnp.sin(angles) * sign


def as_column(row):
    return jnp.broadcast_to(row, (BLK, BLK)).T


def as_row(column):
    return jnp.broadcast_to(column, (BLK, BLK)).T[0:1, :]


def norm_rope(raw, ssq_row, gain, cosine, sine):
    inv = lax.rsqrt(as_column(ssq_row) * (1.0 / (H * HD)) + 1e-06)
    wide = raw.astype(jnp.float32) * inv * gain
    lane = lax.broadcasted_iota(jnp.int32, wide.shape, 1)
    partner = jnp.where(
        lane % 2 == 0, pltpu.roll(wide, HD - 1, 1), pltpu.roll(wide, 1, 1)
    )
    return (wide * cosine + partner * sine).astype(jnp.bfloat16)


def split3(row):
    hi = row.astype(jnp.bfloat16).astype(jnp.float32)
    rest = row - hi
    mid = rest.astype(jnp.bfloat16).astype(jnp.float32)
    return [hi, mid, rest - mid]


PER_STEP = 2


def attention_kernel(
    q_ref, k_ref, v_ref, before_ref, after_ref, sq_ref, sk_ref, sb_ref, sa_ref,
    gq_ref, gk_ref, cos_ref, sin_ref, out_ref, kbuf, vbuf,
):
    step = pl.program_id(0)
    blocks = k_ref.shape[0] // BLK

    @pl.when(step == 0)
    def _():
        def put(head, dest, raw, values, ssq, table):
            rows = pl.ds(pl.multiple_of(table, BLK), BLK)
            to = pl.ds(pl.multiple_of(dest, BLK), BLK)
            kbuf[head, to, :] = norm_rope(
                raw, ssq, gk_ref[:, head * HD : (head + 1) * HD], cos_ref[rows, :], sin_ref[rows, :]
            )
            vbuf[head, to, :] = values

        for i in range(ROUNDS):
            r = pl.ds(i * BLK, BLK)
            put(0, i * BLK, before_ref[r, 0:HD], before_ref[r, HD:], sb_ref[pl.ds(i, 1), :], i * BLK)
            put(
                1, (blocks + i) * BLK, after_ref[r, 0:HD], after_ref[r, HD:], sa_ref[pl.ds(i, 1), :],
                (blocks + ROUNDS + i) * BLK,
            )

        def own(i, carry):
            r = pl.ds(pl.multiple_of(i * BLK, BLK), BLK)
            ssq = sk_ref[pl.ds(i, 1), :]
            table = (i + ROUNDS) * BLK
            put(0, (i + ROUNDS) * BLK, k_ref[r, 0:HD], v_ref[r, 0:HD], ssq, table)
            put(1, i * BLK, k_ref[r, HD:], v_ref[r, HD:], ssq, table)
            return carry

        lax.fori_loop(0, blocks, own, 0, unroll=2)

    for j in range(PER_STEP):
        b = step * PER_STEP + j
        table = pl.ds(pl.multiple_of((b + ROUNDS) * BLK, BLK), BLK)
        window = pl.ds(pl.multiple_of(b * BLK, BLK), (ROUNDS + 1) * BLK)
        stats = []
        for head in range(2):
            cols = slice(head * HD, (head + 1) * HD)
            q = norm_rope(
                q_ref[j * BLK : (j + 1) * BLK, cols], sq_ref[pl.ds(b, 1), :], gq_ref[:, cols],
                cos_ref[table, :], sin_ref[table, :],
            )
            raw = lax.dot_general(
                q, kbuf[head, window, :], (((1,), (1,)), ((), ())), preferred_element_type=jnp.float32
            )
            top = jnp.max(raw, axis=-1, keepdims=True)
            weights = jnp.exp2((raw - top) * (SCALE * LOG2E))
            total = jnp.sum(weights, axis=-1, keepdims=True)
            mixed = jnp.dot(
                weights.astype(jnp.bfloat16), vbuf[head, window, :], preferred_element_type=jnp.float32
            )
            out_ref[j, 0:BLK, cols] = (mixed / total).astype(jnp.bfloat16)
            stats.append(split3(as_row(top * SCALE)) + split3(as_row(total)))
        pad = jnp.zeros((EXTRA - 6, HD), jnp.float32)
        for head in range(2):
            cols = slice(head * HD, (head + 1) * HD)
            out_ref[j, BLK : BLK + EXTRA, cols] = jnp.concatenate(stats[head] + [pad], axis=0).astype(
                jnp.bfloat16
            )


def attention(q, k, v, before, after, sq, sk, sb, sa, gq, gk, cosine, sine):
    rows = q.shape[0]
    blocks = rows // BLK
    whole = lambda a: pl.BlockSpec(a.shape, lambda i, n=a.ndim: (0,) * n)
    return pl.pallas_call(
        attention_kernel,
        grid=(blocks // PER_STEP,),
        in_specs=[pl.BlockSpec((PER_STEP * BLK, 2 * HD), lambda i: (i, 0))]
        + [whole(a) for a in (k, v, before, after, sq, sk, sb, sa, gq, gk, cosine, sine)],
        out_specs=pl.BlockSpec((PER_STEP, BLK + EXTRA, 2 * HD), lambda i: (i, 0, 0)),
        out_shape=jax.ShapeDtypeStruct((blocks, BLK + EXTRA, 2 * HD), jnp.bfloat16),
        scratch_shapes=[
            pltpu.VMEM((2, rows + HALO, HD), jnp.bfloat16),
            pltpu.VMEM((2, rows + HALO, HD), jnp.bfloat16),
        ],
        compiler_params=pltpu.CompilerParams(
            dimension_semantics=("arbitrary",), vmem_limit_bytes=40 * 1024 * 1024
        ),
        cost_estimate=pl.CostEstimate(flops=2 * 10**9, bytes_accessed=10**7, transcendentals=3 * 10**6),
        name="window_attention",
    )(q, k, v, before, after, sq, sk, sb, sa, gq, gk, cosine, sine)


def square_sum(raw):
    wide = raw.astype(jnp.float32)
    return jnp.sum(wide * wide, axis=-1).reshape(-1, BLK)


def along_sx(block, distance):
    n = lax.axis_size("sx")
    return lax.ppermute(block, "sx", [((i - distance) % n, i) for i in range(n)])


def unpack(arrived):
    attended = arrived[:, :BLK].transpose(1, 0, 2).reshape(BLK, H * HD)
    stats = arrived[:, BLK : BLK + 6].astype(jnp.float32)
    best = (stats[:, 0] + stats[:, 1]) + stats[:, 2]
    total = (stats[:, 3] + stats[:, 4]) + stats[:, 5]
    return attended, best.reshape(H, BLK), total.reshape(H, BLK)


def body(tokens, mod_shift, mod_scale, w_query, w_key, w_value, query_gain, key_gain):
    group = lax.axis_index("sx")
    mine = lax.axis_index("sy")
    normed = layer_norm(tokens, mod_shift, mod_scale)
    piece = lax.all_gather(normed, "sy", axis=0, tiled=True)
    rows = piece.shape[0]
    count = rows * lax.axis_size("sx")
    positions = (group * rows - HALO + jnp.arange(rows + 2 * HALO, dtype=jnp.int32) + count) % count
    cosine, sine = rope_tables(positions)
    gq = lax.dynamic_slice(query_gain, (mine * 2 * HD,), (2 * HD,)).reshape(1, 2 * HD)
    gk = lax.dynamic_slice(key_gain, (mine * 2 * HD,), (2 * HD,)).reshape(1, 2 * HD)
    q, k, v = [
        jnp.dot(piece, weight, preferred_element_type=jnp.float32).astype(jnp.bfloat16)
        for weight in (w_query, w_key, w_value)
    ]
    partial = jnp.stack([square_sum(q), square_sum(k)])
    ssq = jnp.sum(lax.all_gather(partial, "sy", axis=0), axis=0)
    before = along_sx(jnp.concatenate([k[-HALO:, :HD], v[-HALO:, :HD]], axis=1), 1)
    after = along_sx(jnp.concatenate([k[:HALO, HD:], v[:HALO, HD:]], axis=1), -1)
    sb = along_sx(ssq[1, -ROUNDS:], 1)
    sa = along_sx(ssq[1, :ROUNDS], -1)
    out = attention(q, k, v, before, after, ssq[0], ssq[1], sb, sa, gq, gk, cosine, sine)
    arrived = lax.all_to_all(out, "sy", split_axis=0, concat_axis=0, tiled=True)
    return unpack(arrived)


def solution(mesh):
    placed = (
        P(("sx", "sy"), None),
        P(),
        P(),
        P(None, "sy"),
        P(None, "sy"),
        P(None, "sy"),
        P(),
        P(),
    )
    return jax.shard_map(
        body,
        mesh=mesh,
        in_specs=placed,
        out_specs=(P(("sx", "sy"), None), P(None, ("sx", "sy")), P(None, ("sx", "sy"))),
        check_vma=False,
    )
```

profile of v0, /device:TPU:1, one launch (start us, length us, event | category | flops | bytes accessed | tf_op | source)
XLA Modules:
  0.0 253.0 jit_solution(13476237412357082738)
XLA Ops:
  7.2 0.9 broadcast_add_fusion
  8.1 1.7 convert_reduce_fusion
  9.8 1.8 fusion.2
  11.6 1.7 fusion.5
  13.4 0.8 dynamic_slice.6
  14.2 0.8 dynamic_slice.7
  15.4 10.2 %sine_multiply_fusion = (f32[3072,128]{1,0:T(8,128)}, f32[3072,128]{1,0:T(8,128)}) fusion(f32[128]{0:T(128)S(1)} %compare_select_fusion, f32[128]{0:T(128)S(1)} %mul.57, f32[3072]{0:T(1024)S(1)} %fusion.11, f32[3072]{0:T(1024)S(1)} %get-tuple-element.26, f32[3072]{0:T(1024)S(1)} %get-tuple-element.25, pred[128]{0:T(512)(128)(4,1)S(1)} %get-tuple-element.27, ...), kind=kLoop, calls=%fused_computation.13 | loop fusion | flops 1572864 | bytes 3183872 | tf_op jit(solution)/shard_map/mul | solution.py:47
  25.6 103.0 %all-gather.3.cloned.1.call-done = bf16[2048,5120]{1,0:T(8,128)(2,1)} async-done(((bf16[128,5120]{1,0:T(8,128)(2,1)}), bf16[2048,5120]{1,0:T(8,128)(2,1)}) %all-gather.3.cloned.1.call-update) | async-done | bytes 20971536 | tf_op jit(solution)/shard_map/all_gather | solution.py:188
  128.6 12.5 %convolution_convert_fusion.v_ref = bf16[2048,256]{1,0:T(8,128)(2,1)S(1)} fusion(bf16[2048,5120]{1,0:T(8,128)(2,1)} %all-gather.3.cloned.1.call-done, bf16[5120,256]{1,0:T(8,128)(2,1)} %param.13), kind=kOutput, calls=%fused_computation.8 | convolution fusion | flops 5369233408 | bytes 24641536 | tf_op jit(solution)/shard_map/dot_general | solution.py:196
  141.2 1.4 copy-done.11
  142.6 6.5 %multiply_reduce_fusion = (f32[2048]{0:T(1024)S(1)}, bf16[2048,256]{1,0:T(8,128)(2,1)S(1)}) fusion(bf16[2048,5120]{1,0:T(8,128)(2,1)S(1)} %copy-done.11, bf16[5120,256]{1,0:T(8,128)(2,1)S(1)} %copy-done), kind=kOutput, calls=%fused_computation.11 | convolution fusion | flops 5370804224 | bytes 24649728 | tf_op jit(solution)/shard_map/dot_general | solution.py:196
  149.1 0.8 pad_maximum_fusion
  149.9 2.6 %collective-permute-start = (bf16[512,256]{1,0:T(8,128)(2,1)}, bf16[512,256]{1,0:T(8,128)(2,1)S(1)}, u32[]{:S(2)}, u32[]{:S(2)}) collective-permute-start(bf16[512,256]{1,0:T(8,128)(2,1)} %pad_maximum_fusion), channel_id=1, source_target_pairs={{112,0},{0,16},{16,32},{32,48},{48,64},{64,80},{80,96},{96,112},{1... | collective-permute-start | bytes 786440 | tf_op jit(solution)/shard_map/ppermute | solution.py:173
  152.5 0.7 pad_maximum_fusion.1
  153.2 2.5 collective-permute-start.1
  155.8 9.1 %multiply_reduce_fusion.1 = (f32[2048]{0:T(1024)S(1)}, bf16[2048,256]{1,0:T(8,128)(2,1)}) fusion(bf16[2048,5120]{1,0:T(8,128)(2,1)S(1)} %copy-done.11, bf16[5120,256]{1,0:T(8,128)(2,1)} %param.11), kind=kOutput, calls=%fused_computation.12 | convolution fusion | flops 5370804224 | bytes 24649728 | tf_op jit(solution)/shard_map/dot_general | solution.py:196
  164.9 20.0 %all-gather = f32[32,16,128]{2,1,0:T(8,128)S(1)} all-gather(f32[2,16,128]{2,1,0:T(8,128)S(1)} %pad_maximum_fusion.2), channel_id=2, replica_groups=mesh['sx'=8,'sy'=16] {'sy'}, dimensions={0}, use_global_device_ids=true | all-gather | bytes 278528 | tf_op jit(solution)/shard_map/all_gather | solution.py:200
  185.6 4.5 %collective-permute-start.3 = (f32[4,128]{1,0:T(4,128)S(1)}, f32[4,128]{1,0:T(4,128)S(1)}, u32[]{:S(2)}, u32[]{:S(2)}) collective-permute-start(f32[4,128]{1,0:T(4,128)S(1)} %get-tuple-element.17), channel_id=1, source_target_pairs={{16,0},{32,16},{48,32},{64,48},{80,64},{96,80},{112,96},{0,112},{1... | collective-permute-start | bytes 6152 | tf_op jit(solution)/shard_map/ppermute | solution.py:173
  190.1 1.0 collective-permute-done.2.sb_ref
  191.1 1.4 copy-done.1
  192.5 1.4 copy-done.2
  193.9 1.2 copy-done.4
  195.1 1.2 copy-done.6
  196.3 1.2 copy-done.7
  197.6 19.3 %window_attention.1 = bf16[16,144,256]{2,1,0:T(8,128)(2,1)S(1)} custom-call(bf16[2048,256]{1,0:T(8,128)(2,1)S(1)} %copy-done.7, bf16[2048,256]{1,0:T(8,128)(2,1)S(1)} %copy-done.6, bf16[2048,256]{1,0:T(8,128)(2,1)S(1)} %copy-done.4, bf16[512,256]{1,0:T(8,128)(2,1)S(1)} %collective-permute-done.before_ref, ...), custom_call_target="tpu_custom_call" | custom-call | flops 2000000000 | bytes 10000000 | tf_op jit(solution)/shard_map/window_attention/pallas_call | solution.py:147
  216.9 21.1 %all_to_all.5 = bf16[16,144,256]{2,1,0:T(8,128)(2,1)S(1)} all-to-all(bf16[16,144,256]{2,1,0:T(8,128)(2,1)S(1)} %window_attention.1), channel_id=1, replica_groups=mesh['sx'=8,'sy'=16] {'sy'}, dimensions={0} | all-to-all | bytes 2359296 | tf_op jit(solution)/shard_map/all_to_all | solution.py:206
  238.0 1.0 copy-done.9
  239.1 1.1 slice_bitcast_fusion
  240.1 2.3 copy.22
  242.4 2.3 copy.23
  244.7 0.8 slice_convert_fusion
  245.5 0.7 slice_add_fusion
  (40 shorter events, 1.3 us)
Async XLA Ops:
  7.2 134.0 %copy-start = (bf16[5120,256]{1,0:T(8,128)(2,1)S(1)}, bf16[5120,256]{1,0:T(8,128)(2,1)}, u32[]{:S(2)}) copy-start(bf16[5120,256]{1,0:T(8,128)(2,1)} %param.12) | copy-start | bytes 7864324
  7.2 4.4 %copy-start.10 = (f32[5120]{0:T(1024)S(1)}, f32[5120]{0:T(1024)}, u32[]{:S(2)}) copy-start(f32[5120]{0:T(1024)} %param.9) | copy-start | bytes 61444
  7.2 121.4 %all-gather.3.cloned.1.call-start = ((), (), s32[]{:S(2)}) async-start(), calls=%async_computation.1 | async-start | bytes 22282240 | tf_op jit(solution)/shard_map/all_gather | solution.py:188
  7.2 4.4 %copy-start.8 = (bf16[128,5120]{1,0:T(8,128)(2,1)S(1)}, bf16[128,5120]{1,0:T(8,128)(2,1)}, u32[]{:S(2)}) copy-start(bf16[128,5120]{1,0:T(8,128)(2,1)} %param.8) | copy-start | bytes 3932164
  128.6 14.0 %copy-start.11 = (bf16[2048,5120]{1,0:T(8,128)(2,1)S(1)}, bf16[2048,5120]{1,0:T(8,128)(2,1)}, u32[]{:S(2)}) copy-start(bf16[2048,5120]{1,0:T(8,128)(2,1)} %all-gather.3.cloned.1.call-done) | copy-start | bytes 62914564
  141.2 7.9 %copy-start.3 = (bf16[2048,256]{1,0:T(8,128)(2,1)}, bf16[2048,256]{1,0:T(8,128)(2,1)S(1)}, u32[]{:S(2)}) copy-start(bf16[2048,256]{1,0:T(8,128)(2,1)S(1)} %convolution_convert_fusion.v_ref) | copy-start | bytes 3145732
  149.1 15.8 %copy-start.5 = (bf16[2048,256]{1,0:T(8,128)(2,1)}, bf16[2048,256]{1,0:T(8,128)(2,1)S(1)}, u32[]{:S(2)}) copy-start(bf16[2048,256]{1,0:T(8,128)(2,1)S(1)} %get-tuple-element.22.k_ref) | copy-start | bytes 3145732
  149.9 41.1 %collective-permute-start = (bf16[512,256]{1,0:T(8,128)(2,1)}, bf16[512,256]{1,0:T(8,128)(2,1)S(1)}, u32[]{:S(2)}, u32[]{:S(2)}) collective-permute-start(bf16[512,256]{1,0:T(8,128)(2,1)} %pad_maximum_fusion), channel_id=1, source_target_pairs={{112,0},{0,16},{16,32},{32,48},{48,64},{64,80},{80,96},{96,112},{1... | collective-permute-start | bytes 786440 | tf_op jit(solution)/shard_map/ppermute | solution.py:173
  153.2 37.8 %collective-permute-start.1 = (bf16[512,256]{1,0:T(8,128)(2,1)}, bf16[512,256]{1,0:T(8,128)(2,1)S(1)}, u32[]{:S(2)}, u32[]{:S(2)}) collective-permute-start(bf16[512,256]{1,0:T(8,128)(2,1)} %pad_maximum_fusion.1), channel_id=1, source_target_pairs={{16,0},{32,16},{48,32},{64,48},{80,64},{96,80},{112,96},{0,112},{1... | collective-permute-start | bytes 786440 | tf_op jit(solution)/shard_map/ppermute | solution.py:173
  184.9 6.1 %collective-permute-start.2 = (f32[4,128]{1,0:T(4,128)S(1)}, f32[4,128]{1,0:T(4,128)S(1)}, u32[]{:S(2)}, u32[]{:S(2)}) collective-permute-start(f32[4,128]{1,0:T(4,128)S(1)} %get-tuple-element.18), channel_id=1, source_target_pairs={{112,0},{0,16},{16,32},{32,48},{48,64},{64,80},{80,96},{96,112},{1... | collective-permute-start | bytes 6152 | tf_op jit(solution)/shard_map/ppermute | solution.py:173
  185.6 5.5 %collective-permute-start.3 = (f32[4,128]{1,0:T(4,128)S(1)}, f32[4,128]{1,0:T(4,128)S(1)}, u32[]{:S(2)}, u32[]{:S(2)}) collective-permute-start(f32[4,128]{1,0:T(4,128)S(1)} %get-tuple-element.17), channel_id=1, source_target_pairs={{16,0},{32,16},{48,32},{64,48},{80,64},{96,80},{112,96},{0,112},{1... | collective-permute-start | bytes 6152 | tf_op jit(solution)/shard_map/ppermute | solution.py:173
  191.1 1.4 copy-start.1
  192.5 1.4 copy-start.2
  193.9 1.2 copy-start.4
  195.1 1.2 copy-start.6
  196.3 1.2 copy-start.7
  238.0 1.0 copy-start.9
Sparse Core Ops, SparseCore 0:
  13.5 115.0 all-gather.2
where the time goes:
time: 254 us; the launch traced here: 253 us
  waiting for transfers between devices  104 us (41%)
  blocking collectives  41.1 us (16%)
  matrix products  28.2 us (11%)
  other arithmetic  19.6 us (8%)
  Pallas kernels  19.3 us (8%)
  local copies, waits for them, and re-layouts  16.3 us (6%)
  between operations  14.2 us (6%)
  starting transfers between devices  10.3 us (4%)
    all_gather x1, waiting for transfers between devices, body(): piece = lax.all_gather(normed, 'sy', axis=0, tiled=True)  103 us
    dot_general x3, matrix products, body(): jnp.dot(piece, weight, preferred_element_type=jnp.float32)  28.2 us
    all_to_all x1, blocking collectives, body(): arrived = lax.all_to_all(out, 'sy', split_axis=0, concat_axis=0, tiled=True)  21.1 us
    all_gather x1, blocking collectives, body(): ssq = jnp.sum(lax.all_gather(partial, 'sy', axis=0), axis=0)  20 us
    pallas_call x1, Pallas kernels, attention(): pl.pallas_call(attention_kernel, grid=(blocks // PER_STEP,), in_specs=[pl...  19.3 us
    unnamed x25, local copies, waits for them, and re-layouts  11.2 us
    ppermute x4, starting transfers between devices, along_sx(): lax.ppermute(block, 'sx', [((i - distance) % n, i) for i in range(n)])  10.2 us
    mul x1, other arithmetic, rope_tables(): return (jnp.cos(angles), jnp.sin(angles) * sign)  10.2 us
  transfers between devices with their start and end apart: 5, of which 2 were waited for; matrix products, arithmetic and copies ran while one was open for 9% of the time, Pallas kernels for 0%

commit v1 on v0

v1 whole, which is shorter than its diff:
```python
import jax
import jax.numpy as jnp
import numpy as np
from jax import lax
from jax.experimental import pallas as pl
from jax.experimental.pallas import tpu as pltpu
from jax.sharding import PartitionSpec as P

H = 32
HD = 128
ROUNDS = 4
GRID_W = 80
GRID_H = 45
BLK = 128
HALO = ROUNDS * BLK
EXTRA = 16
NSY = 16
SCALE = np.float32(1.0) / np.sqrt(np.float32(HD))
LOG2E = np.float32(1.4426950408889634)


def layer_norm(values, mod_shift, mod_scale):
    wide = values.astype(jnp.float32)
    center = jnp.mean(wide, axis=-1, keepdims=True)
    spread = jnp.mean((wide - center) ** 2, axis=-1, keepdims=True)
    scaled = (wide - center) * lax.rsqrt(spread + 1e-06)
    return (scaled * (1.0 + mod_scale) + mod_shift).astype(jnp.bfloat16)


def rope_tables(positions):
    small_pairs = HD // 6
    time_pairs = (HD - 4 * small_pairs) // 2
    frame = (positions // (GRID_H * GRID_W)).astype(jnp.float32)
    row_pos = (positions // GRID_W % GRID_H).astype(jnp.float32)
    col_pos = (positions % GRID_W).astype(jnp.float32)
    time_freq = 10000.0 ** (-jnp.arange(time_pairs, dtype=jnp.float32) / time_pairs)
    space_freq = 10000.0 ** (-jnp.arange(small_pairs, dtype=jnp.float32) / small_pairs)
    freq = jnp.repeat(jnp.concatenate([time_freq, space_freq, space_freq]), 2)
    pair = jnp.arange(HD, dtype=jnp.int32) // 2
    where = jnp.where(
        pair < time_pairs,
        frame[:, None],
        jnp.where(pair < time_pairs + small_pairs, row_pos[:, None], col_pos[:, None]),
    )
    angles = where * freq
    sign = jnp.where(jnp.arange(HD) % 2 == 0, -1.0, 1.0).astype(jnp.float32)
    return jnp.cos(angles), jnp.sin(angles) * sign


def as_column(row):
    return jnp.broadcast_to(row, (BLK, BLK)).T


def as_row(column):
    return jnp.broadcast_to(column, (BLK, BLK)).T[0:1, :]


def norm_rope(raw, ssq_row, gain, cosine, sine):
    inv = lax.rsqrt(as_column(ssq_row) * (1.0 / (H * HD)) + 1e-06)
    wide = raw.astype(jnp.float32) * inv * gain
    lane = lax.broadcasted_iota(jnp.int32, wide.shape, 1)
    partner = jnp.where(
        lane % 2 == 0, pltpu.roll(wide, HD - 1, 1), pltpu.roll(wide, 1, 1)
    )
    return (wide * cosine + partner * sine).astype(jnp.bfloat16)


def split3(row):
    hi = row.astype(jnp.bfloat16).astype(jnp.float32)
    rest = row - hi
    mid = rest.astype(jnp.bfloat16).astype(jnp.float32)
    return [hi, mid, rest - mid]


PER_STEP = 2
SLOTS = ((0, 0), (0, -1), (0, 1), (1, 0), (0, 2), (1, -1), (1, 1), (1, 2))
CHUNKS = (4, 3, 1)


def chip_move(dz, dx, dc):
    return [
        (z * 8 + x * 2 + c, (z + dz) % 2 * 8 + (x + dx) % 4 * 2 + (c + dc) % 2)
        for z in range(2)
        for x in range(4)
        for c in range(2)
    ]


def from_left(block):
    return lax.ppermute(block, "sy", chip_move(0, 1, 0))


def from_right(block):
    return lax.ppermute(block, "sy", chip_move(0, -1, 0))


def from_z(block):
    return lax.ppermute(block, "sy", chip_move(1, 0, 0))


def from_core(block):
    return lax.ppermute(block, "sy", chip_move(0, 0, 1))


def project_kernel(*refs):
    n = len(refs) - 7
    pieces, (own_w, other_w, own_ref, other_ref, ssq_ref, x_ref, sems) = refs[:n], refs[n:]

    @pl.when(pl.program_id(0) == 0)
    def _():
        copies, at = [], 0
        for i, piece in enumerate(pieces):
            rows = piece.shape[0]
            copies.append(pltpu.make_async_copy(piece, x_ref.at[pl.ds(at, rows)], sems.at[i]))
            copies[-1].start()
            at += rows
        for copy in copies:
            copy.wait()

    total = None
    for weight, out in ((own_w, own_ref), (other_w, other_ref)):
        made = jnp.dot(x_ref[...], weight[0], preferred_element_type=jnp.float32).astype(jnp.bfloat16)
        out[0] = made
        wide = made.astype(jnp.float32)
        part = jnp.sum(wide * wide, axis=-1, keepdims=True)
        total = part if total is None else total + part
    for i in range(x_ref.shape[0] // BLK):
        ssq_ref[0, i : i + 1, :] = as_row(total[i * BLK : (i + 1) * BLK])


def project(pieces, own_w, other_w):
    rows = sum(p.shape[0] for p in pieces)
    depth, wide = own_w.shape[1:]
    w_spec = pl.BlockSpec((1, depth, wide), lambda i: (i, 0, 0))
    o_spec = pl.BlockSpec((1, rows, wide), lambda i: (i, 0, 0))
    out = jax.ShapeDtypeStruct((3, rows, wide), jnp.bfloat16)
    return pl.pallas_call(
        project_kernel,
        grid=(3,),
        in_specs=[pl.BlockSpec(memory_space=pl.ANY)] * len(pieces) + [w_spec, w_spec],
        out_specs=[o_spec, o_spec, pl.BlockSpec((1, rows // BLK, BLK), lambda i: (i, 0, 0))],
        out_shape=[out, out, jax.ShapeDtypeStruct((3, rows // BLK, BLK), jnp.float32)],
        scratch_shapes=[pltpu.VMEM((rows, depth), jnp.bfloat16), pltpu.SemaphoreType.DMA((len(pieces),))],
        compiler_params=pltpu.CompilerParams(
            dimension_semantics=("arbitrary",), vmem_limit_bytes=48 * 1024 * 1024
        ),
        cost_estimate=pl.CostEstimate(
            flops=12 * rows * depth * wide, bytes_accessed=12 * depth * wide, transcendentals=0
        ),
        name="project",
    )(*pieces, own_w, other_w)


def sources(refs):
    at = 0
    for chunk, slots in enumerate(CHUNKS):
        for i in range(slots):
            for core in range(2):
                yield (at + i) * 2 + core, refs[chunk * 2 + core], pl.ds(i * BLK, BLK)
        at += slots


def halo_kernel(
    place_ref, fa, ga, fb, gb, fc, gc, ssq_ref, gk_ref, cos_lo, sin_lo, cos_hi, sin_hi,
    before_ref, after_ref, raw, sems,
):
    blocks = 2 * sum(CHUNKS)
    ends = ((lambda n: n >= blocks - ROUNDS, blocks - ROUNDS, 0), (lambda n: n < ROUNDS, 0, 1))

    def each(act):
        for at, ref, rows in sources((fa, ga, fb, gb, fc, gc)):
            n = place_ref[at]
            for inside, first, head in ends:

                @pl.when(inside(n))
                def _(n=n, first=first, head=head, ref=ref, rows=rows, at=at):
                    to = pl.ds(pl.multiple_of((n - first) * BLK, BLK), BLK)
                    cols = pl.ds(head * HD, HD)
                    out = (before_ref, after_ref)[head]
                    act(pltpu.make_async_copy(ref.at[0, rows, cols], raw.at[head, to], sems.at[at, 0]))
                    act(pltpu.make_async_copy(ref.at[2, rows, cols], out.at[to, pl.ds(HD, HD)], sems.at[at, 1]))

    each(lambda copy: copy.start())
    each(lambda copy: copy.wait())
    for head, out, first, cosine, sine in (
        (0, before_ref, blocks - ROUNDS, cos_hi, sin_hi),
        (1, after_ref, 0, cos_lo, sin_lo),
    ):
        for i in range(ROUNDS):
            rows = pl.ds(i * BLK, BLK)
            out[rows, 0:HD] = norm_rope(
                raw[head, rows, :], ssq_ref[pl.ds(first + i, 1), :], gk_ref[:, head * HD : (head + 1) * HD],
                cosine[rows, :], sine[rows, :],
            )


VMEM = pl.BlockSpec(memory_space=pltpu.VMEM)
SMEM = pl.BlockSpec(memory_space=pltpu.SMEM)
ANYWHERE = pl.BlockSpec(memory_space=pl.ANY)


def halo(place, features, ssq_k, gk, cosine, sine):
    rows = cosine.shape[0]
    low = pl.BlockSpec((HALO, HD), lambda i: (0, 0))
    high = pl.BlockSpec((HALO, HD), lambda i: (rows // HALO - 1, 0))
    one = lambda a: pl.BlockSpec(a.shape, lambda i: (0, 0))
    out = jax.ShapeDtypeStruct((HALO, 2 * HD), jnp.bfloat16)
    return pl.pallas_call(
        halo_kernel,
        grid=(1,),
        in_specs=[SMEM] + [ANYWHERE] * 6 + [one(ssq_k), one(gk), low, low, high, high],
        out_specs=[pl.BlockSpec((HALO, 2 * HD), lambda i: (0, 0))] * 2,
        out_shape=[out, out],
        scratch_shapes=[
            pltpu.VMEM((2, HALO, HD), jnp.bfloat16),
            pltpu.SemaphoreType.DMA((2 * sum(CHUNKS), 2)),
        ],
        compiler_params=pltpu.CompilerParams(vmem_limit_bytes=48 * 1024 * 1024),
        cost_estimate=pl.CostEstimate(flops=10**7, bytes_accessed=3 * 10**6, transcendentals=0),
        name="halo_keys",
    )(place, *features, ssq_k, gk, cosine, sine, cosine, sine)


def attention_kernel(
    place_ref, fa, ga, fb, gb, fc, gc, before_ref, after_ref, sk_ref, sq_ref,
    gk_ref, gq_ref, cos_ref, sin_ref, out_ref, raw, kbuf, vbuf, sems,
):
    step = pl.program_id(0)
    blocks = 2 * sum(CHUNKS)
    own_first = (ROUNDS, 0)
    halo_first = (0, blocks)
    columns = [slice(head * HD, (head + 1) * HD) for head in range(2)]

    @pl.when(step == 0)
    def _():
        copies = []
        for at, ref, rows in sources((fa, ga, fb, gb, fc, gc)):
            n = place_ref[at]
            to = pl.ds(pl.multiple_of(n * BLK, BLK), BLK)
            for i in range(2):
                copies.append(pltpu.make_async_copy(ref.at[i, rows], raw.at[i, to], sems.at[at, i]))
            for head in range(2):
                to = pl.ds(pl.multiple_of((n + own_first[head]) * BLK, BLK), BLK)
                copies.append(
                    pltpu.make_async_copy(
                        ref.at[2, rows, pl.ds(head * HD, HD)], vbuf.at[head, to], sems.at[at, 2 + head]
                    )
                )
        for copy in copies:
            copy.start()
        for head, ref in enumerate((before_ref, after_ref)):
            to = pl.ds(halo_first[head] * BLK, HALO)
            kbuf[head, to, :] = ref[:, 0:HD]
            vbuf[head, to, :] = ref[:, HD:]
        for copy in copies:
            copy.wait()

        def own(i, carry):
            rows = pl.ds(pl.multiple_of(i * BLK, BLK), BLK)
            for head in range(2):
                to = pl.ds(pl.multiple_of((i + own_first[head]) * BLK, BLK), BLK)
                kbuf[head, to, :] = norm_rope(
                    raw[0, rows, columns[head]], sk_ref[pl.ds(i, 1), :], gk_ref[:, columns[head]],
                    cos_ref[rows, :], sin_ref[rows, :],
                )
            return carry

        lax.fori_loop(0, blocks, own, 0, unroll=2)

    for j in range(PER_STEP):
        b = step * PER_STEP + j
        rows = pl.ds(pl.multiple_of(b * BLK, BLK), BLK)
        window = pl.ds(pl.multiple_of(b * BLK, BLK), (ROUNDS + 1) * BLK)
        stats = []
        for head in range(2):
            q = norm_rope(
                raw[1, rows, columns[head]], sq_ref[pl.ds(b, 1), :], gq_ref[:, columns[head]],
                cos_ref[rows, :], sin_ref[rows, :],
            )
            scores = lax.dot_general(
                q, kbuf[head, window, :], (((1,), (1,)), ((), ())), preferred_element_type=jnp.float32
            )
            top = jnp.max(scores, axis=-1, keepdims=True)
            weights = jnp.exp2((scores - top) * (SCALE * LOG2E))
            total = jnp.sum(weights, axis=-1, keepdims=True)
            mixed = jnp.dot(
                weights.astype(jnp.bfloat16), vbuf[head, window, :], preferred_element_type=jnp.float32
            )
            out_ref[j, 0:BLK, columns[head]] = (mixed / total).astype(jnp.bfloat16)
            stats.append(split3(as_row(top * SCALE)) + split3(as_row(total)))
        pad = jnp.zeros((EXTRA - 6, HD), jnp.float32)
        for head in range(2):
            out_ref[j, BLK : BLK + EXTRA, columns[head]] = jnp.concatenate(
                stats[head] + [pad], axis=0
            ).astype(jnp.bfloat16)


def attention(place, features, before, after, sk, sq, gk, gq, cosine, sine):
    rows = cosine.shape[0]
    blocks = rows // BLK
    whole = lambda a: pl.BlockSpec(a.shape, lambda i, n=a.ndim: (0,) * n)
    return pl.pallas_call(
        attention_kernel,
        grid=(blocks // PER_STEP,),
        in_specs=[SMEM] + [ANYWHERE] * 6 + [whole(a) for a in (before, after, sk, sq, gk, gq, cosine, sine)],
        out_specs=pl.BlockSpec((PER_STEP, BLK + EXTRA, 2 * HD), lambda i: (i, 0, 0)),
        out_shape=jax.ShapeDtypeStruct((blocks, BLK + EXTRA, 2 * HD), jnp.bfloat16),
        scratch_shapes=[
            pltpu.VMEM((2, rows, 2 * HD), jnp.bfloat16),
            pltpu.VMEM((2, rows + HALO, HD), jnp.bfloat16),
            pltpu.VMEM((2, rows + HALO, HD), jnp.bfloat16),
            pltpu.SemaphoreType.DMA((blocks, 4)),
        ],
        compiler_params=pltpu.CompilerParams(
            dimension_semantics=("arbitrary",), vmem_limit_bytes=48 * 1024 * 1024
        ),
        cost_estimate=pl.CostEstimate(flops=2 * 10**9, bytes_accessed=10**7, transcendentals=3 * 10**6),
        name="window_attention",
    )(place, *features, before, after, sk, sq, gk, gq, cosine, sine)


def along_sx(block, distance):
    n = lax.axis_size("sx")
    return lax.ppermute(block, "sx", [((i - distance) % n, i) for i in range(n)])


def unpack(arrived):
    attended = arrived[:, :BLK].transpose(1, 0, 2).reshape(BLK, H * HD)
    stats = arrived[:, BLK : BLK + 6].astype(jnp.float32)
    best = (stats[:, 0] + stats[:, 1]) + stats[:, 2]
    total = (stats[:, 3] + stats[:, 4]) + stats[:, 5]
    return attended, best.reshape(H, BLK), total.reshape(H, BLK)


def body(tokens, mod_shift, mod_scale, w_query, w_key, w_value, query_gain, key_gain):
    group = lax.axis_index("sx")
    mine = lax.axis_index("sy")
    z, x, core = mine // 8, mine // 2 % 4, mine % 2
    chips = jnp.stack([(z + dz) % 2 * 4 + (x + dx) % 4 for dz, dx in SLOTS])
    place = jnp.stack([chips * 2 + core, chips * 2 + 1 - core], axis=1).reshape(-1).astype(jnp.int32)
    half = BLK // 2

    own = layer_norm(tokens, mod_shift, mod_scale)
    left, right, far_z = from_left(own), from_right(own), from_z(own)
    own_w = jnp.stack([w_key, w_query, w_value])
    other_w = from_core(own_w)
    left_lo, right_hi = left[:half], right[half:]
    far_lo, far_hi = from_left(left_lo), from_right(right_hi)
    z_left_lo, z_right_hi = from_z(left_lo), from_z(right_hi)
    z_left_hi, z_right_lo = from_left(far_z[half:]), from_right(far_z[:half])
    z_far_lo, z_far_hi = from_left(z_left_lo), from_right(z_right_hi)

    rows = BLK * lax.axis_size("sy")
    cosine, sine = rope_tables(group * rows + jnp.arange(rows, dtype=jnp.int32))
    gq = lax.dynamic_slice(query_gain, (mine * 2 * HD,), (2 * HD,)).reshape(1, 2 * HD)
    gk = lax.dynamic_slice(key_gain, (mine * 2 * HD,), (2 * HD,)).reshape(1, 2 * HD)

    features, parts = [], []
    for pieces in (
        (own, left, right, far_z),
        (far_lo, far_hi, z_left_lo, z_left_hi, z_right_lo, z_right_hi),
        (z_far_lo, z_far_hi),
    ):
        made, given, part = project(pieces, own_w, other_w)
        features += [made, from_core(given)]
        parts.append(part[:2])
    part = jnp.concatenate(parts, axis=1)
    here = chips[:, None] == jnp.arange(8)[None, :]
    part = jnp.sum(jnp.where(here[None, :, :, None], part[:, :, None, :], 0.0), axis=1)
    sent = jnp.broadcast_to(part.reshape(1, 16, BLK), (NSY, 16, BLK))
    seen = lax.all_to_all(sent, "sy", split_axis=0, concat_axis=0, tiled=True)
    ssq = jnp.sum(seen.reshape(8, 2, 2, 8, BLK), axis=0).transpose(1, 2, 0, 3).reshape(2, 16, BLK)
    before, after = halo(place, features, ssq[0], gk, cosine, sine)
    before, after = along_sx(before, 1), along_sx(after, -1)
    out = attention(place, features, before, after, ssq[0], ssq[1], gk, gq, cosine, sine)
    arrived = lax.all_to_all(out, "sy", split_axis=0, concat_axis=0, tiled=True)
    return unpack(arrived)


def solution(mesh):
    placed = (
        P(("sx", "sy"), None),
        P(),
        P(),
        P(None, "sy"),
        P(None, "sy"),
        P(None, "sy"),
        P(),
        P(),
    )
    return jax.shard_map(
        body,
        mesh=mesh,
        in_specs=placed,
        out_specs=(P(("sx", "sy"), None), P(None, ("sx", "sy")), P(None, ("sx", "sy"))),
        check_vma=False,
    )
```

time: 254 us -> 197 us (0.78)
  waiting for transfers between devices: 104 us -> 54.1 us
  Pallas kernels: 19.3 us -> 59.6 us
  matrix products: 28.2 us -> 0 us
  blocking collectives: 41.1 us -> 21.4 us
  starting transfers between devices: 10.3 us -> 28.7 us
  between operations: 14.2 us -> 1.05 us
  local copies, waits for them, and re-layouts: 16.3 us -> 11.6 us
    all_gather x1 -> x0, waiting for transfers between devices: 103 us -> none  [body(): piece = lax.all_gather(normed, 'sy', axis=0, tiled=True)]
    pallas_call x1 -> x5, Pallas kernels: 19.3 us -> 59.6 us  [the longest x3 34.2 us: project(): pl.pallas_call(project_kernel, grid=(3,), in_specs=[pl.BlockSpec(memory_s...]
    ppermute x0 -> x15, waiting for transfers between devices: none -> 37.5 us  [the longest x4 27 us: from_left(): return lax.ppermute(block, 'sy', chip_move(0, 1, 0))]
    dot_general x3 -> x0, matrix products: 28.2 us -> none  [body(): jnp.dot(piece, weight, preferred_element_type=jnp.float32)]
    all_gather x1 -> x0, blocking collectives: 20 us -> none  [body(): ssq = jnp.sum(lax.all_gather(partial, 'sy', axis=0), axis=0)]
    ppermute x0 -> x15, starting transfers between devices: none -> 18.3 us  [the longest x4 8.38 us: from_right(): return lax.ppermute(block, 'sy', chip_move(0, -1, 0))]
    ppermute x4 -> x2, waiting for transfers between devices: 0.97 us -> 11.5 us  [along_sx(): lax.ppermute(block, 'sx', [((i - distance) % n, i) for i in range(n)])]
    another operation x1 -> x2, other arithmetic: 0.01 us -> 6.89 us  [the longest x1 6.88 us: body(): own_w = jnp.stack([w_key, w_query, w_value])]
  transfers between devices with their start and end apart: 5 -> 18, of which waited for: 2 -> 6; matrix products, arithmetic and copies ran while one was open for 9% -> 9% of each run, Pallas kernels for 0% -> 17%
where the time goes in v1:
time: 197 us; the launch traced here: 196 us
  Pallas kernels  59.6 us (30%)
  waiting for transfers between devices  54.1 us (27%)
  starting transfers between devices  28.7 us (15%)
  blocking collectives  21.4 us (11%)
  other arithmetic  19.4 us (10%)
  local copies, waits for them, and re-layouts  11.6 us (6%)
    pallas_call x3, Pallas kernels, project(): pl.pallas_call(project_kernel, grid=(3,), in_specs=[pl.BlockSpec(memory_s...  34.2 us
    ppermute x4, waiting for transfers between devices, from_left(): return lax.ppermute(block, 'sy', chip_move(0, 1, 0))  27 us
    pallas_call x1, Pallas kernels, attention(): pl.pallas_call(attention_kernel, grid=(blocks // PER_STEP,), in_specs=[SM...  23.1 us
    all_to_all x1, blocking collectives, body(): arrived = lax.all_to_all(out, 'sy', split_axis=0, concat_axis=0, tiled=True)  21.4 us
    ppermute x2, waiting for transfers between devices, along_sx(): lax.ppermute(block, 'sx', [((i - distance) % n, i) for i in range(n)])  11.5 us
    ppermute x3, waiting for transfers between devices, from_z(): return lax.ppermute(block, 'sy', chip_move(1, 0, 0))  10.5 us
    mul x1, other arithmetic, rope_tables(): return (jnp.cos(angles), jnp.sin(angles) * sign)  9.19 us
    ppermute x4, starting transfers between devices, from_right(): return lax.ppermute(block, 'sy', chip_move(0, -1, 0))  8.38 us
  transfers between devices with their start and end apart: 18, of which 6 were waited for; matrix products, arithmetic and copies ran while one was open for 9% of the time, Pallas kernels for 17%

profile of v1, /device:TPU:1, one launch (start us, length us, event | category | flops | bytes accessed | tf_op | source)
XLA Modules:
  0.0 195.9 jit_solution(9394887165219433230)
XLA Ops:
  0.6 6.9 %pad_maximum_fusion.refs_4_.refs_6_.refs_2_ = bf16[3,5120,256]{2,1,0:T(8,128)(2,1)} fusion(bf16[1,5120,256]{2,1,0:T(8,128)(2,1)} %bitcast.38, bf16[1,5120,256]{2,1,0:T(8,128)(2,1)} %bitcast.39, bf16[1,5120,256]{2,1,0:T(8,128)(2,1)} %bitcast.40), kind=kLoop, calls=%fused_computation | loop fusion | flops 7864320 | bytes 15728640 | tf_op jit(solution)/shard_map/stack | solution.py:345
  7.5 1.4 collective-permute-start.3
  10.4 1.4 collective-permute-start
  11.7 1.4 collective-permute-start.1
  13.1 1.7 collective-permute-start.2
  15.6 9.2 %sine_multiply_fusion = (f32[2048,128]{1,0:T(8,128)S(1)}, f32[2048,128]{1,0:T(8,128)S(1)}) fusion(f32[128]{0:T(128)S(1)} %compare_select_fusion, f32[128]{0:T(128)S(1)} %mul.79, f32[2048]{0:T(1024)S(1)} %fusion.10, f32[2048]{0:T(1024)S(1)} %get-tuple-element.45, f32[2048]{0:T(1024)S(1)} %get-tuple-element.44, pred[128]{0:T(512)(128)(4,1)S(1)} %get-tuple-element.46, ...), kind=kLoop, calls=%fused_computation.10 | loop fusion | flops 1048576 | bytes 2123008 | tf_op jit(solution)/shard_map/mul | solution.py:47
  24.8 17.3 %collective-permute-done.refs_1_ = bf16[128,5120]{1,0:T(8,128)(2,1)} collective-permute-done((bf16[128,5120]{1,0:T(8,128)(2,1)S(1)}, bf16[128,5120]{1,0:T(8,128)(2,1)}, u32[]{:S(2)}, u32[]{:S(2)}) %collective-permute-start) | collective-permute-done | bytes 1310752 | tf_op jit(solution)/shard_map/ppermute | solution.py:90
  42.1 1.1 slice.71
  43.4 1.7 collective-permute-start.7
  45.2 1.1 slice.72
  46.3 2.7 %collective-permute-start.6 = (bf16[64,5120]{1,0:T(8,128)(2,1)S(1)}, bf16[64,5120]{1,0:T(8,128)(2,1)S(1)}, u32[]{:S(2)}, u32[]{:S(2)}) collective-permute-start(bf16[64,5120]{1,0:T(8,128)(2,1)S(1)} %slice.72), channel_id=1, source_target_pairs={{0,6},{1,7},{2,0},{3,1},{4,2},{5,3},{6,4},{7,5},{8,14},{9,15},{10,... | collective-permute-start | bytes 1966088 | tf_op jit(solution)/shard_map/ppermute | solution.py:94
  48.9 1.4 fusion.16
  50.3 9.7 %collective-permute-done.5.refs_0_ = bf16[64,5120]{1,0:T(8,128)(2,1)S(1)} collective-permute-done((bf16[64,5120]{1,0:T(8,128)(2,1)S(1)}, bf16[64,5120]{1,0:T(8,128)(2,1)S(1)}, u32[]{:S(2)}, u32[]{:S(2)}) %collective-permute-start.5) | collective-permute-done | bytes 655392 | tf_op jit(solution)/shard_map/ppermute | solution.py:90
  60.0 2.7 %collective-permute-start.9 = (bf16[64,5120]{1,0:T(8,128)(2,1)S(1)}, bf16[64,5120]{1,0:T(8,128)(2,1)S(1)}, u32[]{:S(2)}, u32[]{:S(2)}) collective-permute-start(bf16[64,5120]{1,0:T(8,128)(2,1)S(1)} %get-tuple-element.34), channel_id=1, source_target_pairs={{0,6},{1,7},{2,0},{3,1},{4,2},{5,3},{6,4},{7,5},{8,14},{9,15},{10,... | collective-permute-start | bytes 1966088 | tf_op jit(solution)/shard_map/ppermute | solution.py:94
  62.7 10.5 %collective-permute-done.10.refs_5_ = bf16[64,5120]{1,0:T(8,128)(2,1)S(1)} collective-permute-done((bf16[64,5120]{1,0:T(8,128)(2,1)S(1)}, bf16[64,5120]{1,0:T(8,128)(2,1)S(1)}, u32[]{:S(2)}, u32[]{:S(2)}) %collective-permute-start.10) | collective-permute-done | bytes 655392 | tf_op jit(solution)/shard_map/ppermute | solution.py:98
  73.2 1.0 collective-permute-start.12
  74.2 1.7 collective-permute-start.13
  75.9 15.1 %project.3 = (bf16[3,512,256]{2,1,0:T(8,128)(2,1)S(1)}, bf16[3,512,256]{2,1,0:T(8,128)(2,1)}, f32[3,4,128]{2,1,0:T(4,128)S(1)}) custom-call(bf16[128,5120]{1,0:T(8,128)(2,1)S(1)} %fusion.5.refs_0_, bf16[128,5120]{1,0:T(8,128)(2,1)} %collective-permute-done.refs_1_, bf16[128,5120]{1,0:T(8,128)(2,1)} %collective-permute-done.1.refs_2_, ...), custom_call_target="tpu_custom_call" | custom-call | flops 8053063680 | bytes 15728640 | tf_op jit(solution)/shard_map/project/pallas_call | solution.py:137
  91.8 2.3 %collective-permute-start.4 = (bf16[3,512,256]{2,1,0:T(8,128)(2,1)}, bf16[3,512,256]{2,1,0:T(8,128)(2,1)}, u32[]{:S(2)}, u32[]{:S(2)}) collective-permute-start(bf16[3,512,256]{2,1,0:T(8,128)(2,1)} %get-tuple-element.15), channel_id=1, source_target_pairs={{0,1},{1,0},{2,3},{3,2},{4,5},{5,4},{6,7},{7,6},{8,9},{9,8},{10,11... | collective-permute-start | bytes 2359304 | tf_op jit(solution)/shard_map/ppermute | solution.py:102
  94.1 11.6 %project.4 = (bf16[3,384,256]{2,1,0:T(8,128)(2,1)S(1)}, bf16[3,384,256]{2,1,0:T(8,128)(2,1)}, f32[3,3,128]{2,1,0:T(4,128)S(1)}) custom-call(bf16[64,5120]{1,0:T(8,128)(2,1)S(1)} %collective-permute-done.5.refs_0_, bf16[64,5120]{1,0:T(8,128)(2,1)S(1)} %collective-permute-done.6.refs_1_, bf16[64,5120]{1,0:T(8,128)(2,1)S(1)} %collective-permute-done.7.refs_2_, ...), custom_call_target="tpu_custom_call" | custom-call | flops 6039797760 | bytes 15728640 | tf_op jit(solution)/shard_map/project/pallas_call | solution.py:137
  105.8 7.5 %project.5 = (bf16[3,128,256]{2,1,0:T(8,128)(2,1)S(1)}, bf16[3,128,256]{2,1,0:T(8,128)(2,1)S(1)}, f32[3,1,128]{2,1,0:T(1,128)S(1)}) custom-call(bf16[64,5120]{1,0:T(8,128)(2,1)S(1)} %collective-permute-done.12.refs_0_, bf16[64,5120]{1,0:T(8,128)(2,1)S(1)} %collective-permute-done.13.refs_1_, bf16[3,5120,256]{2,1,0:T(8,128)(2,1)} %pad_maximum_fusion.refs_4_.refs_6_.refs_2_, ...), custom_call_target="tpu_custom_call" | custom-call | flops 2013265920 | bytes 15728640 | tf_op jit(solution)/shard_map/project/pallas_call | solution.py:137
  115.5 4.5 %all-to-all-start = ((f32[16,16,128]{2,1,0:T(8,128)}), f32[16,16,128]{2,1,0:T(8,128)}, u32[]{:S(2)}, u32[]{:S(2)}) async-start(f32[16,16,128]{2,1,0:T(8,128)} %broadcast_in_dim.86), calls=%async_computation | async-start | bytes 262144 | tf_op jit(solution)/shard_map/all_to_all | solution.py:371
  121.1 5.1 %all-to-all-done = f32[16,16,128]{2,1,0:T(8,128)} async-done(((f32[16,16,128]{2,1,0:T(8,128)}), f32[16,16,128]{2,1,0:T(8,128)}, u32[]{:S(2)}, u32[]{:S(2)}) %all-to-all-start) | async-done | bytes 131104 | tf_op jit(solution)/shard_map/all_to_all | solution.py:371
  126.2 0.9 reduce_sum.39
  128.1 2.3 %halo_keys.1 = (bf16[512,256]{1,0:T(8,128)(2,1)S(1)}, bf16[512,256]{1,0:T(8,128)(2,1)S(1)}) custom-call(s32[16]{0:T(128)S(1)} %reshape.311.place_ref, bf16[3,512,256]{2,1,0:T(8,128)(2,1)S(1)} %copy-done.1, bf16[3,512,256]{2,1,0:T(8,128)(2,1)} %collective-permute-done.4.ga, bf16[3,384,256]{2,1,0:T(8,128)(2,1)S(1)} %get-tuple-element.16.fb, ...), custom_call_target="tpu_custom_call" | custom-call | flops 10000000 | bytes 3000000 | tf_op jit(solution)/shard_map/halo_keys/pallas_call | solution.py:208
  130.4 3.4 %collective-permute-start.15 = (bf16[512,256]{1,0:T(8,128)(2,1)S(1)}, bf16[512,256]{1,0:T(8,128)(2,1)S(1)}, u32[]{:S(2)}, u32[]{:S(2)}) collective-permute-start(bf16[512,256]{1,0:T(8,128)(2,1)S(1)} %get-tuple-element.23), channel_id=1, source_target_pairs={{112,0},{0,16},{16,32},{32,48},{48,64},{64,80},{80,96},{96,112},{1... | collective-permute-start | bytes 786440 | tf_op jit(solution)/shard_map/ppermute | solution.py:324
  133.8 2.5 %collective-permute-start.16 = (bf16[512,256]{1,0:T(8,128)(2,1)S(1)}, bf16[512,256]{1,0:T(8,128)(2,1)S(1)}, u32[]{:S(2)}, u32[]{:S(2)}) collective-permute-start(bf16[512,256]{1,0:T(8,128)(2,1)S(1)} %get-tuple-element.24), channel_id=1, source_target_pairs={{16,0},{32,16},{48,32},{64,48},{80,64},{96,80},{112,96},{0,112},{1... | collective-permute-start | bytes 786440 | tf_op jit(solution)/shard_map/ppermute | solution.py:324
  137.1 7.5 %collective-permute-done.15.before_ref = bf16[512,256]{1,0:T(8,128)(2,1)S(1)} collective-permute-done((bf16[512,256]{1,0:T(8,128)(2,1)S(1)}, bf16[512,256]{1,0:T(8,128)(2,1)S(1)}, u32[]{:S(2)}, u32[]{:S(2)}) %collective-permute-start.15) | collective-permute-done | bytes 262176 | tf_op jit(solution)/shard_map/ppermute | solution.py:324
  144.6 4.0 %collective-permute-done.16.after_ref = bf16[512,256]{1,0:T(8,128)(2,1)S(1)} collective-permute-done((bf16[512,256]{1,0:T(8,128)(2,1)S(1)}, bf16[512,256]{1,0:T(8,128)(2,1)S(1)}, u32[]{:S(2)}, u32[]{:S(2)}) %collective-permute-start.16) | collective-permute-done | bytes 262176 | tf_op jit(solution)/shard_map/ppermute | solution.py:324
  148.7 23.1 %window_attention.1 = bf16[16,144,256]{2,1,0:T(8,128)(2,1)} custom-call(s32[16]{0:T(128)S(1)} %reshape.311.place_ref, bf16[3,512,256]{2,1,0:T(8,128)(2,1)S(1)} %copy-done.1, bf16[3,512,256]{2,1,0:T(8,128)(2,1)} %collective-permute-done.4.ga, bf16[3,384,256]{2,1,0:T(8,128)(2,1)S(1)} %get-tuple-element.16.fb, bf16[3,384,256]{2,1,0:T(8,128)(2,1)} %collective-permute-done.11.gb, ...), custom_call_target="tpu_custom_call" | custom-call | flops 2000000000 | bytes 10000000 | tf_op jit(solution)/shard_map/window_attention/pallas_call | solution.py:302
  171.8 21.4 %all_to_all.10 = bf16[16,144,256]{2,1,0:T(8,128)(2,1)S(1)} all-to-all(bf16[16,144,256]{2,1,0:T(8,128)(2,1)} %window_attention.1), channel_id=1, replica_groups=mesh['sx'=8,'sy'=16] {'sy'}, dimensions={0} | all-to-all | bytes 2359296 | tf_op jit(solution)/shard_map/all_to_all | solution.py:376
  193.9 1.3 copy.20
  (70 shorter events, 9.5 us)
Async XLA Ops:
  0.6 8.3 %copy-start.5 = (bf16[128,5120]{1,0:T(8,128)(2,1)S(1)}, bf16[128,5120]{1,0:T(8,128)(2,1)}, u32[]{:S(2)}) copy-start(bf16[128,5120]{1,0:T(8,128)(2,1)} %param.8) | copy-start | bytes 3932164
  7.5 2.2 %copy-start.7 = (f32[5120]{0:T(1024)S(1)}, f32[5120]{0:T(1024)}, u32[]{:S(2)}) copy-start(f32[5120]{0:T(1024)} %param.10) | copy-start | bytes 61444
  7.5 2.2 %copy-start.6 = (f32[5120]{0:T(1024)S(1)}, f32[5120]{0:T(1024)}, u32[]{:S(2)}) copy-start(f32[5120]{0:T(1024)} %param.9) | copy-start | bytes 61444
  7.5 66.7 %collective-permute-start.3 = (bf16[3,5120,256]{2,1,0:T(8,128)(2,1)}, bf16[3,5120,256]{2,1,0:T(8,128)(2,1)}, u32[]{:S(2)}, u32[]{:S(2)}) collective-permute-start(bf16[3,5120,256]{2,1,0:T(8,128)(2,1)} %pad_maximum_fusion.refs_4_.refs_6_.refs_2_), channel_id=1, source_target_pairs={{0,1},{1,0},{2,3},{3,2},{4,5},{5,4},{6,7},{7,6},{8,9},{9,8},{10,11... | collective-permute-start | bytes 23592968 | tf_op jit(solution)/shard_map/ppermute | solution.py:102
  10.4 31.8 %collective-permute-start = (bf16[128,5120]{1,0:T(8,128)(2,1)S(1)}, bf16[128,5120]{1,0:T(8,128)(2,1)}, u32[]{:S(2)}, u32[]{:S(2)}) collective-permute-start(bf16[128,5120]{1,0:T(8,128)(2,1)S(1)} %fusion.5.refs_0_), channel_id=1, source_target_pairs={{0,2},{1,3},{2,4},{3,5},{4,6},{5,7},{6,0},{7,1},{8,10},{9,11},{10,... | collective-permute-start | bytes 3932168 | tf_op jit(solution)/shard_map/ppermute | solution.py:90
  11.7 33.4 %collective-permute-start.1 = (bf16[128,5120]{1,0:T(8,128)(2,1)S(1)}, bf16[128,5120]{1,0:T(8,128)(2,1)}, u32[]{:S(2)}, u32[]{:S(2)}) collective-permute-start(bf16[128,5120]{1,0:T(8,128)(2,1)S(1)} %fusion.5.refs_0_), channel_id=1, source_target_pairs={{0,6},{1,7},{2,0},{3,1},{4,2},{5,3},{6,4},{7,5},{8,14},{9,15},{10,... | collective-permute-start | bytes 3932168 | tf_op jit(solution)/shard_map/ppermute | solution.py:94
  13.1 35.8 %collective-permute-start.2 = (bf16[128,5120]{1,0:T(8,128)(2,1)S(1)}, bf16[128,5120]{1,0:T(8,128)(2,1)}, u32[]{:S(2)}, u32[]{:S(2)}) collective-permute-start(bf16[128,5120]{1,0:T(8,128)(2,1)S(1)} %fusion.5.refs_0_), channel_id=1, source_target_pairs={{0,8},{1,9},{2,10},{3,11},{4,12},{5,13},{6,14},{7,15},{8,0},{9,1},... | collective-permute-start | bytes 3932168 | tf_op jit(solution)/shard_map/ppermute | solution.py:98
  43.3 16.7 %collective-permute-start.5 = (bf16[64,5120]{1,0:T(8,128)(2,1)S(1)}, bf16[64,5120]{1,0:T(8,128)(2,1)S(1)}, u32[]{:S(2)}, u32[]{:S(2)}) collective-permute-start(bf16[64,5120]{1,0:T(8,128)(2,1)S(1)} %slice.71), channel_id=1, source_target_pairs={{0,2},{1,3},{2,4},{3,5},{4,6},{5,7},{6,0},{7,1},{8,10},{9,11},{10,... | collective-permute-start | bytes 1966088 | tf_op jit(solution)/shard_map/ppermute | solution.py:90
  43.4 16.6 %collective-permute-start.7 = (bf16[64,5120]{1,0:T(8,128)(2,1)S(1)}, bf16[64,5120]{1,0:T(8,128)(2,1)S(1)}, u32[]{:S(2)}, u32[]{:S(2)}) collective-permute-start(bf16[64,5120]{1,0:T(8,128)(2,1)S(1)} %slice.71), channel_id=1, source_target_pairs={{0,8},{1,9},{2,10},{3,11},{4,12},{5,13},{6,14},{7,15},{8,0},{9,1},... | collective-permute-start | bytes 1966088 | tf_op jit(solution)/shard_map/ppermute | solution.py:98
  46.3 45.6 %collective-permute-start.6 = (bf16[64,5120]{1,0:T(8,128)(2,1)S(1)}, bf16[64,5120]{1,0:T(8,128)(2,1)S(1)}, u32[]{:S(2)}, u32[]{:S(2)}) collective-permute-start(bf16[64,5120]{1,0:T(8,128)(2,1)S(1)} %slice.72), channel_id=1, source_target_pairs={{0,6},{1,7},{2,0},{3,1},{4,2},{5,3},{6,4},{7,5},{8,14},{9,15},{10,... | collective-permute-start | bytes 1966088 | tf_op jit(solution)/shard_map/ppermute | solution.py:94
  48.9 24.2 %collective-permute-start.10 = (bf16[64,5120]{1,0:T(8,128)(2,1)S(1)}, bf16[64,5120]{1,0:T(8,128)(2,1)S(1)}, u32[]{:S(2)}, u32[]{:S(2)}) collective-permute-start(bf16[64,5120]{1,0:T(8,128)(2,1)S(1)} %slice.72), channel_id=1, source_target_pairs={{0,8},{1,9},{2,10},{3,11},{4,12},{5,13},{6,14},{7,15},{8,0},{9,1},... | collective-permute-start | bytes 1966088 | tf_op jit(solution)/shard_map/ppermute | solution.py:98
  60.0 34.1 %collective-permute-start.8 = (bf16[64,5120]{1,0:T(8,128)(2,1)S(1)}, bf16[64,5120]{1,0:T(8,128)(2,1)S(1)}, u32[]{:S(2)}, u32[]{:S(2)}) collective-permute-start(bf16[64,5120]{1,0:T(8,128)(2,1)S(1)} %get-tuple-element.35), channel_id=1, source_target_pairs={{0,2},{1,3},{2,4},{3,5},{4,6},{5,7},{6,0},{7,1},{8,10},{9,11},{10,... | collective-permute-start | bytes 1966088 | tf_op jit(solution)/shard_map/ppermute | solution.py:90
  60.0 34.1 %collective-permute-start.9 = (bf16[64,5120]{1,0:T(8,128)(2,1)S(1)}, bf16[64,5120]{1,0:T(8,128)(2,1)S(1)}, u32[]{:S(2)}, u32[]{:S(2)}) collective-permute-start(bf16[64,5120]{1,0:T(8,128)(2,1)S(1)} %get-tuple-element.34), channel_id=1, source_target_pairs={{0,6},{1,7},{2,0},{3,1},{4,2},{5,3},{6,4},{7,5},{8,14},{9,15},{10,... | collective-permute-start | bytes 1966088 | tf_op jit(solution)/shard_map/ppermute | solution.py:94
  73.2 32.6 %collective-permute-start.12 = (bf16[64,5120]{1,0:T(8,128)(2,1)S(1)}, bf16[64,5120]{1,0:T(8,128)(2,1)S(1)}, u32[]{:S(2)}, u32[]{:S(2)}) collective-permute-start(bf16[64,5120]{1,0:T(8,128)(2,1)S(1)} %collective-permute-done.7.refs_2_), channel_id=1, source_target_pairs={{0,2},{1,3},{2,4},{3,5},{4,6},{5,7},{6,0},{7,1},{8,10},{9,11},{10,... | collective-permute-start | bytes 1966088 | tf_op jit(solution)/shard_map/ppermute | solution.py:90
  74.2 31.6 %collective-permute-start.13 = (bf16[64,5120]{1,0:T(8,128)(2,1)S(1)}, bf16[64,5120]{1,0:T(8,128)(2,1)S(1)}, u32[]{:S(2)}, u32[]{:S(2)}) collective-permute-start(bf16[64,5120]{1,0:T(8,128)(2,1)S(1)} %collective-permute-done.10.refs_5_), channel_id=1, source_target_pairs={{0,6},{1,7},{2,0},{3,1},{4,2},{5,3},{6,4},{7,5},{8,14},{9,15},{10,... | collective-permute-start | bytes 1966088 | tf_op jit(solution)/shard_map/ppermute | solution.py:94
  91.0 0.9 copy-start
  91.8 35.3 %collective-permute-start.4 = (bf16[3,512,256]{2,1,0:T(8,128)(2,1)}, bf16[3,512,256]{2,1,0:T(8,128)(2,1)}, u32[]{:S(2)}, u32[]{:S(2)}) collective-permute-start(bf16[3,512,256]{2,1,0:T(8,128)(2,1)} %get-tuple-element.15), channel_id=1, source_target_pairs={{0,1},{1,0},{2,3},{3,2},{4,5},{5,4},{6,7},{7,6},{8,9},{9,8},{10,11... | collective-permute-start | bytes 2359304 | tf_op jit(solution)/shard_map/ppermute | solution.py:102
  105.7 21.5 %copy-start.1 = (bf16[3,512,256]{2,1,0:T(8,128)(2,1)S(1)}, bf16[3,512,256]{2,1,0:T(8,128)(2,1)}, u32[]{:S(2)}) copy-start(bf16[3,512,256]{2,1,0:T(8,128)(2,1)} %copy-done) | copy-start | bytes 2359300
  105.7 21.4 %collective-permute-start.11 = (bf16[3,384,256]{2,1,0:T(8,128)(2,1)}, bf16[3,384,256]{2,1,0:T(8,128)(2,1)}, u32[]{:S(2)}, u32[]{:S(2)}) collective-permute-start(bf16[3,384,256]{2,1,0:T(8,128)(2,1)} %get-tuple-element.17), channel_id=1, source_target_pairs={{0,1},{1,0},{2,3},{3,2},{4,5},{5,4},{6,7},{7,6},{8,9},{9,8},{10,11... | collective-permute-start | bytes 1769480 | tf_op jit(solution)/shard_map/ppermute | solution.py:102
  113.4 0.7 copy-start.2
  114.0 0.7 copy-start.4
  115.5 10.7 %all-to-all-start = ((f32[16,16,128]{2,1,0:T(8,128)}), f32[16,16,128]{2,1,0:T(8,128)}, u32[]{:S(2)}, u32[]{:S(2)}) async-start(f32[16,16,128]{2,1,0:T(8,128)} %broadcast_in_dim.86), calls=%async_computation | async-start | bytes 262144 | tf_op jit(solution)/shard_map/all_to_all | solution.py:371
  120.9 6.2 %collective-permute-start.14 = (bf16[3,128,256]{2,1,0:T(8,128)(2,1)}, bf16[3,128,256]{2,1,0:T(8,128)(2,1)}, u32[]{:S(2)}, u32[]{:S(2)}) collective-permute-start(bf16[3,128,256]{2,1,0:T(8,128)(2,1)} %copy-done.4), channel_id=1, source_target_pairs={{0,1},{1,0},{2,3},{3,2},{4,5},{5,4},{6,7},{7,6},{8,9},{9,8},{10,11... | collective-permute-start | bytes 589832 | tf_op jit(solution)/shard_map/ppermute | solution.py:102
  127.2 0.9 copy-start.3
  130.4 14.2 %collective-permute-start.15 = (bf16[512,256]{1,0:T(8,128)(2,1)S(1)}, bf16[512,256]{1,0:T(8,128)(2,1)S(1)}, u32[]{:S(2)}, u32[]{:S(2)}) collective-permute-start(bf16[512,256]{1,0:T(8,128)(2,1)S(1)} %get-tuple-element.23), channel_id=1, source_target_pairs={{112,0},{0,16},{16,32},{32,48},{48,64},{64,80},{80,96},{96,112},{1... | collective-permute-start | bytes 786440 | tf_op jit(solution)/shard_map/ppermute | solution.py:324
  133.8 14.8 %collective-permute-start.16 = (bf16[512,256]{1,0:T(8,128)(2,1)S(1)}, bf16[512,256]{1,0:T(8,128)(2,1)S(1)}, u32[]{:S(2)}, u32[]{:S(2)}) collective-permute-start(bf16[512,256]{1,0:T(8,128)(2,1)S(1)} %get-tuple-element.24), channel_id=1, source_target_pairs={{16,0},{32,16},{48,32},{64,48},{80,64},{96,80},{112,96},{0,112},{1... | collective-permute-start | bytes 786440 | tf_op jit(solution)/shard_map/ppermute | solution.py:324

commit v2 on v1

--- a/solution.py
+++ b/solution.py
@@ -1,3 +1,5 @@
+import functools
+
 import jax
 import jax.numpy as jnp
 import numpy as np
@@ -72,7 +74,7 @@
     return [hi, mid, rest - mid]
 
 
-PER_STEP = 2
+PER_STEP = 4
 SLOTS = ((0, 0), (0, -1), (0, 1), (1, 0), (0, 2), (1, -1), (1, 1), (1, 2))
 CHUNKS = (4, 3, 1)
 
@@ -142,7 +144,7 @@
         out_shape=[out, out, jax.ShapeDtypeStruct((3, rows // BLK, BLK), jnp.float32)],
         scratch_shapes=[pltpu.VMEM((rows, depth), jnp.bfloat16), pltpu.SemaphoreType.DMA((len(pieces),))],
         compiler_params=pltpu.CompilerParams(
-            dimension_semantics=("arbitrary",), vmem_limit_bytes=48 * 1024 * 1024
+            dimension_semantics=("arbitrary",), vmem_limit_bytes=30 * 1024 * 1024
         ),
         cost_estimate=pl.CostEstimate(
             flops=12 * rows * depth * wide, bytes_accessed=12 * depth * wide, transcendentals=0
@@ -222,101 +224,117 @@
 
 
 def attention_kernel(
-    place_ref, fa, ga, fb, gb, fc, gc, before_ref, after_ref, sk_ref, sq_ref,
-    gk_ref, gq_ref, cos_ref, sin_ref, out_ref, raw, kbuf, vbuf, sems,
+    part, place_ref, fa, ga, fb, gb, fc, gc, before_ref, after_ref, sk_ref, sq_ref,
+    gk_ref, gq_ref, cos_ref, sin_ref, *rest,
 ):
-    step = pl.program_id(0)
+    out_ref, raw, kbuf, vbuf, sems = rest[-5:]
+    step, head = pl.program_id(0), pl.program_id(1)
     blocks = 2 * sum(CHUNKS)
+    columns = [slice(head * HD, (head + 1) * HD) for head in range(2)]
     own_first = (ROUNDS, 0)
-    halo_first = (0, blocks)
-    columns = [slice(head * HD, (head + 1) * HD) for head in range(2)]
-
-    @pl.when(step == 0)
+
+    def wanted(n, head):
+        if part == 0:
+            return None
+        return n < ROUNDS if head == 0 else n >= blocks - ROUNDS
+
+    def guarded(condition, act):
+        if condition is None:
+            act()
+        else:
+            pl.when(condition)(act)
+
+    @pl.when((step == 0) & (head == 0))
     def _():
         copies = []
         for at, ref, rows in sources((fa, ga, fb, gb, fc, gc)):
             n = place_ref[at]
             to = pl.ds(pl.multiple_of(n * BLK, BLK), BLK)
-            for i in range(2):
-                copies.append(pltpu.make_async_copy(ref.at[i, rows], raw.at[i, to], sems.at[at, i]))
-            for head in range(2):
+            needed = None if part == 0 else (n < ROUNDS) | (n >= blocks - ROUNDS)
+            copies.append((n, needed, pltpu.make_async_copy(ref.at[:, rows], raw.at[:, to], sems.at[at])))
+        for _, needed, copy in copies:
+            guarded(needed, copy.start)
+        if part == 1:
+            for head, ref in enumerate((before_ref, after_ref)):
+                to = pl.ds((0, blocks)[head] * BLK, HALO)
+                kbuf[head, to, :] = ref[:, 0:HD]
+                vbuf[head, :, to] = ref[:, HD:].T
+        for n, needed, copy in copies:
+            guarded(needed, copy.wait)
+
+        def prepare(n, head):
+            def act():
+                rows = pl.ds(pl.multiple_of(n * BLK, BLK), BLK)
                 to = pl.ds(pl.multiple_of((n + own_first[head]) * BLK, BLK), BLK)
-                copies.append(
-                    pltpu.make_async_copy(
-                        ref.at[2, rows, pl.ds(head * HD, HD)], vbuf.at[head, to], sems.at[at, 2 + head]
-                    )
-                )
-        for copy in copies:
-            copy.start()
-        for head, ref in enumerate((before_ref, after_ref)):
-            to = pl.ds(halo_first[head] * BLK, HALO)
-            kbuf[head, to, :] = ref[:, 0:HD]
-            vbuf[head, to, :] = ref[:, HD:]
-        for copy in copies:
-            copy.wait()
-
-        def own(i, carry):
-            rows = pl.ds(pl.multiple_of(i * BLK, BLK), BLK)
-            for head in range(2):
-                to = pl.ds(pl.multiple_of((i + own_first[head]) * BLK, BLK), BLK)
                 kbuf[head, to, :] = norm_rope(
-                    raw[0, rows, columns[head]], sk_ref[pl.ds(i, 1), :], gk_ref[:, columns[head]],
+                    raw[0, rows, columns[head]], sk_ref[pl.ds(n, 1), :], gk_ref[:, columns[head]],
                     cos_ref[rows, :], sin_ref[rows, :],
                 )
-            return carry
-
-        lax.fori_loop(0, blocks, own, 0, unroll=2)
-
-    for j in range(PER_STEP):
-        b = step * PER_STEP + j
-        rows = pl.ds(pl.multiple_of(b * BLK, BLK), BLK)
-        window = pl.ds(pl.multiple_of(b * BLK, BLK), (ROUNDS + 1) * BLK)
-        stats = []
-        for head in range(2):
+                vbuf[head, :, to] = raw[2, rows, columns[head]].T
+
+            return act
+
+        for n in range(blocks):
+            for head in range(2):
+                if wanted(n, head) is not False:
+                    prepare(n, head)()
+
+    def attend(first, head):
+        for j in range(PER_STEP):
+            b = first + j
+            rows = pl.ds(pl.multiple_of(b * BLK, BLK), BLK)
+            window = pl.ds(pl.multiple_of(b * BLK, BLK), (ROUNDS + 1) * BLK)
             q = norm_rope(
                 raw[1, rows, columns[head]], sq_ref[pl.ds(b, 1), :], gq_ref[:, columns[head]],
                 cos_ref[rows, :], sin_ref[rows, :],
             )
             scores = lax.dot_general(
-                q, kbuf[head, window, :], (((1,), (1,)), ((), ())), preferred_element_type=jnp.float32
+                kbuf[head, window, :], q, (((1,), (1,)), ((), ())), preferred_element_type=jnp.float32
             )
-            top = jnp.max(scores, axis=-1, keepdims=True)
-            weights = jnp.exp2((scores - top) * (SCALE * LOG2E))
-            total = jnp.sum(weights, axis=-1, keepdims=True)
+            top = jnp.max(scores, axis=0, keepdims=True)
+            weight = jnp.exp2((scores - top) * (SCALE * LOG2E))
+            total = jnp.sum(weight, axis=0, keepdims=True)
             mixed = jnp.dot(
-                weights.astype(jnp.bfloat16), vbuf[head, window, :], preferred_element_type=jnp.float32
+                vbuf[head, :, window], weight.astype(jnp.bfloat16), preferred_element_type=jnp.float32
             )
-            out_ref[j, 0:BLK, columns[head]] = (mixed / total).astype(jnp.bfloat16)
-            stats.append(split3(as_row(top * SCALE)) + split3(as_row(total)))
-        pad = jnp.zeros((EXTRA - 6, HD), jnp.float32)
-        for head in range(2):
-            out_ref[j, BLK : BLK + EXTRA, columns[head]] = jnp.concatenate(
-                stats[head] + [pad], axis=0
-            ).astype(jnp.bfloat16)
-
-
-def attention(place, features, before, after, sk, sq, gk, gq, cosine, sine):
+            out_ref[j, 0, 0:BLK, :] = (mixed / total).T.astype(jnp.bfloat16)
+            stats = split3(top * SCALE) + split3(total) + [jnp.zeros((EXTRA - 6, HD), jnp.float32)]
+            out_ref[j, 0, BLK : BLK + EXTRA, :] = jnp.concatenate(stats, axis=0).astype(jnp.bfloat16)
+
+    for which in range(2):
+        first = (step + 1 - which) * PER_STEP if part == 0 else (0, blocks - ROUNDS)[which]
+        pl.when(head == which)(functools.partial(attend, first, which))
+
+
+def attention(part, place, features, before, after, sk, sq, gk, gq, cosine, sine, held=None):
     rows = cosine.shape[0]
     blocks = rows // BLK
-    whole = lambda a: pl.BlockSpec(a.shape, lambda i, n=a.ndim: (0,) * n)
+    whole = lambda a: pl.BlockSpec(a.shape, lambda i, h, n=a.ndim: (0,) * n)
+    steps = blocks // PER_STEP - 1 if part == 0 else 1
+    which = (lambda i, h: (i + 1 - h, h, 0, 0)) if part == 0 else (lambda i, h: (h * (blocks // PER_STEP - 1), h, 0, 0))
+    small = (before, after, sk, sq, gk, gq, cosine, sine)
+    more = () if held is None else (held,)
     return pl.pallas_call(
-        attention_kernel,
-        grid=(blocks // PER_STEP,),
-        in_specs=[SMEM] + [ANYWHERE] * 6 + [whole(a) for a in (before, after, sk, sq, gk, gq, cosine, sine)],
-        out_specs=pl.BlockSpec((PER_STEP, BLK + EXTRA, 2 * HD), lambda i: (i, 0, 0)),
-        out_shape=jax.ShapeDtypeStruct((blocks, BLK + EXTRA, 2 * HD), jnp.bfloat16),
+        functools.partial(attention_kernel, part),
+        grid=(steps, 2),
+        in_specs=[SMEM] + [ANYWHERE] * 6 + [whole(a) for a in small] + [ANYWHERE] * len(more),
+        out_specs=pl.BlockSpec((PER_STEP, 1, BLK + EXTRA, HD), which),
+        out_shape=jax.ShapeDtypeStruct((blocks, 2, BLK + EXTRA, HD), jnp.bfloat16),
         scratch_shapes=[
-            pltpu.VMEM((2, rows, 2 * HD), jnp.bfloat16),
+            pltpu.VMEM((3, rows, 2 * HD), jnp.bfloat16),
             pltpu.VMEM((2, rows + HALO, HD), jnp.bfloat16),
-            pltpu.VMEM((2, rows + HALO, HD), jnp.bfloat16),
-            pltpu.SemaphoreType.DMA((blocks, 4)),
+            pltpu.VMEM((2, HD, rows + HALO), jnp.bfloat16),
+            pltpu.SemaphoreType.DMA((blocks,)),
         ],
+        input_output_aliases={15: 0} if more else {},
         compiler_params=pltpu.CompilerParams(
-            dimension_semantics=("arbitrary",), vmem_limit_bytes=48 * 1024 * 1024
+            dimension_semantics=("arbitrary", "arbitrary"), vmem_limit_bytes=56 * 1024 * 1024
         ),
-        cost_estimate=pl.CostEstimate(flops=2 * 10**9, bytes_accessed=10**7, transcendentals=3 * 10**6),
-        name="window_attention",
-    )(place, *features, before, after, sk, sq, gk, gq, cosine, sine)
+        cost_estimate=pl.CostEstimate(
+            flops=(1 + 2 * (1 - part)) * 5 * 10**8, bytes_accessed=10**7, transcendentals=10**6
+        ),
+        name=("window_attention", "window_attention_halo")[part],
+    )(place, *features, *small, *more)
 
 
 def along_sx(block, distance):
@@ -325,10 +343,10 @@
 
 
 def unpack(arrived):
-    attended = arrived[:, :BLK].transpose(1, 0, 2).reshape(BLK, H * HD)
-    stats = arrived[:, BLK : BLK + 6].astype(jnp.float32)
-    best = (stats[:, 0] + stats[:, 1]) + stats[:, 2]
-    total = (stats[:, 3] + stats[:, 4]) + stats[:, 5]
+    attended = arrived[:, :, :BLK].transpose(2, 0, 1, 3).reshape(BLK, H * HD)
+    stats = arrived[:, :, BLK : BLK + 6].astype(jnp.float32)
+    best = (stats[:, :, 0] + stats[:, :, 1]) + stats[:, :, 2]
+    total = (stats[:, :, 3] + stats[:, :, 4]) + stats[:, :, 5]
     return attended, best.reshape(H, BLK), total.reshape(H, BLK)
 
 
@@ -339,29 +357,34 @@
     chips = jnp.stack([(z + dz) % 2 * 4 + (x + dx) % 4 for dz, dx in SLOTS])
     place = jnp.stack([chips * 2 + core, chips * 2 + 1 - core], axis=1).reshape(-1).astype(jnp.int32)
     half = BLK // 2
-
-    own = layer_norm(tokens, mod_shift, mod_scale)
-    left, right, far_z = from_left(own), from_right(own), from_z(own)
-    own_w = jnp.stack([w_key, w_query, w_value])
-    other_w = from_core(own_w)
-    left_lo, right_hi = left[:half], right[half:]
-    far_lo, far_hi = from_left(left_lo), from_right(right_hi)
-    z_left_lo, z_right_hi = from_z(left_lo), from_z(right_hi)
-    z_left_hi, z_right_lo = from_left(far_z[half:]), from_right(far_z[:half])
-    z_far_lo, z_far_hi = from_left(z_left_lo), from_right(z_right_hi)
-
     rows = BLK * lax.axis_size("sy")
+
+    own_lo = layer_norm(tokens[:half], mod_shift, mod_scale)
+    own_hi = layer_norm(tokens[half:], mod_shift, mod_scale)
+    left_lo, right_hi, z_lo = from_left(own_lo), from_right(own_hi), from_z(own_lo)
+    left_hi, right_lo, z_hi = from_left(own_hi), from_right(own_lo), from_z(own_hi)
+    weights = lax.optimization_barrier((w_key, w_query, w_value, own_lo, own_hi))[:3]
+    swapped = [from_core(w) for w in weights]
+    weights, swapped, left_lo = lax.optimization_barrier((weights, swapped, left_lo))
+    own_w, other_w = jnp.stack(weights), jnp.stack(swapped)
+    far_lo, z_left_lo = from_left(left_lo), from_z(left_lo)
+    far_hi, z_right_hi = from_right(right_hi), from_z(right_hi)
+    z_left_hi, z_right_lo = from_left(z_hi), from_right(z_lo)
+
     cosine, sine = rope_tables(group * rows + jnp.arange(rows, dtype=jnp.int32))
     gq = lax.dynamic_slice(query_gain, (mine * 2 * HD,), (2 * HD,)).reshape(1, 2 * HD)
     gk = lax.dynamic_slice(key_gain, (mine * 2 * HD,), (2 * HD,)).reshape(1, 2 * HD)
+    own_lo, cosine, sine, gq, gk, place = lax.optimization_barrier((own_lo, cosine, sine, gq, gk, place))
+
+    near = project((own_lo, own_hi, left_lo, left_hi, right_lo, right_hi, z_lo, z_hi), own_w, other_w)
+    near, z_left_lo, z_right_hi = lax.optimization_barrier((near, z_left_lo, z_right_hi))
+    z_far_lo, z_far_hi = from_left(z_left_lo), from_right(z_right_hi)
+    middle = project((far_lo, far_hi, z_left_lo, z_left_hi, z_right_lo, z_right_hi), own_w, other_w)
+    z_far_lo, z_far_hi, middle = lax.optimization_barrier((z_far_lo, z_far_hi, middle))
+    last = project((z_far_lo, z_far_hi), own_w, other_w)
 
     features, parts = [], []
-    for pieces in (
-        (own, left, right, far_z),
-        (far_lo, far_hi, z_left_lo, z_left_hi, z_right_lo, z_right_hi),
-        (z_far_lo, z_far_hi),
-    ):
-        made, given, part = project(pieces, own_w, other_w)
+    for made, given, part in (near, middle, last):
         features += [made, from_core(given)]
         parts.append(part[:2])
     part = jnp.concatenate(parts, axis=1)
@@ -371,8 +394,10 @@
     seen = lax.all_to_all(sent, "sy", split_axis=0, concat_axis=0, tiled=True)
     ssq = jnp.sum(seen.reshape(8, 2, 2, 8, BLK), axis=0).transpose(1, 2, 0, 3).reshape(2, 16, BLK)
     before, after = halo(place, features, ssq[0], gk, cosine, sine)
+    common = (ssq[0], ssq[1], gk, gq, cosine, sine)
+    out = attention(0, place, features, before, after, *common)
     before, after = along_sx(before, 1), along_sx(after, -1)
-    out = attention(place, features, before, after, ssq[0], ssq[1], gk, gq, cosine, sine)
+    out = attention(1, place, features, before, after, *common, held=out)
     arrived = lax.all_to_all(out, "sy", split_axis=0, concat_axis=0, tiled=True)
     return unpack(arrived)
 

time: 197 us -> 176 us (0.89)
  waiting for transfers between devices: 54.1 us -> 38.3 us
  Pallas kernels: 59.6 us -> 48.7 us
  starting transfers between devices: 28.7 us -> 33.9 us
  other arithmetic: 19.4 us -> 22.3 us
    ppermute x4 -> x5, waiting for transfers between devices: 27 us -> 5.35 us  [from_left(): return lax.ppermute(block, 'sy', chip_move(0, 1, 0))]
    ppermute x3 -> x4, waiting for transfers between devices: 10.5 us -> 26.9 us  [from_z(): return lax.ppermute(block, 'sy', chip_move(1, 0, 0))]
    ppermute x2, waiting for transfers between devices: 11.5 us -> 0.01 us  [along_sx(): lax.ppermute(block, 'sx', [((i - distance) % n, i) for i in range(n)])]
    pallas_call x3, Pallas kernels: 34.2 us -> 24.3 us  [project(): pl.pallas_call(project_kernel, grid=(3,), in_specs=[pl.BlockSpec(memory_s...]
    slice x5 -> x2, local copies, waits for them, and re-layouts: 3.64 us -> 0.61 us  [body(): common = (ssq[0], ssq[1], gk, gq, cosine, sine)]
    ppermute x4 -> x6, starting transfers between devices: 3.95 us -> 6.48 us  [from_core(): return lax.ppermute(block, 'sy', chip_move(0, 0, 1))]
    another operation x1 -> x2, other arithmetic: 6.88 us -> 8.33 us  [body(): own_w, other_w = (jnp.stack(weights), jnp.stack(swapped))]
    ppermute x4 -> x5, starting transfers between devices: 8.38 us -> 9.76 us  [from_right(): return lax.ppermute(block, 'sy', chip_move(0, -1, 0))]
  transfers between devices with their start and end apart: 18 -> 23, of which waited for: 6 -> 7; matrix products, arithmetic and copies ran while one was open for 9% -> 13% of each run, Pallas kernels for 17% -> 22%
where the time goes in v2:
time: 176 us
  Pallas kernels  48.7 us (28%)
  waiting for transfers between devices  38.3 us (22%)
  starting transfers between devices  33.9 us (19%)
  other arithmetic  22.3 us (13%)
  blocking collectives  21.6 us (12%)
  local copies, waits for them, and re-layouts  9.81 us (6%)
    ppermute x4, waiting for transfers between devices, from_z(): return lax.ppermute(block, 'sy', chip_move(1, 0, 0))  26.9 us
    pallas_call x3, Pallas kernels, project(): pl.pallas_call(project_kernel, grid=(3,), in_specs=[pl.BlockSpec(memory_s...  24.3 us
    pallas_call x2, Pallas kernels, attention(): pl.pallas_call(functools.partial(attention_kernel, part), grid=(steps, 2)...  22.1 us
    all_to_all x1, blocking collectives, body(): arrived = lax.all_to_all(out, 'sy', split_axis=0, concat_axis=0, tiled=True)  21.6 us
    ppermute x5, starting transfers between devices, from_right(): return lax.ppermute(block, 'sy', chip_move(0, -1, 0))  9.76 us
    mul x1, other arithmetic, rope_tables(): return (jnp.cos(angles), jnp.sin(angles) * sign)  9.21 us
    another operation x2, other arithmetic, body(): own_w, other_w = (jnp.stack(weights), jnp.stack(swapped))  8.33 us
    ppermute x6, starting transfers between devices, from_core(): return lax.ppermute(block, 'sy', chip_move(0, 0, 1))  6.48 us
  transfers between devices with their start and end apart: 23, of which 7 were waited for; matrix products, arithmetic and copies ran while one was open for 13% of the time, Pallas kernels for 22%

profile of v2, /device:TPU:1, one launch (start us, length us, event | category | flops | bytes accessed | tf_op | source)
XLA Modules:
  0.0 175.7 jit_solution(13415504178584122674)
XLA Ops:
  0.7 1.7 convert_reduce_fusion
  3.5 1.5 collective-permute-start
  6.8 1.4 collective-permute-start.6
  8.7 1.4 dynamic_slice.6
  11.0 9.2 %sine_multiply_fusion = (f32[2048,128]{1,0:T(8,128)S(1)}, f32[2048,128]{1,0:T(8,128)S(1)}) fusion(f32[128]{0:T(128)S(1)} %compare_select_fusion, f32[128]{0:T(128)S(1)} %mul.89, f32[2048]{0:T(1024)S(1)} %fusion.16, f32[2048]{0:T(1024)S(1)} %get-tuple-element.103, f32[2048]{0:T(1024)S(1)} %get-tuple-element.102, pred[128]{0:T(512)(128)(4,1)S(1)} %get-tuple-element.104, ...), kind=kLoop, calls=%fused_computation.19 | loop fusion | flops 1048576 | bytes 2123008 | tf_op jit(solution)/shard_map/mul | solution.py:49
  20.4 2.8 %collective-permute-done.3.refs_2_ = bf16[64,5120]{1,0:T(8,128)(2,1)} collective-permute-done((bf16[64,5120]{1,0:T(8,128)(2,1)S(1)}, bf16[64,5120]{1,0:T(8,128)(2,1)}, u32[]{:S(2)}, u32[]{:S(2)}) %collective-permute-start.3) | collective-permute-done | bytes 655392 | tf_op jit(solution)/shard_map/ppermute | solution.py:92
  23.1 1.7 collective-permute-start.7
  25.8 1.9 %collective-permute-start.5 = (bf16[64,5120]{1,0:T(8,128)(2,1)S(1)}, bf16[64,5120]{1,0:T(8,128)(2,1)S(1)}, u32[]{:S(2)}, u32[]{:S(2)}) collective-permute-start(bf16[64,5120]{1,0:T(8,128)(2,1)S(1)} %get-tuple-element.41.refs_0_), channel_id=1, source_target_pairs={{0,6},{1,7},{2,0},{3,1},{4,2},{5,3},{6,4},{7,5},{8,14},{9,15},{10,... | collective-permute-start | bytes 1966088 | tf_op jit(solution)/shard_map/ppermute | solution.py:96
  27.6 1.4 collective-permute-start.10
  29.0 4.1 %pad_maximum_fusion.1.refs_9_.refs_7_.refs_3_ = bf16[3,5120,256]{2,1,0:T(8,128)(2,1)S(1)} fusion(bf16[1,5120,256]{2,1,0:T(8,128)(2,1)} %bitcast.15, bf16[1,5120,256]{2,1,0:T(8,128)(2,1)} %bitcast.14, bf16[1,5120,256]{2,1,0:T(8,128)(2,1)} %bitcast.13), kind=kLoop, calls=%fused_computation.1 | loop fusion | flops 7864320 | bytes 15728640 | tf_op jit(solution)/shard_map/stack | solution.py:369
  33.2 4.2 %pad_maximum_fusion.refs_8_.refs_6_.refs_2_ = bf16[3,5120,256]{2,1,0:T(8,128)(2,1)S(1)} fusion(bf16[1,5120,256]{2,1,0:T(8,128)(2,1)} %bitcast.12, bf16[1,5120,256]{2,1,0:T(8,128)(2,1)} %bitcast.11, bf16[1,5120,256]{2,1,0:T(8,128)(2,1)} %bitcast.10), kind=kLoop, calls=%fused_computation | loop fusion | flops 7864320 | bytes 15728640 | tf_op jit(solution)/shard_map/stack | solution.py:369
  37.4 1.7 collective-permute-done.7.refs_6_
  40.2 12.9 %collective-permute-done.8.refs_7_ = bf16[64,5120]{1,0:T(8,128)(2,1)S(1)} collective-permute-done((bf16[64,5120]{1,0:T(8,128)(2,1)S(1)}, bf16[64,5120]{1,0:T(8,128)(2,1)S(1)}, u32[]{:S(2)}, u32[]{:S(2)}) %collective-permute-start.8) | collective-permute-done | bytes 655392 | tf_op jit(solution)/shard_map/ppermute | solution.py:100
  53.1 2.7 %collective-permute-start.17 = (bf16[64,5120]{1,0:T(8,128)(2,1)S(1)}, bf16[64,5120]{1,0:T(8,128)(2,1)S(1)}, u32[]{:S(2)}, u32[]{:S(2)}) collective-permute-start(bf16[64,5120]{1,0:T(8,128)(2,1)S(1)} %collective-permute-done.7.refs_6_), channel_id=1, source_target_pairs={{0,6},{1,7},{2,0},{3,1},{4,2},{5,3},{6,4},{7,5},{8,14},{9,15},{10,... | collective-permute-start | bytes 1966088 | tf_op jit(solution)/shard_map/ppermute | solution.py:96
  57.0 10.2 %collective-permute-done.10.refs_5_ = bf16[64,5120]{1,0:T(8,128)(2,1)S(1)} collective-permute-done((bf16[64,5120]{1,0:T(8,128)(2,1)}, bf16[64,5120]{1,0:T(8,128)(2,1)S(1)}, u32[]{:S(2)}, u32[]{:S(2)}) %collective-permute-start.10) | collective-permute-done | bytes 655392 | tf_op jit(solution)/shard_map/ppermute | solution.py:100
  67.2 11.9 %project.3 = (bf16[3,512,256]{2,1,0:T(8,128)(2,1)S(1)}, bf16[3,512,256]{2,1,0:T(8,128)(2,1)}, f32[3,4,128]{2,1,0:T(4,128)S(1)}) custom-call(bf16[64,5120]{1,0:T(8,128)(2,1)S(1)} %copy-done.7, bf16[64,5120]{1,0:T(8,128)(2,1)S(1)} %get-tuple-element.90.refs_1_, bf16[64,5120]{1,0:T(8,128)(2,1)} %collective-permute-done.3.refs_2_, ...), custom_call_target="tpu_custom_call" | custom-call | flops 8053063680 | bytes 15728640 | tf_op jit(solution)/shard_map/project/pallas_call | solution.py:139
  79.0 2.2 %collective-permute-done.9.refs_2_ = bf16[64,5120]{1,0:T(8,128)(2,1)S(1)} collective-permute-done((bf16[64,5120]{1,0:T(8,128)(2,1)}, bf16[64,5120]{1,0:T(8,128)(2,1)S(1)}, u32[]{:S(2)}, u32[]{:S(2)}) %collective-permute-start.9) | collective-permute-done | bytes 655392 | tf_op jit(solution)/shard_map/ppermute | solution.py:100
  81.2 2.7 %collective-permute-start.13 = (bf16[64,5120]{1,0:T(8,128)(2,1)S(1)}, bf16[64,5120]{1,0:T(8,128)(2,1)S(1)}, u32[]{:S(2)}, u32[]{:S(2)}) collective-permute-start(bf16[64,5120]{1,0:T(8,128)(2,1)S(1)} %collective-permute-done.10.refs_5_), channel_id=1, source_target_pairs={{0,6},{1,7},{2,0},{3,1},{4,2},{5,3},{6,4},{7,5},{8,14},{9,15},{10,... | collective-permute-start | bytes 1966088 | tf_op jit(solution)/shard_map/ppermute | solution.py:96
  84.0 2.1 %collective-permute-start.11 = (bf16[3,512,256]{2,1,0:T(8,128)(2,1)}, bf16[3,512,256]{2,1,0:T(8,128)(2,1)}, u32[]{:S(2)}, u32[]{:S(2)}) collective-permute-start(bf16[3,512,256]{2,1,0:T(8,128)(2,1)} %get-tuple-element.56), channel_id=1, source_target_pairs={{0,1},{1,0},{2,3},{3,2},{4,5},{5,4},{6,7},{7,6},{8,9},{9,8},{10,11... | collective-permute-start | bytes 2359304 | tf_op jit(solution)/shard_map/ppermute | solution.py:104
  86.0 9.0 %project.4 = (bf16[3,384,256]{2,1,0:T(8,128)(2,1)S(1)}, bf16[3,384,256]{2,1,0:T(8,128)(2,1)}, f32[3,3,128]{2,1,0:T(4,128)S(1)}) custom-call(bf16[64,5120]{1,0:T(8,128)(2,1)S(1)} %collective-permute-done.14.refs_0_, bf16[64,5120]{1,0:T(8,128)(2,1)S(1)} %collective-permute-done.15.refs_1_, bf16[64,5120]{1,0:T(8,128)(2,1)S(1)} %collective-permute-done.9.refs_2_, ...), custom_call_target="tpu_custom_call" | custom-call | flops 6039797760 | bytes 15728640 | tf_op jit(solution)/shard_map/project/pallas_call | solution.py:139
  95.0 2.6 %collective-permute-done.12.refs_0_ = bf16[64,5120]{1,0:T(8,128)(2,1)S(1)} collective-permute-done((bf16[64,5120]{1,0:T(8,128)(2,1)S(1)}, bf16[64,5120]{1,0:T(8,128)(2,1)S(1)}, u32[]{:S(2)}, u32[]{:S(2)}) %collective-permute-start.12) | collective-permute-done | bytes 655392 | tf_op jit(solution)/shard_map/ppermute | solution.py:92
  97.6 2.2 %collective-permute-start.18 = (bf16[3,384,256]{2,1,0:T(8,128)(2,1)}, bf16[3,384,256]{2,1,0:T(8,128)(2,1)}, u32[]{:S(2)}, u32[]{:S(2)}) collective-permute-start(bf16[3,384,256]{2,1,0:T(8,128)(2,1)} %get-tuple-element.63), channel_id=1, source_target_pairs={{0,1},{1,0},{2,3},{3,2},{4,5},{5,4},{6,7},{7,6},{8,9},{9,8},{10,11... | collective-permute-start | bytes 1769480 | tf_op jit(solution)/shard_map/ppermute | solution.py:104
  99.8 3.5 %project.5 = (bf16[3,128,256]{2,1,0:T(8,128)(2,1)S(1)}, bf16[3,128,256]{2,1,0:T(8,128)(2,1)S(1)}, f32[3,1,128]{2,1,0:T(1,128)S(1)}) custom-call(bf16[64,5120]{1,0:T(8,128)(2,1)S(1)} %collective-permute-done.12.refs_0_, bf16[64,5120]{1,0:T(8,128)(2,1)S(1)} %collective-permute-done.13.refs_1_, ...), custom_call_target="tpu_custom_call" | custom-call | flops 2013265920 | bytes 15728640 | tf_op jit(solution)/shard_map/project/pallas_call | solution.py:139
  105.4 5.0 %all-to-all-start = ((f32[16,16,128]{2,1,0:T(8,128)}), f32[16,16,128]{2,1,0:T(8,128)}, u32[]{:S(2)}, u32[]{:S(2)}) async-start(f32[16,16,128]{2,1,0:T(8,128)} %broadcast_in_dim.98), calls=%async_computation | async-start | bytes 262144 | tf_op jit(solution)/shard_map/all_to_all | solution.py:394
  110.7 6.0 %all-to-all-done = f32[16,16,128]{2,1,0:T(8,128)} async-done(((f32[16,16,128]{2,1,0:T(8,128)}), f32[16,16,128]{2,1,0:T(8,128)}, u32[]{:S(2)}, u32[]{:S(2)}) %all-to-all-start) | async-done | bytes 131104 | tf_op jit(solution)/shard_map/all_to_all | solution.py:394
  118.6 2.3 %halo_keys.1 = (bf16[512,256]{1,0:T(8,128)(2,1)S(1)}, bf16[512,256]{1,0:T(8,128)(2,1)S(1)}) custom-call(s32[16]{0:T(128)S(1)} %reshape.325.place_ref, bf16[3,512,256]{2,1,0:T(8,128)(2,1)S(1)} %get-tuple-element.55.fa, bf16[3,512,256]{2,1,0:T(8,128)(2,1)} %collective-permute-done.11.ga, bf16[3,384,256]{2,1,0:T(8,128)(2,1)S(1)} %get-tuple-element.62.fb, ...), custom_call_target="tpu_custom_call" | custom-call | flops 10000000 | bytes 3000000 | tf_op jit(solution)/shard_map/halo_keys/pallas_call | solution.py:210
  121.0 3.4 %collective-permute-start.20 = (bf16[512,256]{1,0:T(8,128)(2,1)S(1)}, bf16[512,256]{1,0:T(8,128)(2,1)S(1)}, u32[]{:S(2)}, u32[]{:S(2)}) collective-permute-start(bf16[512,256]{1,0:T(8,128)(2,1)S(1)} %get-tuple-element.74.before_ref), channel_id=1, source_target_pairs={{112,0},{0,16},{16,32},{32,48},{48,64},{64,80},{80,96},{96,112},{1... | collective-permute-start | bytes 786440 | tf_op jit(solution)/shard_map/ppermute | solution.py:342
  124.4 2.7 %collective-permute-start.21 = (bf16[512,256]{1,0:T(8,128)(2,1)S(1)}, bf16[512,256]{1,0:T(8,128)(2,1)S(1)}, u32[]{:S(2)}, u32[]{:S(2)}) collective-permute-start(bf16[512,256]{1,0:T(8,128)(2,1)S(1)} %get-tuple-element.75.after_ref), channel_id=1, source_target_pairs={{16,0},{32,16},{48,32},{64,48},{80,64},{96,80},{112,96},{0,112},{1... | collective-permute-start | bytes 786440 | tf_op jit(solution)/shard_map/ppermute | solution.py:342
  127.7 14.8 %window_attention.1.rest_0_ = bf16[16,2,144,128]{3,2,1,0:T(8,128)(2,1)} custom-call(s32[16]{0:T(128)} %copy-done.12, bf16[3,512,256]{2,1,0:T(8,128)(2,1)} %copy-done.2, bf16[3,512,256]{2,1,0:T(8,128)(2,1)} %collective-permute-done.11.ga, bf16[3,384,256]{2,1,0:T(8,128)(2,1)} %copy-done.3, bf16[3,384,256]{2,1,0:T(8,128)(2,1)} %collective-permute-done.18.gb, ...), custom_call_target="tpu_custom_call" | custom-call | flops 1500000000 | bytes 10000000 | tf_op jit(solution)/shard_map/window_attention/pallas_call | solution.py:317
  143.9 7.3 %window_attention_halo.1 = bf16[16,2,144,128]{3,2,1,0:T(8,128)(2,1)} custom-call(s32[16]{0:T(128)} %copy-done.12, bf16[3,512,256]{2,1,0:T(8,128)(2,1)} %copy-done.2, bf16[3,512,256]{2,1,0:T(8,128)(2,1)} %collective-permute-done.11.ga, bf16[3,384,256]{2,1,0:T(8,128)(2,1)} %copy-done.3, ...), custom_call_target="tpu_custom_call", output_to_operand_aliasing={{}: (15, {})} | custom-call | flops 500000000 | bytes 10000000 | tf_op jit(solution)/shard_map/window_attention_halo/pallas_call | solution.py:317
  151.2 21.6 %all_to_all.10 = bf16[16,2,144,128]{3,2,1,0:T(8,128)(2,1)S(1)} all-to-all(bf16[16,2,144,128]{3,2,1,0:T(8,128)(2,1)} %window_attention_halo.1), channel_id=1, replica_groups=mesh['sx'=8,'sy'=16] {'sy'}, dimensions={0} | all-to-all | bytes 2359296 | tf_op jit(solution)/shard_map/all_to_all | solution.py:401
  173.7 1.3 copy.21
  (102 shorter events, 15.5 us)
Async XLA Ops:
  3.5 29.6 %copy-start.6 = (bf16[64,5120]{1,0:T(8,128)(2,1)}, bf16[64,5120]{1,0:T(8,128)(2,1)S(1)}, u32[]{:S(2)}) copy-start(bf16[64,5120]{1,0:T(8,128)(2,1)S(1)} %get-tuple-element.41.refs_0_) | copy-start | bytes 1966084
  3.5 21.4 %collective-permute-start = (bf16[5120,256]{1,0:T(8,128)(2,1)}, bf16[5120,256]{1,0:T(8,128)(2,1)}, u32[]{:S(2)}, u32[]{:S(2)}) collective-permute-start(bf16[5120,256]{1,0:T(8,128)(2,1)} %param.12), channel_id=1, source_target_pairs={{0,1},{1,0},{2,3},{3,2},{4,5},{5,4},{6,7},{7,6},{8,9},{9,8},{10,11... | collective-permute-start | bytes 7864328 | tf_op jit(solution)/shard_map/ppermute | solution.py:104
  5.0 20.7 %collective-permute-start.1 = (bf16[5120,256]{1,0:T(8,128)(2,1)}, bf16[5120,256]{1,0:T(8,128)(2,1)}, u32[]{:S(2)}, u32[]{:S(2)}) collective-permute-start(bf16[5120,256]{1,0:T(8,128)(2,1)} %param.11), channel_id=1, source_target_pairs={{0,1},{1,0},{2,3},{3,2},{4,5},{5,4},{6,7},{7,6},{8,9},{9,8},{10,11... | collective-permute-start | bytes 7864328 | tf_op jit(solution)/shard_map/ppermute | solution.py:104
  5.1 22.5 %collective-permute-start.2 = (bf16[5120,256]{1,0:T(8,128)(2,1)}, bf16[5120,256]{1,0:T(8,128)(2,1)}, u32[]{:S(2)}, u32[]{:S(2)}) collective-permute-start(bf16[5120,256]{1,0:T(8,128)(2,1)} %param.13), channel_id=1, source_target_pairs={{0,1},{1,0},{2,3},{3,2},{4,5},{5,4},{6,7},{7,6},{8,9},{9,8},{10,11... | collective-permute-start | bytes 7864328 | tf_op jit(solution)/shard_map/ppermute | solution.py:104
  5.5 17.6 %collective-permute-start.3 = (bf16[64,5120]{1,0:T(8,128)(2,1)S(1)}, bf16[64,5120]{1,0:T(8,128)(2,1)}, u32[]{:S(2)}, u32[]{:S(2)}) collective-permute-start(bf16[64,5120]{1,0:T(8,128)(2,1)S(1)} %get-tuple-element.41.refs_0_), channel_id=1, source_target_pairs={{0,2},{1,3},{2,4},{3,5},{4,6},{5,7},{6,0},{7,1},{8,10},{9,11},{10,... | collective-permute-start | bytes 1966088 | tf_op jit(solution)/shard_map/ppermute | solution.py:92
  6.8 18.0 %collective-permute-start.6 = (bf16[64,5120]{1,0:T(8,128)(2,1)S(1)}, bf16[64,5120]{1,0:T(8,128)(2,1)}, u32[]{:S(2)}, u32[]{:S(2)}) collective-permute-start(bf16[64,5120]{1,0:T(8,128)(2,1)S(1)} %get-tuple-element.90.refs_1_), channel_id=1, source_target_pairs={{0,6},{1,7},{2,0},{3,1},{4,2},{5,3},{6,4},{7,5},{8,14},{9,15},{10,... | collective-permute-start | bytes 1966088 | tf_op jit(solution)/shard_map/ppermute | solution.py:96
  8.7 109.0 %copy-start.12 = (s32[16]{0:T(128)}, s32[16]{0:T(128)S(1)}, u32[]{:S(2)}) copy-start(s32[16]{0:T(128)S(1)} %reshape.325.place_ref) | copy-start | bytes 196
  10.8 106.9 %copy-start.11 = (f32[256]{0:T(256)}, f32[256]{0:T(256)S(1)}, u32[]{:S(2)}) copy-start(f32[256]{0:T(256)S(1)} %dynamic_slice.7) | copy-start | bytes 3076
  20.3 97.4 %copy-start = (f32[2048,128]{1,0:T(8,128)}, f32[2048,128]{1,0:T(8,128)S(1)}, u32[]{:S(2)}) copy-start(f32[2048,128]{1,0:T(8,128)S(1)} %get-tuple-element.73.sin_lo.sin_hi.sin_ref) | copy-start | bytes 3145732
  20.3 97.4 %copy-start.1 = (f32[2048,128]{1,0:T(8,128)}, f32[2048,128]{1,0:T(8,128)S(1)}, u32[]{:S(2)}) copy-start(f32[2048,128]{1,0:T(8,128)S(1)} %get-tuple-element.72.cos_lo.cos_hi.cos_ref) | copy-start | bytes 3145732
  23.1 15.9 %collective-permute-start.7 = (bf16[64,5120]{1,0:T(8,128)(2,1)S(1)}, bf16[64,5120]{1,0:T(8,128)(2,1)S(1)}, u32[]{:S(2)}, u32[]{:S(2)}) collective-permute-start(bf16[64,5120]{1,0:T(8,128)(2,1)S(1)} %get-tuple-element.41.refs_0_), channel_id=1, source_target_pairs={{0,8},{1,9},{2,10},{3,11},{4,12},{5,13},{6,14},{7,15},{8,0},{9,1},... | collective-permute-start | bytes 1966088 | tf_op jit(solution)/shard_map/ppermute | solution.py:100
  24.9 28.2 %collective-permute-start.8 = (bf16[64,5120]{1,0:T(8,128)(2,1)S(1)}, bf16[64,5120]{1,0:T(8,128)(2,1)S(1)}, u32[]{:S(2)}, u32[]{:S(2)}) collective-permute-start(bf16[64,5120]{1,0:T(8,128)(2,1)S(1)} %get-tuple-element.90.refs_1_), channel_id=1, source_target_pairs={{0,8},{1,9},{2,10},{3,11},{4,12},{5,13},{6,14},{7,15},{8,0},{9,1},... | collective-permute-start | bytes 1966088 | tf_op jit(solution)/shard_map/ppermute | solution.py:100
  24.9 28.2 %collective-permute-start.4 = (bf16[64,5120]{1,0:T(8,128)(2,1)S(1)}, bf16[64,5120]{1,0:T(8,128)(2,1)S(1)}, u32[]{:S(2)}, u32[]{:S(2)}) collective-permute-start(bf16[64,5120]{1,0:T(8,128)(2,1)S(1)} %get-tuple-element.90.refs_1_), channel_id=1, source_target_pairs={{0,2},{1,3},{2,4},{3,5},{4,6},{5,7},{6,0},{7,1},{8,10},{9,11},{10,... | collective-permute-start | bytes 1966088 | tf_op jit(solution)/shard_map/ppermute | solution.py:92
  25.8 30.0 %collective-permute-start.5 = (bf16[64,5120]{1,0:T(8,128)(2,1)S(1)}, bf16[64,5120]{1,0:T(8,128)(2,1)S(1)}, u32[]{:S(2)}, u32[]{:S(2)}) collective-permute-start(bf16[64,5120]{1,0:T(8,128)(2,1)S(1)} %get-tuple-element.41.refs_0_), channel_id=1, source_target_pairs={{0,6},{1,7},{2,0},{3,1},{4,2},{5,3},{6,4},{7,5},{8,14},{9,15},{10,... | collective-permute-start | bytes 1966088 | tf_op jit(solution)/shard_map/ppermute | solution.py:96
  27.6 39.5 %collective-permute-start.10 = (bf16[64,5120]{1,0:T(8,128)(2,1)}, bf16[64,5120]{1,0:T(8,128)(2,1)S(1)}, u32[]{:S(2)}, u32[]{:S(2)}) collective-permute-start(bf16[64,5120]{1,0:T(8,128)(2,1)} %collective-permute-done.6.refs_5_), channel_id=1, source_target_pairs={{0,8},{1,9},{2,10},{3,11},{4,12},{5,13},{6,14},{7,15},{8,0},{9,1},... | collective-permute-start | bytes 1966088 | tf_op jit(solution)/shard_map/ppermute | solution.py:100
  33.2 34.0 %copy-start.7 = (bf16[64,5120]{1,0:T(8,128)(2,1)S(1)}, bf16[64,5120]{1,0:T(8,128)(2,1)}, u32[]{:S(2)}) copy-start(bf16[64,5120]{1,0:T(8,128)(2,1)} %copy-done.6) | copy-start | bytes 1966084
  39.1 42.1 %collective-permute-start.15 = (bf16[64,5120]{1,0:T(8,128)(2,1)}, bf16[64,5120]{1,0:T(8,128)(2,1)S(1)}, u32[]{:S(2)}, u32[]{:S(2)}) collective-permute-start(bf16[64,5120]{1,0:T(8,128)(2,1)} %collective-permute-done.6.refs_5_), channel_id=1, source_target_pairs={{0,6},{1,7},{2,0},{3,1},{4,2},{5,3},{6,4},{7,5},{8,14},{9,15},{10,... | collective-permute-start | bytes 1966088 | tf_op jit(solution)/shard_map/ppermute | solution.py:96
  53.1 30.8 %collective-permute-start.16 = (bf16[64,5120]{1,0:T(8,128)(2,1)S(1)}, bf16[64,5120]{1,0:T(8,128)(2,1)S(1)}, u32[]{:S(2)}, u32[]{:S(2)}) collective-permute-start(bf16[64,5120]{1,0:T(8,128)(2,1)S(1)} %collective-permute-done.8.refs_7_), channel_id=1, source_target_pairs={{0,2},{1,3},{2,4},{3,5},{4,6},{5,7},{6,0},{7,1},{8,10},{9,11},{10,... | collective-permute-start | bytes 1966088 | tf_op jit(solution)/shard_map/ppermute | solution.py:92
  53.1 32.9 %collective-permute-start.17 = (bf16[64,5120]{1,0:T(8,128)(2,1)S(1)}, bf16[64,5120]{1,0:T(8,128)(2,1)S(1)}, u32[]{:S(2)}, u32[]{:S(2)}) collective-permute-start(bf16[64,5120]{1,0:T(8,128)(2,1)S(1)} %collective-permute-done.7.refs_6_), channel_id=1, source_target_pairs={{0,6},{1,7},{2,0},{3,1},{4,2},{5,3},{6,4},{7,5},{8,14},{9,15},{10,... | collective-permute-start | bytes 1966088 | tf_op jit(solution)/shard_map/ppermute | solution.py:96
  55.8 25.4 %collective-permute-start.9 = (bf16[64,5120]{1,0:T(8,128)(2,1)}, bf16[64,5120]{1,0:T(8,128)(2,1)S(1)}, u32[]{:S(2)}, u32[]{:S(2)}) collective-permute-start(bf16[64,5120]{1,0:T(8,128)(2,1)} %collective-permute-done.3.refs_2_), channel_id=1, source_target_pairs={{0,8},{1,9},{2,10},{3,11},{4,12},{5,13},{6,14},{7,15},{8,0},{9,1},... | collective-permute-start | bytes 1966088 | tf_op jit(solution)/shard_map/ppermute | solution.py:100
  67.2 18.9 %collective-permute-start.14 = (bf16[64,5120]{1,0:T(8,128)(2,1)}, bf16[64,5120]{1,0:T(8,128)(2,1)S(1)}, u32[]{:S(2)}, u32[]{:S(2)}) collective-permute-start(bf16[64,5120]{1,0:T(8,128)(2,1)} %collective-permute-done.3.refs_2_), channel_id=1, source_target_pairs={{0,2},{1,3},{2,4},{3,5},{4,6},{5,7},{6,0},{7,1},{8,10},{9,11},{10,... | collective-permute-start | bytes 1966088 | tf_op jit(solution)/shard_map/ppermute | solution.py:92
  79.0 38.6 %copy-start.2 = (bf16[3,512,256]{2,1,0:T(8,128)(2,1)}, bf16[3,512,256]{2,1,0:T(8,128)(2,1)S(1)}, u32[]{:S(2)}) copy-start(bf16[3,512,256]{2,1,0:T(8,128)(2,1)S(1)} %get-tuple-element.55.fa) | copy-start | bytes 2359300
  81.2 16.4 %collective-permute-start.12 = (bf16[64,5120]{1,0:T(8,128)(2,1)S(1)}, bf16[64,5120]{1,0:T(8,128)(2,1)S(1)}, u32[]{:S(2)}, u32[]{:S(2)}) collective-permute-start(bf16[64,5120]{1,0:T(8,128)(2,1)S(1)} %collective-permute-done.9.refs_2_), channel_id=1, source_target_pairs={{0,2},{1,3},{2,4},{3,5},{4,6},{5,7},{6,0},{7,1},{8,10},{9,11},{10,... | collective-permute-start | bytes 1966088 | tf_op jit(solution)/shard_map/ppermute | solution.py:92
  81.2 16.4 %collective-permute-start.13 = (bf16[64,5120]{1,0:T(8,128)(2,1)S(1)}, bf16[64,5120]{1,0:T(8,128)(2,1)S(1)}, u32[]{:S(2)}, u32[]{:S(2)}) collective-permute-start(bf16[64,5120]{1,0:T(8,128)(2,1)S(1)} %collective-permute-done.10.refs_5_), channel_id=1, source_target_pairs={{0,6},{1,7},{2,0},{3,1},{4,2},{5,3},{6,4},{7,5},{8,14},{9,15},{10,... | collective-permute-start | bytes 1966088 | tf_op jit(solution)/shard_map/ppermute | solution.py:96
  84.0 33.6 %collective-permute-start.11 = (bf16[3,512,256]{2,1,0:T(8,128)(2,1)}, bf16[3,512,256]{2,1,0:T(8,128)(2,1)}, u32[]{:S(2)}, u32[]{:S(2)}) collective-permute-start(bf16[3,512,256]{2,1,0:T(8,128)(2,1)} %get-tuple-element.56), channel_id=1, source_target_pairs={{0,1},{1,0},{2,3},{3,2},{4,5},{5,4},{6,7},{7,6},{8,9},{9,8},{10,11... | collective-permute-start | bytes 2359304 | tf_op jit(solution)/shard_map/ppermute | solution.py:104
  95.0 22.7 %copy-start.3 = (bf16[3,384,256]{2,1,0:T(8,128)(2,1)}, bf16[3,384,256]{2,1,0:T(8,128)(2,1)S(1)}, u32[]{:S(2)}) copy-start(bf16[3,384,256]{2,1,0:T(8,128)(2,1)S(1)} %get-tuple-element.62.fb) | copy-start | bytes 1769476
  97.6 20.0 %collective-permute-start.18 = (bf16[3,384,256]{2,1,0:T(8,128)(2,1)}, bf16[3,384,256]{2,1,0:T(8,128)(2,1)}, u32[]{:S(2)}, u32[]{:S(2)}) collective-permute-start(bf16[3,384,256]{2,1,0:T(8,128)(2,1)} %get-tuple-element.63), channel_id=1, source_target_pairs={{0,1},{1,0},{2,3},{3,2},{4,5},{5,4},{6,7},{7,6},{8,9},{9,8},{10,11... | collective-permute-start | bytes 1769480 | tf_op jit(solution)/shard_map/ppermute | solution.py:104
  105.4 11.2 %all-to-all-start = ((f32[16,16,128]{2,1,0:T(8,128)}), f32[16,16,128]{2,1,0:T(8,128)}, u32[]{:S(2)}, u32[]{:S(2)}) async-start(f32[16,16,128]{2,1,0:T(8,128)} %broadcast_in_dim.98), calls=%async_computation | async-start | bytes 262144 | tf_op jit(solution)/shard_map/all_to_all | solution.py:394
  110.4 7.2 %collective-permute-start.19 = (bf16[3,128,256]{2,1,0:T(8,128)(2,1)}, bf16[3,128,256]{2,1,0:T(8,128)(2,1)}, u32[]{:S(2)}, u32[]{:S(2)}) collective-permute-start(bf16[3,128,256]{2,1,0:T(8,128)(2,1)} %copy-done.13), channel_id=1, source_target_pairs={{0,1},{1,0},{2,3},{3,2},{4,5},{5,4},{6,7},{7,6},{8,9},{9,8},{10,11... | collective-permute-start | bytes 589832 | tf_op jit(solution)/shard_map/ppermute | solution.py:104
  121.0 6.7 %copy-start.8 = (bf16[512,256]{1,0:T(8,128)(2,1)}, bf16[512,256]{1,0:T(8,128)(2,1)S(1)}, u32[]{:S(2)}) copy-start(bf16[512,256]{1,0:T(8,128)(2,1)S(1)} %get-tuple-element.75.after_ref) | copy-start | bytes 786436
  121.0 21.5 %collective-permute-start.20 = (bf16[512,256]{1,0:T(8,128)(2,1)S(1)}, bf16[512,256]{1,0:T(8,128)(2,1)S(1)}, u32[]{:S(2)}, u32[]{:S(2)}) collective-permute-start(bf16[512,256]{1,0:T(8,128)(2,1)S(1)} %get-tuple-element.74.before_ref), channel_id=1, source_target_pairs={{112,0},{0,16},{16,32},{32,48},{48,64},{64,80},{80,96},{96,112},{1... | collective-permute-start | bytes 786440 | tf_op jit(solution)/shard_map/ppermute | solution.py:342
  124.4 18.2 %collective-permute-start.21 = (bf16[512,256]{1,0:T(8,128)(2,1)S(1)}, bf16[512,256]{1,0:T(8,128)(2,1)S(1)}, u32[]{:S(2)}, u32[]{:S(2)}) collective-permute-start(bf16[512,256]{1,0:T(8,128)(2,1)S(1)} %get-tuple-element.75.after_ref), channel_id=1, source_target_pairs={{16,0},{32,16},{48,32},{64,48},{80,64},{96,80},{112,96},{0,112},{1... | collective-permute-start | bytes 786440 | tf_op jit(solution)/shard_map/ppermute | solution.py:342
  (10 other events, 20.0 us)

commit v3 on v1

v3 whole, which is shorter than its diff:
```python
import functools

import jax
import jax.numpy as jnp
import numpy as np
from jax import lax
from jax.experimental import pallas as pl
from jax.experimental.pallas import tpu as pltpu
from jax.sharding import PartitionSpec as P

H = 32
HD = 128
ROUNDS = 4
GRID_W = 80
GRID_H = 45
BLK = 128
HALO = ROUNDS * BLK
EXTRA = 16
NSY = 16
SCALE = np.float32(1.0) / np.sqrt(np.float32(HD))
LOG2E = np.float32(1.4426950408889634)


def layer_norm(values, mod_shift, mod_scale):
    wide = values.astype(jnp.float32)
    center = jnp.mean(wide, axis=-1, keepdims=True)
    spread = jnp.mean((wide - center) ** 2, axis=-1, keepdims=True)
    scaled = (wide - center) * lax.rsqrt(spread + 1e-06)
    return (scaled * (1.0 + mod_scale) + mod_shift).astype(jnp.bfloat16)


def rope_tables(positions):
    small_pairs = HD // 6
    time_pairs = (HD - 4 * small_pairs) // 2
    frame = (positions // (GRID_H * GRID_W)).astype(jnp.float32)
    row_pos = (positions // GRID_W % GRID_H).astype(jnp.float32)
    col_pos = (positions % GRID_W).astype(jnp.float32)
    time_freq = 10000.0 ** (-jnp.arange(time_pairs, dtype=jnp.float32) / time_pairs)
    space_freq = 10000.0 ** (-jnp.arange(small_pairs, dtype=jnp.float32) / small_pairs)
    freq = jnp.repeat(jnp.concatenate([time_freq, space_freq, space_freq]), 2)
    pair = jnp.arange(HD, dtype=jnp.int32) // 2
    where = jnp.where(
        pair < time_pairs,
        frame[:, None],
        jnp.where(pair < time_pairs + small_pairs, row_pos[:, None], col_pos[:, None]),
    )
    angles = where * freq
    sign = jnp.where(jnp.arange(HD) % 2 == 0, -1.0, 1.0).astype(jnp.float32)
    return jnp.cos(angles), jnp.sin(angles) * sign


def as_column(row):
    return jnp.broadcast_to(row, (BLK, BLK)).T


def as_row(column):
    return jnp.broadcast_to(column, (BLK, BLK)).T[0:1, :]


def inverse_norm(ssq_row):
    return as_column(lax.rsqrt(ssq_row * (1.0 / (H * HD)) + 1e-06))


def norm_rope(raw, inv, gain, cosine, sine):
    wide = raw.astype(jnp.float32) * inv * gain
    lane = lax.broadcasted_iota(jnp.int32, wide.shape, 1)
    partner = jnp.where(
        lane % 2 == 0, pltpu.roll(wide, HD - 1, 1), pltpu.roll(wide, 1, 1)
    )
    return (wide * cosine + partner * sine).astype(jnp.bfloat16)


def split3(row):
    hi = row.astype(jnp.bfloat16).astype(jnp.float32)
    rest = row - hi
    mid = rest.astype(jnp.bfloat16).astype(jnp.float32)
    return [hi, mid, rest - mid]


PER_STEP = 4
SLOTS = ((0, 0), (0, -1), (0, 1), (1, 0), (0, 2), (1, -1), (1, 1), (1, 2))
CHUNKS = (4, 3, 1)


def chip_move(dz, dx, dc):
    return [
        (z * 8 + x * 2 + c, (z + dz) % 2 * 8 + (x + dx) % 4 * 2 + (c + dc) % 2)
        for z in range(2)
        for x in range(4)
        for c in range(2)
    ]


def from_left(block):
    return lax.ppermute(block, "sy", chip_move(0, 1, 0))


def from_right(block):
    return lax.ppermute(block, "sy", chip_move(0, -1, 0))


def from_z(block):
    return lax.ppermute(block, "sy", chip_move(1, 0, 0))


def from_core(block):
    return lax.ppermute(block, "sy", chip_move(0, 0, 1))


ANYWHERE = pl.BlockSpec(memory_space=pl.ANY)
SMEM = pl.BlockSpec(memory_space=pltpu.SMEM)


def project_kernel(cuts, *refs):
    n = len(refs) - 7
    arrays, (own_w, other_w, own_ref, other_ref, ssq_ref, x_ref, sems) = refs[:n], refs[n:]

    @pl.when(pl.program_id(0) == 0)
    def _():
        copies, at = [], 0
        for i, (which, first, count) in enumerate(cuts):
            source = arrays[which].at[pl.ds(first, count)]
            copies.append(pltpu.make_async_copy(source, x_ref.at[pl.ds(at, count)], sems.at[i]))
            copies[-1].start()
            at += count
        for copy in copies:
            copy.wait()

    total = None
    for weight, out in ((own_w, own_ref), (other_w, other_ref)):
        made = jnp.dot(x_ref[...], weight[0], preferred_element_type=jnp.float32).astype(jnp.bfloat16)
        out[0] = made
        wide = made.astype(jnp.float32)
        part = jnp.sum(wide * wide, axis=-1, keepdims=True)
        total = part if total is None else total + part
    for i in range(x_ref.shape[0] // BLK):
        ssq_ref[0, i : i + 1, :] = as_row(total[i * BLK : (i + 1) * BLK])


def project(arrays, cuts, own_w, other_w):
    rows = sum(count for _, _, count in cuts)
    depth, wide = own_w.shape[1:]
    w_spec = pl.BlockSpec((1, depth, wide), lambda i: (i, 0, 0))
    o_spec = pl.BlockSpec((1, rows, wide), lambda i: (i, 0, 0))
    out = jax.ShapeDtypeStruct((3, rows, wide), jnp.bfloat16)
    return pl.pallas_call(
        functools.partial(project_kernel, cuts),
        grid=(3,),
        in_specs=[ANYWHERE] * len(arrays) + [w_spec, w_spec],
        out_specs=[o_spec, o_spec, pl.BlockSpec((1, rows // BLK, BLK), lambda i: (i, 0, 0))],
        out_shape=[out, out, jax.ShapeDtypeStruct((3, rows // BLK, BLK), jnp.float32)],
        scratch_shapes=[pltpu.VMEM((rows, depth), jnp.bfloat16), pltpu.SemaphoreType.DMA((len(cuts),))],
        compiler_params=pltpu.CompilerParams(
            dimension_semantics=("arbitrary",), vmem_limit_bytes=30 * 1024 * 1024
        ),
        cost_estimate=pl.CostEstimate(
            flops=12 * rows * depth * wide, bytes_accessed=12 * depth * wide, transcendentals=0
        ),
        name="project",
    )(*arrays, own_w, other_w)


def sources(refs):
    at = 0
    for chunk, slots in enumerate(CHUNKS):
        for i in range(slots):
            for core in range(2):
                yield (at + i) * 2 + core, refs[chunk * 2 + core], pl.ds(i * BLK, BLK)
        at += slots


def halo_kernel(place_ref, fa, ga, fb, gb, fc, gc, before_ref, after_ref, sems):
    blocks = 2 * sum(CHUNKS)
    ends = ((lambda n: n >= blocks - ROUNDS, blocks - ROUNDS, 0), (lambda n: n < ROUNDS, 0, 1))

    def each(act):
        for at, ref, rows in sources((fa, ga, fb, gb, fc, gc)):
            n = place_ref[at]
            for inside, first, head in ends:

                @pl.when(inside(n))
                def _(n=n, first=first, head=head, ref=ref, rows=rows, at=at):
                    to = pl.ds(pl.multiple_of((n - first) * BLK, BLK), BLK)
                    out = (before_ref, after_ref)[head]
                    for i, kind in enumerate((0, 2)):
                        source = ref.at[kind, rows, pl.ds(head * HD, HD)]
                        act(pltpu.make_async_copy(source, out.at[i, to], sems.at[at, i]))

    each(lambda copy: copy.start())
    each(lambda copy: copy.wait())


def halo(place, features):
    out = jax.ShapeDtypeStruct((2, HALO, HD), jnp.bfloat16)
    return pl.pallas_call(
        halo_kernel,
        in_specs=[SMEM] + [ANYWHERE] * 6,
        out_specs=[ANYWHERE] * 2,
        out_shape=[out, out],
        scratch_shapes=[pltpu.SemaphoreType.DMA((2 * sum(CHUNKS), 2))],
        compiler_params=pltpu.CompilerParams(vmem_limit_bytes=16 * 1024 * 1024),
        cost_estimate=pl.CostEstimate(flops=10**6, bytes_accessed=10**6, transcendentals=0),
        name="halo_rows",
    )(place, *features)


def attention_kernel(
    place_ref, fa, ga, fb, gb, fc, gc, before_ref, after_ref, sk_ref, sq_ref, sb_ref, sa_ref,
    gk_ref, gq_ref, cos_ref, sin_ref, out_ref, raw, kbuf, vbuf, sems,
):
    step = pl.program_id(0)
    blocks = 2 * sum(CHUNKS)
    columns = [slice(head * HD, (head + 1) * HD) for head in range(2)]

    @pl.when(step == 0)
    def _():
        copies = []
        for at, ref, rows in sources((fa, ga, fb, gb, fc, gc)):
            to = pl.ds(pl.multiple_of(place_ref[at] * BLK, BLK), BLK)
            copies.append(pltpu.make_async_copy(ref.at[:, rows], raw.at[:, to], sems.at[at]))
        for copy in copies:
            copy.start()

        def put(head, n, keys, values, inv):
            to = slice(n * BLK, (n + 1) * BLK)
            table = slice((n + head * ROUNDS) * BLK, (n + head * ROUNDS + 1) * BLK)
            kbuf[head, to, :] = norm_rope(keys, inv, gk_ref[:, columns[head]], cos_ref[table, :], sin_ref[table, :])
            vbuf[head, :, to] = values.T

        for head, ref, ssq in ((0, before_ref, sb_ref), (1, after_ref, sa_ref)):
            for i in range(ROUNDS):
                rows = slice(i * BLK, (i + 1) * BLK)
                put(head, head * blocks + i, ref[0, rows, :], ref[1, rows, :], inverse_norm(ssq[i : i + 1, :]))
        for copy in copies:
            copy.wait()
        for n in range(blocks):
            rows = slice(n * BLK, (n + 1) * BLK)
            inv = inverse_norm(sk_ref[n : n + 1, :])
            for head in range(2):
                put(head, n + (1 - head) * ROUNDS, raw[0, rows, columns[head]], raw[2, rows, columns[head]], inv)

    for j in range(PER_STEP):
        b = step * PER_STEP + j
        rows = pl.ds(pl.multiple_of(b * BLK, BLK), BLK)
        table = pl.ds(pl.multiple_of((b + ROUNDS) * BLK, BLK), BLK)
        window = pl.ds(pl.multiple_of(b * BLK, BLK), (ROUNDS + 1) * BLK)
        inv = inverse_norm(sq_ref[pl.ds(b, 1), :])
        for head in range(2):
            q = norm_rope(
                raw[1, rows, columns[head]], inv, gq_ref[:, columns[head]], cos_ref[table, :], sin_ref[table, :]
            )
            scores = lax.dot_general(
                kbuf[head, window, :], q, (((1,), (1,)), ((), ())), preferred_element_type=jnp.float32
            )
            top = jnp.max(scores, axis=0, keepdims=True)
            weight = jnp.exp2((scores - top) * (SCALE * LOG2E))
            total = jnp.sum(weight, axis=0, keepdims=True)
            mixed = jnp.dot(
                vbuf[head, :, window], weight.astype(jnp.bfloat16), preferred_element_type=jnp.float32
            )
            out_ref[j, 0:BLK, columns[head]] = (mixed / total).T.astype(jnp.bfloat16)
            stats = split3(top * SCALE) + split3(total) + [jnp.zeros((EXTRA - 6, HD), jnp.float32)]
            out_ref[j, BLK : BLK + EXTRA, columns[head]] = jnp.concatenate(stats, axis=0).astype(jnp.bfloat16)


def attention(place, features, before, after, sk, sq, sb, sa, gk, gq, cosine, sine):
    rows = sk.shape[0] * BLK
    blocks = rows // BLK
    whole = lambda a: pl.BlockSpec(a.shape, lambda i, n=a.ndim: (0,) * n)
    small = (before, after, sk, sq, sb, sa, gk, gq, cosine, sine)
    return pl.pallas_call(
        attention_kernel,
        grid=(blocks // PER_STEP,),
        in_specs=[SMEM] + [ANYWHERE] * 6 + [whole(a) for a in small],
        out_specs=pl.BlockSpec((PER_STEP, BLK + EXTRA, 2 * HD), lambda i: (i, 0, 0)),
        out_shape=jax.ShapeDtypeStruct((blocks, BLK + EXTRA, 2 * HD), jnp.bfloat16),
        scratch_shapes=[
            pltpu.VMEM((3, rows, 2 * HD), jnp.bfloat16),
            pltpu.VMEM((2, rows + HALO, HD), jnp.bfloat16),
            pltpu.VMEM((2, HD, rows + HALO), jnp.bfloat16),
            pltpu.SemaphoreType.DMA((blocks,)),
        ],
        compiler_params=pltpu.CompilerParams(
            dimension_semantics=("arbitrary",), vmem_limit_bytes=56 * 1024 * 1024
        ),
        cost_estimate=pl.CostEstimate(flops=2 * 10**9, bytes_accessed=10**7, transcendentals=10**6),
        name="window_attention",
    )(place, *features, *small)


def along_sx(block, distance):
    n = lax.axis_size("sx")
    return lax.ppermute(block, "sx", [((i - distance) % n, i) for i in range(n)])


def unpack(arrived):
    attended = arrived[:, :BLK].transpose(1, 0, 2).reshape(BLK, H * HD)
    stats = arrived[:, BLK : BLK + 6].astype(jnp.float32)
    best = (stats[:, 0] + stats[:, 1]) + stats[:, 2]
    total = (stats[:, 3] + stats[:, 4]) + stats[:, 5]
    return attended, best.reshape(H, BLK), total.reshape(H, BLK)


def body(tokens, mod_shift, mod_scale, w_query, w_key, w_value, query_gain, key_gain):
    group = lax.axis_index("sx")
    mine = lax.axis_index("sy")
    z, x, core = mine // 8, mine // 2 % 4, mine % 2
    chips = jnp.stack([(z + dz) % 2 * 4 + (x + dx) % 4 for dz, dx in SLOTS])
    place = jnp.stack([chips * 2 + core, chips * 2 + 1 - core], axis=1).reshape(-1).astype(jnp.int32)
    half = BLK // 2
    rows = BLK * lax.axis_size("sy")
    count = rows * lax.axis_size("sx")
    barrier = lax.optimization_barrier

    own = layer_norm(tokens, mod_shift, mod_scale)
    left, right, beside = from_left(own), from_right(own), from_z(own)
    weights = barrier((w_key, w_query, w_value, own))[:3]
    own_w, other_w = jnp.stack(weights), jnp.stack([from_core(w) for w in weights])
    positions = (group * rows - HALO + jnp.arange(rows + 2 * HALO, dtype=jnp.int32) + count) % count
    cosine, sine = rope_tables(positions)
    gq = lax.dynamic_slice(query_gain, (mine * 2 * HD,), (2 * HD,)).reshape(1, 2 * HD)
    gk = lax.dynamic_slice(key_gain, (mine * 2 * HD,), (2 * HD,)).reshape(1, 2 * HD)
    (left, right, beside), (own_w, other_w), (cosine, sine, gq, gk, place) = barrier(
        ((left, right, beside), (own_w, other_w), (cosine, sine, gq, gk, place))
    )

    by_z = from_z(jnp.concatenate([left[:half], right[half:]]))
    by_left = from_left(jnp.concatenate([left[:half], beside[half:]]))
    by_right = from_right(jnp.concatenate([right[half:], beside[:half]]))
    near = project((own, left, right, beside), tuple((i, 0, BLK) for i in range(4)), own_w, other_w)

    near, by_z = barrier((near, by_z))
    far_lo, far_hi = from_left(by_z[:half]), from_right(by_z[half:])
    middle = project(
        (by_left, by_right, by_z),
        ((0, 0, half), (1, 0, half), (2, 0, half), (0, half, half), (1, half, half), (2, half, half)),
        own_w, other_w,
    )
    far_lo, far_hi, middle = barrier((far_lo, far_hi, middle))
    last = project((far_lo, far_hi), ((0, 0, half), (1, 0, half)), own_w, other_w)

    features, parts = [], []
    for made, given, part in (near, middle, last):
        features += [made, from_core(given)]
        parts.append(part[:2])
    part = jnp.concatenate(parts, axis=1)
    here = chips[:, None] == jnp.arange(8)[None, :]
    part = jnp.sum(jnp.where(here[None, :, :, None], part[:, :, None, :], 0.0), axis=1)
    sent = jnp.broadcast_to(part.reshape(1, 16, BLK), (NSY, 16, BLK))
    seen = lax.all_to_all(sent, "sy", split_axis=0, concat_axis=0, tiled=True)
    ssq = jnp.sum(seen.reshape(8, 2, 2, 8, BLK), axis=0).transpose(1, 2, 0, 3).reshape(2, 16, BLK)
    before, after = halo(place, features)
    before, after = along_sx(before, 1), along_sx(after, -1)
    sb, sa = along_sx(ssq[0, -ROUNDS:], 1), along_sx(ssq[0, :ROUNDS], -1)
    out = attention(place, features, before, after, ssq[0], ssq[1], sb, sa, gk, gq, cosine, sine)
    arrived = lax.all_to_all(out, "sy", split_axis=0, concat_axis=0, tiled=True)
    return unpack(arrived)


def solution(mesh):
    placed = (
        P(("sx", "sy"), None),
        P(),
        P(),
        P(None, "sy"),
        P(None, "sy"),
        P(None, "sy"),
        P(),
        P(),
    )
    return jax.shard_map(
        body,
        mesh=mesh,
        in_specs=placed,
        out_specs=(P(("sx", "sy"), None), P(None, ("sx", "sy")), P(None, ("sx", "sy"))),
        check_vma=False,
    )
```

time: 197 us -> 181 us (0.919)
  Pallas kernels: 59.6 us -> 38.2 us
  waiting for transfers between devices: 54.1 us -> 41.4 us
  local copies, waits for them, and re-layouts: 11.6 us -> 22.4 us
  blocking collectives: 21.4 us -> 30 us
  starting transfers between devices: 28.7 us -> 21.6 us
  other arithmetic: 19.4 us -> 26 us
    ppermute x4 -> x3, waiting for transfers between devices: 27 us -> 11.5 us  [from_left(): return lax.ppermute(block, 'sy', chip_move(0, 1, 0))]
    pallas_call x4, Pallas kernels: 36.5 us -> 24.6 us  [the longest x3 23.3 us: project(): pl.pallas_call(functools.partial(project_kernel, cuts), grid=(3,), in_spe...]
    unnamed x17 -> x51, local copies, waits for them, and re-layouts: 4.45 us -> 14.8 us
    ppermute x3 -> x2, waiting for transfers between devices: 10.5 us -> 20.5 us  [from_z(): return lax.ppermute(block, 'sy', chip_move(1, 0, 0))]
    pallas_call x1, Pallas kernels: 23.1 us -> 13.6 us  [attention(): pl.pallas_call(attention_kernel, grid=(blocks // PER_STEP,), in_specs=[SM...]
    all_to_all x0 -> x1, blocking collectives: none -> 8.59 us  [body(): seen = lax.all_to_all(sent, 'sy', split_axis=0, concat_axis=0, tiled=True)]
    ppermute x4 -> x3, starting transfers between devices: 8.38 us -> 2.48 us  [from_right(): return lax.ppermute(block, 'sy', chip_move(0, -1, 0))]
    all_to_all x1 -> x0, waiting for transfers between devices: 5.08 us -> none  [body(): seen = lax.all_to_all(sent, 'sy', split_axis=0, concat_axis=0, tiled=True)]
  transfers between devices with their start and end apart: 18 -> 18, of which waited for: 6 -> 5; matrix products, arithmetic and copies ran while one was open for 9% -> 14% of each run, Pallas kernels for 17% -> 13%
where the time goes in v3:
time: 181 us
  waiting for transfers between devices  41.4 us (23%)
  Pallas kernels  38.2 us (21%)
  blocking collectives  30 us (17%)
  other arithmetic  26 us (14%)
  local copies, waits for them, and re-layouts  22.4 us (12%)
  starting transfers between devices  21.6 us (12%)
    pallas_call x3, Pallas kernels, project(): pl.pallas_call(functools.partial(project_kernel, cuts), grid=(3,), in_spe...  23.3 us
    all_to_all x1, blocking collectives, body(): arrived = lax.all_to_all(out, 'sy', split_axis=0, concat_axis=0, tiled=True)  21.4 us
    ppermute x2, waiting for transfers between devices, from_z(): return lax.ppermute(block, 'sy', chip_move(1, 0, 0))  20.5 us
    unnamed x51, local copies, waits for them, and re-layouts  14.8 us
    pallas_call x1, Pallas kernels, attention(): pl.pallas_call(attention_kernel, grid=(blocks // PER_STEP,), in_specs=[SM...  13.6 us
    ppermute x3, waiting for transfers between devices, from_left(): return lax.ppermute(block, 'sy', chip_move(0, 1, 0))  11.5 us
    mul x1, other arithmetic, rope_tables(): return (jnp.cos(angles), jnp.sin(angles) * sign)  10.5 us
    ppermute x4, starting transfers between devices, along_sx(): lax.ppermute(block, 'sx', [((i - distance) % n, i) for i in range(n)])  8.87 us
  transfers between devices with their start and end apart: 18, of which 5 were waited for; matrix products, arithmetic and copies ran while one was open for 14% of the time, Pallas kernels for 13%

profile of v3, /device:TPU:1, one launch (start us, length us, event | category | flops | bytes accessed | tf_op | source)
XLA Modules:
  0.0 180.6 jit_solution(2586073375338473311)
XLA Ops:
  0.7 1.7 convert_reduce_fusion
  2.4 1.8 %fusion.2 = f32[128]{0:T(128)S(1)} fusion(bf16[128,5120]{1,0:T(8,128)(2,1)} %param.8, f32[128]{0:T(128)S(1)} %broadcast_multiply_fusion), kind=kLoop, calls=%fused_computation.6 | loop fusion | flops 2621312 | bytes 1311744 | tf_op jit(solution)/shard_map/reduce_sum | solution.py:27
  4.8 1.5 collective-permute-start.3
  6.3 1.7 collective-permute-start.2
  8.0 2.5 %collective-permute-start.1 = (bf16[128,5120]{1,0:T(8,128)(2,1)S(1)}, bf16[128,5120]{1,0:T(8,128)(2,1)}, u32[]{:S(2)}, u32[]{:S(2)}) collective-permute-start(bf16[128,5120]{1,0:T(8,128)(2,1)S(1)} %fusion.5.refs_0_), channel_id=1, source_target_pairs={{0,6},{1,7},{2,0},{3,1},{4,2},{5,3},{6,4},{7,5},{8,14},{9,15},{10,... | collective-permute-start | bytes 3932168 | tf_op jit(solution)/shard_map/ppermute | solution.py:99
  11.2 1.3 dynamic_slice.6
  12.5 1.3 dynamic_slice.7
  14.5 4.1 %pad_maximum_fusion.refs_4_.refs_3_.refs_2_ = bf16[3,5120,256]{2,1,0:T(8,128)(2,1)S(1)} fusion(bf16[1,5120,256]{2,1,0:T(8,128)(2,1)} %bitcast.2, bf16[1,5120,256]{2,1,0:T(8,128)(2,1)} %bitcast.1, bf16[1,5120,256]{2,1,0:T(8,128)(2,1)} %bitcast), kind=kLoop, calls=%fused_computation | loop fusion | flops 7864320 | bytes 15728640 | tf_op jit(solution)/shard_map/stack | solution.py:318
  18.7 10.5 %sine_multiply_fusion = (f32[3072,128]{1,0:T(8,128)}, f32[3072,128]{1,0:T(8,128)}) fusion(f32[128]{0:T(128)S(1)} %compare_select_fusion, f32[128]{0:T(128)S(1)} %mul.75, f32[3072]{0:T(1024)S(1)} %fusion.11, f32[3072]{0:T(1024)S(1)} %get-tuple-element.96, f32[3072]{0:T(1024)S(1)} %get-tuple-element.95, pred[128]{0:T(512)(128)(4,1)S(1)} %get-tuple-element.97, ...), kind=kLoop, calls=%fused_computation.10 | loop fusion | flops 1572864 | bytes 3183872 | tf_op jit(solution)/shard_map/mul | solution.py:49
  29.3 4.1 %pad_maximum_fusion.1.refs_5_.refs_4_.refs_3_ = bf16[3,5120,256]{2,1,0:T(8,128)(2,1)S(1)} fusion(bf16[1,5120,256]{2,1,0:T(8,128)(2,1)} %bitcast.5, bf16[1,5120,256]{2,1,0:T(8,128)(2,1)} %bitcast.4, bf16[1,5120,256]{2,1,0:T(8,128)(2,1)} %bitcast.3), kind=kLoop, calls=%fused_computation.1 | loop fusion | flops 7864320 | bytes 15728640 | tf_op jit(solution)/shard_map/stack | solution.py:318
  33.4 3.7 %collective-permute-done.2.refs_3_ = bf16[128,5120]{1,0:T(8,128)(2,1)S(1)} collective-permute-done((bf16[128,5120]{1,0:T(8,128)(2,1)S(1)}, bf16[128,5120]{1,0:T(8,128)(2,1)S(1)}, u32[]{:S(2)}, u32[]{:S(2)}) %collective-permute-start.2) | collective-permute-done | bytes 1310752 | tf_op jit(solution)/shard_map/ppermute | solution.py:103
  38.3 11.4 %collective-permute-done.refs_1_ = bf16[128,5120]{1,0:T(8,128)(2,1)S(1)} collective-permute-done((bf16[128,5120]{1,0:T(8,128)(2,1)S(1)}, bf16[128,5120]{1,0:T(8,128)(2,1)S(1)}, u32[]{:S(2)}, u32[]{:S(2)}) %collective-permute-start) | collective-permute-done | bytes 1310752 | tf_op jit(solution)/shard_map/ppermute | solution.py:95
  51.1 2.0 %pad_maximum_fusion.4 = (bf16[128,5120]{1,0:T(8,128)(2,1)}, bf16[128,5120]{1,0:T(8,128)(2,1)S(1)}, bf16[128,5120]{1,0:T(8,128)(2,1)}) fusion(bf16[64,5120]{1,0:T(8,128)(2,1)S(1)} %get-tuple-element.78, bf16[64,5120]{1,0:T(8,128)(2,1)S(1)} %slice.68, bf16[64,5120]{1,0:T(8,128)(2,1)S(1)} %slice.67, bf16[64,5120]{1,0:T(8,128)(2,1)S(1)} %get-tuple-element.79), kind=kLoop, calls=%fused_computation.15 | loop fusion | flops 7208960 | bytes 6553600 | tf_op jit(solution)/shard_map/concatenate | solution.py:329
  53.1 1.5 collective-permute-start.10
  54.6 10.7 %project.3 = (bf16[3,512,256]{2,1,0:T(8,128)(2,1)S(1)}, bf16[3,512,256]{2,1,0:T(8,128)(2,1)S(1)}, f32[3,4,128]{2,1,0:T(4,128)S(1)}) custom-call(bf16[128,5120]{1,0:T(8,128)(2,1)S(1)} %fusion.5.refs_0_, bf16[128,5120]{1,0:T(8,128)(2,1)S(1)} %collective-permute-done.refs_1_, bf16[128,5120]{1,0:T(8,128)(2,1)} %collective-permute-done.1.refs_2_, ...), custom_call_target="tpu_custom_call" | custom-call | flops 8053063680 | bytes 15728640 | tf_op jit(solution)/shard_map/project/pallas_call | solution.py:146
  65.3 16.8 %collective-permute-done.6.refs_2_ = bf16[128,5120]{1,0:T(8,128)(2,1)S(1)} collective-permute-done((bf16[128,5120]{1,0:T(8,128)(2,1)S(1)}, bf16[128,5120]{1,0:T(8,128)(2,1)S(1)}, u32[]{:S(2)}, u32[]{:S(2)}) %collective-permute-start.6) | collective-permute-done | bytes 1310752 | tf_op jit(solution)/shard_map/ppermute | solution.py:103
  84.3 1.5 collective-permute-start.8
  85.9 2.8 %collective-permute-start.7 = (bf16[3,512,256]{2,1,0:T(8,128)(2,1)}, bf16[3,512,256]{2,1,0:T(8,128)(2,1)S(1)}, u32[]{:S(2)}, u32[]{:S(2)}) collective-permute-start(bf16[3,512,256]{2,1,0:T(8,128)(2,1)} %copy-done.17), channel_id=1, source_target_pairs={{0,1},{1,0},{2,3},{3,2},{4,5},{5,4},{6,7},{7,6},{8,9},{9,8},{10,11... | collective-permute-start | bytes 2359304 | tf_op jit(solution)/shard_map/ppermute | solution.py:107
  88.6 3.2 %copy-done.1 = bf16[3,5120,256]{2,1,0:T(8,128)(2,1)S(1)} copy-done((bf16[3,5120,256]{2,1,0:T(8,128)(2,1)S(1)}, bf16[3,5120,256]{2,1,0:T(8,128)(2,1)}, u32[]{:S(2)}) %copy-start.1) | copy-done | bytes 7864344
  91.9 3.2 %copy-done.3 = bf16[3,5120,256]{2,1,0:T(8,128)(2,1)S(1)} copy-done((bf16[3,5120,256]{2,1,0:T(8,128)(2,1)S(1)}, bf16[3,5120,256]{2,1,0:T(8,128)(2,1)}, u32[]{:S(2)}) %copy-start.3) | copy-done | bytes 7864344
  95.1 1.3 copy-done.9
  96.4 9.3 %project.4 = (bf16[3,384,256]{2,1,0:T(8,128)(2,1)S(1)}, bf16[3,384,256]{2,1,0:T(8,128)(2,1)}, f32[3,3,128]{2,1,0:T(4,128)S(1)}) custom-call(bf16[128,5120]{1,0:T(8,128)(2,1)} %collective-permute-done.10.refs_0_, bf16[128,5120]{1,0:T(8,128)(2,1)} %collective-permute-done.11.refs_1_, bf16[128,5120]{1,0:T(8,128)(2,1)S(1)} %copy-done.9, ...), custom_call_target="tpu_custom_call" | custom-call | flops 6039797760 | bytes 15728640 | tf_op jit(solution)/shard_map/project/pallas_call | solution.py:146
  109.8 3.3 %project.5 = (bf16[3,128,256]{2,1,0:T(8,128)(2,1)S(1)}, bf16[3,128,256]{2,1,0:T(8,128)(2,1)S(1)}, f32[3,1,128]{2,1,0:T(1,128)S(1)}) custom-call(bf16[64,5120]{1,0:T(8,128)(2,1)S(1)} %copy-done.15, bf16[64,5120]{1,0:T(8,128)(2,1)S(1)} %copy-done.13, bf16[3,5120,256]{2,1,0:T(8,128)(2,1)S(1)} %copy-done.1, bf16[3,5120,256]{2,1,0:T(8,128)(2,1)S(1)} %copy-done.3), custom_call_target="tpu_custom_call" | custom-call | flops 2013265920 | bytes 15728640 | tf_op jit(solution)/shard_map/project/pallas_call | solution.py:146
  113.8 8.6 %all_to_all.10 = f32[16,16,128]{2,1,0:T(8,128)S(1)} all-to-all(f32[16,16,128]{2,1,0:T(8,128)S(1)} %broadcast_in_dim.94), channel_id=1, replica_groups=mesh['sx'=8,'sy'=16] {'sy'}, dimensions={0} | all-to-all | bytes 262144 | tf_op jit(solution)/shard_map/all_to_all | solution.py:350
  122.5 1.2 halo_rows.1
  123.8 3.4 %collective-permute-start.14 = (bf16[2,512,128]{2,1,0:T(8,128)(2,1)S(1)}, bf16[2,512,128]{2,1,0:T(8,128)(2,1)S(1)}, u32[]{:S(2)}, u32[]{:S(2)}) collective-permute-start(bf16[2,512,128]{2,1,0:T(8,128)(2,1)S(1)} %get-tuple-element.60), channel_id=1, source_target_pairs={{112,0},{0,16},{16,32},{32,48},{48,64},{64,80},{80,96},{96,112},{1... | collective-permute-start | bytes 786440 | tf_op jit(solution)/shard_map/ppermute | solution.py:293
  127.1 2.5 %collective-permute-start.15 = (bf16[2,512,128]{2,1,0:T(8,128)(2,1)S(1)}, bf16[2,512,128]{2,1,0:T(8,128)(2,1)S(1)}, u32[]{:S(2)}, u32[]{:S(2)}) collective-permute-start(bf16[2,512,128]{2,1,0:T(8,128)(2,1)S(1)} %get-tuple-element.61), channel_id=1, source_target_pairs={{16,0},{32,16},{48,32},{64,48},{80,64},{96,80},{112,96},{0,112},{1... | collective-permute-start | bytes 786440 | tf_op jit(solution)/shard_map/ppermute | solution.py:293
  129.7 2.9 %collective-permute-start.17 = (f32[4,128]{1,0:T(4,128)S(1)}, f32[4,128]{1,0:T(4,128)S(1)}, u32[]{:S(2)}, u32[]{:S(2)}) collective-permute-start(f32[4,128]{1,0:T(4,128)S(1)} %get-tuple-element.89), channel_id=1, source_target_pairs={{16,0},{32,16},{48,32},{64,48},{80,64},{96,80},{112,96},{0,112},{1... | collective-permute-start | bytes 6152 | tf_op jit(solution)/shard_map/ppermute | solution.py:293
  133.9 8.2 %collective-permute-done.17.sa_ref = f32[4,128]{1,0:T(4,128)S(1)} collective-permute-done((f32[4,128]{1,0:T(4,128)S(1)}, f32[4,128]{1,0:T(4,128)S(1)}, u32[]{:S(2)}, u32[]{:S(2)}) %collective-permute-start.17) | collective-permute-done | bytes 2080 | tf_op jit(solution)/shard_map/ppermute | solution.py:293
  142.9 13.6 %window_attention.1 = bf16[16,144,256]{2,1,0:T(8,128)(2,1)} custom-call(s32[16]{0:T(128)} %copy-done.16, bf16[3,512,256]{2,1,0:T(8,128)(2,1)} %copy-done.4, bf16[3,512,256]{2,1,0:T(8,128)(2,1)} %copy-done.5, bf16[3,384,256]{2,1,0:T(8,128)(2,1)} %copy-done.6, bf16[3,384,256]{2,1,0:T(8,128)(2,1)} %copy-done.7, bf16[3,128,256]{2,1,0:T(8,128)(2,1)} %copy-done.10, ...), custom_call_target="tpu_custom_call" | custom-call | flops 2000000000 | bytes 10000000 | tf_op jit(solution)/shard_map/window_attention/pallas_call | solution.py:271
  156.5 21.4 %all_to_all.11 = bf16[16,144,256]{2,1,0:T(8,128)(2,1)S(1)} all-to-all(bf16[16,144,256]{2,1,0:T(8,128)(2,1)} %window_attention.1), channel_id=1, replica_groups=mesh['sx'=8,'sy'=16] {'sy'}, dimensions={0} | all-to-all | bytes 2359296 | tf_op jit(solution)/shard_map/all_to_all | solution.py:356
  179.3 1.3 copy.21
  (110 shorter events, 15.0 us)
Async XLA Ops:
  0.6 3.6 %copy-start.18 = (bf16[128,5120]{1,0:T(8,128)(2,1)S(1)}, bf16[128,5120]{1,0:T(8,128)(2,1)}, u32[]{:S(2)}) copy-start(bf16[128,5120]{1,0:T(8,128)(2,1)} %param.8) | copy-start | bytes 3932164
  0.6 3.5 %copy-start.22 = (f32[5120]{0:T(1024)S(1)}, f32[5120]{0:T(1024)}, u32[]{:S(2)}) copy-start(f32[5120]{0:T(1024)} %param.10) | copy-start | bytes 61444
  0.7 3.6 %copy-start.21 = (f32[5120]{0:T(1024)S(1)}, f32[5120]{0:T(1024)}, u32[]{:S(2)}) copy-start(f32[5120]{0:T(1024)} %param.9) | copy-start | bytes 61444
  4.8 13.8 %collective-permute-start.3 = (bf16[5120,256]{1,0:T(8,128)(2,1)}, bf16[5120,256]{1,0:T(8,128)(2,1)}, u32[]{:S(2)}, u32[]{:S(2)}) collective-permute-start(bf16[5120,256]{1,0:T(8,128)(2,1)} %param.12), channel_id=1, source_target_pairs={{0,1},{1,0},{2,3},{3,2},{4,5},{5,4},{6,7},{7,6},{8,9},{9,8},{10,11... | collective-permute-start | bytes 7864328 | tf_op jit(solution)/shard_map/ppermute | solution.py:107
  6.3 30.9 %collective-permute-start.2 = (bf16[128,5120]{1,0:T(8,128)(2,1)S(1)}, bf16[128,5120]{1,0:T(8,128)(2,1)S(1)}, u32[]{:S(2)}, u32[]{:S(2)}) collective-permute-start(bf16[128,5120]{1,0:T(8,128)(2,1)S(1)} %fusion.5.refs_0_), channel_id=1, source_target_pairs={{0,8},{1,9},{2,10},{3,11},{4,12},{5,13},{6,14},{7,15},{8,0},{9,1},... | collective-permute-start | bytes 3932168 | tf_op jit(solution)/shard_map/ppermute | solution.py:103
  8.0 30.3 %collective-permute-start.1 = (bf16[128,5120]{1,0:T(8,128)(2,1)S(1)}, bf16[128,5120]{1,0:T(8,128)(2,1)}, u32[]{:S(2)}, u32[]{:S(2)}) collective-permute-start(bf16[128,5120]{1,0:T(8,128)(2,1)S(1)} %fusion.5.refs_0_), channel_id=1, source_target_pairs={{0,6},{1,7},{2,0},{3,1},{4,2},{5,3},{6,4},{7,5},{8,14},{9,15},{10,... | collective-permute-start | bytes 3932168 | tf_op jit(solution)/shard_map/ppermute | solution.py:99
  10.5 18.8 %collective-permute-start.4 = (bf16[5120,256]{1,0:T(8,128)(2,1)}, bf16[5120,256]{1,0:T(8,128)(2,1)}, u32[]{:S(2)}, u32[]{:S(2)}) collective-permute-start(bf16[5120,256]{1,0:T(8,128)(2,1)} %param.11), channel_id=1, source_target_pairs={{0,1},{1,0},{2,3},{3,2},{4,5},{5,4},{6,7},{7,6},{8,9},{9,8},{10,11... | collective-permute-start | bytes 7864328 | tf_op jit(solution)/shard_map/ppermute | solution.py:107
  11.2 18.1 %collective-permute-start.5 = (bf16[5120,256]{1,0:T(8,128)(2,1)}, bf16[5120,256]{1,0:T(8,128)(2,1)}, u32[]{:S(2)}, u32[]{:S(2)}) collective-permute-start(bf16[5120,256]{1,0:T(8,128)(2,1)} %param.13), channel_id=1, source_target_pairs={{0,1},{1,0},{2,3},{3,2},{4,5},{5,4},{6,7},{7,6},{8,9},{9,8},{10,11... | collective-permute-start | bytes 7864328 | tf_op jit(solution)/shard_map/ppermute | solution.py:107
  14.0 108.4 %copy-start.16 = (s32[16]{0:T(128)}, s32[16]{0:T(128)S(1)}, u32[]{:S(2)}) copy-start(s32[16]{0:T(128)S(1)} %reshape.327.place_ref) | copy-start | bytes 196
  18.6 35.9 %copy-start = (bf16[3,5120,256]{2,1,0:T(8,128)(2,1)}, bf16[3,5120,256]{2,1,0:T(8,128)(2,1)S(1)}, u32[]{:S(2)}) copy-start(bf16[3,5120,256]{2,1,0:T(8,128)(2,1)S(1)} %pad_maximum_fusion.refs_4_.refs_3_.refs_2_) | copy-start | bytes 23592964
  18.7 31.1 %collective-permute-start = (bf16[128,5120]{1,0:T(8,128)(2,1)S(1)}, bf16[128,5120]{1,0:T(8,128)(2,1)S(1)}, u32[]{:S(2)}, u32[]{:S(2)}) collective-permute-start(bf16[128,5120]{1,0:T(8,128)(2,1)S(1)} %fusion.5.refs_0_), channel_id=1, source_target_pairs={{0,2},{1,3},{2,4},{3,5},{4,6},{5,7},{6,0},{7,1},{8,10},{9,11},{10,... | collective-permute-start | bytes 3932168 | tf_op jit(solution)/shard_map/ppermute | solution.py:95
  33.4 21.1 %copy-start.2 = (bf16[3,5120,256]{2,1,0:T(8,128)(2,1)}, bf16[3,5120,256]{2,1,0:T(8,128)(2,1)S(1)}, u32[]{:S(2)}) copy-start(bf16[3,5120,256]{2,1,0:T(8,128)(2,1)S(1)} %pad_maximum_fusion.1.refs_5_.refs_4_.refs_3_) | copy-start | bytes 23592964
  53.1 29.0 %collective-permute-start.6 = (bf16[128,5120]{1,0:T(8,128)(2,1)S(1)}, bf16[128,5120]{1,0:T(8,128)(2,1)S(1)}, u32[]{:S(2)}, u32[]{:S(2)}) collective-permute-start(bf16[128,5120]{1,0:T(8,128)(2,1)S(1)} %get-tuple-element.83), channel_id=1, source_target_pairs={{0,8},{1,9},{2,10},{3,11},{4,12},{5,13},{6,14},{7,15},{8,0},{9,1},... | collective-permute-start | bytes 3932168 | tf_op jit(solution)/shard_map/ppermute | solution.py:103
  53.1 35.5 %collective-permute-start.11 = (bf16[128,5120]{1,0:T(8,128)(2,1)}, bf16[128,5120]{1,0:T(8,128)(2,1)}, u32[]{:S(2)}, u32[]{:S(2)}) collective-permute-start(bf16[128,5120]{1,0:T(8,128)(2,1)} %get-tuple-element.82), channel_id=1, source_target_pairs={{0,6},{1,7},{2,0},{3,1},{4,2},{5,3},{6,4},{7,5},{8,14},{9,15},{10,... | collective-permute-start | bytes 3932168 | tf_op jit(solution)/shard_map/ppermute | solution.py:99
  53.1 35.5 %collective-permute-start.10 = (bf16[128,5120]{1,0:T(8,128)(2,1)}, bf16[128,5120]{1,0:T(8,128)(2,1)}, u32[]{:S(2)}, u32[]{:S(2)}) collective-permute-start(bf16[128,5120]{1,0:T(8,128)(2,1)} %get-tuple-element.84), channel_id=1, source_target_pairs={{0,2},{1,3},{2,4},{3,5},{4,6},{5,7},{6,0},{7,1},{8,10},{9,11},{10,... | collective-permute-start | bytes 3932168 | tf_op jit(solution)/shard_map/ppermute | solution.py:95
  65.3 19.0 %copy-start.17 = (bf16[3,512,256]{2,1,0:T(8,128)(2,1)}, bf16[3,512,256]{2,1,0:T(8,128)(2,1)S(1)}, u32[]{:S(2)}) copy-start(bf16[3,512,256]{2,1,0:T(8,128)(2,1)S(1)} %get-tuple-element.49) | copy-start | bytes 2359300
  65.3 57.2 %copy-start.4 = (bf16[3,512,256]{2,1,0:T(8,128)(2,1)}, bf16[3,512,256]{2,1,0:T(8,128)(2,1)S(1)}, u32[]{:S(2)}) copy-start(bf16[3,512,256]{2,1,0:T(8,128)(2,1)S(1)} %get-tuple-element.48.fa) | copy-start | bytes 2359300
  84.3 21.4 %collective-permute-start.9 = (bf16[64,5120]{1,0:T(8,128)(2,1)}, bf16[64,5120]{1,0:T(8,128)(2,1)S(1)}, u32[]{:S(2)}, u32[]{:S(2)}) collective-permute-start(bf16[64,5120]{1,0:T(8,128)(2,1)} %get-tuple-element.80), channel_id=1, source_target_pairs={{0,6},{1,7},{2,0},{3,1},{4,2},{5,3},{6,4},{7,5},{8,14},{9,15},{10,... | collective-permute-start | bytes 1966088 | tf_op jit(solution)/shard_map/ppermute | solution.py:99
  84.3 22.3 %collective-permute-start.8 = (bf16[64,5120]{1,0:T(8,128)(2,1)}, bf16[64,5120]{1,0:T(8,128)(2,1)S(1)}, u32[]{:S(2)}, u32[]{:S(2)}) collective-permute-start(bf16[64,5120]{1,0:T(8,128)(2,1)} %get-tuple-element.81), channel_id=1, source_target_pairs={{0,2},{1,3},{2,4},{3,5},{4,6},{5,7},{6,0},{7,1},{8,10},{9,11},{10,... | collective-permute-start | bytes 1966088 | tf_op jit(solution)/shard_map/ppermute | solution.py:95
  85.9 36.6 %collective-permute-start.7 = (bf16[3,512,256]{2,1,0:T(8,128)(2,1)}, bf16[3,512,256]{2,1,0:T(8,128)(2,1)S(1)}, u32[]{:S(2)}, u32[]{:S(2)}) collective-permute-start(bf16[3,512,256]{2,1,0:T(8,128)(2,1)} %copy-done.17), channel_id=1, source_target_pairs={{0,1},{1,0},{2,3},{3,2},{4,5},{5,4},{6,7},{7,6},{8,9},{9,8},{10,11... | collective-permute-start | bytes 2359304 | tf_op jit(solution)/shard_map/ppermute | solution.py:107
  88.6 3.2 %copy-start.1 = (bf16[3,5120,256]{2,1,0:T(8,128)(2,1)S(1)}, bf16[3,5120,256]{2,1,0:T(8,128)(2,1)}, u32[]{:S(2)}) copy-start(bf16[3,5120,256]{2,1,0:T(8,128)(2,1)} %copy-done) | copy-start | bytes 23592964
  105.7 16.8 %copy-start.6 = (bf16[3,384,256]{2,1,0:T(8,128)(2,1)}, bf16[3,384,256]{2,1,0:T(8,128)(2,1)S(1)}, u32[]{:S(2)}) copy-start(bf16[3,384,256]{2,1,0:T(8,128)(2,1)S(1)} %get-tuple-element.54.fb) | copy-start | bytes 1769476
  107.5 15.0 %collective-permute-start.12 = (bf16[3,384,256]{2,1,0:T(8,128)(2,1)}, bf16[3,384,256]{2,1,0:T(8,128)(2,1)S(1)}, u32[]{:S(2)}, u32[]{:S(2)}) collective-permute-start(bf16[3,384,256]{2,1,0:T(8,128)(2,1)} %get-tuple-element.55), channel_id=1, source_target_pairs={{0,1},{1,0},{2,3},{3,2},{4,5},{5,4},{6,7},{7,6},{8,9},{9,8},{10,11... | collective-permute-start | bytes 1769480 | tf_op jit(solution)/shard_map/ppermute | solution.py:107
  113.1 29.0 %copy-start.10 = (bf16[3,128,256]{2,1,0:T(8,128)(2,1)}, bf16[3,128,256]{2,1,0:T(8,128)(2,1)S(1)}, u32[]{:S(2)}) copy-start(bf16[3,128,256]{2,1,0:T(8,128)(2,1)S(1)} %get-tuple-element.58.fc) | copy-start | bytes 589828
  113.1 9.3 %collective-permute-start.13 = (bf16[3,128,256]{2,1,0:T(8,128)(2,1)S(1)}, bf16[3,128,256]{2,1,0:T(8,128)(2,1)S(1)}, u32[]{:S(2)}, u32[]{:S(2)}) collective-permute-start(bf16[3,128,256]{2,1,0:T(8,128)(2,1)S(1)} %get-tuple-element.59), channel_id=1, source_target_pairs={{0,1},{1,0},{2,3},{3,2},{4,5},{5,4},{6,7},{7,6},{8,9},{9,8},{10,11... | collective-permute-start | bytes 589832 | tf_op jit(solution)/shard_map/ppermute | solution.py:107
  122.4 19.7 %copy-start.5 = (bf16[3,512,256]{2,1,0:T(8,128)(2,1)}, bf16[3,512,256]{2,1,0:T(8,128)(2,1)S(1)}, u32[]{:S(2)}) copy-start(bf16[3,512,256]{2,1,0:T(8,128)(2,1)S(1)} %collective-permute-done.7.ga) | copy-start | bytes 2359300
  122.5 19.7 %copy-start.11 = (bf16[3,128,256]{2,1,0:T(8,128)(2,1)}, bf16[3,128,256]{2,1,0:T(8,128)(2,1)S(1)}, u32[]{:S(2)}) copy-start(bf16[3,128,256]{2,1,0:T(8,128)(2,1)S(1)} %collective-permute-done.13.gc) | copy-start | bytes 589828
  122.5 19.7 %copy-start.7 = (bf16[3,384,256]{2,1,0:T(8,128)(2,1)}, bf16[3,384,256]{2,1,0:T(8,128)(2,1)S(1)}, u32[]{:S(2)}) copy-start(bf16[3,384,256]{2,1,0:T(8,128)(2,1)S(1)} %collective-permute-done.12.gb) | copy-start | bytes 1769476
  123.8 18.3 %collective-permute-start.14 = (bf16[2,512,128]{2,1,0:T(8,128)(2,1)S(1)}, bf16[2,512,128]{2,1,0:T(8,128)(2,1)S(1)}, u32[]{:S(2)}, u32[]{:S(2)}) collective-permute-start(bf16[2,512,128]{2,1,0:T(8,128)(2,1)S(1)} %get-tuple-element.60), channel_id=1, source_target_pairs={{112,0},{0,16},{16,32},{32,48},{48,64},{64,80},{80,96},{96,112},{1... | collective-permute-start | bytes 786440 | tf_op jit(solution)/shard_map/ppermute | solution.py:293
  127.1 14.9 %collective-permute-start.15 = (bf16[2,512,128]{2,1,0:T(8,128)(2,1)S(1)}, bf16[2,512,128]{2,1,0:T(8,128)(2,1)S(1)}, u32[]{:S(2)}, u32[]{:S(2)}) collective-permute-start(bf16[2,512,128]{2,1,0:T(8,128)(2,1)S(1)} %get-tuple-element.61), channel_id=1, source_target_pairs={{16,0},{32,16},{48,32},{64,48},{80,64},{96,80},{112,96},{0,112},{1... | collective-permute-start | bytes 786440 | tf_op jit(solution)/shard_map/ppermute | solution.py:293
  129.7 12.4 %collective-permute-start.17 = (f32[4,128]{1,0:T(4,128)S(1)}, f32[4,128]{1,0:T(4,128)S(1)}, u32[]{:S(2)}, u32[]{:S(2)}) collective-permute-start(f32[4,128]{1,0:T(4,128)S(1)} %get-tuple-element.89), channel_id=1, source_target_pairs={{16,0},{32,16},{48,32},{64,48},{80,64},{96,80},{112,96},{0,112},{1... | collective-permute-start | bytes 6152 | tf_op jit(solution)/shard_map/ppermute | solution.py:293
  132.6 9.5 %collective-permute-start.16 = (f32[4,128]{1,0:T(4,128)S(1)}, f32[4,128]{1,0:T(4,128)S(1)}, u32[]{:S(2)}, u32[]{:S(2)}) collective-permute-start(f32[4,128]{1,0:T(4,128)S(1)} %get-tuple-element.90), channel_id=1, source_target_pairs={{112,0},{0,16},{16,32},{32,48},{48,64},{64,80},{80,96},{96,112},{1... | collective-permute-start | bytes 6152 | tf_op jit(solution)/shard_map/ppermute | solution.py:293
  (11 other events, 12.2 us)

commit v4 on v2

--- a/solution.py
+++ b/solution.py
@@ -21,12 +21,29 @@
 LOG2E = np.float32(1.4426950408889634)
 
 
+def layer_norm_kernel(tokens_ref, shift_ref, scale_ref, out_ref):
+    wide = tokens_ref[...].astype(jnp.float32)
+    center = jnp.mean(wide, axis=-1, keepdims=True)
+    apart = wide - center
+    spread = jnp.mean(apart * apart, axis=-1, keepdims=True)
+    scaled = apart * lax.rsqrt(spread + 1e-06)
+    out_ref[...] = (scaled * (1.0 + scale_ref[...]) + shift_ref[...]).astype(jnp.bfloat16)
+
+
 def layer_norm(values, mod_shift, mod_scale):
-    wide = values.astype(jnp.float32)
-    center = jnp.mean(wide, axis=-1, keepdims=True)
-    spread = jnp.mean((wide - center) ** 2, axis=-1, keepdims=True)
-    scaled = (wide - center) * lax.rsqrt(spread + 1e-06)
-    return (scaled * (1.0 + mod_scale) + mod_shift).astype(jnp.bfloat16)
+    rows, wide = values.shape
+    block = pl.BlockSpec((32, wide), lambda i: (i, 0))
+    vector = pl.BlockSpec((1, wide), lambda i: (0, 0))
+    return pl.pallas_call(
+        layer_norm_kernel,
+        grid=(rows // 32,),
+        in_specs=[block, vector, vector],
+        out_specs=block,
+        out_shape=jax.ShapeDtypeStruct((rows, wide), jnp.bfloat16),
+        compiler_params=pltpu.CompilerParams(vmem_limit_bytes=16 * 1024 * 1024),
+        cost_estimate=pl.CostEstimate(flops=10 * rows * wide, bytes_accessed=4 * rows * wide, transcendentals=rows),
+        name="layer_norm",
+    )(values, mod_shift.reshape(1, wide), mod_scale.reshape(1, wide))
 
 
 def rope_tables(positions):
@@ -57,8 +74,11 @@
     return jnp.broadcast_to(column, (BLK, BLK)).T[0:1, :]
 
 
-def norm_rope(raw, ssq_row, gain, cosine, sine):
-    inv = lax.rsqrt(as_column(ssq_row) * (1.0 / (H * HD)) + 1e-06)
+def inverse_norm(ssq_row):
+    return as_column(lax.rsqrt(ssq_row * (1.0 / (H * HD)) + 1e-06))
+
+
+def norm_rope(raw, inv, gain, cosine, sine):
     wide = raw.astype(jnp.float32) * inv * gain
     lane = lax.broadcasted_iota(jnp.int32, wide.shape, 1)
     partner = jnp.where(
@@ -104,18 +124,22 @@
     return lax.ppermute(block, "sy", chip_move(0, 0, 1))
 
 
-def project_kernel(*refs):
+ANYWHERE = pl.BlockSpec(memory_space=pltpu.HBM)
+SMEM = pl.BlockSpec(memory_space=pltpu.SMEM)
+
+
+def project_kernel(cuts, *refs):
     n = len(refs) - 7
-    pieces, (own_w, other_w, own_ref, other_ref, ssq_ref, x_ref, sems) = refs[:n], refs[n:]
+    arrays, (own_w, other_w, own_ref, other_ref, ssq_ref, x_ref, sems) = refs[:n], refs[n:]
 
     @pl.when(pl.program_id(0) == 0)
     def _():
         copies, at = [], 0
-        for i, piece in enumerate(pieces):
-            rows = piece.shape[0]
-            copies.append(pltpu.make_async_copy(piece, x_ref.at[pl.ds(at, rows)], sems.at[i]))
+        for i, (which, first, count) in enumerate(cuts):
+            source = arrays[which].at[pl.ds(first, count)]
+            copies.append(pltpu.make_async_copy(source, x_ref.at[pl.ds(at, count)], sems.at[i]))
             copies[-1].start()
-            at += rows
+            at += count
         for copy in copies:
             copy.wait()
 
@@ -130,27 +154,27 @@
         ssq_ref[0, i : i + 1, :] = as_row(total[i * BLK : (i + 1) * BLK])
 
 
-def project(pieces, own_w, other_w):
-    rows = sum(p.shape[0] for p in pieces)
+def project(arrays, cuts, own_w, other_w):
+    rows = sum(count for _, _, count in cuts)
     depth, wide = own_w.shape[1:]
     w_spec = pl.BlockSpec((1, depth, wide), lambda i: (i, 0, 0))
     o_spec = pl.BlockSpec((1, rows, wide), lambda i: (i, 0, 0))
     out = jax.ShapeDtypeStruct((3, rows, wide), jnp.bfloat16)
     return pl.pallas_call(
-        project_kernel,
+        functools.partial(project_kernel, cuts),
         grid=(3,),
-        in_specs=[pl.BlockSpec(memory_space=pl.ANY)] * len(pieces) + [w_spec, w_spec],
+        in_specs=[ANYWHERE] * len(arrays) + [w_spec, w_spec],
         out_specs=[o_spec, o_spec, pl.BlockSpec((1, rows // BLK, BLK), lambda i: (i, 0, 0))],
         out_shape=[out, out, jax.ShapeDtypeStruct((3, rows // BLK, BLK), jnp.float32)],
-        scratch_shapes=[pltpu.VMEM((rows, depth), jnp.bfloat16), pltpu.SemaphoreType.DMA((len(pieces),))],
+        scratch_shapes=[pltpu.VMEM((rows, depth), jnp.bfloat16), pltpu.SemaphoreType.DMA((len(cuts),))],
         compiler_params=pltpu.CompilerParams(
-            dimension_semantics=("arbitrary",), vmem_limit_bytes=30 * 1024 * 1024
+            dimension_semantics=("arbitrary",), vmem_limit_bytes=26 * 1024 * 1024
         ),
         cost_estimate=pl.CostEstimate(
             flops=12 * rows * depth * wide, bytes_accessed=12 * depth * wide, transcendentals=0
         ),
         name="project",
-    )(*pieces, own_w, other_w)
+    )(*arrays, own_w, other_w)
 
 
 def sources(refs):
@@ -191,14 +215,10 @@
         for i in range(ROUNDS):
             rows = pl.ds(i * BLK, BLK)
             out[rows, 0:HD] = norm_rope(
-                raw[head, rows, :], ssq_ref[pl.ds(first + i, 1), :], gk_ref[:, head * HD : (head + 1) * HD],
+                raw[head, rows, :], inverse_norm(ssq_ref[pl.ds(first + i, 1), :]),
+                gk_ref[:, head * HD : (head + 1) * HD],
                 cosine[rows, :], sine[rows, :],
             )
-
-
-VMEM = pl.BlockSpec(memory_space=pltpu.VMEM)
-SMEM = pl.BlockSpec(memory_space=pltpu.SMEM)
-ANYWHERE = pl.BlockSpec(memory_space=pl.ANY)
 
 
 def halo(place, features, ssq_k, gk, cosine, sine):
@@ -217,7 +237,7 @@
             pltpu.VMEM((2, HALO, HD), jnp.bfloat16),
             pltpu.SemaphoreType.DMA((2 * sum(CHUNKS), 2)),
         ],
-        compiler_params=pltpu.CompilerParams(vmem_limit_bytes=48 * 1024 * 1024),
+        compiler_params=pltpu.CompilerParams(vmem_limit_bytes=16 * 1024 * 1024),
         cost_estimate=pl.CostEstimate(flops=10**7, bytes_accessed=3 * 10**6, transcendentals=0),
         name="halo_keys",
     )(place, *features, ssq_k, gk, cosine, sine, cosine, sine)
@@ -232,11 +252,6 @@
     blocks = 2 * sum(CHUNKS)
     columns = [slice(head * HD, (head + 1) * HD) for head in range(2)]
     own_first = (ROUNDS, 0)
-
-    def wanted(n, head):
-        if part == 0:
-            return None
-        return n < ROUNDS if head == 0 else n >= blocks - ROUNDS
 
     def guarded(condition, act):
         if condition is None:
@@ -262,22 +277,16 @@
         for n, needed, copy in copies:
             guarded(needed, copy.wait)
 
-        def prepare(n, head):
-            def act():
-                rows = pl.ds(pl.multiple_of(n * BLK, BLK), BLK)
-                to = pl.ds(pl.multiple_of((n + own_first[head]) * BLK, BLK), BLK)
+        for n in range(blocks):
+            heads = [head for head in range(2) if part == 0 or (n < ROUNDS, n >= blocks - ROUNDS)[head]]
+            rows = slice(n * BLK, (n + 1) * BLK)
+            inv = inverse_norm(sk_ref[n : n + 1, :]) if heads else None
+            for head in heads:
+                to = slice((n + own_first[head]) * BLK, (n + own_first[head] + 1) * BLK)
                 kbuf[head, to, :] = norm_rope(
-                    raw[0, rows, columns[head]], sk_ref[pl.ds(n, 1), :], gk_ref[:, columns[head]],
-                    cos_ref[rows, :], sin_ref[rows, :],
+                    raw[0, rows, columns[head]], inv, gk_ref[:, columns[head]], cos_ref[rows, :], sin_ref[rows, :]
                 )
                 vbuf[head, :, to] = raw[2, rows, columns[head]].T
-
-            return act
-
-        for n in range(blocks):
-            for head in range(2):
-                if wanted(n, head) is not False:
-                    prepare(n, head)()
 
     def attend(first, head):
         for j in range(PER_STEP):
@@ -285,7 +294,7 @@
             rows = pl.ds(pl.multiple_of(b * BLK, BLK), BLK)
             window = pl.ds(pl.multiple_of(b * BLK, BLK), (ROUNDS + 1) * BLK)
             q = norm_rope(
-                raw[1, rows, columns[head]], sq_ref[pl.ds(b, 1), :], gq_ref[:, columns[head]],
+                raw[1, rows, columns[head]], inverse_norm(sq_ref[pl.ds(b, 1), :]), gq_ref[:, columns[head]],
                 cos_ref[rows, :], sin_ref[rows, :],
             )
             scores = lax.dot_general(
@@ -328,7 +337,7 @@
         ],
         input_output_aliases={15: 0} if more else {},
         compiler_params=pltpu.CompilerParams(
-            dimension_semantics=("arbitrary", "arbitrary"), vmem_limit_bytes=56 * 1024 * 1024
+            dimension_semantics=("arbitrary", "arbitrary"), vmem_limit_bytes=24 * 1024 * 1024
         ),
         cost_estimate=pl.CostEstimate(
             flops=(1 + 2 * (1 - part)) * 5 * 10**8, bytes_accessed=10**7, transcendentals=10**6
@@ -356,32 +365,29 @@
     z, x, core = mine // 8, mine // 2 % 4, mine % 2
     chips = jnp.stack([(z + dz) % 2 * 4 + (x + dx) % 4 for dz, dx in SLOTS])
     place = jnp.stack([chips * 2 + core, chips * 2 + 1 - core], axis=1).reshape(-1).astype(jnp.int32)
-    half = BLK // 2
     rows = BLK * lax.axis_size("sy")
-
-    own_lo = layer_norm(tokens[:half], mod_shift, mod_scale)
-    own_hi = layer_norm(tokens[half:], mod_shift, mod_scale)
-    left_lo, right_hi, z_lo = from_left(own_lo), from_right(own_hi), from_z(own_lo)
-    left_hi, right_lo, z_hi = from_left(own_hi), from_right(own_lo), from_z(own_hi)
-    weights = lax.optimization_barrier((w_key, w_query, w_value, own_lo, own_hi))[:3]
-    swapped = [from_core(w) for w in weights]
-    weights, swapped, left_lo = lax.optimization_barrier((weights, swapped, left_lo))
-    own_w, other_w = jnp.stack(weights), jnp.stack(swapped)
-    far_lo, z_left_lo = from_left(left_lo), from_z(left_lo)
-    far_hi, z_right_hi = from_right(right_hi), from_z(right_hi)
-    z_left_hi, z_right_lo = from_left(z_hi), from_right(z_lo)
-
+    barrier = lax.optimization_barrier
+
+    own = layer_norm(tokens, mod_shift, mod_scale)
+    left, right, beside = from_left(own), from_right(own), from_z(own)
+    own_w = jnp.stack(barrier((w_key, w_query, w_value, own))[:3])
     cosine, sine = rope_tables(group * rows + jnp.arange(rows, dtype=jnp.int32))
     gq = lax.dynamic_slice(query_gain, (mine * 2 * HD,), (2 * HD,)).reshape(1, 2 * HD)
     gk = lax.dynamic_slice(key_gain, (mine * 2 * HD,), (2 * HD,)).reshape(1, 2 * HD)
-    own_lo, cosine, sine, gq, gk, place = lax.optimization_barrier((own_lo, cosine, sine, gq, gk, place))
-
-    near = project((own_lo, own_hi, left_lo, left_hi, right_lo, right_hi, z_lo, z_hi), own_w, other_w)
-    near, z_left_lo, z_right_hi = lax.optimization_barrier((near, z_left_lo, z_right_hi))
-    z_far_lo, z_far_hi = from_left(z_left_lo), from_right(z_right_hi)
-    middle = project((far_lo, far_hi, z_left_lo, z_left_hi, z_right_lo, z_right_hi), own_w, other_w)
-    z_far_lo, z_far_hi, middle = lax.optimization_barrier((z_far_lo, z_far_hi, middle))
-    last = project((z_far_lo, z_far_hi), own_w, other_w)
+    (left, right, beside), own_w, (cosine, sine, gq, gk, place) = barrier(
+        ((left, right, beside), own_w, (cosine, sine, gq, gk, place))
+    )
+
+    far, z_right, z_left = from_left(left), from_right(beside), from_z(left)
+    other_w = from_core(own_w)
+    near = project((own, left, right, beside), tuple((i, 0, BLK) for i in range(4)), own_w, other_w)
+    near, far, z_right, z_left = barrier((near, far, z_right, z_left))
+
+    cuts = (48, 96)
+    z_far = (from_left(z_left[: cuts[0]]), from_right(z_right[cuts[0] : cuts[1]]), from_z(far[cuts[1] :]))
+    middle = project((far, z_left, z_right), tuple((i, 0, BLK) for i in range(3)), own_w, other_w)
+    z_far, middle = barrier((z_far, middle))
+    last = project(z_far, tuple((i, 0, p.shape[0]) for i, p in enumerate(z_far)), own_w, other_w)
 
     features, parts = [], []
     for made, given, part in (near, middle, last):

time: 176 us -> 168 us (0.955)
  waiting for transfers between devices: 38.3 us -> 27.9 us
  Pallas kernels: 48.7 us -> 57.3 us
  starting transfers between devices: 33.9 us -> 28.6 us
  local copies, waits for them, and re-layouts: 9.81 us -> 14.3 us
  other arithmetic: 22.3 us -> 18 us
    ppermute x4 -> x3, waiting for transfers between devices: 26.9 us -> 2.43 us  [from_z(): return lax.ppermute(block, 'sy', chip_move(1, 0, 0))]
    pallas_call x3 -> x4, Pallas kernels: 24.3 us -> 37.6 us  [the longest x3 35.9 us: project(): pl.pallas_call(functools.partial(project_kernel, cuts), grid=(3,), in_spe...]
    ppermute x6 -> x4, waiting for transfers between devices: 0.02 us -> 8.08 us  [from_core(): return lax.ppermute(block, 'sy', chip_move(0, 0, 1))]
    ppermute x5 -> x3, waiting for transfers between devices: 5.35 us -> 11.2 us  [from_left(): return lax.ppermute(block, 'sy', chip_move(0, 1, 0))]
    pallas_call x2, Pallas kernels: 22.1 us -> 17.3 us  [attention(): pl.pallas_call(functools.partial(attention_kernel, part), grid=(steps, 2)...]
    slice x0 -> x3, local copies, waits for them, and re-layouts: none -> 3.12 us  [the longest x1 1.06 us: body(): z_right[cuts[0]:cuts[1]]]
    ppermute x5 -> x3, starting transfers between devices: 9.76 us -> 6.75 us  [from_right(): return lax.ppermute(block, 'sy', chip_move(0, -1, 0))]
    unnamed x39 -> x19, local copies, waits for them, and re-layouts: 5.07 us -> 7.67 us
  transfers between devices with their start and end apart: 23 -> 16, of which waited for: 7 -> 7; matrix products, arithmetic and copies ran while one was open for 13% -> 13% of each run, Pallas kernels for 22% -> 29%
where the time goes in v4:
time: 168 us; the launch traced here: 167 us
  Pallas kernels  57.3 us (34%)
  starting transfers between devices  28.6 us (17%)
  waiting for transfers between devices  27.9 us (17%)
  blocking collectives  20.3 us (12%)
  other arithmetic  18 us (11%)
  local copies, waits for them, and re-layouts  14.3 us (9%)
    pallas_call x3, Pallas kernels, project(): pl.pallas_call(functools.partial(project_kernel, cuts), grid=(3,), in_spe...  35.9 us
    all_to_all x1, blocking collectives, body(): arrived = lax.all_to_all(out, 'sy', split_axis=0, concat_axis=0, tiled=True)  20.3 us
    pallas_call x2, Pallas kernels, attention(): pl.pallas_call(functools.partial(attention_kernel, part), grid=(steps, 2)...  17.3 us
    ppermute x3, waiting for transfers between devices, from_left(): return lax.ppermute(block, 'sy', chip_move(0, 1, 0))  11.2 us
    mul x1, other arithmetic, rope_tables(): return (jnp.cos(angles), jnp.sin(angles) * sign)  9.21 us
    ppermute x4, waiting for transfers between devices, from_core(): return lax.ppermute(block, 'sy', chip_move(0, 0, 1))  8.08 us
    unnamed x19, local copies, waits for them, and re-layouts  7.67 us
    another operation x1, other arithmetic, body(): own_w = jnp.stack(barrier((w_key, w_query, w_value, own))[:3])  6.82 us
  transfers between devices with their start and end apart: 16, of which 7 were waited for; matrix products, arithmetic and copies ran while one was open for 13% of the time, Pallas kernels for 29%

profile of v4, /device:TPU:1, one launch (start us, length us, event | category | flops | bytes accessed | tf_op | source)
XLA Modules:
  0.0 167.3 jit_solution(8099646092294482477)
XLA Ops:
  0.6 1.3 copy-done.3
  3.4 1.7 %layer_norm.1.refs_0_ = bf16[128,5120]{1,0:T(8,128)(2,1)S(1)} custom-call(bf16[128,5120]{1,0:T(8,128)(2,1)S(1)} %copy-done.3, f32[1,5120]{1,0:T(1,128)S(1)} %bitcast.38, f32[1,5120]{1,0:T(1,128)S(1)} %bitcast.39), custom_call_target="tpu_custom_call" | custom-call | flops 6553600 | bytes 2621440 | tf_op jit(solution)/shard_map/layer_norm/pallas_call | solution.py:37
  5.1 2.1 %collective-permute-start = (bf16[128,5120]{1,0:T(8,128)(2,1)S(1)}, bf16[128,5120]{1,0:T(8,128)(2,1)}, u32[]{:S(2)}, u32[]{:S(2)}) collective-permute-start(bf16[128,5120]{1,0:T(8,128)(2,1)S(1)} %layer_norm.1.refs_0_), channel_id=1, source_target_pairs={{0,2},{1,3},{2,4},{3,5},{4,6},{5,7},{6,0},{7,1},{8,10},{9,11},{10,... | collective-permute-start | bytes 3932168 | tf_op jit(solution)/shard_map/ppermute | solution.py:112
  7.2 1.4 collective-permute-start.1
  8.6 1.8 %collective-permute-start.2 = (bf16[128,5120]{1,0:T(8,128)(2,1)S(1)}, bf16[128,5120]{1,0:T(8,128)(2,1)}, u32[]{:S(2)}, u32[]{:S(2)}) collective-permute-start(bf16[128,5120]{1,0:T(8,128)(2,1)S(1)} %layer_norm.1.refs_0_), channel_id=1, source_target_pairs={{0,8},{1,9},{2,10},{3,11},{4,12},{5,13},{6,14},{7,15},{8,0},{9,1},... | collective-permute-start | bytes 3932168 | tf_op jit(solution)/shard_map/ppermute | solution.py:120
  12.6 9.2 %sine_multiply_fusion = (f32[2048,128]{1,0:T(8,128)S(1)}, f32[2048,128]{1,0:T(8,128)S(1)}) fusion(f32[128]{0:T(128)S(1)} %compare_select_fusion, f32[128]{0:T(128)S(1)} %mul.55, f32[2048]{0:T(1024)S(1)} %fusion.4, f32[2048]{0:T(1024)S(1)} %get-tuple-element.91, f32[2048]{0:T(1024)S(1)} %get-tuple-element.90, pred[128]{0:T(512)(128)(4,1)S(1)} %get-tuple-element.92, ...), kind=kLoop, calls=%fused_computation.2 | loop fusion | flops 1048576 | bytes 2123008 | tf_op jit(solution)/shard_map/mul | solution.py:66
  21.8 6.8 %pad_maximum_fusion.refs_4_.refs_3_ = bf16[3,5120,256]{2,1,0:T(8,128)(2,1)} fusion(bf16[1,5120,256]{2,1,0:T(8,128)(2,1)} %bitcast.46, bf16[1,5120,256]{2,1,0:T(8,128)(2,1)} %bitcast.47, bf16[1,5120,256]{2,1,0:T(8,128)(2,1)} %bitcast.48), kind=kLoop, calls=%fused_computation | loop fusion | flops 7864320 | bytes 15728640 | tf_op jit(solution)/shard_map/stack | solution.py:373
  28.6 8.1 %collective-permute-done.refs_1_ = bf16[128,5120]{1,0:T(8,128)(2,1)} collective-permute-done((bf16[128,5120]{1,0:T(8,128)(2,1)S(1)}, bf16[128,5120]{1,0:T(8,128)(2,1)}, u32[]{:S(2)}, u32[]{:S(2)}) %collective-permute-start) | collective-permute-done | bytes 1310752 | tf_op jit(solution)/shard_map/ppermute | solution.py:112
  36.7 1.6 collective-permute-done.2.refs_3_
  38.3 1.9 %collective-permute-start.3 = (bf16[3,5120,256]{2,1,0:T(8,128)(2,1)}, bf16[3,5120,256]{2,1,0:T(8,128)(2,1)}, u32[]{:S(2)}, u32[]{:S(2)}) collective-permute-start(bf16[3,5120,256]{2,1,0:T(8,128)(2,1)} %pad_maximum_fusion.refs_4_.refs_3_), channel_id=1, source_target_pairs={{0,1},{1,0},{2,3},{3,2},{4,5},{5,4},{6,7},{7,6},{8,9},{9,8},{10,11... | collective-permute-start | bytes 23592968 | tf_op jit(solution)/shard_map/ppermute | solution.py:124
  40.2 2.7 %collective-permute-start.5 = (bf16[128,5120]{1,0:T(8,128)(2,1)}, bf16[128,5120]{1,0:T(8,128)(2,1)}, u32[]{:S(2)}, u32[]{:S(2)}) collective-permute-start(bf16[128,5120]{1,0:T(8,128)(2,1)} %collective-permute-done.2.refs_3_), channel_id=1, source_target_pairs={{0,6},{1,7},{2,0},{3,1},{4,2},{5,3},{6,4},{7,5},{8,14},{9,15},{10,... | collective-permute-start | bytes 3932168 | tf_op jit(solution)/shard_map/ppermute | solution.py:116
  42.8 1.5 collective-permute-start.6
  44.5 8.1 %collective-permute-done.3.refs_5_.refs_4_ = bf16[3,5120,256]{2,1,0:T(8,128)(2,1)} collective-permute-done((bf16[3,5120,256]{2,1,0:T(8,128)(2,1)}, bf16[3,5120,256]{2,1,0:T(8,128)(2,1)}, u32[]{:S(2)}, u32[]{:S(2)}) %collective-permute-start.3) | collective-permute-done | bytes 7864352 | tf_op jit(solution)/shard_map/ppermute | solution.py:124
  52.5 1.3 copy-done.5
  53.9 15.1 %project.3 = (bf16[3,512,256]{2,1,0:T(8,128)(2,1)S(1)}, bf16[3,512,256]{2,1,0:T(8,128)(2,1)}, f32[3,4,128]{2,1,0:T(4,128)S(1)}) custom-call(bf16[128,5120]{1,0:T(8,128)(2,1)S(1)} %copy-done.5, bf16[128,5120]{1,0:T(8,128)(2,1)} %collective-permute-done.refs_1_, bf16[128,5120]{1,0:T(8,128)(2,1)} %collective-permute-done.1.refs_2_, ...), custom_call_target="tpu_custom_call" | custom-call | flops 8053063680 | bytes 15728640 | tf_op jit(solution)/shard_map/project/pallas_call | solution.py:163
  69.0 3.1 %collective-permute-done.4.refs_0_ = bf16[128,5120]{1,0:T(8,128)(2,1)} collective-permute-done((bf16[128,5120]{1,0:T(8,128)(2,1)}, bf16[128,5120]{1,0:T(8,128)(2,1)}, u32[]{:S(2)}, u32[]{:S(2)}) %collective-permute-start.4) | collective-permute-done | bytes 1310752 | tf_op jit(solution)/shard_map/ppermute | solution.py:112
  72.9 1.1 slice.51
  74.1 1.1 slice.52
  75.1 2.7 %collective-permute-start.9 = (bf16[48,5120]{1,0:T(8,128)(2,1)S(1)}, bf16[48,5120]{1,0:T(8,128)(2,1)S(1)}, u32[]{:S(2)}, u32[]{:S(2)}) collective-permute-start(bf16[48,5120]{1,0:T(8,128)(2,1)S(1)} %slice.52), channel_id=1, source_target_pairs={{0,6},{1,7},{2,0},{3,1},{4,2},{5,3},{6,4},{7,5},{8,14},{9,15},{10,... | collective-permute-start | bytes 1474568 | tf_op jit(solution)/shard_map/ppermute | solution.py:116
  78.9 1.5 collective-permute-start.10
  80.4 2.3 %collective-permute-start.7 = (bf16[3,512,256]{2,1,0:T(8,128)(2,1)}, bf16[3,512,256]{2,1,0:T(8,128)(2,1)}, u32[]{:S(2)}, u32[]{:S(2)}) collective-permute-start(bf16[3,512,256]{2,1,0:T(8,128)(2,1)} %get-tuple-element.50), channel_id=1, source_target_pairs={{0,1},{1,0},{2,3},{3,2},{4,5},{5,4},{6,7},{7,6},{8,9},{9,8},{10,11... | collective-permute-start | bytes 2359304 | tf_op jit(solution)/shard_map/ppermute | solution.py:124
  82.7 13.1 %project.4 = (bf16[3,384,256]{2,1,0:T(8,128)(2,1)S(1)}, bf16[3,384,256]{2,1,0:T(8,128)(2,1)}, f32[3,3,128]{2,1,0:T(4,128)S(1)}) custom-call(bf16[128,5120]{1,0:T(8,128)(2,1)} %collective-permute-done.4.refs_0_, bf16[128,5120]{1,0:T(8,128)(2,1)} %collective-permute-done.6.refs_1_, bf16[128,5120]{1,0:T(8,128)(2,1)} %collective-permute-done.5.refs_2_, ...), custom_call_target="tpu_custom_call" | custom-call | flops 6039797760 | bytes 15728640 | tf_op jit(solution)/shard_map/project/pallas_call | solution.py:163
  95.9 7.8 %project.5 = (bf16[3,128,256]{2,1,0:T(8,128)(2,1)S(1)}, bf16[3,128,256]{2,1,0:T(8,128)(2,1)S(1)}, f32[3,1,128]{2,1,0:T(1,128)S(1)}) custom-call(bf16[48,5120]{1,0:T(8,128)(2,1)S(1)} %collective-permute-done.8.refs_0_, bf16[48,5120]{1,0:T(8,128)(2,1)S(1)} %collective-permute-done.9.refs_1_, bf16[32,5120]{1,0:T(8,128)(2,1)S(1)} %collective-permute-done.10.refs_2_, ...), custom_call_target="tpu_custom_call" | custom-call | flops 2013265920 | bytes 15728640 | tf_op jit(solution)/shard_map/project/pallas_call | solution.py:163
  105.8 4.4 %all-to-all-start = ((f32[16,16,128]{2,1,0:T(8,128)}), f32[16,16,128]{2,1,0:T(8,128)}, u32[]{:S(2)}, u32[]{:S(2)}) async-start(f32[16,16,128]{2,1,0:T(8,128)} %broadcast_in_dim.90), calls=%async_computation | async-start | bytes 262144 | tf_op jit(solution)/shard_map/all_to_all | solution.py:400
  110.5 5.9 %all-to-all-done = f32[16,16,128]{2,1,0:T(8,128)} async-done(((f32[16,16,128]{2,1,0:T(8,128)}), f32[16,16,128]{2,1,0:T(8,128)}, u32[]{:S(2)}, u32[]{:S(2)}) %all-to-all-start) | async-done | bytes 131104 | tf_op jit(solution)/shard_map/all_to_all | solution.py:400
  118.4 2.3 %halo_keys.1 = (bf16[512,256]{1,0:T(8,128)(2,1)S(1)}, bf16[512,256]{1,0:T(8,128)(2,1)S(1)}) custom-call(s32[16]{0:T(128)S(1)} %reshape.307.place_ref, bf16[3,512,256]{2,1,0:T(8,128)(2,1)S(1)} %get-tuple-element.49.fa, bf16[3,512,256]{2,1,0:T(8,128)(2,1)} %collective-permute-done.7.ga, bf16[3,384,256]{2,1,0:T(8,128)(2,1)S(1)} %get-tuple-element.57.fb, ...), custom_call_target="tpu_custom_call" | custom-call | flops 10000000 | bytes 3000000 | tf_op jit(solution)/shard_map/halo_keys/pallas_call | solution.py:230
  120.7 3.4 %collective-permute-start.13 = (bf16[512,256]{1,0:T(8,128)(2,1)S(1)}, bf16[512,256]{1,0:T(8,128)(2,1)S(1)}, u32[]{:S(2)}, u32[]{:S(2)}) collective-permute-start(bf16[512,256]{1,0:T(8,128)(2,1)S(1)} %get-tuple-element.70.before_ref), channel_id=1, source_target_pairs={{112,0},{0,16},{16,32},{32,48},{48,64},{64,80},{80,96},{96,112},{1... | collective-permute-start | bytes 786440 | tf_op jit(solution)/shard_map/ppermute | solution.py:351
  124.1 2.5 %collective-permute-start.14 = (bf16[512,256]{1,0:T(8,128)(2,1)S(1)}, bf16[512,256]{1,0:T(8,128)(2,1)S(1)}, u32[]{:S(2)}, u32[]{:S(2)}) collective-permute-start(bf16[512,256]{1,0:T(8,128)(2,1)S(1)} %get-tuple-element.71.after_ref), channel_id=1, source_target_pairs={{16,0},{32,16},{48,32},{64,48},{80,64},{96,80},{112,96},{0,112},{1... | collective-permute-start | bytes 786440 | tf_op jit(solution)/shard_map/ppermute | solution.py:351
  126.6 12.0 %window_attention.1.rest_0_ = bf16[16,2,144,128]{3,2,1,0:T(8,128)(2,1)S(1)} custom-call(s32[16]{0:T(128)S(1)} %reshape.307.place_ref, bf16[3,512,256]{2,1,0:T(8,128)(2,1)S(1)} %get-tuple-element.49.fa, bf16[3,512,256]{2,1,0:T(8,128)(2,1)} %collective-permute-done.7.ga, bf16[3,384,256]{2,1,0:T(8,128)(2,1)S(1)} %get-tuple-element.57.fb, ...), custom_call_target="tpu_custom_call" | custom-call | flops 1500000000 | bytes 10000000 | tf_op jit(solution)/shard_map/window_attention/pallas_call | solution.py:326
  138.9 5.3 %window_attention_halo.1 = bf16[16,2,144,128]{3,2,1,0:T(8,128)(2,1)S(1)} custom-call(s32[16]{0:T(128)S(1)} %reshape.307.place_ref, bf16[3,512,256]{2,1,0:T(8,128)(2,1)S(1)} %get-tuple-element.49.fa, bf16[3,512,256]{2,1,0:T(8,128)(2,1)} %collective-permute-done.7.ga, bf16[3,384,256]{2,1,0:T(8,128)(2,1)S(1)} %get-tuple-element.57.fb, ...), custom_call_target="tpu_custom_call", output_to_operand_aliasing={{}: (15, {})} | custom-call | flops 500000000 | bytes 10000000 | tf_op jit(solution)/shard_map/window_attention_halo/pallas_call | solution.py:326
  144.2 20.3 %all_to_all.10 = bf16[16,2,144,128]{3,2,1,0:T(8,128)(2,1)S(1)} all-to-all(bf16[16,2,144,128]{3,2,1,0:T(8,128)(2,1)S(1)} %window_attention_halo.1), channel_id=1, replica_groups=mesh['sx'=8,'sy'=16] {'sy'}, dimensions={0} | all-to-all | bytes 2359296 | tf_op jit(solution)/shard_map/all_to_all | solution.py:407
  165.3 1.3 copy.21
  (64 shorter events, 11.9 us)
Async XLA Ops:
  0.6 1.3 copy-start.3
  1.9 0.7 copy-start.6
  2.7 0.7 copy-start.7
  5.1 23.5 %copy-start.4 = (bf16[128,5120]{1,0:T(8,128)(2,1)}, bf16[128,5120]{1,0:T(8,128)(2,1)S(1)}, u32[]{:S(2)}) copy-start(bf16[128,5120]{1,0:T(8,128)(2,1)S(1)} %layer_norm.1.refs_0_) | copy-start | bytes 3932164
  5.1 31.5 %collective-permute-start = (bf16[128,5120]{1,0:T(8,128)(2,1)S(1)}, bf16[128,5120]{1,0:T(8,128)(2,1)}, u32[]{:S(2)}, u32[]{:S(2)}) collective-permute-start(bf16[128,5120]{1,0:T(8,128)(2,1)S(1)} %layer_norm.1.refs_0_), channel_id=1, source_target_pairs={{0,2},{1,3},{2,4},{3,5},{4,6},{5,7},{6,0},{7,1},{8,10},{9,11},{10,... | collective-permute-start | bytes 3932168 | tf_op jit(solution)/shard_map/ppermute | solution.py:112
  7.2 29.4 %collective-permute-start.1 = (bf16[128,5120]{1,0:T(8,128)(2,1)S(1)}, bf16[128,5120]{1,0:T(8,128)(2,1)}, u32[]{:S(2)}, u32[]{:S(2)}) collective-permute-start(bf16[128,5120]{1,0:T(8,128)(2,1)S(1)} %layer_norm.1.refs_0_), channel_id=1, source_target_pairs={{0,6},{1,7},{2,0},{3,1},{4,2},{5,3},{6,4},{7,5},{8,14},{9,15},{10,... | collective-permute-start | bytes 3932168 | tf_op jit(solution)/shard_map/ppermute | solution.py:116
  8.6 29.7 %collective-permute-start.2 = (bf16[128,5120]{1,0:T(8,128)(2,1)S(1)}, bf16[128,5120]{1,0:T(8,128)(2,1)}, u32[]{:S(2)}, u32[]{:S(2)}) collective-permute-start(bf16[128,5120]{1,0:T(8,128)(2,1)S(1)} %layer_norm.1.refs_0_), channel_id=1, source_target_pairs={{0,8},{1,9},{2,10},{3,11},{4,12},{5,13},{6,14},{7,15},{8,0},{9,1},... | collective-permute-start | bytes 3932168 | tf_op jit(solution)/shard_map/ppermute | solution.py:120
  38.3 14.3 %collective-permute-start.3 = (bf16[3,5120,256]{2,1,0:T(8,128)(2,1)}, bf16[3,5120,256]{2,1,0:T(8,128)(2,1)}, u32[]{:S(2)}, u32[]{:S(2)}) collective-permute-start(bf16[3,5120,256]{2,1,0:T(8,128)(2,1)} %pad_maximum_fusion.refs_4_.refs_3_), channel_id=1, source_target_pairs={{0,1},{1,0},{2,3},{3,2},{4,5},{5,4},{6,7},{7,6},{8,9},{9,8},{10,11... | collective-permute-start | bytes 23592968 | tf_op jit(solution)/shard_map/ppermute | solution.py:124
  40.2 31.9 %collective-permute-start.4 = (bf16[128,5120]{1,0:T(8,128)(2,1)}, bf16[128,5120]{1,0:T(8,128)(2,1)}, u32[]{:S(2)}, u32[]{:S(2)}) collective-permute-start(bf16[128,5120]{1,0:T(8,128)(2,1)} %collective-permute-done.refs_1_), channel_id=1, source_target_pairs={{0,2},{1,3},{2,4},{3,5},{4,6},{5,7},{6,0},{7,1},{8,10},{9,11},{10,... | collective-permute-start | bytes 3932168 | tf_op jit(solution)/shard_map/ppermute | solution.py:112
  40.2 31.9 %collective-permute-start.5 = (bf16[128,5120]{1,0:T(8,128)(2,1)}, bf16[128,5120]{1,0:T(8,128)(2,1)}, u32[]{:S(2)}, u32[]{:S(2)}) collective-permute-start(bf16[128,5120]{1,0:T(8,128)(2,1)} %collective-permute-done.2.refs_3_), channel_id=1, source_target_pairs={{0,6},{1,7},{2,0},{3,1},{4,2},{5,3},{6,4},{7,5},{8,14},{9,15},{10,... | collective-permute-start | bytes 3932168 | tf_op jit(solution)/shard_map/ppermute | solution.py:116
  42.8 30.1 %collective-permute-start.6 = (bf16[128,5120]{1,0:T(8,128)(2,1)}, bf16[128,5120]{1,0:T(8,128)(2,1)}, u32[]{:S(2)}, u32[]{:S(2)}) collective-permute-start(bf16[128,5120]{1,0:T(8,128)(2,1)} %collective-permute-done.refs_1_), channel_id=1, source_target_pairs={{0,8},{1,9},{2,10},{3,11},{4,12},{5,13},{6,14},{7,15},{8,0},{9,1},... | collective-permute-start | bytes 3932168 | tf_op jit(solution)/shard_map/ppermute | solution.py:120
  52.5 1.3 copy-start.5
  74.0 21.8 %collective-permute-start.8 = (bf16[48,5120]{1,0:T(8,128)(2,1)S(1)}, bf16[48,5120]{1,0:T(8,128)(2,1)S(1)}, u32[]{:S(2)}, u32[]{:S(2)}) collective-permute-start(bf16[48,5120]{1,0:T(8,128)(2,1)S(1)} %slice.51), channel_id=1, source_target_pairs={{0,2},{1,3},{2,4},{3,5},{4,6},{5,7},{6,0},{7,1},{8,10},{9,11},{10,... | collective-permute-start | bytes 1474568 | tf_op jit(solution)/shard_map/ppermute | solution.py:112
  75.1 20.7 %collective-permute-start.9 = (bf16[48,5120]{1,0:T(8,128)(2,1)S(1)}, bf16[48,5120]{1,0:T(8,128)(2,1)S(1)}, u32[]{:S(2)}, u32[]{:S(2)}) collective-permute-start(bf16[48,5120]{1,0:T(8,128)(2,1)S(1)} %slice.52), channel_id=1, source_target_pairs={{0,6},{1,7},{2,0},{3,1},{4,2},{5,3},{6,4},{7,5},{8,14},{9,15},{10,... | collective-permute-start | bytes 1474568 | tf_op jit(solution)/shard_map/ppermute | solution.py:116
  78.9 16.9 %collective-permute-start.10 = (bf16[32,5120]{1,0:T(8,128)(2,1)S(1)}, bf16[32,5120]{1,0:T(8,128)(2,1)S(1)}, u32[]{:S(2)}, u32[]{:S(2)}) collective-permute-start(bf16[32,5120]{1,0:T(8,128)(2,1)S(1)} %slice.53), channel_id=1, source_target_pairs={{0,8},{1,9},{2,10},{3,11},{4,12},{5,13},{6,14},{7,15},{8,0},{9,1},... | collective-permute-start | bytes 983048 | tf_op jit(solution)/shard_map/ppermute | solution.py:120
  80.4 37.0 %collective-permute-start.7 = (bf16[3,512,256]{2,1,0:T(8,128)(2,1)}, bf16[3,512,256]{2,1,0:T(8,128)(2,1)}, u32[]{:S(2)}, u32[]{:S(2)}) collective-permute-start(bf16[3,512,256]{2,1,0:T(8,128)(2,1)} %get-tuple-element.50), channel_id=1, source_target_pairs={{0,1},{1,0},{2,3},{3,2},{4,5},{5,4},{6,7},{7,6},{8,9},{9,8},{10,11... | collective-permute-start | bytes 2359304 | tf_op jit(solution)/shard_map/ppermute | solution.py:124
  95.8 21.6 %collective-permute-start.11 = (bf16[3,384,256]{2,1,0:T(8,128)(2,1)}, bf16[3,384,256]{2,1,0:T(8,128)(2,1)}, u32[]{:S(2)}, u32[]{:S(2)}) collective-permute-start(bf16[3,384,256]{2,1,0:T(8,128)(2,1)} %get-tuple-element.58), channel_id=1, source_target_pairs={{0,1},{1,0},{2,3},{3,2},{4,5},{5,4},{6,7},{7,6},{8,9},{9,8},{10,11... | collective-permute-start | bytes 1769480 | tf_op jit(solution)/shard_map/ppermute | solution.py:124
  103.7 0.7 copy-start
  104.4 0.7 copy-start.8
  105.8 10.6 %all-to-all-start = ((f32[16,16,128]{2,1,0:T(8,128)}), f32[16,16,128]{2,1,0:T(8,128)}, u32[]{:S(2)}, u32[]{:S(2)}) async-start(f32[16,16,128]{2,1,0:T(8,128)} %broadcast_in_dim.90), calls=%async_computation | async-start | bytes 262144 | tf_op jit(solution)/shard_map/all_to_all | solution.py:400
  110.2 7.2 %collective-permute-start.12 = (bf16[3,128,256]{2,1,0:T(8,128)(2,1)}, bf16[3,128,256]{2,1,0:T(8,128)(2,1)}, u32[]{:S(2)}, u32[]{:S(2)}) collective-permute-start(bf16[3,128,256]{2,1,0:T(8,128)(2,1)} %copy-done.8), channel_id=1, source_target_pairs={{0,1},{1,0},{2,3},{3,2},{4,5},{5,4},{6,7},{7,6},{8,9},{9,8},{10,11... | collective-permute-start | bytes 589832 | tf_op jit(solution)/shard_map/ppermute | solution.py:124
  117.4 0.9 copy-start.1
  118.4 8.3 %copy-start.2 = (bf16[3,128,256]{2,1,0:T(8,128)(2,1)S(1)}, bf16[3,128,256]{2,1,0:T(8,128)(2,1)}, u32[]{:S(2)}) copy-start(bf16[3,128,256]{2,1,0:T(8,128)(2,1)} %copy-done) | copy-start | bytes 589828
  120.7 17.9 %collective-permute-start.13 = (bf16[512,256]{1,0:T(8,128)(2,1)S(1)}, bf16[512,256]{1,0:T(8,128)(2,1)S(1)}, u32[]{:S(2)}, u32[]{:S(2)}) collective-permute-start(bf16[512,256]{1,0:T(8,128)(2,1)S(1)} %get-tuple-element.70.before_ref), channel_id=1, source_target_pairs={{112,0},{0,16},{16,32},{32,48},{48,64},{64,80},{80,96},{96,112},{1... | collective-permute-start | bytes 786440 | tf_op jit(solution)/shard_map/ppermute | solution.py:351
  124.1 14.8 %collective-permute-start.14 = (bf16[512,256]{1,0:T(8,128)(2,1)S(1)}, bf16[512,256]{1,0:T(8,128)(2,1)S(1)}, u32[]{:S(2)}, u32[]{:S(2)}) collective-permute-start(bf16[512,256]{1,0:T(8,128)(2,1)S(1)} %get-tuple-element.71.after_ref), channel_id=1, source_target_pairs={{16,0},{32,16},{48,32},{64,48},{80,64},{96,80},{112,96},{0,112},{1... | collective-permute-start | bytes 786440 | tf_op jit(solution)/shard_map/ppermute | solution.py:351

commit v5 on v4

--- a/solution.py
+++ b/solution.py
@@ -40,7 +40,7 @@
         in_specs=[block, vector, vector],
         out_specs=block,
         out_shape=jax.ShapeDtypeStruct((rows, wide), jnp.bfloat16),
-        compiler_params=pltpu.CompilerParams(vmem_limit_bytes=16 * 1024 * 1024),
+        compiler_params=pltpu.CompilerParams(vmem_limit_bytes=60 * 1024 * 1024),
         cost_estimate=pl.CostEstimate(flops=10 * rows * wide, bytes_accessed=4 * rows * wide, transcendentals=rows),
         name="layer_norm",
     )(values, mod_shift.reshape(1, wide), mod_scale.reshape(1, wide))
@@ -175,6 +175,30 @@
         ),
         name="project",
     )(*arrays, own_w, other_w)
+
+
+def cut_kernel(cuts, *refs):
+    n = len(cuts)
+    copies = [
+        pltpu.make_async_copy(refs[i].at[pl.ds(first, count)], refs[n + i], refs[2 * n].at[i])
+        for i, (first, count) in enumerate(cuts)
+    ]
+    for copy in copies:
+        copy.start()
+    for copy in copies:
+        copy.wait()
+
+
+def cut(arrays, cuts):
+    return pl.pallas_call(
+        functools.partial(cut_kernel, cuts),
+        in_specs=[ANYWHERE] * len(cuts),
+        out_specs=[ANYWHERE] * len(cuts),
+        out_shape=[jax.ShapeDtypeStruct((count, a.shape[1]), a.dtype) for a, (_, count) in zip(arrays, cuts)],
+        scratch_shapes=[pltpu.SemaphoreType.DMA((len(cuts),))],
+        cost_estimate=pl.CostEstimate(flops=10**5, bytes_accessed=3 * 10**6, transcendentals=0),
+        name="cut_rows",
+    )(*arrays)
 
 
 def sources(refs):
@@ -370,21 +394,22 @@
 
     own = layer_norm(tokens, mod_shift, mod_scale)
     left, right, beside = from_left(own), from_right(own), from_z(own)
-    own_w = jnp.stack(barrier((w_key, w_query, w_value, own))[:3])
+    key_w, query_w, value_w = barrier((w_key, w_query, w_value, own))[:3]
+    own_w, sent_w = jnp.stack([key_w, query_w, value_w]), jnp.stack([value_w, query_w, key_w])
     cosine, sine = rope_tables(group * rows + jnp.arange(rows, dtype=jnp.int32))
     gq = lax.dynamic_slice(query_gain, (mine * 2 * HD,), (2 * HD,)).reshape(1, 2 * HD)
     gk = lax.dynamic_slice(key_gain, (mine * 2 * HD,), (2 * HD,)).reshape(1, 2 * HD)
-    (left, right, beside), own_w, (cosine, sine, gq, gk, place) = barrier(
-        ((left, right, beside), own_w, (cosine, sine, gq, gk, place))
+    (left, right, beside), own_w, sent_w, (cosine, sine, gq, gk, place) = barrier(
+        ((left, right, beside), own_w, sent_w, (cosine, sine, gq, gk, place))
     )
 
     far, z_right, z_left = from_left(left), from_right(beside), from_z(left)
-    other_w = from_core(own_w)
+    other_w = lax.rev(from_core(sent_w), (0,))
     near = project((own, left, right, beside), tuple((i, 0, BLK) for i in range(4)), own_w, other_w)
     near, far, z_right, z_left = barrier((near, far, z_right, z_left))
 
-    cuts = (48, 96)
-    z_far = (from_left(z_left[: cuts[0]]), from_right(z_right[cuts[0] : cuts[1]]), from_z(far[cuts[1] :]))
+    part_left, part_right, part_z = cut((z_left, z_right, far), ((0, 48), (48, 48), (96, 32)))
+    z_far = (from_left(part_left), from_right(part_right), from_z(part_z))
     middle = project((far, z_left, z_right), tuple((i, 0, BLK) for i in range(3)), own_w, other_w)
     z_far, middle = barrier((z_far, middle))
     last = project(z_far, tuple((i, 0, p.shape[0]) for i, p in enumerate(z_far)), own_w, other_w)

time: 168 us -> 211 us (1.26)
  Pallas kernels: 57.3 us -> 89.1 us
  local copies, waits for them, and re-layouts: 14.3 us -> 31.5 us
  waiting for transfers between devices: 27.9 us -> 18.5 us
  other arithmetic: 18 us -> 22.7 us
    pallas_call x0 -> x1, Pallas kernels: none -> 40.8 us  [cut(): pl.pallas_call(functools.partial(cut_kernel, cuts), in_specs=[ANYWHERE] *...]
    unnamed x19 -> x25, local copies, waits for them, and re-layouts: 7.67 us -> 21.1 us
    pallas_call x3, Pallas kernels: 35.9 us -> 24.4 us  [project(): pl.pallas_call(functools.partial(project_kernel, cuts), grid=(3,), in_spe...]
    ppermute x3, waiting for transfers between devices: 11.2 us -> 3.57 us  [from_left(): return lax.ppermute(block, 'sy', chip_move(0, 1, 0))]
    rev x0 -> x1, local copies, waits for them, and re-layouts: none -> 6.83 us  [body(): other_w = lax.rev(from_core(sent_w), (0,))]
    another operation x1, other arithmetic: 6.82 us -> 11.5 us  [body(): jnp.stack([value_w, query_w, key_w])]
    slice x3 -> x0, local copies, waits for them, and re-layouts: 3.12 us -> none  [the longest x1 1.06 us: body(): z_right[cuts[0]:cuts[1]]]
    pallas_call x1, Pallas kernels: 1.7 us -> 4.27 us  [layer_norm(): pl.pallas_call(layer_norm_kernel, grid=(rows // 32,), in_specs=[block, ve...]
  transfers between devices with their start and end apart: 16 -> 16, of which waited for: 7 -> 5; matrix products, arithmetic and copies ran while one was open for 13% -> 15% of each run, Pallas kernels for 29% -> 17%
where the time goes in v5:
time: 211 us; the launch traced here: 210 us
  Pallas kernels  89.1 us (42%)
  local copies, waits for them, and re-layouts  31.5 us (15%)
  starting transfers between devices  27.2 us (13%)
  other arithmetic  22.7 us (11%)
  blocking collectives  20.3 us (10%)
  waiting for transfers between devices  18.5 us (9%)
    pallas_call x1, Pallas kernels, cut(): pl.pallas_call(functools.partial(cut_kernel, cuts), in_specs=[ANYWHERE] *...  40.8 us
    pallas_call x3, Pallas kernels, project(): pl.pallas_call(functools.partial(project_kernel, cuts), grid=(3,), in_spe...  24.4 us
    unnamed x25, local copies, waits for them, and re-layouts  21.1 us
    all_to_all x1, blocking collectives, body(): arrived = lax.all_to_all(out, 'sy', split_axis=0, concat_axis=0, tiled=True)  20.3 us
    pallas_call x2, Pallas kernels, attention(): pl.pallas_call(functools.partial(attention_kernel, part), grid=(steps, 2)...  17.3 us
    another operation x1, other arithmetic, body(): jnp.stack([value_w, query_w, key_w])  11.5 us
    mul x1, other arithmetic, rope_tables(): return (jnp.cos(angles), jnp.sin(angles) * sign)  9.21 us
    ppermute x4, waiting for transfers between devices, from_core(): return lax.ppermute(block, 'sy', chip_move(0, 0, 1))  8.12 us
  transfers between devices with their start and end apart: 16, of which 5 were waited for; matrix products, arithmetic and copies ran while one was open for 15% of the time, Pallas kernels for 17%

profile of v5, /device:TPU:1, one launch (start us, length us, event | category | flops | bytes accessed | tf_op | source)
XLA Modules:
  0.0 210.2 jit_solution(10691123423987309456)
XLA Ops:
  0.6 4.3 %layer_norm.1.refs_0_ = bf16[128,5120]{1,0:T(8,128)(2,1)} custom-call(bf16[128,5120]{1,0:T(8,128)(2,1)} %tokens_ref.1, f32[1,5120]{1,0:T(1,128)} %bitcast.49, f32[1,5120]{1,0:T(1,128)} %bitcast.50), custom_call_target="tpu_custom_call" | custom-call | flops 6553600 | bytes 2621440 | tf_op jit(solution)/shard_map/layer_norm/pallas_call | solution.py:37
  4.9 2.0 collective-permute-start
  8.2 1.8 collective-permute-start.2
  12.3 9.2 %sine_multiply_fusion = (f32[2048,128]{1,0:T(8,128)S(1)}, f32[2048,128]{1,0:T(8,128)S(1)}) fusion(f32[128]{0:T(128)S(1)} %compare_select_fusion, f32[128]{0:T(128)S(1)} %mul.55, f32[2048]{0:T(1024)S(1)} %fusion.6, f32[2048]{0:T(1024)S(1)} %get-tuple-element.101, f32[2048]{0:T(1024)S(1)} %get-tuple-element.100, pred[128]{0:T(512)(128)(4,1)S(1)} %get-tuple-element.102, ...), kind=kLoop, calls=%fused_computation.5 | loop fusion | flops 1048576 | bytes 2123008 | tf_op jit(solution)/shard_map/mul | solution.py:66
  21.5 11.5 %fusion.1 = (bf16[3,5120,256]{2,1,0:T(8,128)(2,1)}, bf16[3,5120,256]{2,1,0:T(8,128)(2,1)}) fusion(bf16[1,5120,256]{2,1,0:T(8,128)(2,1)} %bitcast.44, bf16[1,5120,256]{2,1,0:T(8,128)(2,1)} %bitcast.45, bf16[1,5120,256]{2,1,0:T(8,128)(2,1)} %bitcast.46), kind=kLoop, calls=%fused_computation.3 | loop fusion | flops 15728640 | bytes 23592960 | tf_op jit(solution)/shard_map/stack | solution.py:398
  33.0 3.6 %collective-permute-done.refs_1_ = bf16[128,5120]{1,0:T(8,128)(2,1)} collective-permute-done((bf16[128,5120]{1,0:T(8,128)(2,1)}, bf16[128,5120]{1,0:T(8,128)(2,1)}, u32[]{:S(2)}, u32[]{:S(2)}) %collective-permute-start) | collective-permute-done | bytes 1310752 | tf_op jit(solution)/shard_map/ppermute | solution.py:112
  38.3 1.9 collective-permute-start.3
  40.6 2.2 %collective-permute-start.5 = (bf16[128,5120]{1,0:T(8,128)(2,1)}, bf16[128,5120]{1,0:T(8,128)(2,1)}, u32[]{:S(2)}, u32[]{:S(2)}) collective-permute-start(bf16[128,5120]{1,0:T(8,128)(2,1)} %collective-permute-done.2.refs_3_), channel_id=1, source_target_pairs={{0,6},{1,7},{2,0},{3,1},{4,2},{5,3},{6,4},{7,5},{8,14},{9,15},{10,... | collective-permute-start | bytes 3932168 | tf_op jit(solution)/shard_map/ppermute | solution.py:116
  42.8 1.4 collective-permute-start.6
  44.4 8.1 %collective-permute-done.3 = bf16[3,5120,256]{2,1,0:T(8,128)(2,1)} collective-permute-done((bf16[3,5120,256]{2,1,0:T(8,128)(2,1)}, bf16[3,5120,256]{2,1,0:T(8,128)(2,1)}, u32[]{:S(2)}, u32[]{:S(2)}) %collective-permute-start.3) | collective-permute-done | bytes 7864352 | tf_op jit(solution)/shard_map/ppermute | solution.py:124
  52.5 6.8 %rev.3.refs_5_.refs_4_ = bf16[3,5120,256]{2,1,0:T(8,128)(2,1)} reverse(bf16[3,5120,256]{2,1,0:T(8,128)(2,1)} %collective-permute-done.3), dimensions={0} | reverse | bytes 15728640 | tf_op jit(solution)/shard_map/rev | solution.py:407
  59.3 3.2 %copy-done = bf16[3,5120,256]{2,1,0:T(8,128)(2,1)S(1)} copy-done((bf16[3,5120,256]{2,1,0:T(8,128)(2,1)S(1)}, bf16[3,5120,256]{2,1,0:T(8,128)(2,1)}, u32[]{:S(2)}) %copy-start) | copy-done | bytes 7864344
  62.6 3.2 %copy-done.2 = bf16[3,5120,256]{2,1,0:T(8,128)(2,1)S(1)} copy-done((bf16[3,5120,256]{2,1,0:T(8,128)(2,1)S(1)}, bf16[3,5120,256]{2,1,0:T(8,128)(2,1)}, u32[]{:S(2)}) %copy-start.2) | copy-done | bytes 7864344
  65.8 1.3 copy-done.7
  67.1 1.3 copy-done.9
  68.4 11.0 %project.3 = (bf16[3,512,256]{2,1,0:T(8,128)(2,1)S(1)}, bf16[3,512,256]{2,1,0:T(8,128)(2,1)S(1)}, f32[3,4,128]{2,1,0:T(4,128)S(1)}) custom-call(bf16[128,5120]{1,0:T(8,128)(2,1)S(1)} %copy-done.7, bf16[128,5120]{1,0:T(8,128)(2,1)} %collective-permute-done.refs_1_, bf16[128,5120]{1,0:T(8,128)(2,1)S(1)} %copy-done.9, ...), custom_call_target="tpu_custom_call" | custom-call | flops 8053063680 | bytes 15728640 | tf_op jit(solution)/shard_map/project/pallas_call | solution.py:163
  80.4 40.8 %cut_rows.1 = (bf16[48,5120]{1,0:T(8,128)(2,1)}, bf16[48,5120]{1,0:T(8,128)(2,1)}, bf16[32,5120]{1,0:T(8,128)(2,1)}) custom-call(bf16[128,5120]{1,0:T(8,128)(2,1)} %collective-permute-done.6.refs_0_.refs_1_, bf16[128,5120]{1,0:T(8,128)(2,1)} %collective-permute-done.5.refs_1_.refs_2_, bf16[128,5120]{1,0:T(8,128)(2,1)} %collective-permute-done.4.refs_2_.refs_0_), custom_call_target="tpu_custom_call" | custom-call | flops 100000 | bytes 3000000 | tf_op jit(solution)/shard_map/cut_rows/pallas_call | solution.py:193
  121.8 2.2 %collective-permute-start.9 = (bf16[48,5120]{1,0:T(8,128)(2,1)}, bf16[48,5120]{1,0:T(8,128)(2,1)S(1)}, u32[]{:S(2)}, u32[]{:S(2)}) collective-permute-start(bf16[48,5120]{1,0:T(8,128)(2,1)} %get-tuple-element.60), channel_id=1, source_target_pairs={{0,6},{1,7},{2,0},{3,1},{4,2},{5,3},{6,4},{7,5},{8,14},{9,15},{10,... | collective-permute-start | bytes 1474568 | tf_op jit(solution)/shard_map/ppermute | solution.py:116
  124.0 1.4 collective-permute-start.10
  126.6 3.2 %copy-done.1 = bf16[3,5120,256]{2,1,0:T(8,128)(2,1)S(1)} copy-done((bf16[3,5120,256]{2,1,0:T(8,128)(2,1)S(1)}, bf16[3,5120,256]{2,1,0:T(8,128)(2,1)}, u32[]{:S(2)}) %copy-start.1) | copy-done | bytes 7864344
  129.8 3.2 %copy-done.3 = bf16[3,5120,256]{2,1,0:T(8,128)(2,1)S(1)} copy-done((bf16[3,5120,256]{2,1,0:T(8,128)(2,1)S(1)}, bf16[3,5120,256]{2,1,0:T(8,128)(2,1)}, u32[]{:S(2)}) %copy-start.3) | copy-done | bytes 7864344
  133.1 9.6 %project.4 = (bf16[3,384,256]{2,1,0:T(8,128)(2,1)S(1)}, bf16[3,384,256]{2,1,0:T(8,128)(2,1)}, f32[3,3,128]{2,1,0:T(4,128)S(1)}) custom-call(bf16[128,5120]{1,0:T(8,128)(2,1)} %collective-permute-done.4.refs_2_.refs_0_, bf16[128,5120]{1,0:T(8,128)(2,1)} %collective-permute-done.6.refs_0_.refs_1_, bf16[128,5120]{1,0:T(8,128)(2,1)} %collective-permute-done.5.refs_1_.refs_2_, ...), custom_call_target="tpu_custom_call" | custom-call | flops 6039797760 | bytes 15728640 | tf_op jit(solution)/shard_map/project/pallas_call | solution.py:163
  142.9 3.7 %project.5 = (bf16[3,128,256]{2,1,0:T(8,128)(2,1)S(1)}, bf16[3,128,256]{2,1,0:T(8,128)(2,1)S(1)}, f32[3,1,128]{2,1,0:T(1,128)S(1)}) custom-call(bf16[48,5120]{1,0:T(8,128)(2,1)S(1)} %collective-permute-done.8.refs_0_, bf16[48,5120]{1,0:T(8,128)(2,1)S(1)} %collective-permute-done.9.refs_1_, bf16[32,5120]{1,0:T(8,128)(2,1)S(1)} %collective-permute-done.10.refs_2_, ...), custom_call_target="tpu_custom_call" | custom-call | flops 2013265920 | bytes 15728640 | tf_op jit(solution)/shard_map/project/pallas_call | solution.py:163
  148.7 4.4 %all-to-all-start = ((f32[16,16,128]{2,1,0:T(8,128)}), f32[16,16,128]{2,1,0:T(8,128)}, u32[]{:S(2)}, u32[]{:S(2)}) async-start(f32[16,16,128]{2,1,0:T(8,128)} %broadcast_in_dim.90), calls=%async_computation | async-start | bytes 262144 | tf_op jit(solution)/shard_map/all_to_all | solution.py:425
  153.4 5.9 %all-to-all-done = f32[16,16,128]{2,1,0:T(8,128)} async-done(((f32[16,16,128]{2,1,0:T(8,128)}), f32[16,16,128]{2,1,0:T(8,128)}, u32[]{:S(2)}, u32[]{:S(2)}) %all-to-all-start) | async-done | bytes 131104 | tf_op jit(solution)/shard_map/all_to_all | solution.py:425
  161.2 2.3 %halo_keys.1 = (bf16[512,256]{1,0:T(8,128)(2,1)S(1)}, bf16[512,256]{1,0:T(8,128)(2,1)S(1)}) custom-call(s32[16]{0:T(128)S(1)} %reshape.307.place_ref, bf16[3,512,256]{2,1,0:T(8,128)(2,1)S(1)} %get-tuple-element.54.fa, bf16[3,512,256]{2,1,0:T(8,128)(2,1)} %collective-permute-done.7.ga, bf16[3,384,256]{2,1,0:T(8,128)(2,1)S(1)} %get-tuple-element.65.fb, ...), custom_call_target="tpu_custom_call" | custom-call | flops 10000000 | bytes 3000000 | tf_op jit(solution)/shard_map/halo_keys/pallas_call | solution.py:254
  163.5 3.4 %collective-permute-start.13 = (bf16[512,256]{1,0:T(8,128)(2,1)S(1)}, bf16[512,256]{1,0:T(8,128)(2,1)S(1)}, u32[]{:S(2)}, u32[]{:S(2)}) collective-permute-start(bf16[512,256]{1,0:T(8,128)(2,1)S(1)} %get-tuple-element.78.before_ref), channel_id=1, source_target_pairs={{112,0},{0,16},{16,32},{32,48},{48,64},{64,80},{80,96},{96,112},{1... | collective-permute-start | bytes 786440 | tf_op jit(solution)/shard_map/ppermute | solution.py:375
  166.9 2.5 %collective-permute-start.14 = (bf16[512,256]{1,0:T(8,128)(2,1)S(1)}, bf16[512,256]{1,0:T(8,128)(2,1)S(1)}, u32[]{:S(2)}, u32[]{:S(2)}) collective-permute-start(bf16[512,256]{1,0:T(8,128)(2,1)S(1)} %get-tuple-element.79.after_ref), channel_id=1, source_target_pairs={{16,0},{32,16},{48,32},{64,48},{80,64},{96,80},{112,96},{0,112},{1... | collective-permute-start | bytes 786440 | tf_op jit(solution)/shard_map/ppermute | solution.py:375
  169.4 12.0 %window_attention.1.rest_0_ = bf16[16,2,144,128]{3,2,1,0:T(8,128)(2,1)S(1)} custom-call(s32[16]{0:T(128)S(1)} %reshape.307.place_ref, bf16[3,512,256]{2,1,0:T(8,128)(2,1)S(1)} %get-tuple-element.54.fa, bf16[3,512,256]{2,1,0:T(8,128)(2,1)} %collective-permute-done.7.ga, bf16[3,384,256]{2,1,0:T(8,128)(2,1)S(1)} %get-tuple-element.65.fb, ...), custom_call_target="tpu_custom_call" | custom-call | flops 1500000000 | bytes 10000000 | tf_op jit(solution)/shard_map/window_attention/pallas_call | solution.py:350
  181.7 5.3 %window_attention_halo.1 = bf16[16,2,144,128]{3,2,1,0:T(8,128)(2,1)S(1)} custom-call(s32[16]{0:T(128)S(1)} %reshape.307.place_ref, bf16[3,512,256]{2,1,0:T(8,128)(2,1)S(1)} %get-tuple-element.54.fa, bf16[3,512,256]{2,1,0:T(8,128)(2,1)} %collective-permute-done.7.ga, bf16[3,384,256]{2,1,0:T(8,128)(2,1)S(1)} %get-tuple-element.65.fb, ...), custom_call_target="tpu_custom_call", output_to_operand_aliasing={{}: (15, {})} | custom-call | flops 500000000 | bytes 10000000 | tf_op jit(solution)/shard_map/window_attention_halo/pallas_call | solution.py:350
  187.1 20.3 %all_to_all.10 = bf16[16,2,144,128]{3,2,1,0:T(8,128)(2,1)S(1)} all-to-all(bf16[16,2,144,128]{3,2,1,0:T(8,128)(2,1)S(1)} %window_attention_halo.1), channel_id=1, replica_groups=mesh['sx'=8,'sy'=16] {'sy'}, dimensions={0} | all-to-all | bytes 2359296 | tf_op jit(solution)/shard_map/all_to_all | solution.py:432
  208.2 1.3 copy.21
  (69 shorter events, 14.7 us)
Async XLA Ops:
  4.9 31.7 %collective-permute-start = (bf16[128,5120]{1,0:T(8,128)(2,1)}, bf16[128,5120]{1,0:T(8,128)(2,1)}, u32[]{:S(2)}, u32[]{:S(2)}) collective-permute-start(bf16[128,5120]{1,0:T(8,128)(2,1)} %layer_norm.1.refs_0_), channel_id=1, source_target_pairs={{0,2},{1,3},{2,4},{3,5},{4,6},{5,7},{6,0},{7,1},{8,10},{9,11},{10,... | collective-permute-start | bytes 3932168 | tf_op jit(solution)/shard_map/ppermute | solution.py:112
  6.9 29.6 %collective-permute-start.1 = (bf16[128,5120]{1,0:T(8,128)(2,1)}, bf16[128,5120]{1,0:T(8,128)(2,1)S(1)}, u32[]{:S(2)}, u32[]{:S(2)}) collective-permute-start(bf16[128,5120]{1,0:T(8,128)(2,1)} %layer_norm.1.refs_0_), channel_id=1, source_target_pairs={{0,6},{1,7},{2,0},{3,1},{4,2},{5,3},{6,4},{7,5},{8,14},{9,15},{10,... | collective-permute-start | bytes 3932168 | tf_op jit(solution)/shard_map/ppermute | solution.py:116
  8.2 30.0 %collective-permute-start.2 = (bf16[128,5120]{1,0:T(8,128)(2,1)}, bf16[128,5120]{1,0:T(8,128)(2,1)}, u32[]{:S(2)}, u32[]{:S(2)}) collective-permute-start(bf16[128,5120]{1,0:T(8,128)(2,1)} %layer_norm.1.refs_0_), channel_id=1, source_target_pairs={{0,8},{1,9},{2,10},{3,11},{4,12},{5,13},{6,14},{7,15},{8,0},{9,1},... | collective-permute-start | bytes 3932168 | tf_op jit(solution)/shard_map/ppermute | solution.py:120
  36.6 1.1 copy-start.8
  38.3 14.2 %collective-permute-start.3 = (bf16[3,5120,256]{2,1,0:T(8,128)(2,1)}, bf16[3,5120,256]{2,1,0:T(8,128)(2,1)}, u32[]{:S(2)}, u32[]{:S(2)}) collective-permute-start(bf16[3,5120,256]{2,1,0:T(8,128)(2,1)} %get-tuple-element.50), channel_id=1, source_target_pairs={{0,1},{1,0},{2,3},{3,2},{4,5},{5,4},{6,7},{7,6},{8,9},{9,8},{10,11... | collective-permute-start | bytes 23592968 | tf_op jit(solution)/shard_map/ppermute | solution.py:124
  40.1 40.2 %collective-permute-start.4 = (bf16[128,5120]{1,0:T(8,128)(2,1)}, bf16[128,5120]{1,0:T(8,128)(2,1)}, u32[]{:S(2)}, u32[]{:S(2)}) collective-permute-start(bf16[128,5120]{1,0:T(8,128)(2,1)} %collective-permute-done.refs_1_), channel_id=1, source_target_pairs={{0,2},{1,3},{2,4},{3,5},{4,6},{5,7},{6,0},{7,1},{8,10},{9,11},{10,... | collective-permute-start | bytes 3932168 | tf_op jit(solution)/shard_map/ppermute | solution.py:112
  40.6 39.7 %collective-permute-start.5 = (bf16[128,5120]{1,0:T(8,128)(2,1)}, bf16[128,5120]{1,0:T(8,128)(2,1)}, u32[]{:S(2)}, u32[]{:S(2)}) collective-permute-start(bf16[128,5120]{1,0:T(8,128)(2,1)} %collective-permute-done.2.refs_3_), channel_id=1, source_target_pairs={{0,6},{1,7},{2,0},{3,1},{4,2},{5,3},{6,4},{7,5},{8,14},{9,15},{10,... | collective-permute-start | bytes 3932168 | tf_op jit(solution)/shard_map/ppermute | solution.py:116
  42.8 37.6 %collective-permute-start.6 = (bf16[128,5120]{1,0:T(8,128)(2,1)}, bf16[128,5120]{1,0:T(8,128)(2,1)}, u32[]{:S(2)}, u32[]{:S(2)}) collective-permute-start(bf16[128,5120]{1,0:T(8,128)(2,1)} %collective-permute-done.refs_1_), channel_id=1, source_target_pairs={{0,8},{1,9},{2,10},{3,11},{4,12},{5,13},{6,14},{7,15},{8,0},{9,1},... | collective-permute-start | bytes 3932168 | tf_op jit(solution)/shard_map/ppermute | solution.py:120
  59.3 3.2 %copy-start = (bf16[3,5120,256]{2,1,0:T(8,128)(2,1)S(1)}, bf16[3,5120,256]{2,1,0:T(8,128)(2,1)}, u32[]{:S(2)}) copy-start(bf16[3,5120,256]{2,1,0:T(8,128)(2,1)} %get-tuple-element.49.refs_4_.refs_3_) | copy-start | bytes 23592964
  62.6 3.2 %copy-start.2 = (bf16[3,5120,256]{2,1,0:T(8,128)(2,1)S(1)}, bf16[3,5120,256]{2,1,0:T(8,128)(2,1)}, u32[]{:S(2)}) copy-start(bf16[3,5120,256]{2,1,0:T(8,128)(2,1)} %rev.3.refs_5_.refs_4_) | copy-start | bytes 23592964
  65.8 1.3 copy-start.7
  67.1 1.3 copy-start.9
  79.5 0.9 copy-start.10
  121.2 21.5 %collective-permute-start.8 = (bf16[48,5120]{1,0:T(8,128)(2,1)}, bf16[48,5120]{1,0:T(8,128)(2,1)S(1)}, u32[]{:S(2)}, u32[]{:S(2)}) collective-permute-start(bf16[48,5120]{1,0:T(8,128)(2,1)} %get-tuple-element.59), channel_id=1, source_target_pairs={{0,2},{1,3},{2,4},{3,5},{4,6},{5,7},{6,0},{7,1},{8,10},{9,11},{10,... | collective-permute-start | bytes 1474568 | tf_op jit(solution)/shard_map/ppermute | solution.py:112
  121.8 21.0 %collective-permute-start.9 = (bf16[48,5120]{1,0:T(8,128)(2,1)}, bf16[48,5120]{1,0:T(8,128)(2,1)S(1)}, u32[]{:S(2)}, u32[]{:S(2)}) collective-permute-start(bf16[48,5120]{1,0:T(8,128)(2,1)} %get-tuple-element.60), channel_id=1, source_target_pairs={{0,6},{1,7},{2,0},{3,1},{4,2},{5,3},{6,4},{7,5},{8,14},{9,15},{10,... | collective-permute-start | bytes 1474568 | tf_op jit(solution)/shard_map/ppermute | solution.py:116
  124.0 18.8 %collective-permute-start.10 = (bf16[32,5120]{1,0:T(8,128)(2,1)}, bf16[32,5120]{1,0:T(8,128)(2,1)S(1)}, u32[]{:S(2)}, u32[]{:S(2)}) collective-permute-start(bf16[32,5120]{1,0:T(8,128)(2,1)} %get-tuple-element.61), channel_id=1, source_target_pairs={{0,8},{1,9},{2,10},{3,11},{4,12},{5,13},{6,14},{7,15},{8,0},{9,1},... | collective-permute-start | bytes 983048 | tf_op jit(solution)/shard_map/ppermute | solution.py:120
  125.4 34.8 %collective-permute-start.7 = (bf16[3,512,256]{2,1,0:T(8,128)(2,1)}, bf16[3,512,256]{2,1,0:T(8,128)(2,1)}, u32[]{:S(2)}, u32[]{:S(2)}) collective-permute-start(bf16[3,512,256]{2,1,0:T(8,128)(2,1)} %copy-done.10), channel_id=1, source_target_pairs={{0,1},{1,0},{2,3},{3,2},{4,5},{5,4},{6,7},{7,6},{8,9},{9,8},{10,11... | collective-permute-start | bytes 2359304 | tf_op jit(solution)/shard_map/ppermute | solution.py:124
  126.6 3.2 %copy-start.1 = (bf16[3,5120,256]{2,1,0:T(8,128)(2,1)S(1)}, bf16[3,5120,256]{2,1,0:T(8,128)(2,1)}, u32[]{:S(2)}) copy-start(bf16[3,5120,256]{2,1,0:T(8,128)(2,1)} %get-tuple-element.49.refs_4_.refs_3_) | copy-start | bytes 23592964
  129.8 3.2 %copy-start.3 = (bf16[3,5120,256]{2,1,0:T(8,128)(2,1)S(1)}, bf16[3,5120,256]{2,1,0:T(8,128)(2,1)}, u32[]{:S(2)}) copy-start(bf16[3,5120,256]{2,1,0:T(8,128)(2,1)} %rev.3.refs_5_.refs_4_) | copy-start | bytes 23592964
  142.8 17.5 %collective-permute-start.11 = (bf16[3,384,256]{2,1,0:T(8,128)(2,1)}, bf16[3,384,256]{2,1,0:T(8,128)(2,1)}, u32[]{:S(2)}, u32[]{:S(2)}) collective-permute-start(bf16[3,384,256]{2,1,0:T(8,128)(2,1)} %get-tuple-element.66), channel_id=1, source_target_pairs={{0,1},{1,0},{2,3},{3,2},{4,5},{5,4},{6,7},{7,6},{8,9},{9,8},{10,11... | collective-permute-start | bytes 1769480 | tf_op jit(solution)/shard_map/ppermute | solution.py:124
  146.6 0.7 copy-start.4
  147.2 0.7 copy-start.11
  148.7 10.6 %all-to-all-start = ((f32[16,16,128]{2,1,0:T(8,128)}), f32[16,16,128]{2,1,0:T(8,128)}, u32[]{:S(2)}, u32[]{:S(2)}) async-start(f32[16,16,128]{2,1,0:T(8,128)} %broadcast_in_dim.90), calls=%async_computation | async-start | bytes 262144 | tf_op jit(solution)/shard_map/all_to_all | solution.py:425
  153.0 7.2 %collective-permute-start.12 = (bf16[3,128,256]{2,1,0:T(8,128)(2,1)}, bf16[3,128,256]{2,1,0:T(8,128)(2,1)}, u32[]{:S(2)}, u32[]{:S(2)}) collective-permute-start(bf16[3,128,256]{2,1,0:T(8,128)(2,1)} %copy-done.11), channel_id=1, source_target_pairs={{0,1},{1,0},{2,3},{3,2},{4,5},{5,4},{6,7},{7,6},{8,9},{9,8},{10,11... | collective-permute-start | bytes 589832 | tf_op jit(solution)/shard_map/ppermute | solution.py:124
  160.3 0.9 copy-start.5
  161.2 8.3 %copy-start.6 = (bf16[3,128,256]{2,1,0:T(8,128)(2,1)S(1)}, bf16[3,128,256]{2,1,0:T(8,128)(2,1)}, u32[]{:S(2)}) copy-start(bf16[3,128,256]{2,1,0:T(8,128)(2,1)} %copy-done.4) | copy-start | bytes 589828
  163.5 17.9 %collective-permute-start.13 = (bf16[512,256]{1,0:T(8,128)(2,1)S(1)}, bf16[512,256]{1,0:T(8,128)(2,1)S(1)}, u32[]{:S(2)}, u32[]{:S(2)}) collective-permute-start(bf16[512,256]{1,0:T(8,128)(2,1)S(1)} %get-tuple-element.78.before_ref), channel_id=1, source_target_pairs={{112,0},{0,16},{16,32},{32,48},{48,64},{64,80},{80,96},{96,112},{1... | collective-permute-start | bytes 786440 | tf_op jit(solution)/shard_map/ppermute | solution.py:375
  166.9 14.8 %collective-permute-start.14 = (bf16[512,256]{1,0:T(8,128)(2,1)S(1)}, bf16[512,256]{1,0:T(8,128)(2,1)S(1)}, u32[]{:S(2)}, u32[]{:S(2)}) collective-permute-start(bf16[512,256]{1,0:T(8,128)(2,1)S(1)} %get-tuple-element.79.after_ref), channel_id=1, source_target_pairs={{16,0},{32,16},{48,32},{64,48},{80,64},{96,80},{112,96},{0,112},{1... | collective-permute-start | bytes 786440 | tf_op jit(solution)/shard_map/ppermute | solution.py:375

commit v6 on v4

--- a/solution.py
+++ b/solution.py
@@ -32,15 +32,15 @@
 
 def layer_norm(values, mod_shift, mod_scale):
     rows, wide = values.shape
-    block = pl.BlockSpec((32, wide), lambda i: (i, 0))
+    block = pl.BlockSpec((64, wide), lambda i: (i, 0))
     vector = pl.BlockSpec((1, wide), lambda i: (0, 0))
     return pl.pallas_call(
         layer_norm_kernel,
-        grid=(rows // 32,),
+        grid=(rows // 64,),
         in_specs=[block, vector, vector],
         out_specs=block,
         out_shape=jax.ShapeDtypeStruct((rows, wide), jnp.bfloat16),
-        compiler_params=pltpu.CompilerParams(vmem_limit_bytes=16 * 1024 * 1024),
+        compiler_params=pltpu.CompilerParams(vmem_limit_bytes=60 * 1024 * 1024),
         cost_estimate=pl.CostEstimate(flops=10 * rows * wide, bytes_accessed=4 * rows * wide, transcendentals=rows),
         name="layer_norm",
     )(values, mod_shift.reshape(1, wide), mod_scale.reshape(1, wide))
@@ -175,6 +175,26 @@
         ),
         name="project",
     )(*arrays, own_w, other_w)
+
+
+def cut_kernel(*refs):
+    n = len(refs) // 2
+    for source, out in zip(refs[:n], refs[n:]):
+        out[...] = source[...]
+
+
+def cut(arrays, cuts):
+    wide = arrays[0].shape[1]
+    return pl.pallas_call(
+        cut_kernel,
+        grid=(1,),
+        in_specs=[pl.BlockSpec((count, wide), lambda i, first=first: (first, 0)) for first, count in cuts],
+        out_specs=[pl.BlockSpec((count, wide), lambda i: (0, 0)) for _, count in cuts],
+        out_shape=[jax.ShapeDtypeStruct((count, wide), jnp.bfloat16) for _, count in cuts],
+        compiler_params=pltpu.CompilerParams(vmem_limit_bytes=10 * 1024 * 1024),
+        cost_estimate=pl.CostEstimate(flops=10**5, bytes_accessed=3 * 10**6, transcendentals=0),
+        name="cut_rows",
+    )(*arrays)
 
 
 def sources(refs):
@@ -370,21 +390,24 @@
 
     own = layer_norm(tokens, mod_shift, mod_scale)
     left, right, beside = from_left(own), from_right(own), from_z(own)
-    own_w = jnp.stack(barrier((w_key, w_query, w_value, own))[:3])
+    key_w, query_w, value_w = barrier((w_key, w_query, w_value, own))[:3]
+    one = barrier(jnp.bfloat16(1))
+    sent_w = jnp.stack([key_w, query_w, value_w])
+    own_w = sent_w * one
     cosine, sine = rope_tables(group * rows + jnp.arange(rows, dtype=jnp.int32))
     gq = lax.dynamic_slice(query_gain, (mine * 2 * HD,), (2 * HD,)).reshape(1, 2 * HD)
     gk = lax.dynamic_slice(key_gain, (mine * 2 * HD,), (2 * HD,)).reshape(1, 2 * HD)
-    (left, right, beside), own_w, (cosine, sine, gq, gk, place) = barrier(
-        ((left, right, beside), own_w, (cosine, sine, gq, gk, place))
+    (left, right, beside), own_w, sent_w, (cosine, sine, gq, gk, place) = barrier(
+        ((left, right, beside), own_w, sent_w, (cosine, sine, gq, gk, place))
     )
 
     far, z_right, z_left = from_left(left), from_right(beside), from_z(left)
-    other_w = from_core(own_w)
+    other_w = from_core(sent_w) * one
     near = project((own, left, right, beside), tuple((i, 0, BLK) for i in range(4)), own_w, other_w)
     near, far, z_right, z_left = barrier((near, far, z_right, z_left))
 
-    cuts = (48, 96)
-    z_far = (from_left(z_left[: cuts[0]]), from_right(z_right[cuts[0] : cuts[1]]), from_z(far[cuts[1] :]))
+    part_left, part_right, part_z = cut((z_left, z_right, far), ((0, 48), (1, 48), (3, 32)))
+    z_far = (from_left(part_left), from_right(part_right), from_z(part_z))
     middle = project((far, z_left, z_right), tuple((i, 0, BLK) for i in range(3)), own_w, other_w)
     z_far, middle = barrier((z_far, middle))
     last = project(z_far, tuple((i, 0, p.shape[0]) for i, p in enumerate(z_far)), own_w, other_w)

time: 168 us -> 159 us (0.946)
  Pallas kernels: 57.3 us -> 49.1 us
  waiting for transfers between devices: 27.9 us -> 20.4 us
  other arithmetic: 18 us -> 22.6 us
  local copies, waits for them, and re-layouts: 14.3 us -> 16.5 us
    pallas_call x3, Pallas kernels: 35.9 us -> 25.1 us  [project(): pl.pallas_call(functools.partial(project_kernel, cuts), grid=(3,), in_spe...]
    ppermute x3, waiting for transfers between devices: 11.2 us -> 5.93 us  [from_left(): return lax.ppermute(block, 'sy', chip_move(0, 1, 0))]
    unnamed x19 -> x29, local copies, waits for them, and re-layouts: 7.67 us -> 11.8 us
    mul x0 -> x1, other arithmetic: none -> 3.74 us  [body(): other_w = from_core(sent_w) * one]
    slice x3 -> x0, local copies, waits for them, and re-layouts: 3.12 us -> none  [the longest x1 1.06 us: body(): z_right[cuts[0]:cuts[1]]]
    pallas_call x1 -> x2, Pallas kernels: 1.7 us -> 4.65 us  [the longest x1 3.29 us: layer_norm(): pl.pallas_call(layer_norm_kernel, grid=(rows // 64,), in_specs=[block, ve...]
    another operation x1, other arithmetic: 6.82 us -> 9.12 us  [body(): sent_w = jnp.stack([key_w, query_w, value_w])]
    ppermute x3, waiting for transfers between devices: 2.43 us -> 0.6 us  [from_z(): return lax.ppermute(block, 'sy', chip_move(1, 0, 0))]
  transfers between devices with their start and end apart: 16 -> 16, of which waited for: 7 -> 5; matrix products, arithmetic and copies ran while one was open for 13% -> 16% of each run, Pallas kernels for 29% -> 23%
where the time goes in v6:
time: 159 us; the launch traced here: 158 us
  Pallas kernels  49.1 us (31%)
  starting transfers between devices  27.8 us (17%)
  other arithmetic  22.6 us (14%)
  waiting for transfers between devices  20.4 us (13%)
  blocking collectives  20.4 us (13%)
  local copies, waits for them, and re-layouts  16.5 us (10%)
    pallas_call x3, Pallas kernels, project(): pl.pallas_call(functools.partial(project_kernel, cuts), grid=(3,), in_spe...  25.1 us
    all_to_all x1, blocking collectives, body(): arrived = lax.all_to_all(out, 'sy', split_axis=0, concat_axis=0, tiled=True)  20.4 us
    pallas_call x2, Pallas kernels, attention(): pl.pallas_call(functools.partial(attention_kernel, part), grid=(steps, 2)...  17.1 us
    unnamed x29, local copies, waits for them, and re-layouts  11.8 us
    another operation x1, other arithmetic, body(): sent_w = jnp.stack([key_w, query_w, value_w])  9.12 us
    mul x1, other arithmetic, rope_tables(): return (jnp.cos(angles), jnp.sin(angles) * sign)  8.15 us
    ppermute x4, waiting for transfers between devices, from_core(): return lax.ppermute(block, 'sy', chip_move(0, 0, 1))  7.55 us
    ppermute x3, waiting for transfers between devices, from_left(): return lax.ppermute(block, 'sy', chip_move(0, 1, 0))  5.93 us
  transfers between devices with their start and end apart: 16, of which 5 were waited for; matrix products, arithmetic and copies ran while one was open for 16% of the time, Pallas kernels for 23%

profile of v6, /device:TPU:1, one launch (start us, length us, event | category | flops | bytes accessed | tf_op | source)
XLA Modules:
  0.0 157.8 jit_solution(16407628423065388655)
XLA Ops:
  0.6 3.3 %layer_norm.1.refs_0_ = bf16[128,5120]{1,0:T(8,128)(2,1)} custom-call(bf16[128,5120]{1,0:T(8,128)(2,1)} %tokens_ref.1, f32[1,5120]{1,0:T(1,128)} %bitcast.50, f32[1,5120]{1,0:T(1,128)} %bitcast.51), custom_call_target="tpu_custom_call" | custom-call | flops 6553600 | bytes 2621440 | tf_op jit(solution)/shard_map/layer_norm/pallas_call | solution.py:37
  3.9 2.0 %collective-permute-start = (bf16[128,5120]{1,0:T(8,128)(2,1)}, bf16[128,5120]{1,0:T(8,128)(2,1)}, u32[]{:S(2)}, u32[]{:S(2)}) collective-permute-start(bf16[128,5120]{1,0:T(8,128)(2,1)} %layer_norm.1.refs_0_), channel_id=1, source_target_pairs={{0,2},{1,3},{2,4},{3,5},{4,6},{5,7},{6,0},{7,1},{8,10},{9,11},{10,... | collective-permute-start | bytes 3932168 | tf_op jit(solution)/shard_map/ppermute | solution.py:112
  6.0 1.3 collective-permute-start.1
  7.2 1.8 %collective-permute-start.2 = (bf16[128,5120]{1,0:T(8,128)(2,1)}, bf16[128,5120]{1,0:T(8,128)(2,1)}, u32[]{:S(2)}, u32[]{:S(2)}) collective-permute-start(bf16[128,5120]{1,0:T(8,128)(2,1)} %layer_norm.1.refs_0_), channel_id=1, source_target_pairs={{0,8},{1,9},{2,10},{3,11},{4,12},{5,13},{6,14},{7,15},{8,0},{9,1},... | collective-permute-start | bytes 3932168 | tf_op jit(solution)/shard_map/ppermute | solution.py:120
  10.0 1.3 dynamic_slice.6
  12.4 8.2 %sine_multiply_fusion = (f32[2048,128]{1,0:T(8,128)S(1)}, f32[2048,128]{1,0:T(8,128)}) fusion(f32[128]{0:T(128)S(1)} %compare_select_fusion, f32[128]{0:T(128)S(1)} %mul.67, f32[2048]{0:T(1024)S(1)} %fusion.4, f32[2048]{0:T(1024)S(1)} %get-tuple-element.101, f32[2048]{0:T(1024)S(1)} %get-tuple-element.100, pred[128]{0:T(512)(128)(4,1)S(1)} %get-tuple-element.102, ...), kind=kLoop, calls=%fused_computation.4 | loop fusion | flops 1048576 | bytes 2123008 | tf_op jit(solution)/shard_map/mul | solution.py:66
  20.5 9.1 %pad_maximum_fusion = (bf16[3,5120,256]{2,1,0:T(8,128)(2,1)}, bf16[3,5120,256]{2,1,0:T(8,128)(2,1)}) fusion(bf16[1,5120,256]{2,1,0:T(8,128)(2,1)} %bitcast.44, bf16[1,5120,256]{2,1,0:T(8,128)(2,1)} %bitcast.45, bf16[1,5120,256]{2,1,0:T(8,128)(2,1)} %bitcast.46, bf16[]{:T(256)} %constant.157.clone.1), kind=kLoop, calls=%fused_computation | loop fusion | flops 11796480 | bytes 23592962 | tf_op jit(solution)/shard_map/stack | solution.py:395
  29.7 5.9 %collective-permute-done.refs_1_ = bf16[128,5120]{1,0:T(8,128)(2,1)} collective-permute-done((bf16[128,5120]{1,0:T(8,128)(2,1)}, bf16[128,5120]{1,0:T(8,128)(2,1)}, u32[]{:S(2)}, u32[]{:S(2)}) %collective-permute-start) | collective-permute-done | bytes 1310752 | tf_op jit(solution)/shard_map/ppermute | solution.py:112
  37.3 1.9 %collective-permute-start.3 = (bf16[3,5120,256]{2,1,0:T(8,128)(2,1)}, bf16[3,5120,256]{2,1,0:T(8,128)(2,1)}, u32[]{:S(2)}, u32[]{:S(2)}) collective-permute-start(bf16[3,5120,256]{2,1,0:T(8,128)(2,1)} %get-tuple-element.50), channel_id=1, source_target_pairs={{0,1},{1,0},{2,3},{3,2},{4,5},{5,4},{6,7},{7,6},{8,9},{9,8},{10,11... | collective-permute-start | bytes 23592968 | tf_op jit(solution)/shard_map/ppermute | solution.py:124
  40.4 1.6 %collective-permute-start.6 = (bf16[128,5120]{1,0:T(8,128)(2,1)}, bf16[128,5120]{1,0:T(8,128)(2,1)}, u32[]{:S(2)}, u32[]{:S(2)}) collective-permute-start(bf16[128,5120]{1,0:T(8,128)(2,1)} %collective-permute-done.refs_1_), channel_id=1, source_target_pairs={{0,8},{1,9},{2,10},{3,11},{4,12},{5,13},{6,14},{7,15},{8,0},{9,1},... | collective-permute-start | bytes 3932168 | tf_op jit(solution)/shard_map/ppermute | solution.py:120
  42.0 2.0 %collective-permute-start.5 = (bf16[128,5120]{1,0:T(8,128)(2,1)}, bf16[128,5120]{1,0:T(8,128)(2,1)}, u32[]{:S(2)}, u32[]{:S(2)}) collective-permute-start(bf16[128,5120]{1,0:T(8,128)(2,1)} %collective-permute-done.2.refs_3_), channel_id=1, source_target_pairs={{0,6},{1,7},{2,0},{3,1},{4,2},{5,3},{6,4},{7,5},{8,14},{9,15},{10,... | collective-permute-start | bytes 3932168 | tf_op jit(solution)/shard_map/ppermute | solution.py:116
  44.0 7.5 %collective-permute-done.3 = bf16[3,5120,256]{2,1,0:T(8,128)(2,1)} collective-permute-done((bf16[3,5120,256]{2,1,0:T(8,128)(2,1)}, bf16[3,5120,256]{2,1,0:T(8,128)(2,1)}, u32[]{:S(2)}, u32[]{:S(2)}) %collective-permute-start.3) | collective-permute-done | bytes 7864352 | tf_op jit(solution)/shard_map/ppermute | solution.py:124
  51.5 3.7 %broadcast_multiply_fusion.refs_5_.refs_4_ = bf16[3,5120,256]{2,1,0:T(8,128)(2,1)S(1)} fusion(bf16[3,5120,256]{2,1,0:T(8,128)(2,1)} %collective-permute-done.3, bf16[]{:T(256)} %constant.157.clone.1), kind=kLoop, calls=%fused_computation.1 | loop fusion | flops 3932160 | bytes 15728642 | tf_op jit(solution)/shard_map/mul | solution.py:405
  55.3 3.2 %copy-done = bf16[3,5120,256]{2,1,0:T(8,128)(2,1)S(1)} copy-done((bf16[3,5120,256]{2,1,0:T(8,128)(2,1)S(1)}, bf16[3,5120,256]{2,1,0:T(8,128)(2,1)}, u32[]{:S(2)}) %copy-start) | copy-done | bytes 7864344
  58.5 1.3 copy-done.6
  59.8 1.3 copy-done.11
  61.1 11.6 %project.3 = (bf16[3,512,256]{2,1,0:T(8,128)(2,1)S(1)}, bf16[3,512,256]{2,1,0:T(8,128)(2,1)}, f32[3,4,128]{2,1,0:T(4,128)S(1)}) custom-call(bf16[128,5120]{1,0:T(8,128)(2,1)S(1)} %copy-done.6, bf16[128,5120]{1,0:T(8,128)(2,1)} %collective-permute-done.refs_1_, bf16[128,5120]{1,0:T(8,128)(2,1)S(1)} %copy-done.11, ...), custom_call_target="tpu_custom_call" | custom-call | flops 8053063680 | bytes 15728640 | tf_op jit(solution)/shard_map/project/pallas_call | solution.py:163
  72.8 1.4 cut_rows.1
  74.7 2.2 %collective-permute-start.9 = (bf16[48,5120]{1,0:T(8,128)(2,1)S(1)}, bf16[48,5120]{1,0:T(8,128)(2,1)S(1)}, u32[]{:S(2)}, u32[]{:S(2)}) collective-permute-start(bf16[48,5120]{1,0:T(8,128)(2,1)S(1)} %get-tuple-element.60), channel_id=1, source_target_pairs={{0,6},{1,7},{2,0},{3,1},{4,2},{5,3},{6,4},{7,5},{8,14},{9,15},{10,... | collective-permute-start | bytes 1474568 | tf_op jit(solution)/shard_map/ppermute | solution.py:116
  76.9 1.4 collective-permute-start.10
  79.5 9.8 %project.4 = (bf16[3,384,256]{2,1,0:T(8,128)(2,1)S(1)}, bf16[3,384,256]{2,1,0:T(8,128)(2,1)}, f32[3,3,128]{2,1,0:T(4,128)S(1)}) custom-call(bf16[128,5120]{1,0:T(8,128)(2,1)} %collective-permute-done.4.refs_2_.refs_0_, bf16[128,5120]{1,0:T(8,128)(2,1)} %collective-permute-done.6.refs_0_.refs_1_, bf16[128,5120]{1,0:T(8,128)(2,1)} %collective-permute-done.5.refs_1_.refs_2_, ...), custom_call_target="tpu_custom_call" | custom-call | flops 6039797760 | bytes 15728640 | tf_op jit(solution)/shard_map/project/pallas_call | solution.py:163
  89.6 3.8 %project.5 = (bf16[3,128,256]{2,1,0:T(8,128)(2,1)S(1)}, bf16[3,128,256]{2,1,0:T(8,128)(2,1)S(1)}, f32[3,1,128]{2,1,0:T(1,128)S(1)}) custom-call(bf16[48,5120]{1,0:T(8,128)(2,1)S(1)} %collective-permute-done.8.refs_0_, bf16[48,5120]{1,0:T(8,128)(2,1)S(1)} %collective-permute-done.9.refs_1_, bf16[32,5120]{1,0:T(8,128)(2,1)S(1)} %collective-permute-done.10.refs_2_, ...), custom_call_target="tpu_custom_call" | custom-call | flops 2013265920 | bytes 15728640 | tf_op jit(solution)/shard_map/project/pallas_call | solution.py:163
  94.9 4.9 %all-to-all-start = ((f32[16,16,128]{2,1,0:T(8,128)}), f32[16,16,128]{2,1,0:T(8,128)S(1)}, u32[]{:S(2)}, u32[]{:S(2)}) async-start(f32[16,16,128]{2,1,0:T(8,128)} %broadcast_in_dim.90), calls=%async_computation | async-start | bytes 262144 | tf_op jit(solution)/shard_map/all_to_all | solution.py:423
  99.9 5.9 %all-to-all-done = f32[16,16,128]{2,1,0:T(8,128)S(1)} async-done(((f32[16,16,128]{2,1,0:T(8,128)}), f32[16,16,128]{2,1,0:T(8,128)S(1)}, u32[]{:S(2)}, u32[]{:S(2)}) %all-to-all-start) | async-done | bytes 131104 | tf_op jit(solution)/shard_map/all_to_all | solution.py:423
  105.9 1.2 copy-done.1
  108.9 2.3 %halo_keys.1 = (bf16[512,256]{1,0:T(8,128)(2,1)S(1)}, bf16[512,256]{1,0:T(8,128)(2,1)S(1)}) custom-call(s32[16]{0:T(128)S(1)} %copy-done.8, bf16[3,512,256]{2,1,0:T(8,128)(2,1)S(1)} %get-tuple-element.54.fa, bf16[3,512,256]{2,1,0:T(8,128)(2,1)} %collective-permute-done.7.ga, bf16[3,384,256]{2,1,0:T(8,128)(2,1)S(1)} %copy-done.4, ...), custom_call_target="tpu_custom_call" | custom-call | flops 10000000 | bytes 3000000 | tf_op jit(solution)/shard_map/halo_keys/pallas_call | solution.py:250
  111.2 3.4 %collective-permute-start.13 = (bf16[512,256]{1,0:T(8,128)(2,1)S(1)}, bf16[512,256]{1,0:T(8,128)(2,1)S(1)}, u32[]{:S(2)}, u32[]{:S(2)}) collective-permute-start(bf16[512,256]{1,0:T(8,128)(2,1)S(1)} %get-tuple-element.78.before_ref), channel_id=1, source_target_pairs={{112,0},{0,16},{16,32},{32,48},{48,64},{64,80},{80,96},{96,112},{1... | collective-permute-start | bytes 786440 | tf_op jit(solution)/shard_map/ppermute | solution.py:371
  114.6 2.5 %collective-permute-start.14 = (bf16[512,256]{1,0:T(8,128)(2,1)S(1)}, bf16[512,256]{1,0:T(8,128)(2,1)S(1)}, u32[]{:S(2)}, u32[]{:S(2)}) collective-permute-start(bf16[512,256]{1,0:T(8,128)(2,1)S(1)} %get-tuple-element.79.after_ref), channel_id=1, source_target_pairs={{16,0},{32,16},{48,32},{64,48},{80,64},{96,80},{112,96},{0,112},{1... | collective-permute-start | bytes 786440 | tf_op jit(solution)/shard_map/ppermute | solution.py:371
  117.1 11.9 %window_attention.1.rest_0_ = bf16[16,2,144,128]{3,2,1,0:T(8,128)(2,1)S(1)} custom-call(s32[16]{0:T(128)S(1)} %copy-done.9, bf16[3,512,256]{2,1,0:T(8,128)(2,1)S(1)} %get-tuple-element.54.fa, bf16[3,512,256]{2,1,0:T(8,128)(2,1)} %collective-permute-done.7.ga, bf16[3,384,256]{2,1,0:T(8,128)(2,1)S(1)} %copy-done.5, ...), custom_call_target="tpu_custom_call" | custom-call | flops 1500000000 | bytes 10000000 | tf_op jit(solution)/shard_map/window_attention/pallas_call | solution.py:346
  129.4 5.2 %window_attention_halo.1 = bf16[16,2,144,128]{3,2,1,0:T(8,128)(2,1)S(1)} custom-call(s32[16]{0:T(128)S(1)} %copy-done.9, bf16[3,512,256]{2,1,0:T(8,128)(2,1)S(1)} %get-tuple-element.54.fa, bf16[3,512,256]{2,1,0:T(8,128)(2,1)} %collective-permute-done.7.ga, bf16[3,384,256]{2,1,0:T(8,128)(2,1)S(1)} %copy-done.5, ...), custom_call_target="tpu_custom_call", output_to_operand_aliasing={{}: (15, {})} | custom-call | flops 500000000 | bytes 10000000 | tf_op jit(solution)/shard_map/window_attention_halo/pallas_call | solution.py:346
  134.6 20.4 %all_to_all.10 = bf16[16,2,144,128]{3,2,1,0:T(8,128)(2,1)S(1)} all-to-all(bf16[16,2,144,128]{3,2,1,0:T(8,128)(2,1)S(1)} %window_attention_halo.1), channel_id=1, replica_groups=mesh['sx'=8,'sy'=16] {'sy'}, dimensions={0} | all-to-all | bytes 2359296 | tf_op jit(solution)/shard_map/all_to_all | solution.py:430
  155.8 1.3 copy.21
  (73 shorter events, 12.2 us)
Async XLA Ops:
  3.9 31.7 %collective-permute-start = (bf16[128,5120]{1,0:T(8,128)(2,1)}, bf16[128,5120]{1,0:T(8,128)(2,1)}, u32[]{:S(2)}, u32[]{:S(2)}) collective-permute-start(bf16[128,5120]{1,0:T(8,128)(2,1)} %layer_norm.1.refs_0_), channel_id=1, source_target_pairs={{0,2},{1,3},{2,4},{3,5},{4,6},{5,7},{6,0},{7,1},{8,10},{9,11},{10,... | collective-permute-start | bytes 3932168 | tf_op jit(solution)/shard_map/ppermute | solution.py:112
  6.0 29.6 %collective-permute-start.1 = (bf16[128,5120]{1,0:T(8,128)(2,1)}, bf16[128,5120]{1,0:T(8,128)(2,1)S(1)}, u32[]{:S(2)}, u32[]{:S(2)}) collective-permute-start(bf16[128,5120]{1,0:T(8,128)(2,1)} %layer_norm.1.refs_0_), channel_id=1, source_target_pairs={{0,6},{1,7},{2,0},{3,1},{4,2},{5,3},{6,4},{7,5},{8,14},{9,15},{10,... | collective-permute-start | bytes 3932168 | tf_op jit(solution)/shard_map/ppermute | solution.py:116
  7.2 30.0 %collective-permute-start.2 = (bf16[128,5120]{1,0:T(8,128)(2,1)}, bf16[128,5120]{1,0:T(8,128)(2,1)}, u32[]{:S(2)}, u32[]{:S(2)}) collective-permute-start(bf16[128,5120]{1,0:T(8,128)(2,1)} %layer_norm.1.refs_0_), channel_id=1, source_target_pairs={{0,8},{1,9},{2,10},{3,11},{4,12},{5,13},{6,14},{7,15},{8,0},{9,1},... | collective-permute-start | bytes 3932168 | tf_op jit(solution)/shard_map/ppermute | solution.py:120
  35.6 1.1 copy-start.10
  37.3 14.2 %collective-permute-start.3 = (bf16[3,5120,256]{2,1,0:T(8,128)(2,1)}, bf16[3,5120,256]{2,1,0:T(8,128)(2,1)}, u32[]{:S(2)}, u32[]{:S(2)}) collective-permute-start(bf16[3,5120,256]{2,1,0:T(8,128)(2,1)} %get-tuple-element.50), channel_id=1, source_target_pairs={{0,1},{1,0},{2,3},{3,2},{4,5},{5,4},{6,7},{7,6},{8,9},{9,8},{10,11... | collective-permute-start | bytes 23592968 | tf_op jit(solution)/shard_map/ppermute | solution.py:124
  39.9 32.9 %collective-permute-start.4 = (bf16[128,5120]{1,0:T(8,128)(2,1)}, bf16[128,5120]{1,0:T(8,128)(2,1)}, u32[]{:S(2)}, u32[]{:S(2)}) collective-permute-start(bf16[128,5120]{1,0:T(8,128)(2,1)} %collective-permute-done.refs_1_), channel_id=1, source_target_pairs={{0,2},{1,3},{2,4},{3,5},{4,6},{5,7},{6,0},{7,1},{8,10},{9,11},{10,... | collective-permute-start | bytes 3932168 | tf_op jit(solution)/shard_map/ppermute | solution.py:112
  40.4 32.4 %collective-permute-start.6 = (bf16[128,5120]{1,0:T(8,128)(2,1)}, bf16[128,5120]{1,0:T(8,128)(2,1)}, u32[]{:S(2)}, u32[]{:S(2)}) collective-permute-start(bf16[128,5120]{1,0:T(8,128)(2,1)} %collective-permute-done.refs_1_), channel_id=1, source_target_pairs={{0,8},{1,9},{2,10},{3,11},{4,12},{5,13},{6,14},{7,15},{8,0},{9,1},... | collective-permute-start | bytes 3932168 | tf_op jit(solution)/shard_map/ppermute | solution.py:120
  42.0 30.7 %collective-permute-start.5 = (bf16[128,5120]{1,0:T(8,128)(2,1)}, bf16[128,5120]{1,0:T(8,128)(2,1)}, u32[]{:S(2)}, u32[]{:S(2)}) collective-permute-start(bf16[128,5120]{1,0:T(8,128)(2,1)} %collective-permute-done.2.refs_3_), channel_id=1, source_target_pairs={{0,6},{1,7},{2,0},{3,1},{4,2},{5,3},{6,4},{7,5},{8,14},{9,15},{10,... | collective-permute-start | bytes 3932168 | tf_op jit(solution)/shard_map/ppermute | solution.py:116
  55.3 3.2 %copy-start = (bf16[3,5120,256]{2,1,0:T(8,128)(2,1)S(1)}, bf16[3,5120,256]{2,1,0:T(8,128)(2,1)}, u32[]{:S(2)}) copy-start(bf16[3,5120,256]{2,1,0:T(8,128)(2,1)} %get-tuple-element.49.refs_4_.refs_3_) | copy-start | bytes 23592964
  58.5 1.3 copy-start.6
  59.8 1.3 copy-start.11
  74.1 15.2 %collective-permute-start.8 = (bf16[48,5120]{1,0:T(8,128)(2,1)S(1)}, bf16[48,5120]{1,0:T(8,128)(2,1)S(1)}, u32[]{:S(2)}, u32[]{:S(2)}) collective-permute-start(bf16[48,5120]{1,0:T(8,128)(2,1)S(1)} %get-tuple-element.59), channel_id=1, source_target_pairs={{0,2},{1,3},{2,4},{3,5},{4,6},{5,7},{6,0},{7,1},{8,10},{9,11},{10,... | collective-permute-start | bytes 1474568 | tf_op jit(solution)/shard_map/ppermute | solution.py:112
  74.7 14.6 %collective-permute-start.9 = (bf16[48,5120]{1,0:T(8,128)(2,1)S(1)}, bf16[48,5120]{1,0:T(8,128)(2,1)S(1)}, u32[]{:S(2)}, u32[]{:S(2)}) collective-permute-start(bf16[48,5120]{1,0:T(8,128)(2,1)S(1)} %get-tuple-element.60), channel_id=1, source_target_pairs={{0,6},{1,7},{2,0},{3,1},{4,2},{5,3},{6,4},{7,5},{8,14},{9,15},{10,... | collective-permute-start | bytes 1474568 | tf_op jit(solution)/shard_map/ppermute | solution.py:116
  76.9 12.4 %collective-permute-start.10 = (bf16[32,5120]{1,0:T(8,128)(2,1)S(1)}, bf16[32,5120]{1,0:T(8,128)(2,1)S(1)}, u32[]{:S(2)}, u32[]{:S(2)}) collective-permute-start(bf16[32,5120]{1,0:T(8,128)(2,1)S(1)} %get-tuple-element.61), channel_id=1, source_target_pairs={{0,8},{1,9},{2,10},{3,11},{4,12},{5,13},{6,14},{7,15},{8,0},{9,1},... | collective-permute-start | bytes 983048 | tf_op jit(solution)/shard_map/ppermute | solution.py:120
  78.3 27.6 %collective-permute-start.7 = (bf16[3,512,256]{2,1,0:T(8,128)(2,1)}, bf16[3,512,256]{2,1,0:T(8,128)(2,1)}, u32[]{:S(2)}, u32[]{:S(2)}) collective-permute-start(bf16[3,512,256]{2,1,0:T(8,128)(2,1)} %get-tuple-element.55), channel_id=1, source_target_pairs={{0,1},{1,0},{2,3},{3,2},{4,5},{5,4},{6,7},{7,6},{8,9},{9,8},{10,11... | collective-permute-start | bytes 2359304 | tf_op jit(solution)/shard_map/ppermute | solution.py:124
  89.3 4.2 %copy-start.3 = (bf16[3,384,256]{2,1,0:T(8,128)(2,1)}, bf16[3,384,256]{2,1,0:T(8,128)(2,1)S(1)}, u32[]{:S(2)}) copy-start(bf16[3,384,256]{2,1,0:T(8,128)(2,1)S(1)} %get-tuple-element.65.fb) | copy-start | bytes 1769476
  89.3 4.8 %copy-start.13 = (pred[8,8]{1,0:T(8,128)(4,1)S(1)}, pred[8,8]{1,0:T(8,128)(4,1)}, u32[]{:S(2)}) copy-start(pred[8,8]{1,0:T(8,128)(4,1)} %iota_compare_fusion) | copy-start | bytes 196
  89.3 16.6 %collective-permute-start.11 = (bf16[3,384,256]{2,1,0:T(8,128)(2,1)}, bf16[3,384,256]{2,1,0:T(8,128)(2,1)}, u32[]{:S(2)}, u32[]{:S(2)}) collective-permute-start(bf16[3,384,256]{2,1,0:T(8,128)(2,1)} %get-tuple-element.66), channel_id=1, source_target_pairs={{0,1},{1,0},{2,3},{3,2},{4,5},{5,4},{6,7},{7,6},{8,9},{9,8},{10,11... | collective-permute-start | bytes 1769480 | tf_op jit(solution)/shard_map/ppermute | solution.py:124
  93.4 0.7 copy-start.12
  94.9 11.0 %all-to-all-start = ((f32[16,16,128]{2,1,0:T(8,128)}), f32[16,16,128]{2,1,0:T(8,128)S(1)}, u32[]{:S(2)}, u32[]{:S(2)}) async-start(f32[16,16,128]{2,1,0:T(8,128)} %broadcast_in_dim.90), calls=%async_computation | async-start | bytes 262144 | tf_op jit(solution)/shard_map/all_to_all | solution.py:423
  99.8 6.1 %collective-permute-start.12 = (bf16[3,128,256]{2,1,0:T(8,128)(2,1)}, bf16[3,128,256]{2,1,0:T(8,128)(2,1)S(1)}, u32[]{:S(2)}, u32[]{:S(2)}) collective-permute-start(bf16[3,128,256]{2,1,0:T(8,128)(2,1)} %copy-done.12), channel_id=1, source_target_pairs={{0,1},{1,0},{2,3},{3,2},{4,5},{5,4},{6,7},{7,6},{8,9},{9,8},{10,11... | collective-permute-start | bytes 589832 | tf_op jit(solution)/shard_map/ppermute | solution.py:124
  105.9 1.2 copy-start.1
  107.1 1.1 copy-start.4
  108.2 0.6 copy-start.8
  108.8 8.3 %copy-start.2 = (f32[2048,128]{1,0:T(8,128)S(1)}, f32[2048,128]{1,0:T(8,128)}, u32[]{:S(2)}) copy-start(f32[2048,128]{1,0:T(8,128)} %get-tuple-element.76.cos_lo.cos_hi.cos_ref) | copy-start | bytes 3145732
  108.9 8.3 %copy-start.5 = (bf16[3,384,256]{2,1,0:T(8,128)(2,1)S(1)}, bf16[3,384,256]{2,1,0:T(8,128)(2,1)}, u32[]{:S(2)}) copy-start(bf16[3,384,256]{2,1,0:T(8,128)(2,1)} %copy-done.3) | copy-start | bytes 1769476
  108.9 8.3 %copy-start.7 = (f32[256]{0:T(256)S(1)}, f32[256]{0:T(256)}, u32[]{:S(2)}) copy-start(f32[256]{0:T(256)} %dynamic_slice.6) | copy-start | bytes 3076
  108.9 8.3 %copy-start.9 = (s32[16]{0:T(128)S(1)}, s32[16]{0:T(128)}, u32[]{:S(2)}) copy-start(s32[16]{0:T(128)} %reshape.307.place_ref) | copy-start | bytes 196
  111.2 17.8 %collective-permute-start.13 = (bf16[512,256]{1,0:T(8,128)(2,1)S(1)}, bf16[512,256]{1,0:T(8,128)(2,1)S(1)}, u32[]{:S(2)}, u32[]{:S(2)}) collective-permute-start(bf16[512,256]{1,0:T(8,128)(2,1)S(1)} %get-tuple-element.78.before_ref), channel_id=1, source_target_pairs={{112,0},{0,16},{16,32},{32,48},{48,64},{64,80},{80,96},{96,112},{1... | collective-permute-start | bytes 786440 | tf_op jit(solution)/shard_map/ppermute | solution.py:371
  114.6 14.8 %collective-permute-start.14 = (bf16[512,256]{1,0:T(8,128)(2,1)S(1)}, bf16[512,256]{1,0:T(8,128)(2,1)S(1)}, u32[]{:S(2)}, u32[]{:S(2)}) collective-permute-start(bf16[512,256]{1,0:T(8,128)(2,1)S(1)} %get-tuple-element.79.after_ref), channel_id=1, source_target_pairs={{16,0},{32,16},{48,32},{64,48},{80,64},{96,80},{112,96},{0,112},{1... | collective-permute-start | bytes 786440 | tf_op jit(solution)/shard_map/ppermute | solution.py:371

commit v7 on v6

--- a/solution.py
+++ b/solution.py
@@ -125,7 +125,6 @@
 
 
 ANYWHERE = pl.BlockSpec(memory_space=pltpu.HBM)
-SMEM = pl.BlockSpec(memory_space=pltpu.SMEM)
 
 
 def project_kernel(cuts, *refs):
@@ -168,7 +167,8 @@
         out_shape=[out, out, jax.ShapeDtypeStruct((3, rows // BLK, BLK), jnp.float32)],
         scratch_shapes=[pltpu.VMEM((rows, depth), jnp.bfloat16), pltpu.SemaphoreType.DMA((len(cuts),))],
         compiler_params=pltpu.CompilerParams(
-            dimension_semantics=("arbitrary",), vmem_limit_bytes=26 * 1024 * 1024
+            dimension_semantics=("arbitrary",),
+            vmem_limit_bytes=2 * rows * depth + 8 * depth * wide + 4 * 1024 * 1024,
         ),
         cost_estimate=pl.CostEstimate(
             flops=12 * rows * depth * wide, bytes_accessed=12 * depth * wide, transcendentals=0
@@ -198,24 +198,28 @@
 
 
 def sources(refs):
+    mine = lax.axis_index("sy")
+    z, x, core = mine // 8, mine // 2 % 4, mine % 2
     at = 0
     for chunk, slots in enumerate(CHUNKS):
         for i in range(slots):
-            for core in range(2):
-                yield (at + i) * 2 + core, refs[chunk * 2 + core], pl.ds(i * BLK, BLK)
-        at += slots
+            dz, dx = SLOTS[at]
+            chip = (z + dz) % 2 * 4 + (x + dx) % 4
+            for other in range(2):
+                n = chip * 2 + (core + other) % 2
+                yield at * 2 + other, n, refs[chunk * 2 + other], pl.ds(i * BLK, BLK)
+            at += 1
 
 
 def halo_kernel(
-    place_ref, fa, ga, fb, gb, fc, gc, ssq_ref, gk_ref, cos_lo, sin_lo, cos_hi, sin_hi,
+    fa, ga, fb, gb, fc, gc, ssq_ref, gk_ref, cos_lo, sin_lo, cos_hi, sin_hi,
     before_ref, after_ref, raw, sems,
 ):
     blocks = 2 * sum(CHUNKS)
     ends = ((lambda n: n >= blocks - ROUNDS, blocks - ROUNDS, 0), (lambda n: n < ROUNDS, 0, 1))
 
     def each(act):
-        for at, ref, rows in sources((fa, ga, fb, gb, fc, gc)):
-            n = place_ref[at]
+        for at, n, ref, rows in sources((fa, ga, fb, gb, fc, gc)):
             for inside, first, head in ends:
 
                 @pl.when(inside(n))
@@ -241,7 +245,7 @@
             )
 
 
-def halo(place, features, ssq_k, gk, cosine, sine):
+def halo(features, ssq_k, gk, cosine, sine):
     rows = cosine.shape[0]
     low = pl.BlockSpec((HALO, HD), lambda i: (0, 0))
     high = pl.BlockSpec((HALO, HD), lambda i: (rows // HALO - 1, 0))
@@ -250,7 +254,7 @@
     return pl.pallas_call(
         halo_kernel,
         grid=(1,),
-        in_specs=[SMEM] + [ANYWHERE] * 6 + [one(ssq_k), one(gk), low, low, high, high],
+        in_specs=[ANYWHERE] * 6 + [one(ssq_k), one(gk), low, low, high, high],
         out_specs=[pl.BlockSpec((HALO, 2 * HD), lambda i: (0, 0))] * 2,
         out_shape=[out, out],
         scratch_shapes=[
@@ -260,12 +264,11 @@
         compiler_params=pltpu.CompilerParams(vmem_limit_bytes=16 * 1024 * 1024),
         cost_estimate=pl.CostEstimate(flops=10**7, bytes_accessed=3 * 10**6, transcendentals=0),
         name="halo_keys",
-    )(place, *features, ssq_k, gk, cosine, sine, cosine, sine)
+    )(*features, ssq_k, gk, cosine, sine, cosine, sine)
 
 
 def attention_kernel(
-    part, place_ref, fa, ga, fb, gb, fc, gc, before_ref, after_ref, sk_ref, sq_ref,
-    gk_ref, gq_ref, cos_ref, sin_ref, *rest,
+    part, fa, ga, fb, gb, fc, gc, sk_ref, sq_ref, gk_ref, gq_ref, cos_ref, sin_ref, *rest
 ):
     out_ref, raw, kbuf, vbuf, sems = rest[-5:]
     step, head = pl.program_id(0), pl.program_id(1)
@@ -282,15 +285,14 @@
     @pl.when((step == 0) & (head == 0))
     def _():
         copies = []
-        for at, ref, rows in sources((fa, ga, fb, gb, fc, gc)):
-            n = place_ref[at]
+        for at, n, ref, rows in sources((fa, ga, fb, gb, fc, gc)):
             to = pl.ds(pl.multiple_of(n * BLK, BLK), BLK)
             needed = None if part == 0 else (n < ROUNDS) | (n >= blocks - ROUNDS)
             copies.append((n, needed, pltpu.make_async_copy(ref.at[:, rows], raw.at[:, to], sems.at[at])))
         for _, needed, copy in copies:
             guarded(needed, copy.start)
         if part == 1:
-            for head, ref in enumerate((before_ref, after_ref)):
+            for head, ref in enumerate(rest[:2]):
                 to = pl.ds((0, blocks)[head] * BLK, HALO)
                 kbuf[head, to, :] = ref[:, 0:HD]
                 vbuf[head, :, to] = ref[:, HD:].T
@@ -309,7 +311,7 @@
                 vbuf[head, :, to] = raw[2, rows, columns[head]].T
 
     def attend(first, head):
-        for j in range(PER_STEP):
+        def score(j):
             b = first + j
             rows = pl.ds(pl.multiple_of(b * BLK, BLK), BLK)
             window = pl.ds(pl.multiple_of(b * BLK, BLK), (ROUNDS + 1) * BLK)
@@ -317,9 +319,12 @@
                 raw[1, rows, columns[head]], inverse_norm(sq_ref[pl.ds(b, 1), :]), gq_ref[:, columns[head]],
                 cos_ref[rows, :], sin_ref[rows, :],
             )
-            scores = lax.dot_general(
+            return lax.dot_general(
                 kbuf[head, window, :], q, (((1,), (1,)), ((), ())), preferred_element_type=jnp.float32
             )
+
+        def finish(j, scores):
+            window = pl.ds(pl.multiple_of((first + j) * BLK, BLK), (ROUNDS + 1) * BLK)
             top = jnp.max(scores, axis=0, keepdims=True)
             weight = jnp.exp2((scores - top) * (SCALE * LOG2E))
             total = jnp.sum(weight, axis=0, keepdims=True)
@@ -330,23 +335,26 @@
             stats = split3(top * SCALE) + split3(total) + [jnp.zeros((EXTRA - 6, HD), jnp.float32)]
             out_ref[j, 0, BLK : BLK + EXTRA, :] = jnp.concatenate(stats, axis=0).astype(jnp.bfloat16)
 
+        scores = [score(j) for j in range(PER_STEP)]
+        for j in range(PER_STEP):
+            finish(j, scores[j])
     for which in range(2):
         first = (step + 1 - which) * PER_STEP if part == 0 else (0, blocks - ROUNDS)[which]
         pl.when(head == which)(functools.partial(attend, first, which))
 
 
-def attention(part, place, features, before, after, sk, sq, gk, gq, cosine, sine, held=None):
+def attention(part, features, sk, sq, gk, gq, cosine, sine, before=None, after=None, held=None):
     rows = cosine.shape[0]
     blocks = rows // BLK
     whole = lambda a: pl.BlockSpec(a.shape, lambda i, h, n=a.ndim: (0,) * n)
     steps = blocks // PER_STEP - 1 if part == 0 else 1
     which = (lambda i, h: (i + 1 - h, h, 0, 0)) if part == 0 else (lambda i, h: (h * (blocks // PER_STEP - 1), h, 0, 0))
-    small = (before, after, sk, sq, gk, gq, cosine, sine)
+    small = (sk, sq, gk, gq, cosine, sine) + (() if held is None else (before, after))
     more = () if held is None else (held,)
     return pl.pallas_call(
         functools.partial(attention_kernel, part),
         grid=(steps, 2),
-        in_specs=[SMEM] + [ANYWHERE] * 6 + [whole(a) for a in small] + [ANYWHERE] * len(more),
+        in_specs=[ANYWHERE] * 6 + [whole(a) for a in small] + [ANYWHERE] * len(more),
         out_specs=pl.BlockSpec((PER_STEP, 1, BLK + EXTRA, HD), which),
         out_shape=jax.ShapeDtypeStruct((blocks, 2, BLK + EXTRA, HD), jnp.bfloat16),
         scratch_shapes=[
@@ -355,7 +363,7 @@
             pltpu.VMEM((2, HD, rows + HALO), jnp.bfloat16),
             pltpu.SemaphoreType.DMA((blocks,)),
         ],
-        input_output_aliases={15: 0} if more else {},
+        input_output_aliases={14: 0} if more else {},
         compiler_params=pltpu.CompilerParams(
             dimension_semantics=("arbitrary", "arbitrary"), vmem_limit_bytes=24 * 1024 * 1024
         ),
@@ -363,7 +371,7 @@
             flops=(1 + 2 * (1 - part)) * 5 * 10**8, bytes_accessed=10**7, transcendentals=10**6
         ),
         name=("window_attention", "window_attention_halo")[part],
-    )(place, *features, *small, *more)
+    )(*features, *small, *more)
 
 
 def along_sx(block, distance):
@@ -371,20 +379,40 @@
     return lax.ppermute(block, "sx", [((i - distance) % n, i) for i in range(n)])
 
 
+def unpack_kernel(arrived_ref, attended_ref, best_ref, total_ref):
+    classes, heads = arrived_ref.shape[:2]
+    for c in range(classes):
+        for h in range(heads):
+            head = c * heads + h
+            attended_ref[:, head * HD : (head + 1) * HD] = arrived_ref[c, h, 0:BLK, :]
+            stats = arrived_ref[c, h, BLK : BLK + EXTRA, :].astype(jnp.float32)
+            best_ref[head : head + 1, :] = (stats[0:1] + stats[1:2]) + stats[2:3]
+            total_ref[head : head + 1, :] = (stats[3:4] + stats[4:5]) + stats[5:6]
+
+
 def unpack(arrived):
-    attended = arrived[:, :, :BLK].transpose(2, 0, 1, 3).reshape(BLK, H * HD)
-    stats = arrived[:, :, BLK : BLK + 6].astype(jnp.float32)
-    best = (stats[:, :, 0] + stats[:, :, 1]) + stats[:, :, 2]
-    total = (stats[:, :, 3] + stats[:, :, 4]) + stats[:, :, 5]
-    return attended, best.reshape(H, BLK), total.reshape(H, BLK)
+    shapes = [
+        jax.ShapeDtypeStruct((BLK, H * HD), jnp.bfloat16),
+        jax.ShapeDtypeStruct((H, BLK), jnp.float32),
+        jax.ShapeDtypeStruct((H, BLK), jnp.float32),
+    ]
+    return pl.pallas_call(
+        unpack_kernel,
+        grid=(1,),
+        in_specs=[pl.BlockSpec(arrived.shape, lambda i: (0, 0, 0, 0))],
+        out_specs=[pl.BlockSpec(a.shape, lambda i: (0, 0)) for a in shapes],
+        out_shape=shapes,
+        compiler_params=pltpu.CompilerParams(vmem_limit_bytes=16 * 1024 * 1024),
+        name="unpack",
+    )(arrived)
 
 
 def body(tokens, mod_shift, mod_scale, w_query, w_key, w_value, query_gain, key_gain):
     group = lax.axis_index("sx")
     mine = lax.axis_index("sy")
-    z, x, core = mine // 8, mine // 2 % 4, mine % 2
+    z, x = mine // 8, mine // 2 % 4
     chips = jnp.stack([(z + dz) % 2 * 4 + (x + dx) % 4 for dz, dx in SLOTS])
-    place = jnp.stack([chips * 2 + core, chips * 2 + 1 - core], axis=1).reshape(-1).astype(jnp.int32)
+    here = (chips[:, None] == jnp.arange(8)[None, :]).astype(jnp.float32)
     rows = BLK * lax.axis_size("sy")
     barrier = lax.optimization_barrier
 
@@ -397,8 +425,8 @@
     cosine, sine = rope_tables(group * rows + jnp.arange(rows, dtype=jnp.int32))
     gq = lax.dynamic_slice(query_gain, (mine * 2 * HD,), (2 * HD,)).reshape(1, 2 * HD)
     gk = lax.dynamic_slice(key_gain, (mine * 2 * HD,), (2 * HD,)).reshape(1, 2 * HD)
-    (left, right, beside), own_w, sent_w, (cosine, sine, gq, gk, place) = barrier(
-        ((left, right, beside), own_w, sent_w, (cosine, sine, gq, gk, place))
+    (left, right, beside), own_w, sent_w, (cosine, sine, gq, gk, here) = barrier(
+        ((left, right, beside), own_w, sent_w, (cosine, sine, gq, gk, here))
     )
 
     far, z_right, z_left = from_left(left), from_right(beside), from_z(left)
@@ -417,16 +445,15 @@
         features += [made, from_core(given)]
         parts.append(part[:2])
     part = jnp.concatenate(parts, axis=1)
-    here = chips[:, None] == jnp.arange(8)[None, :]
-    part = jnp.sum(jnp.where(here[None, :, :, None], part[:, :, None, :], 0.0), axis=1)
+    part = jnp.sum(here[None, :, :, None] * part[:, :, None, :], axis=1)
     sent = jnp.broadcast_to(part.reshape(1, 16, BLK), (NSY, 16, BLK))
     seen = lax.all_to_all(sent, "sy", split_axis=0, concat_axis=0, tiled=True)
     ssq = jnp.sum(seen.reshape(8, 2, 2, 8, BLK), axis=0).transpose(1, 2, 0, 3).reshape(2, 16, BLK)
-    before, after = halo(place, features, ssq[0], gk, cosine, sine)
+    before, after = halo(features, ssq[0], gk, cosine, sine)
     common = (ssq[0], ssq[1], gk, gq, cosine, sine)
-    out = attention(0, place, features, before, after, *common)
+    out = attention(0, features, *common)
     before, after = along_sx(before, 1), along_sx(after, -1)
-    out = attention(1, place, features, before, after, *common, held=out)
+    out = attention(1, features, *common, before=before, after=after, held=out)
     arrived = lax.all_to_all(out, "sy", split_axis=0, concat_axis=0, tiled=True)
     return unpack(arrived)
 

time: 159 us -> 155 us (0.975)
  waiting for transfers between devices: 20.4 us -> 24.3 us
  local copies, waits for them, and re-layouts: 16.5 us -> 13 us
  other arithmetic: 22.6 us -> 19.8 us
    ppermute x3, waiting for transfers between devices: 5.93 us -> 8.13 us  [from_left(): return lax.ppermute(block, 'sy', chip_move(0, 1, 0))]
    another operation x1, other arithmetic: 9.12 us -> 7.01 us  [body(): sent_w = jnp.stack([key_w, query_w, value_w])]
    pallas_call x2, Pallas kernels: 17.1 us -> 15 us  [attention(): pl.pallas_call(functools.partial(attention_kernel, part), grid=(steps, 2)...]
    unnamed x29 -> x24, local copies, waits for them, and re-layouts: 11.8 us -> 9.95 us
  transfers between devices with their start and end apart: 16 -> 16, of which waited for: 5 -> 5; matrix products, arithmetic and copies ran while one was open for 16% -> 15% of each run, Pallas kernels for 23% -> 23%
where the time goes in v7:
time: 155 us; the launch traced here: 154 us
  Pallas kernels  48.2 us (31%)
  starting transfers between devices  27.7 us (18%)
  waiting for transfers between devices  24.3 us (16%)
  blocking collectives  20.3 us (13%)
  other arithmetic  19.8 us (13%)
  local copies, waits for them, and re-layouts  13 us (8%)
    pallas_call x3, Pallas kernels, project(): pl.pallas_call(functools.partial(project_kernel, cuts), grid=(3,), in_spe...  25.4 us
    all_to_all x1, blocking collectives, body(): arrived = lax.all_to_all(out, 'sy', split_axis=0, concat_axis=0, tiled=True)  20.3 us
    pallas_call x2, Pallas kernels, attention(): pl.pallas_call(functools.partial(attention_kernel, part), grid=(steps, 2)...  15 us
    unnamed x24, local copies, waits for them, and re-layouts  9.95 us
    mul x1, other arithmetic, rope_tables(): return (jnp.cos(angles), jnp.sin(angles) * sign)  8.15 us
    ppermute x3, waiting for transfers between devices, from_left(): return lax.ppermute(block, 'sy', chip_move(0, 1, 0))  8.13 us
    ppermute x4, waiting for transfers between devices, from_core(): return lax.ppermute(block, 'sy', chip_move(0, 0, 1))  8.07 us
    another operation x1, other arithmetic, body(): sent_w = jnp.stack([key_w, query_w, value_w])  7.01 us
  transfers between devices with their start and end apart: 16, of which 5 were waited for; matrix products, arithmetic and copies ran while one was open for 15% of the time, Pallas kernels for 23%

profile of v7, /device:TPU:1, one launch (start us, length us, event | category | flops | bytes accessed | tf_op | source)
XLA Modules:
  0.0 154.2 jit_solution(11818970911296956371)
XLA Ops:
  0.6 3.3 %layer_norm.1.refs_0_ = bf16[128,5120]{1,0:T(8,128)(2,1)} custom-call(bf16[128,5120]{1,0:T(8,128)(2,1)} %tokens_ref.1, f32[1,5120]{1,0:T(1,128)} %bitcast.36, f32[1,5120]{1,0:T(1,128)} %bitcast.37), custom_call_target="tpu_custom_call" | custom-call | flops 6553600 | bytes 2621440 | tf_op jit(solution)/shard_map/layer_norm/pallas_call | solution.py:37
  3.9 2.0 %collective-permute-start = (bf16[128,5120]{1,0:T(8,128)(2,1)}, bf16[128,5120]{1,0:T(8,128)(2,1)}, u32[]{:S(2)}, u32[]{:S(2)}) collective-permute-start(bf16[128,5120]{1,0:T(8,128)(2,1)} %layer_norm.1.refs_0_), channel_id=1, source_target_pairs={{0,2},{1,3},{2,4},{3,5},{4,6},{5,7},{6,0},{7,1},{8,10},{9,11},{10,... | collective-permute-start | bytes 3932168 | tf_op jit(solution)/shard_map/ppermute | solution.py:112
  6.0 1.3 collective-permute-start.1
  7.2 1.8 %collective-permute-start.2 = (bf16[128,5120]{1,0:T(8,128)(2,1)}, bf16[128,5120]{1,0:T(8,128)(2,1)}, u32[]{:S(2)}, u32[]{:S(2)}) collective-permute-start(bf16[128,5120]{1,0:T(8,128)(2,1)} %layer_norm.1.refs_0_), channel_id=1, source_target_pairs={{0,8},{1,9},{2,10},{3,11},{4,12},{5,13},{6,14},{7,15},{8,0},{9,1},... | collective-permute-start | bytes 3932168 | tf_op jit(solution)/shard_map/ppermute | solution.py:120
  9.5 8.2 %sine_multiply_fusion = (f32[2048,128]{1,0:T(8,128)S(1)}, f32[2048,128]{1,0:T(8,128)}) fusion(f32[128]{0:T(128)S(1)} %compare_select_fusion, f32[128]{0:T(128)S(1)} %mul.65, f32[2048]{0:T(1024)S(1)} %fusion.4, f32[2048]{0:T(1024)S(1)} %get-tuple-element.88, f32[2048]{0:T(1024)S(1)} %get-tuple-element.87, pred[128]{0:T(512)(128)(4,1)S(1)} %get-tuple-element.89, ...), kind=kLoop, calls=%fused_computation.3 | loop fusion | flops 1048576 | bytes 2123008 | tf_op jit(solution)/shard_map/mul | solution.py:66
  17.6 1.3 dynamic_slice.6
  20.5 7.0 %pad_maximum_fusion = (bf16[3,5120,256]{2,1,0:T(8,128)(2,1)S(1)}, bf16[3,5120,256]{2,1,0:T(8,128)(2,1)}) fusion(bf16[1,5120,256]{2,1,0:T(8,128)(2,1)} %bitcast.30, bf16[1,5120,256]{2,1,0:T(8,128)(2,1)} %bitcast.31, bf16[1,5120,256]{2,1,0:T(8,128)(2,1)} %bitcast.32, bf16[]{:T(256)} %constant.151.clone.1), kind=kLoop, calls=%fused_computation | loop fusion | flops 11796480 | bytes 23592962 | tf_op jit(solution)/shard_map/stack | solution.py:423
  27.5 8.1 %collective-permute-done.refs_1_ = bf16[128,5120]{1,0:T(8,128)(2,1)} collective-permute-done((bf16[128,5120]{1,0:T(8,128)(2,1)}, bf16[128,5120]{1,0:T(8,128)(2,1)}, u32[]{:S(2)}, u32[]{:S(2)}) %collective-permute-start) | collective-permute-done | bytes 1310752 | tf_op jit(solution)/shard_map/ppermute | solution.py:112
  37.3 1.9 %collective-permute-start.3 = (bf16[3,5120,256]{2,1,0:T(8,128)(2,1)S(1)}, bf16[3,5120,256]{2,1,0:T(8,128)(2,1)}, u32[]{:S(2)}, u32[]{:S(2)}) collective-permute-start(bf16[3,5120,256]{2,1,0:T(8,128)(2,1)S(1)} %get-tuple-element.49), channel_id=1, source_target_pairs={{0,1},{1,0},{2,3},{3,2},{4,5},{5,4},{6,7},{7,6},{8,9},{9,8},{10,11... | collective-permute-start | bytes 23592968 | tf_op jit(solution)/shard_map/ppermute | solution.py:124
  39.7 1.6 %collective-permute-start.6 = (bf16[128,5120]{1,0:T(8,128)(2,1)}, bf16[128,5120]{1,0:T(8,128)(2,1)}, u32[]{:S(2)}, u32[]{:S(2)}) collective-permute-start(bf16[128,5120]{1,0:T(8,128)(2,1)} %collective-permute-done.refs_1_), channel_id=1, source_target_pairs={{0,8},{1,9},{2,10},{3,11},{4,12},{5,13},{6,14},{7,15},{8,0},{9,1},... | collective-permute-start | bytes 3932168 | tf_op jit(solution)/shard_map/ppermute | solution.py:120
  41.3 1.9 %collective-permute-start.5 = (bf16[128,5120]{1,0:T(8,128)(2,1)}, bf16[128,5120]{1,0:T(8,128)(2,1)}, u32[]{:S(2)}, u32[]{:S(2)}) collective-permute-start(bf16[128,5120]{1,0:T(8,128)(2,1)} %collective-permute-done.2.refs_3_), channel_id=1, source_target_pairs={{0,6},{1,7},{2,0},{3,1},{4,2},{5,3},{6,4},{7,5},{8,14},{9,15},{10,... | collective-permute-start | bytes 3932168 | tf_op jit(solution)/shard_map/ppermute | solution.py:116
  43.3 8.1 %collective-permute-done.3 = bf16[3,5120,256]{2,1,0:T(8,128)(2,1)} collective-permute-done((bf16[3,5120,256]{2,1,0:T(8,128)(2,1)S(1)}, bf16[3,5120,256]{2,1,0:T(8,128)(2,1)}, u32[]{:S(2)}, u32[]{:S(2)}) %collective-permute-start.3) | collective-permute-done | bytes 7864352 | tf_op jit(solution)/shard_map/ppermute | solution.py:124
  51.3 3.7 %broadcast_multiply_fusion.refs_5_.refs_4_ = bf16[3,5120,256]{2,1,0:T(8,128)(2,1)S(1)} fusion(bf16[3,5120,256]{2,1,0:T(8,128)(2,1)} %collective-permute-done.3, bf16[]{:T(256)} %constant.151.clone.1), kind=kLoop, calls=%fused_computation.1 | loop fusion | flops 3932160 | bytes 15728642 | tf_op jit(solution)/shard_map/mul | solution.py:433
  55.1 3.2 %copy-done = bf16[3,5120,256]{2,1,0:T(8,128)(2,1)S(1)} copy-done((bf16[3,5120,256]{2,1,0:T(8,128)(2,1)S(1)}, bf16[3,5120,256]{2,1,0:T(8,128)(2,1)}, u32[]{:S(2)}) %copy-start) | copy-done | bytes 7864344
  58.3 1.3 copy-done.6
  59.6 1.3 copy-done.9
  60.9 11.7 %project.3 = (bf16[3,512,256]{2,1,0:T(8,128)(2,1)S(1)}, bf16[3,512,256]{2,1,0:T(8,128)(2,1)}, f32[3,4,128]{2,1,0:T(4,128)S(1)}) custom-call(bf16[128,5120]{1,0:T(8,128)(2,1)S(1)} %copy-done.6, bf16[128,5120]{1,0:T(8,128)(2,1)} %collective-permute-done.refs_1_, bf16[128,5120]{1,0:T(8,128)(2,1)S(1)} %copy-done.9, ...), custom_call_target="tpu_custom_call" | custom-call | flops 8053063680 | bytes 15728640 | tf_op jit(solution)/shard_map/project/pallas_call | solution.py:162
  72.6 1.4 cut_rows.1
  74.6 2.1 %collective-permute-start.9 = (bf16[48,5120]{1,0:T(8,128)(2,1)S(1)}, bf16[48,5120]{1,0:T(8,128)(2,1)S(1)}, u32[]{:S(2)}, u32[]{:S(2)}) collective-permute-start(bf16[48,5120]{1,0:T(8,128)(2,1)S(1)} %get-tuple-element.59), channel_id=1, source_target_pairs={{0,6},{1,7},{2,0},{3,1},{4,2},{5,3},{6,4},{7,5},{8,14},{9,15},{10,... | collective-permute-start | bytes 1474568 | tf_op jit(solution)/shard_map/ppermute | solution.py:116
  76.7 1.4 collective-permute-start.10
  79.4 9.9 %project.4 = (bf16[3,384,256]{2,1,0:T(8,128)(2,1)S(1)}, bf16[3,384,256]{2,1,0:T(8,128)(2,1)}, f32[3,3,128]{2,1,0:T(4,128)S(1)}) custom-call(bf16[128,5120]{1,0:T(8,128)(2,1)} %collective-permute-done.4.refs_2_.refs_0_, bf16[128,5120]{1,0:T(8,128)(2,1)} %collective-permute-done.6.refs_0_.refs_1_, bf16[128,5120]{1,0:T(8,128)(2,1)} %collective-permute-done.5.refs_1_.refs_2_, ...), custom_call_target="tpu_custom_call" | custom-call | flops 6039797760 | bytes 15728640 | tf_op jit(solution)/shard_map/project/pallas_call | solution.py:162
  89.6 3.9 %project.5 = (bf16[3,128,256]{2,1,0:T(8,128)(2,1)S(1)}, bf16[3,128,256]{2,1,0:T(8,128)(2,1)S(1)}, f32[3,1,128]{2,1,0:T(1,128)S(1)}) custom-call(bf16[48,5120]{1,0:T(8,128)(2,1)S(1)} %collective-permute-done.8.refs_0_, bf16[48,5120]{1,0:T(8,128)(2,1)S(1)} %collective-permute-done.9.refs_1_, bf16[32,5120]{1,0:T(8,128)(2,1)S(1)} %collective-permute-done.10.refs_2_, ...), custom_call_target="tpu_custom_call" | custom-call | flops 2013265920 | bytes 15728640 | tf_op jit(solution)/shard_map/project/pallas_call | solution.py:162
  94.9 4.8 %all-to-all-start = ((f32[16,16,128]{2,1,0:T(8,128)}), f32[16,16,128]{2,1,0:T(8,128)S(1)}, u32[]{:S(2)}, u32[]{:S(2)}) async-start(f32[16,16,128]{2,1,0:T(8,128)} %broadcast_in_dim.67), calls=%async_computation | async-start | bytes 262144 | tf_op jit(solution)/shard_map/all_to_all | solution.py:450
  99.9 5.9 %all-to-all-done = f32[16,16,128]{2,1,0:T(8,128)S(1)} async-done(((f32[16,16,128]{2,1,0:T(8,128)}), f32[16,16,128]{2,1,0:T(8,128)S(1)}, u32[]{:S(2)}, u32[]{:S(2)}) %all-to-all-start) | async-done | bytes 131104 | tf_op jit(solution)/shard_map/all_to_all | solution.py:450
  108.2 1.9 %halo_keys.1 = (bf16[512,256]{1,0:T(8,128)(2,1)S(1)}, bf16[512,256]{1,0:T(8,128)(2,1)S(1)}) custom-call(bf16[3,512,256]{2,1,0:T(8,128)(2,1)S(1)} %get-tuple-element.53.fa, bf16[3,512,256]{2,1,0:T(8,128)(2,1)} %collective-permute-done.7.ga, bf16[3,384,256]{2,1,0:T(8,128)(2,1)S(1)} %copy-done.4, bf16[3,384,256]{2,1,0:T(8,128)(2,1)} %collective-permute-done.11.gb, ...), custom_call_target="tpu_custom_call" | custom-call | flops 10000000 | bytes 3000000 | tf_op jit(solution)/shard_map/halo_keys/pallas_call | solution.py:254
  110.1 3.4 %collective-permute-start.13 = (bf16[512,256]{1,0:T(8,128)(2,1)S(1)}, bf16[512,256]{1,0:T(8,128)(2,1)S(1)}, u32[]{:S(2)}, u32[]{:S(2)}) collective-permute-start(bf16[512,256]{1,0:T(8,128)(2,1)S(1)} %get-tuple-element.79), channel_id=1, source_target_pairs={{112,0},{0,16},{16,32},{32,48},{48,64},{64,80},{80,96},{96,112},{1... | collective-permute-start | bytes 786440 | tf_op jit(solution)/shard_map/ppermute | solution.py:379
  113.5 2.5 %collective-permute-start.14 = (bf16[512,256]{1,0:T(8,128)(2,1)S(1)}, bf16[512,256]{1,0:T(8,128)(2,1)S(1)}, u32[]{:S(2)}, u32[]{:S(2)}) collective-permute-start(bf16[512,256]{1,0:T(8,128)(2,1)S(1)} %get-tuple-element.80), channel_id=1, source_target_pairs={{16,0},{32,16},{48,32},{64,48},{80,64},{96,80},{112,96},{0,112},{1... | collective-permute-start | bytes 786440 | tf_op jit(solution)/shard_map/ppermute | solution.py:379
  116.0 10.6 %window_attention.1.rest_2_ = bf16[16,2,144,128]{3,2,1,0:T(8,128)(2,1)S(1)} custom-call(bf16[3,512,256]{2,1,0:T(8,128)(2,1)S(1)} %get-tuple-element.53.fa, bf16[3,512,256]{2,1,0:T(8,128)(2,1)} %collective-permute-done.7.ga, bf16[3,384,256]{2,1,0:T(8,128)(2,1)S(1)} %copy-done.5, bf16[3,384,256]{2,1,0:T(8,128)(2,1)} %collective-permute-done.11.gb, ...), custom_call_target="tpu_custom_call" | custom-call | flops 1500000000 | bytes 10000000 | tf_op jit(solution)/shard_map/window_attention/pallas_call | solution.py:354
  126.7 1.6 %collective-permute-done.14.rest_1_ = bf16[512,256]{1,0:T(8,128)(2,1)S(1)} collective-permute-done((bf16[512,256]{1,0:T(8,128)(2,1)S(1)}, bf16[512,256]{1,0:T(8,128)(2,1)S(1)}, u32[]{:S(2)}, u32[]{:S(2)}) %collective-permute-start.14) | collective-permute-done | bytes 262176 | tf_op jit(solution)/shard_map/ppermute | solution.py:379
  128.3 4.4 %window_attention_halo.1 = bf16[16,2,144,128]{3,2,1,0:T(8,128)(2,1)S(1)} custom-call(bf16[3,512,256]{2,1,0:T(8,128)(2,1)S(1)} %get-tuple-element.53.fa, bf16[3,512,256]{2,1,0:T(8,128)(2,1)} %collective-permute-done.7.ga, bf16[3,384,256]{2,1,0:T(8,128)(2,1)S(1)} %copy-done.5, ...), custom_call_target="tpu_custom_call", output_to_operand_aliasing={{}: (14, {})} | custom-call | flops 500000000 | bytes 10000000 | tf_op jit(solution)/shard_map/window_attention_halo/pallas_call | solution.py:354
  132.7 20.3 %all_to_all.10.arrived_ref = bf16[16,2,144,128]{3,2,1,0:T(8,128)(2,1)S(1)} all-to-all(bf16[16,2,144,128]{3,2,1,0:T(8,128)(2,1)S(1)} %window_attention_halo.1), channel_id=1, replica_groups=mesh['sx'=8,'sy'=16] {'sy'}, dimensions={0} | all-to-all | bytes 2359296 | tf_op jit(solution)/shard_map/all_to_all | solution.py:457
  153.0 1.3 unpack.1
  (60 shorter events, 10.2 us)
Async XLA Ops:
  3.9 31.7 %collective-permute-start = (bf16[128,5120]{1,0:T(8,128)(2,1)}, bf16[128,5120]{1,0:T(8,128)(2,1)}, u32[]{:S(2)}, u32[]{:S(2)}) collective-permute-start(bf16[128,5120]{1,0:T(8,128)(2,1)} %layer_norm.1.refs_0_), channel_id=1, source_target_pairs={{0,2},{1,3},{2,4},{3,5},{4,6},{5,7},{6,0},{7,1},{8,10},{9,11},{10,... | collective-permute-start | bytes 3932168 | tf_op jit(solution)/shard_map/ppermute | solution.py:112
  6.0 29.6 %collective-permute-start.1 = (bf16[128,5120]{1,0:T(8,128)(2,1)}, bf16[128,5120]{1,0:T(8,128)(2,1)S(1)}, u32[]{:S(2)}, u32[]{:S(2)}) collective-permute-start(bf16[128,5120]{1,0:T(8,128)(2,1)} %layer_norm.1.refs_0_), channel_id=1, source_target_pairs={{0,6},{1,7},{2,0},{3,1},{4,2},{5,3},{6,4},{7,5},{8,14},{9,15},{10,... | collective-permute-start | bytes 3932168 | tf_op jit(solution)/shard_map/ppermute | solution.py:116
  7.2 30.0 %collective-permute-start.2 = (bf16[128,5120]{1,0:T(8,128)(2,1)}, bf16[128,5120]{1,0:T(8,128)(2,1)}, u32[]{:S(2)}, u32[]{:S(2)}) collective-permute-start(bf16[128,5120]{1,0:T(8,128)(2,1)} %layer_norm.1.refs_0_), channel_id=1, source_target_pairs={{0,8},{1,9},{2,10},{3,11},{4,12},{5,13},{6,14},{7,15},{8,0},{9,1},... | collective-permute-start | bytes 3932168 | tf_op jit(solution)/shard_map/ppermute | solution.py:120
  35.6 1.1 copy-start.8
  37.3 14.0 %collective-permute-start.3 = (bf16[3,5120,256]{2,1,0:T(8,128)(2,1)S(1)}, bf16[3,5120,256]{2,1,0:T(8,128)(2,1)}, u32[]{:S(2)}, u32[]{:S(2)}) collective-permute-start(bf16[3,5120,256]{2,1,0:T(8,128)(2,1)S(1)} %get-tuple-element.49), channel_id=1, source_target_pairs={{0,1},{1,0},{2,3},{3,2},{4,5},{5,4},{6,7},{7,6},{8,9},{9,8},{10,11... | collective-permute-start | bytes 23592968 | tf_op jit(solution)/shard_map/ppermute | solution.py:124
  39.1 33.5 %collective-permute-start.4 = (bf16[128,5120]{1,0:T(8,128)(2,1)}, bf16[128,5120]{1,0:T(8,128)(2,1)}, u32[]{:S(2)}, u32[]{:S(2)}) collective-permute-start(bf16[128,5120]{1,0:T(8,128)(2,1)} %collective-permute-done.refs_1_), channel_id=1, source_target_pairs={{0,2},{1,3},{2,4},{3,5},{4,6},{5,7},{6,0},{7,1},{8,10},{9,11},{10,... | collective-permute-start | bytes 3932168 | tf_op jit(solution)/shard_map/ppermute | solution.py:112
  39.7 32.9 %collective-permute-start.6 = (bf16[128,5120]{1,0:T(8,128)(2,1)}, bf16[128,5120]{1,0:T(8,128)(2,1)}, u32[]{:S(2)}, u32[]{:S(2)}) collective-permute-start(bf16[128,5120]{1,0:T(8,128)(2,1)} %collective-permute-done.refs_1_), channel_id=1, source_target_pairs={{0,8},{1,9},{2,10},{3,11},{4,12},{5,13},{6,14},{7,15},{8,0},{9,1},... | collective-permute-start | bytes 3932168 | tf_op jit(solution)/shard_map/ppermute | solution.py:120
  41.3 31.3 %collective-permute-start.5 = (bf16[128,5120]{1,0:T(8,128)(2,1)}, bf16[128,5120]{1,0:T(8,128)(2,1)}, u32[]{:S(2)}, u32[]{:S(2)}) collective-permute-start(bf16[128,5120]{1,0:T(8,128)(2,1)} %collective-permute-done.2.refs_3_), channel_id=1, source_target_pairs={{0,6},{1,7},{2,0},{3,1},{4,2},{5,3},{6,4},{7,5},{8,14},{9,15},{10,... | collective-permute-start | bytes 3932168 | tf_op jit(solution)/shard_map/ppermute | solution.py:116
  55.1 3.2 %copy-start = (bf16[3,5120,256]{2,1,0:T(8,128)(2,1)S(1)}, bf16[3,5120,256]{2,1,0:T(8,128)(2,1)}, u32[]{:S(2)}) copy-start(bf16[3,5120,256]{2,1,0:T(8,128)(2,1)} %get-tuple-element.48.refs_4_.refs_3_) | copy-start | bytes 23592964
  58.3 1.3 copy-start.6
  59.6 1.3 copy-start.9
  74.0 15.3 %collective-permute-start.8 = (bf16[48,5120]{1,0:T(8,128)(2,1)S(1)}, bf16[48,5120]{1,0:T(8,128)(2,1)S(1)}, u32[]{:S(2)}, u32[]{:S(2)}) collective-permute-start(bf16[48,5120]{1,0:T(8,128)(2,1)S(1)} %get-tuple-element.58), channel_id=1, source_target_pairs={{0,2},{1,3},{2,4},{3,5},{4,6},{5,7},{6,0},{7,1},{8,10},{9,11},{10,... | collective-permute-start | bytes 1474568 | tf_op jit(solution)/shard_map/ppermute | solution.py:112
  74.6 14.7 %collective-permute-start.9 = (bf16[48,5120]{1,0:T(8,128)(2,1)S(1)}, bf16[48,5120]{1,0:T(8,128)(2,1)S(1)}, u32[]{:S(2)}, u32[]{:S(2)}) collective-permute-start(bf16[48,5120]{1,0:T(8,128)(2,1)S(1)} %get-tuple-element.59), channel_id=1, source_target_pairs={{0,6},{1,7},{2,0},{3,1},{4,2},{5,3},{6,4},{7,5},{8,14},{9,15},{10,... | collective-permute-start | bytes 1474568 | tf_op jit(solution)/shard_map/ppermute | solution.py:116
  76.7 12.5 %collective-permute-start.10 = (bf16[32,5120]{1,0:T(8,128)(2,1)S(1)}, bf16[32,5120]{1,0:T(8,128)(2,1)S(1)}, u32[]{:S(2)}, u32[]{:S(2)}) collective-permute-start(bf16[32,5120]{1,0:T(8,128)(2,1)S(1)} %get-tuple-element.60), channel_id=1, source_target_pairs={{0,8},{1,9},{2,10},{3,11},{4,12},{5,13},{6,14},{7,15},{8,0},{9,1},... | collective-permute-start | bytes 983048 | tf_op jit(solution)/shard_map/ppermute | solution.py:120
  78.2 27.7 %collective-permute-start.7 = (bf16[3,512,256]{2,1,0:T(8,128)(2,1)}, bf16[3,512,256]{2,1,0:T(8,128)(2,1)}, u32[]{:S(2)}, u32[]{:S(2)}) collective-permute-start(bf16[3,512,256]{2,1,0:T(8,128)(2,1)} %get-tuple-element.54), channel_id=1, source_target_pairs={{0,1},{1,0},{2,3},{3,2},{4,5},{5,4},{6,7},{7,6},{8,9},{9,8},{10,11... | collective-permute-start | bytes 2359304 | tf_op jit(solution)/shard_map/ppermute | solution.py:124
  89.2 4.2 %copy-start.3 = (bf16[3,384,256]{2,1,0:T(8,128)(2,1)}, bf16[3,384,256]{2,1,0:T(8,128)(2,1)S(1)}, u32[]{:S(2)}) copy-start(bf16[3,384,256]{2,1,0:T(8,128)(2,1)S(1)} %get-tuple-element.64.fb) | copy-start | bytes 1769476
  89.3 4.9 %copy-start.11 = (f32[8,8]{1,0:T(8,128)S(1)}, f32[8,8]{1,0:T(8,128)}, u32[]{:S(2)}) copy-start(f32[8,8]{1,0:T(8,128)} %fusion.10) | copy-start | bytes 772
  89.3 16.6 %collective-permute-start.11 = (bf16[3,384,256]{2,1,0:T(8,128)(2,1)}, bf16[3,384,256]{2,1,0:T(8,128)(2,1)}, u32[]{:S(2)}, u32[]{:S(2)}) collective-permute-start(bf16[3,384,256]{2,1,0:T(8,128)(2,1)} %get-tuple-element.65), channel_id=1, source_target_pairs={{0,1},{1,0},{2,3},{3,2},{4,5},{5,4},{6,7},{7,6},{8,9},{9,8},{10,11... | collective-permute-start | bytes 1769480 | tf_op jit(solution)/shard_map/ppermute | solution.py:124
  93.5 0.7 copy-start.10
  94.9 10.9 %all-to-all-start = ((f32[16,16,128]{2,1,0:T(8,128)}), f32[16,16,128]{2,1,0:T(8,128)S(1)}, u32[]{:S(2)}, u32[]{:S(2)}) async-start(f32[16,16,128]{2,1,0:T(8,128)} %broadcast_in_dim.67), calls=%async_computation | async-start | bytes 262144 | tf_op jit(solution)/shard_map/all_to_all | solution.py:450
  99.7 6.1 %collective-permute-start.12 = (bf16[3,128,256]{2,1,0:T(8,128)(2,1)}, bf16[3,128,256]{2,1,0:T(8,128)(2,1)S(1)}, u32[]{:S(2)}, u32[]{:S(2)}) collective-permute-start(bf16[3,128,256]{2,1,0:T(8,128)(2,1)} %copy-done.10), channel_id=1, source_target_pairs={{0,1},{1,0},{2,3},{3,2},{4,5},{5,4},{6,7},{7,6},{8,9},{9,8},{10,11... | collective-permute-start | bytes 589832 | tf_op jit(solution)/shard_map/ppermute | solution.py:124
  105.9 1.2 copy-start.1
  107.1 1.1 copy-start.4
  108.2 7.8 %copy-start.2 = (f32[2048,128]{1,0:T(8,128)S(1)}, f32[2048,128]{1,0:T(8,128)}, u32[]{:S(2)}) copy-start(f32[2048,128]{1,0:T(8,128)} %get-tuple-element.77.cos_lo.cos_hi.cos_ref) | copy-start | bytes 3145732
  108.2 7.8 %copy-start.5 = (bf16[3,384,256]{2,1,0:T(8,128)(2,1)S(1)}, bf16[3,384,256]{2,1,0:T(8,128)(2,1)}, u32[]{:S(2)}) copy-start(bf16[3,384,256]{2,1,0:T(8,128)(2,1)} %copy-done.3) | copy-start | bytes 1769476
  108.2 7.8 %copy-start.7 = (f32[256]{0:T(256)S(1)}, f32[256]{0:T(256)}, u32[]{:S(2)}) copy-start(f32[256]{0:T(256)} %dynamic_slice.6) | copy-start | bytes 3076
  110.1 16.6 %collective-permute-start.13 = (bf16[512,256]{1,0:T(8,128)(2,1)S(1)}, bf16[512,256]{1,0:T(8,128)(2,1)S(1)}, u32[]{:S(2)}, u32[]{:S(2)}) collective-permute-start(bf16[512,256]{1,0:T(8,128)(2,1)S(1)} %get-tuple-element.79), channel_id=1, source_target_pairs={{112,0},{0,16},{16,32},{32,48},{48,64},{64,80},{80,96},{96,112},{1... | collective-permute-start | bytes 786440 | tf_op jit(solution)/shard_map/ppermute | solution.py:379
  113.5 14.8 %collective-permute-start.14 = (bf16[512,256]{1,0:T(8,128)(2,1)S(1)}, bf16[512,256]{1,0:T(8,128)(2,1)S(1)}, u32[]{:S(2)}, u32[]{:S(2)}) collective-permute-start(bf16[512,256]{1,0:T(8,128)(2,1)S(1)} %get-tuple-element.80), channel_id=1, source_target_pairs={{16,0},{32,16},{48,32},{64,48},{80,64},{96,80},{112,96},{0,112},{1... | collective-permute-start | bytes 786440 | tf_op jit(solution)/shard_map/ppermute | solution.py:379

commit v8 on v7

--- a/solution.py
+++ b/solution.py
@@ -15,7 +15,7 @@
 GRID_H = 45
 BLK = 128
 HALO = ROUNDS * BLK
-EXTRA = 16
+EXTRA = 8
 NSY = 16
 SCALE = np.float32(1.0) / np.sqrt(np.float32(HD))
 LOG2E = np.float32(1.4426950408889634)
@@ -211,6 +211,35 @@
             at += 1
 
 
+def payload_kernel(*refs):
+    parts, out_ref, held = refs[:-2], refs[-2], refs[-1]
+    mine = lax.axis_index("sy")
+    z, x = mine // 8, mine // 2 % 4
+    at = 0
+    for part, slots in zip(parts, CHUNKS):
+        for i in range(slots):
+            dz, dx = SLOTS[at]
+            chip = (z + dz) % 2 * 4 + (x + dx) % 4
+            for kind in range(2):
+                held[pl.ds(kind * 8 + chip, 1), :] = part[kind, i : i + 1, :]
+            at += 1
+    for i in range(out_ref.shape[0]):
+        out_ref[i] = held[...]
+
+
+def payload(parts):
+    return pl.pallas_call(
+        payload_kernel,
+        grid=(1,),
+        in_specs=[pl.BlockSpec(p.shape, lambda i: (0, 0, 0)) for p in parts],
+        out_specs=pl.BlockSpec((NSY, 16, BLK), lambda i: (0, 0, 0)),
+        out_shape=jax.ShapeDtypeStruct((NSY, 16, BLK), jnp.float32),
+        scratch_shapes=[pltpu.VMEM((16, BLK), jnp.float32)],
+        compiler_params=pltpu.CompilerParams(vmem_limit_bytes=4 * 1024 * 1024),
+        name="square_sums",
+    )(*parts)
+
+
 def halo_kernel(
     fa, ga, fb, gb, fc, gc, ssq_ref, gk_ref, cos_lo, sin_lo, cos_hi, sin_hi,
     before_ref, after_ref, raw, sems,
@@ -262,7 +291,7 @@
             pltpu.SemaphoreType.DMA((2 * sum(CHUNKS), 2)),
         ],
         compiler_params=pltpu.CompilerParams(vmem_limit_bytes=16 * 1024 * 1024),
-        cost_estimate=pl.CostEstimate(flops=10**7, bytes_accessed=3 * 10**6, transcendentals=0),
+        cost_estimate=pl.CostEstimate(flops=10**9, bytes_accessed=10**4, transcendentals=0),
         name="halo_keys",
     )(*features, ssq_k, gk, cosine, sine, cosine, sine)
 
@@ -368,7 +397,7 @@
             dimension_semantics=("arbitrary", "arbitrary"), vmem_limit_bytes=24 * 1024 * 1024
         ),
         cost_estimate=pl.CostEstimate(
-            flops=(1 + 2 * (1 - part)) * 5 * 10**8, bytes_accessed=10**7, transcendentals=10**6
+            flops=(1 + 2 * (1 - part)) * 10**9, bytes_accessed=10**4, transcendentals=10**6
         ),
         name=("window_attention", "window_attention_halo")[part],
     )(*features, *small, *more)
@@ -410,9 +439,6 @@
 def body(tokens, mod_shift, mod_scale, w_query, w_key, w_value, query_gain, key_gain):
     group = lax.axis_index("sx")
     mine = lax.axis_index("sy")
-    z, x = mine // 8, mine // 2 % 4
-    chips = jnp.stack([(z + dz) % 2 * 4 + (x + dx) % 4 for dz, dx in SLOTS])
-    here = (chips[:, None] == jnp.arange(8)[None, :]).astype(jnp.float32)
     rows = BLK * lax.axis_size("sy")
     barrier = lax.optimization_barrier
 
@@ -425,8 +451,8 @@
     cosine, sine = rope_tables(group * rows + jnp.arange(rows, dtype=jnp.int32))
     gq = lax.dynamic_slice(query_gain, (mine * 2 * HD,), (2 * HD,)).reshape(1, 2 * HD)
     gk = lax.dynamic_slice(key_gain, (mine * 2 * HD,), (2 * HD,)).reshape(1, 2 * HD)
-    (left, right, beside), own_w, sent_w, (cosine, sine, gq, gk, here) = barrier(
-        ((left, right, beside), own_w, sent_w, (cosine, sine, gq, gk, here))
+    (left, right, beside), own_w, sent_w, (cosine, sine, gq, gk) = barrier(
+        ((left, right, beside), own_w, sent_w, (cosine, sine, gq, gk))
     )
 
     far, z_right, z_left = from_left(left), from_right(beside), from_z(left)
@@ -443,10 +469,8 @@
     features, parts = [], []
     for made, given, part in (near, middle, last):
         features += [made, from_core(given)]
-        parts.append(part[:2])
-    part = jnp.concatenate(parts, axis=1)
-    part = jnp.sum(here[None, :, :, None] * part[:, :, None, :], axis=1)
-    sent = jnp.broadcast_to(part.reshape(1, 16, BLK), (NSY, 16, BLK))
+        parts.append(part)
+    sent = payload(parts)
     seen = lax.all_to_all(sent, "sy", split_axis=0, concat_axis=0, tiled=True)
     ssq = jnp.sum(seen.reshape(8, 2, 2, 8, BLK), axis=0).transpose(1, 2, 0, 3).reshape(2, 16, BLK)
     before, after = halo(features, ssq[0], gk, cosine, sine)

time: 155 us -> 154 us (level)
    unnamed x24 -> x22, local copies, waits for them, and re-layouts: 9.95 us -> 9.95 us
  transfers between devices with their start and end apart: 16 -> 16, of which waited for: 5 -> 5; matrix products, arithmetic and copies ran while one was open for 15% -> 14% of each run, Pallas kernels for 23% -> 24%
where the time goes in v8:
time: 154 us
  Pallas kernels  48.9 us (32%)
  starting transfers between devices  27.7 us (18%)
  waiting for transfers between devices  25 us (16%)
  blocking collectives  19.9 us (13%)
  other arithmetic  19.1 us (12%)
  local copies, waits for them, and re-layouts  12.3 us (8%)
    pallas_call x3, Pallas kernels, project(): pl.pallas_call(functools.partial(project_kernel, cuts), grid=(3,), in_spe...  25.4 us
    all_to_all x1, blocking collectives, body(): arrived = lax.all_to_all(out, 'sy', split_axis=0, concat_axis=0, tiled=True)  19.9 us
    pallas_call x2, Pallas kernels, attention(): pl.pallas_call(functools.partial(attention_kernel, part), grid=(steps, 2)...  15 us
    unnamed x22, local copies, waits for them, and re-layouts  9.95 us
    ppermute x3, waiting for transfers between devices, from_left(): return lax.ppermute(block, 'sy', chip_move(0, 1, 0))  8.88 us
    mul x1, other arithmetic, rope_tables(): return (jnp.cos(angles), jnp.sin(angles) * sign)  8.12 us
    ppermute x4, waiting for transfers between devices, from_core(): return lax.ppermute(block, 'sy', chip_move(0, 0, 1))  8.07 us
    another operation x1, other arithmetic, body(): sent_w = jnp.stack([key_w, query_w, value_w])  7.03 us
  transfers between devices with their start and end apart: 16, of which 5 were waited for; matrix products, arithmetic and copies ran while one was open for 14% of the time, Pallas kernels for 24%

profile of v8, /device:TPU:1, one launch (start us, length us, event | category | flops | bytes accessed | tf_op | source)
XLA Modules:
  0.0 153.7 jit_solution(16024830580827857020)
XLA Ops:
  0.6 3.3 %layer_norm.1.refs_0_ = bf16[128,5120]{1,0:T(8,128)(2,1)} custom-call(bf16[128,5120]{1,0:T(8,128)(2,1)} %tokens_ref.1, f32[1,5120]{1,0:T(1,128)} %bitcast.26, f32[1,5120]{1,0:T(1,128)} %bitcast.27), custom_call_target="tpu_custom_call" | custom-call | flops 6553600 | bytes 2621440 | tf_op jit(solution)/shard_map/layer_norm/pallas_call | solution.py:37
  3.9 2.0 %collective-permute-start = (bf16[128,5120]{1,0:T(8,128)(2,1)}, bf16[128,5120]{1,0:T(8,128)(2,1)}, u32[]{:S(2)}, u32[]{:S(2)}) collective-permute-start(bf16[128,5120]{1,0:T(8,128)(2,1)} %layer_norm.1.refs_0_), channel_id=1, source_target_pairs={{0,2},{1,3},{2,4},{3,5},{4,6},{5,7},{6,0},{7,1},{8,10},{9,11},{10,... | collective-permute-start | bytes 3932168 | tf_op jit(solution)/shard_map/ppermute | solution.py:112
  6.0 1.3 collective-permute-start.1
  7.3 1.8 %collective-permute-start.2 = (bf16[128,5120]{1,0:T(8,128)(2,1)}, bf16[128,5120]{1,0:T(8,128)(2,1)}, u32[]{:S(2)}, u32[]{:S(2)}) collective-permute-start(bf16[128,5120]{1,0:T(8,128)(2,1)} %layer_norm.1.refs_0_), channel_id=1, source_target_pairs={{0,8},{1,9},{2,10},{3,11},{4,12},{5,13},{6,14},{7,15},{8,0},{9,1},... | collective-permute-start | bytes 3932168 | tf_op jit(solution)/shard_map/ppermute | solution.py:120
  9.5 1.3 dynamic_slice.6
  11.6 8.1 %sine_multiply_fusion = (f32[2048,128]{1,0:T(8,128)S(1)}, f32[2048,128]{1,0:T(8,128)}) fusion(f32[128]{0:T(128)S(1)} %compare_select_fusion, f32[128]{0:T(128)S(1)} %mul.40, f32[2048]{0:T(1024)S(1)} %fusion.4, f32[2048]{0:T(1024)S(1)} %get-tuple-element.86, f32[2048]{0:T(1024)S(1)} %get-tuple-element.85, pred[128]{0:T(512)(128)(4,1)S(1)} %get-tuple-element.87, ...), kind=kLoop, calls=%fused_computation.3 | loop fusion | flops 1048576 | bytes 2123008 | tf_op jit(solution)/shard_map/mul | solution.py:66
  19.7 7.0 %pad_maximum_fusion = (bf16[3,5120,256]{2,1,0:T(8,128)(2,1)S(1)}, bf16[3,5120,256]{2,1,0:T(8,128)(2,1)}) fusion(bf16[1,5120,256]{2,1,0:T(8,128)(2,1)} %bitcast.21, bf16[1,5120,256]{2,1,0:T(8,128)(2,1)} %bitcast.22, bf16[1,5120,256]{2,1,0:T(8,128)(2,1)} %bitcast.23, bf16[]{:T(256)} %constant.77.clone.1), kind=kLoop, calls=%fused_computation | loop fusion | flops 11796480 | bytes 23592962 | tf_op jit(solution)/shard_map/stack | solution.py:449
  26.7 8.9 %collective-permute-done.refs_1_ = bf16[128,5120]{1,0:T(8,128)(2,1)} collective-permute-done((bf16[128,5120]{1,0:T(8,128)(2,1)}, bf16[128,5120]{1,0:T(8,128)(2,1)}, u32[]{:S(2)}, u32[]{:S(2)}) %collective-permute-start) | collective-permute-done | bytes 1310752 | tf_op jit(solution)/shard_map/ppermute | solution.py:112
  37.3 1.9 %collective-permute-start.3 = (bf16[3,5120,256]{2,1,0:T(8,128)(2,1)S(1)}, bf16[3,5120,256]{2,1,0:T(8,128)(2,1)}, u32[]{:S(2)}, u32[]{:S(2)}) collective-permute-start(bf16[3,5120,256]{2,1,0:T(8,128)(2,1)S(1)} %get-tuple-element.48), channel_id=1, source_target_pairs={{0,1},{1,0},{2,3},{3,2},{4,5},{5,4},{6,7},{7,6},{8,9},{9,8},{10,11... | collective-permute-start | bytes 23592968 | tf_op jit(solution)/shard_map/ppermute | solution.py:124
  39.7 1.6 %collective-permute-start.6 = (bf16[128,5120]{1,0:T(8,128)(2,1)}, bf16[128,5120]{1,0:T(8,128)(2,1)}, u32[]{:S(2)}, u32[]{:S(2)}) collective-permute-start(bf16[128,5120]{1,0:T(8,128)(2,1)} %collective-permute-done.refs_1_), channel_id=1, source_target_pairs={{0,8},{1,9},{2,10},{3,11},{4,12},{5,13},{6,14},{7,15},{8,0},{9,1},... | collective-permute-start | bytes 3932168 | tf_op jit(solution)/shard_map/ppermute | solution.py:120
  41.4 1.9 %collective-permute-start.5 = (bf16[128,5120]{1,0:T(8,128)(2,1)}, bf16[128,5120]{1,0:T(8,128)(2,1)}, u32[]{:S(2)}, u32[]{:S(2)}) collective-permute-start(bf16[128,5120]{1,0:T(8,128)(2,1)} %collective-permute-done.2.refs_3_), channel_id=1, source_target_pairs={{0,6},{1,7},{2,0},{3,1},{4,2},{5,3},{6,4},{7,5},{8,14},{9,15},{10,... | collective-permute-start | bytes 3932168 | tf_op jit(solution)/shard_map/ppermute | solution.py:116
  43.3 8.1 %collective-permute-done.3 = bf16[3,5120,256]{2,1,0:T(8,128)(2,1)} collective-permute-done((bf16[3,5120,256]{2,1,0:T(8,128)(2,1)S(1)}, bf16[3,5120,256]{2,1,0:T(8,128)(2,1)}, u32[]{:S(2)}, u32[]{:S(2)}) %collective-permute-start.3) | collective-permute-done | bytes 7864352 | tf_op jit(solution)/shard_map/ppermute | solution.py:124
  51.3 3.7 %broadcast_multiply_fusion.refs_5_.refs_4_ = bf16[3,5120,256]{2,1,0:T(8,128)(2,1)S(1)} fusion(bf16[3,5120,256]{2,1,0:T(8,128)(2,1)} %collective-permute-done.3, bf16[]{:T(256)} %constant.77.clone.1), kind=kLoop, calls=%fused_computation.1 | loop fusion | flops 3932160 | bytes 15728642 | tf_op jit(solution)/shard_map/mul | solution.py:459
  55.1 3.2 %copy-done = bf16[3,5120,256]{2,1,0:T(8,128)(2,1)S(1)} copy-done((bf16[3,5120,256]{2,1,0:T(8,128)(2,1)S(1)}, bf16[3,5120,256]{2,1,0:T(8,128)(2,1)}, u32[]{:S(2)}) %copy-start) | copy-done | bytes 7864344
  58.3 1.3 copy-done.6
  59.6 1.3 copy-done.9
  60.9 11.6 %project.3 = (bf16[3,512,256]{2,1,0:T(8,128)(2,1)S(1)}, bf16[3,512,256]{2,1,0:T(8,128)(2,1)}, f32[3,4,128]{2,1,0:T(4,128)S(1)}) custom-call(bf16[128,5120]{1,0:T(8,128)(2,1)S(1)} %copy-done.6, bf16[128,5120]{1,0:T(8,128)(2,1)} %collective-permute-done.refs_1_, bf16[128,5120]{1,0:T(8,128)(2,1)S(1)} %copy-done.9, ...), custom_call_target="tpu_custom_call" | custom-call | flops 8053063680 | bytes 15728640 | tf_op jit(solution)/shard_map/project/pallas_call | solution.py:162
  72.6 1.4 cut_rows.1
  74.6 2.1 %collective-permute-start.9 = (bf16[48,5120]{1,0:T(8,128)(2,1)S(1)}, bf16[48,5120]{1,0:T(8,128)(2,1)S(1)}, u32[]{:S(2)}, u32[]{:S(2)}) collective-permute-start(bf16[48,5120]{1,0:T(8,128)(2,1)S(1)} %get-tuple-element.58), channel_id=1, source_target_pairs={{0,6},{1,7},{2,0},{3,1},{4,2},{5,3},{6,4},{7,5},{8,14},{9,15},{10,... | collective-permute-start | bytes 1474568 | tf_op jit(solution)/shard_map/ppermute | solution.py:116
  76.7 1.4 collective-permute-start.10
  79.4 9.8 %project.4 = (bf16[3,384,256]{2,1,0:T(8,128)(2,1)S(1)}, bf16[3,384,256]{2,1,0:T(8,128)(2,1)}, f32[3,3,128]{2,1,0:T(4,128)S(1)}) custom-call(bf16[128,5120]{1,0:T(8,128)(2,1)} %collective-permute-done.4.refs_2_.refs_0_, bf16[128,5120]{1,0:T(8,128)(2,1)} %collective-permute-done.6.refs_0_.refs_1_, bf16[128,5120]{1,0:T(8,128)(2,1)} %collective-permute-done.5.refs_1_.refs_2_, ...), custom_call_target="tpu_custom_call" | custom-call | flops 6039797760 | bytes 15728640 | tf_op jit(solution)/shard_map/project/pallas_call | solution.py:162
  89.5 3.9 %project.5 = (bf16[3,128,256]{2,1,0:T(8,128)(2,1)S(1)}, bf16[3,128,256]{2,1,0:T(8,128)(2,1)S(1)}, f32[3,1,128]{2,1,0:T(1,128)S(1)}) custom-call(bf16[48,5120]{1,0:T(8,128)(2,1)S(1)} %collective-permute-done.8.refs_0_, bf16[48,5120]{1,0:T(8,128)(2,1)S(1)} %collective-permute-done.9.refs_1_, bf16[32,5120]{1,0:T(8,128)(2,1)S(1)} %collective-permute-done.10.refs_2_, ...), custom_call_target="tpu_custom_call" | custom-call | flops 2013265920 | bytes 15728640 | tf_op jit(solution)/shard_map/project/pallas_call | solution.py:162
  94.8 4.8 %all-to-all-start = ((f32[16,16,128]{2,1,0:T(8,128)}), f32[16,16,128]{2,1,0:T(8,128)S(1)}, u32[]{:S(2)}, u32[]{:S(2)}) async-start(f32[16,16,128]{2,1,0:T(8,128)} %square_sums.1), calls=%async_computation | async-start | bytes 262144 | tf_op jit(solution)/shard_map/all_to_all | solution.py:474
  99.8 5.9 %all-to-all-done = f32[16,16,128]{2,1,0:T(8,128)S(1)} async-done(((f32[16,16,128]{2,1,0:T(8,128)}), f32[16,16,128]{2,1,0:T(8,128)S(1)}, u32[]{:S(2)}, u32[]{:S(2)}) %all-to-all-start) | async-done | bytes 131104 | tf_op jit(solution)/shard_map/all_to_all | solution.py:474
  108.1 1.9 %halo_keys.1 = (bf16[512,256]{1,0:T(8,128)(2,1)S(1)}, bf16[512,256]{1,0:T(8,128)(2,1)S(1)}) custom-call(bf16[3,512,256]{2,1,0:T(8,128)(2,1)S(1)} %get-tuple-element.52.fa, bf16[3,512,256]{2,1,0:T(8,128)(2,1)} %collective-permute-done.7.ga, bf16[3,384,256]{2,1,0:T(8,128)(2,1)S(1)} %copy-done.4, bf16[3,384,256]{2,1,0:T(8,128)(2,1)} %collective-permute-done.11.gb, ...), custom_call_target="tpu_custom_call" | custom-call | flops 1000000000 | bytes 10000 | tf_op jit(solution)/shard_map/halo_keys/pallas_call | solution.py:283
  110.0 3.4 %collective-permute-start.13 = (bf16[512,256]{1,0:T(8,128)(2,1)S(1)}, bf16[512,256]{1,0:T(8,128)(2,1)S(1)}, u32[]{:S(2)}, u32[]{:S(2)}) collective-permute-start(bf16[512,256]{1,0:T(8,128)(2,1)S(1)} %get-tuple-element.77), channel_id=1, source_target_pairs={{112,0},{0,16},{16,32},{32,48},{48,64},{64,80},{80,96},{96,112},{1... | collective-permute-start | bytes 786440 | tf_op jit(solution)/shard_map/ppermute | solution.py:408
  113.4 2.5 %collective-permute-start.14 = (bf16[512,256]{1,0:T(8,128)(2,1)S(1)}, bf16[512,256]{1,0:T(8,128)(2,1)S(1)}, u32[]{:S(2)}, u32[]{:S(2)}) collective-permute-start(bf16[512,256]{1,0:T(8,128)(2,1)S(1)} %get-tuple-element.78), channel_id=1, source_target_pairs={{16,0},{32,16},{48,32},{64,48},{80,64},{96,80},{112,96},{0,112},{1... | collective-permute-start | bytes 786440 | tf_op jit(solution)/shard_map/ppermute | solution.py:408
  115.9 10.7 %window_attention.1.rest_2_ = bf16[16,2,136,128]{3,2,1,0:T(8,128)(2,1)S(1)} custom-call(bf16[3,512,256]{2,1,0:T(8,128)(2,1)S(1)} %get-tuple-element.52.fa, bf16[3,512,256]{2,1,0:T(8,128)(2,1)} %collective-permute-done.7.ga, bf16[3,384,256]{2,1,0:T(8,128)(2,1)S(1)} %copy-done.5, bf16[3,384,256]{2,1,0:T(8,128)(2,1)} %collective-permute-done.11.gb, ...), custom_call_target="tpu_custom_call" | custom-call | flops 3000000000 | bytes 10000 | tf_op jit(solution)/shard_map/window_attention/pallas_call | solution.py:383
  126.6 1.6 %collective-permute-done.14.rest_1_ = bf16[512,256]{1,0:T(8,128)(2,1)S(1)} collective-permute-done((bf16[512,256]{1,0:T(8,128)(2,1)S(1)}, bf16[512,256]{1,0:T(8,128)(2,1)S(1)}, u32[]{:S(2)}, u32[]{:S(2)}) %collective-permute-start.14) | collective-permute-done | bytes 262176 | tf_op jit(solution)/shard_map/ppermute | solution.py:408
  128.2 4.3 %window_attention_halo.1 = bf16[16,2,136,128]{3,2,1,0:T(8,128)(2,1)S(1)} custom-call(bf16[3,512,256]{2,1,0:T(8,128)(2,1)S(1)} %get-tuple-element.52.fa, bf16[3,512,256]{2,1,0:T(8,128)(2,1)} %collective-permute-done.7.ga, bf16[3,384,256]{2,1,0:T(8,128)(2,1)S(1)} %copy-done.5, ...), custom_call_target="tpu_custom_call", output_to_operand_aliasing={{}: (14, {})} | custom-call | flops 1000000000 | bytes 10000 | tf_op jit(solution)/shard_map/window_attention_halo/pallas_call | solution.py:383
  132.5 19.9 %all_to_all.10.arrived_ref = bf16[16,2,136,128]{3,2,1,0:T(8,128)(2,1)S(1)} all-to-all(bf16[16,2,136,128]{3,2,1,0:T(8,128)(2,1)S(1)} %window_attention_halo.1), channel_id=1, replica_groups=mesh['sx'=8,'sy'=16] {'sy'}, dimensions={0} | all-to-all | bytes 2228224 | tf_op jit(solution)/shard_map/all_to_all | solution.py:481
  152.4 1.3 unpack.1
  (51 shorter events, 9.4 us)
Async XLA Ops:
  3.9 31.7 %collective-permute-start = (bf16[128,5120]{1,0:T(8,128)(2,1)}, bf16[128,5120]{1,0:T(8,128)(2,1)}, u32[]{:S(2)}, u32[]{:S(2)}) collective-permute-start(bf16[128,5120]{1,0:T(8,128)(2,1)} %layer_norm.1.refs_0_), channel_id=1, source_target_pairs={{0,2},{1,3},{2,4},{3,5},{4,6},{5,7},{6,0},{7,1},{8,10},{9,11},{10,... | collective-permute-start | bytes 3932168 | tf_op jit(solution)/shard_map/ppermute | solution.py:112
  6.0 29.6 %collective-permute-start.1 = (bf16[128,5120]{1,0:T(8,128)(2,1)}, bf16[128,5120]{1,0:T(8,128)(2,1)S(1)}, u32[]{:S(2)}, u32[]{:S(2)}) collective-permute-start(bf16[128,5120]{1,0:T(8,128)(2,1)} %layer_norm.1.refs_0_), channel_id=1, source_target_pairs={{0,6},{1,7},{2,0},{3,1},{4,2},{5,3},{6,4},{7,5},{8,14},{9,15},{10,... | collective-permute-start | bytes 3932168 | tf_op jit(solution)/shard_map/ppermute | solution.py:116
  7.3 30.0 %collective-permute-start.2 = (bf16[128,5120]{1,0:T(8,128)(2,1)}, bf16[128,5120]{1,0:T(8,128)(2,1)}, u32[]{:S(2)}, u32[]{:S(2)}) collective-permute-start(bf16[128,5120]{1,0:T(8,128)(2,1)} %layer_norm.1.refs_0_), channel_id=1, source_target_pairs={{0,8},{1,9},{2,10},{3,11},{4,12},{5,13},{6,14},{7,15},{8,0},{9,1},... | collective-permute-start | bytes 3932168 | tf_op jit(solution)/shard_map/ppermute | solution.py:120
  35.6 1.1 copy-start.8
  37.3 14.0 %collective-permute-start.3 = (bf16[3,5120,256]{2,1,0:T(8,128)(2,1)S(1)}, bf16[3,5120,256]{2,1,0:T(8,128)(2,1)}, u32[]{:S(2)}, u32[]{:S(2)}) collective-permute-start(bf16[3,5120,256]{2,1,0:T(8,128)(2,1)S(1)} %get-tuple-element.48), channel_id=1, source_target_pairs={{0,1},{1,0},{2,3},{3,2},{4,5},{5,4},{6,7},{7,6},{8,9},{9,8},{10,11... | collective-permute-start | bytes 23592968 | tf_op jit(solution)/shard_map/ppermute | solution.py:124
  39.2 33.4 %collective-permute-start.4 = (bf16[128,5120]{1,0:T(8,128)(2,1)}, bf16[128,5120]{1,0:T(8,128)(2,1)}, u32[]{:S(2)}, u32[]{:S(2)}) collective-permute-start(bf16[128,5120]{1,0:T(8,128)(2,1)} %collective-permute-done.refs_1_), channel_id=1, source_target_pairs={{0,2},{1,3},{2,4},{3,5},{4,6},{5,7},{6,0},{7,1},{8,10},{9,11},{10,... | collective-permute-start | bytes 3932168 | tf_op jit(solution)/shard_map/ppermute | solution.py:112
  39.7 32.9 %collective-permute-start.6 = (bf16[128,5120]{1,0:T(8,128)(2,1)}, bf16[128,5120]{1,0:T(8,128)(2,1)}, u32[]{:S(2)}, u32[]{:S(2)}) collective-permute-start(bf16[128,5120]{1,0:T(8,128)(2,1)} %collective-permute-done.refs_1_), channel_id=1, source_target_pairs={{0,8},{1,9},{2,10},{3,11},{4,12},{5,13},{6,14},{7,15},{8,0},{9,1},... | collective-permute-start | bytes 3932168 | tf_op jit(solution)/shard_map/ppermute | solution.py:120
  41.4 31.3 %collective-permute-start.5 = (bf16[128,5120]{1,0:T(8,128)(2,1)}, bf16[128,5120]{1,0:T(8,128)(2,1)}, u32[]{:S(2)}, u32[]{:S(2)}) collective-permute-start(bf16[128,5120]{1,0:T(8,128)(2,1)} %collective-permute-done.2.refs_3_), channel_id=1, source_target_pairs={{0,6},{1,7},{2,0},{3,1},{4,2},{5,3},{6,4},{7,5},{8,14},{9,15},{10,... | collective-permute-start | bytes 3932168 | tf_op jit(solution)/shard_map/ppermute | solution.py:116
  55.1 3.2 %copy-start = (bf16[3,5120,256]{2,1,0:T(8,128)(2,1)S(1)}, bf16[3,5120,256]{2,1,0:T(8,128)(2,1)}, u32[]{:S(2)}) copy-start(bf16[3,5120,256]{2,1,0:T(8,128)(2,1)} %get-tuple-element.47.refs_4_.refs_3_) | copy-start | bytes 23592964
  58.3 1.3 copy-start.6
  59.6 1.3 copy-start.9
  74.0 15.3 %collective-permute-start.8 = (bf16[48,5120]{1,0:T(8,128)(2,1)S(1)}, bf16[48,5120]{1,0:T(8,128)(2,1)S(1)}, u32[]{:S(2)}, u32[]{:S(2)}) collective-permute-start(bf16[48,5120]{1,0:T(8,128)(2,1)S(1)} %get-tuple-element.57), channel_id=1, source_target_pairs={{0,2},{1,3},{2,4},{3,5},{4,6},{5,7},{6,0},{7,1},{8,10},{9,11},{10,... | collective-permute-start | bytes 1474568 | tf_op jit(solution)/shard_map/ppermute | solution.py:112
  74.6 14.6 %collective-permute-start.9 = (bf16[48,5120]{1,0:T(8,128)(2,1)S(1)}, bf16[48,5120]{1,0:T(8,128)(2,1)S(1)}, u32[]{:S(2)}, u32[]{:S(2)}) collective-permute-start(bf16[48,5120]{1,0:T(8,128)(2,1)S(1)} %get-tuple-element.58), channel_id=1, source_target_pairs={{0,6},{1,7},{2,0},{3,1},{4,2},{5,3},{6,4},{7,5},{8,14},{9,15},{10,... | collective-permute-start | bytes 1474568 | tf_op jit(solution)/shard_map/ppermute | solution.py:116
  76.7 12.5 %collective-permute-start.10 = (bf16[32,5120]{1,0:T(8,128)(2,1)S(1)}, bf16[32,5120]{1,0:T(8,128)(2,1)S(1)}, u32[]{:S(2)}, u32[]{:S(2)}) collective-permute-start(bf16[32,5120]{1,0:T(8,128)(2,1)S(1)} %get-tuple-element.59), channel_id=1, source_target_pairs={{0,8},{1,9},{2,10},{3,11},{4,12},{5,13},{6,14},{7,15},{8,0},{9,1},... | collective-permute-start | bytes 983048 | tf_op jit(solution)/shard_map/ppermute | solution.py:120
  78.2 27.6 %collective-permute-start.7 = (bf16[3,512,256]{2,1,0:T(8,128)(2,1)}, bf16[3,512,256]{2,1,0:T(8,128)(2,1)}, u32[]{:S(2)}, u32[]{:S(2)}) collective-permute-start(bf16[3,512,256]{2,1,0:T(8,128)(2,1)} %get-tuple-element.53), channel_id=1, source_target_pairs={{0,1},{1,0},{2,3},{3,2},{4,5},{5,4},{6,7},{7,6},{8,9},{9,8},{10,11... | collective-permute-start | bytes 2359304 | tf_op jit(solution)/shard_map/ppermute | solution.py:124
  89.2 4.2 %copy-start.3 = (bf16[3,384,256]{2,1,0:T(8,128)(2,1)}, bf16[3,384,256]{2,1,0:T(8,128)(2,1)S(1)}, u32[]{:S(2)}) copy-start(bf16[3,384,256]{2,1,0:T(8,128)(2,1)S(1)} %get-tuple-element.63.fb) | copy-start | bytes 1769476
  89.3 16.5 %collective-permute-start.11 = (bf16[3,384,256]{2,1,0:T(8,128)(2,1)}, bf16[3,384,256]{2,1,0:T(8,128)(2,1)}, u32[]{:S(2)}, u32[]{:S(2)}) collective-permute-start(bf16[3,384,256]{2,1,0:T(8,128)(2,1)} %get-tuple-element.64), channel_id=1, source_target_pairs={{0,1},{1,0},{2,3},{3,2},{4,5},{5,4},{6,7},{7,6},{8,9},{9,8},{10,11... | collective-permute-start | bytes 1769480 | tf_op jit(solution)/shard_map/ppermute | solution.py:124
  93.5 0.7 copy-start.10
  94.8 10.9 %all-to-all-start = ((f32[16,16,128]{2,1,0:T(8,128)}), f32[16,16,128]{2,1,0:T(8,128)S(1)}, u32[]{:S(2)}, u32[]{:S(2)}) async-start(f32[16,16,128]{2,1,0:T(8,128)} %square_sums.1), calls=%async_computation | async-start | bytes 262144 | tf_op jit(solution)/shard_map/all_to_all | solution.py:474
  99.6 6.1 %collective-permute-start.12 = (bf16[3,128,256]{2,1,0:T(8,128)(2,1)}, bf16[3,128,256]{2,1,0:T(8,128)(2,1)S(1)}, u32[]{:S(2)}, u32[]{:S(2)}) collective-permute-start(bf16[3,128,256]{2,1,0:T(8,128)(2,1)} %copy-done.10), channel_id=1, source_target_pairs={{0,1},{1,0},{2,3},{3,2},{4,5},{5,4},{6,7},{7,6},{8,9},{9,8},{10,11... | collective-permute-start | bytes 589832 | tf_op jit(solution)/shard_map/ppermute | solution.py:124
  105.8 1.2 copy-start.1
  107.0 1.1 copy-start.4
  108.1 7.8 %copy-start.2 = (f32[2048,128]{1,0:T(8,128)S(1)}, f32[2048,128]{1,0:T(8,128)}, u32[]{:S(2)}) copy-start(f32[2048,128]{1,0:T(8,128)} %get-tuple-element.75.cos_lo.cos_hi.cos_ref) | copy-start | bytes 3145732
  108.1 7.8 %copy-start.5 = (bf16[3,384,256]{2,1,0:T(8,128)(2,1)S(1)}, bf16[3,384,256]{2,1,0:T(8,128)(2,1)}, u32[]{:S(2)}) copy-start(bf16[3,384,256]{2,1,0:T(8,128)(2,1)} %copy-done.3) | copy-start | bytes 1769476
  108.1 7.8 %copy-start.7 = (f32[256]{0:T(256)S(1)}, f32[256]{0:T(256)}, u32[]{:S(2)}) copy-start(f32[256]{0:T(256)} %dynamic_slice.6) | copy-start | bytes 3076
  110.0 16.6 %collective-permute-start.13 = (bf16[512,256]{1,0:T(8,128)(2,1)S(1)}, bf16[512,256]{1,0:T(8,128)(2,1)S(1)}, u32[]{:S(2)}, u32[]{:S(2)}) collective-permute-start(bf16[512,256]{1,0:T(8,128)(2,1)S(1)} %get-tuple-element.77), channel_id=1, source_target_pairs={{112,0},{0,16},{16,32},{32,48},{48,64},{64,80},{80,96},{96,112},{1... | collective-permute-start | bytes 786440 | tf_op jit(solution)/shard_map/ppermute | solution.py:408
  113.4 14.8 %collective-permute-start.14 = (bf16[512,256]{1,0:T(8,128)(2,1)S(1)}, bf16[512,256]{1,0:T(8,128)(2,1)S(1)}, u32[]{:S(2)}, u32[]{:S(2)}) collective-permute-start(bf16[512,256]{1,0:T(8,128)(2,1)S(1)} %get-tuple-element.78), channel_id=1, source_target_pairs={{16,0},{32,16},{48,32},{64,48},{80,64},{96,80},{112,96},{0,112},{1... | collective-permute-start | bytes 786440 | tf_op jit(solution)/shard_map/ppermute | solution.py:408

commit v9 on v8

--- a/solution.py
+++ b/solution.py
@@ -360,7 +360,7 @@
             mixed = jnp.dot(
                 vbuf[head, :, window], weight.astype(jnp.bfloat16), preferred_element_type=jnp.float32
             )
-            out_ref[j, 0, 0:BLK, :] = (mixed / total).T.astype(jnp.bfloat16)
+            out_ref[j, 0, 0:BLK, :] = (mixed * (1.0 / total)).T.astype(jnp.bfloat16)
             stats = split3(top * SCALE) + split3(total) + [jnp.zeros((EXTRA - 6, HD), jnp.float32)]
             out_ref[j, 0, BLK : BLK + EXTRA, :] = jnp.concatenate(stats, axis=0).astype(jnp.bfloat16)
 

time: 154 us -> 154 us (level)
  no operation moved by 1% of the time
where the time goes in v9:
time: 154 us
  Pallas kernels  48.9 us (32%)
  starting transfers between devices  27.7 us (18%)
  waiting for transfers between devices  25 us (16%)
  blocking collectives  19.9 us (13%)
  other arithmetic  19.1 us (12%)
  local copies, waits for them, and re-layouts  12.3 us (8%)
    pallas_call x3, Pallas kernels, project(): pl.pallas_call(functools.partial(project_kernel, cuts), grid=(3,), in_spe...  25.4 us
    all_to_all x1, blocking collectives, body(): arrived = lax.all_to_all(out, 'sy', split_axis=0, concat_axis=0, tiled=True)  19.9 us
    pallas_call x2, Pallas kernels, attention(): pl.pallas_call(functools.partial(attention_kernel, part), grid=(steps, 2)...  15 us
    unnamed x22, local copies, waits for them, and re-layouts  9.95 us
    ppermute x3, waiting for transfers between devices, from_left(): return lax.ppermute(block, 'sy', chip_move(0, 1, 0))  8.88 us
    mul x1, other arithmetic, rope_tables(): return (jnp.cos(angles), jnp.sin(angles) * sign)  8.12 us
    ppermute x4, waiting for transfers between devices, from_core(): return lax.ppermute(block, 'sy', chip_move(0, 0, 1))  8.07 us
    another operation x1, other arithmetic, body(): sent_w = jnp.stack([key_w, query_w, value_w])  7.03 us
  transfers between devices with their start and end apart: 16, of which 5 were waited for; matrix products, arithmetic and copies ran while one was open for 14% of the time, Pallas kernels for 24%

profile of v9, /device:TPU:1, one launch (start us, length us, event | category | flops | bytes accessed | tf_op | source)
XLA Modules:
  0.0 153.7 jit_solution(16024830580827857020)
XLA Ops:
  0.6 3.3 %layer_norm.1.refs_0_ = bf16[128,5120]{1,0:T(8,128)(2,1)} custom-call(bf16[128,5120]{1,0:T(8,128)(2,1)} %tokens_ref.1, f32[1,5120]{1,0:T(1,128)} %bitcast.26, f32[1,5120]{1,0:T(1,128)} %bitcast.27), custom_call_target="tpu_custom_call" | custom-call | flops 6553600 | bytes 2621440 | tf_op jit(solution)/shard_map/layer_norm/pallas_call | solution.py:37
  3.9 2.0 %collective-permute-start = (bf16[128,5120]{1,0:T(8,128)(2,1)}, bf16[128,5120]{1,0:T(8,128)(2,1)}, u32[]{:S(2)}, u32[]{:S(2)}) collective-permute-start(bf16[128,5120]{1,0:T(8,128)(2,1)} %layer_norm.1.refs_0_), channel_id=1, source_target_pairs={{0,2},{1,3},{2,4},{3,5},{4,6},{5,7},{6,0},{7,1},{8,10},{9,11},{10,... | collective-permute-start | bytes 3932168 | tf_op jit(solution)/shard_map/ppermute | solution.py:112
  6.0 1.3 collective-permute-start.1
  7.3 1.8 %collective-permute-start.2 = (bf16[128,5120]{1,0:T(8,128)(2,1)}, bf16[128,5120]{1,0:T(8,128)(2,1)}, u32[]{:S(2)}, u32[]{:S(2)}) collective-permute-start(bf16[128,5120]{1,0:T(8,128)(2,1)} %layer_norm.1.refs_0_), channel_id=1, source_target_pairs={{0,8},{1,9},{2,10},{3,11},{4,12},{5,13},{6,14},{7,15},{8,0},{9,1},... | collective-permute-start | bytes 3932168 | tf_op jit(solution)/shard_map/ppermute | solution.py:120
  9.5 1.3 dynamic_slice.6
  11.6 8.1 %sine_multiply_fusion = (f32[2048,128]{1,0:T(8,128)S(1)}, f32[2048,128]{1,0:T(8,128)}) fusion(f32[128]{0:T(128)S(1)} %compare_select_fusion, f32[128]{0:T(128)S(1)} %mul.40, f32[2048]{0:T(1024)S(1)} %fusion.4, f32[2048]{0:T(1024)S(1)} %get-tuple-element.86, f32[2048]{0:T(1024)S(1)} %get-tuple-element.85, pred[128]{0:T(512)(128)(4,1)S(1)} %get-tuple-element.87, ...), kind=kLoop, calls=%fused_computation.3 | loop fusion | flops 1048576 | bytes 2123008 | tf_op jit(solution)/shard_map/mul | solution.py:66
  19.7 7.0 %pad_maximum_fusion = (bf16[3,5120,256]{2,1,0:T(8,128)(2,1)S(1)}, bf16[3,5120,256]{2,1,0:T(8,128)(2,1)}) fusion(bf16[1,5120,256]{2,1,0:T(8,128)(2,1)} %bitcast.21, bf16[1,5120,256]{2,1,0:T(8,128)(2,1)} %bitcast.22, bf16[1,5120,256]{2,1,0:T(8,128)(2,1)} %bitcast.23, bf16[]{:T(256)} %constant.77.clone.1), kind=kLoop, calls=%fused_computation | loop fusion | flops 11796480 | bytes 23592962 | tf_op jit(solution)/shard_map/stack | solution.py:449
  26.7 8.9 %collective-permute-done.refs_1_ = bf16[128,5120]{1,0:T(8,128)(2,1)} collective-permute-done((bf16[128,5120]{1,0:T(8,128)(2,1)}, bf16[128,5120]{1,0:T(8,128)(2,1)}, u32[]{:S(2)}, u32[]{:S(2)}) %collective-permute-start) | collective-permute-done | bytes 1310752 | tf_op jit(solution)/shard_map/ppermute | solution.py:112
  37.3 1.9 %collective-permute-start.3 = (bf16[3,5120,256]{2,1,0:T(8,128)(2,1)S(1)}, bf16[3,5120,256]{2,1,0:T(8,128)(2,1)}, u32[]{:S(2)}, u32[]{:S(2)}) collective-permute-start(bf16[3,5120,256]{2,1,0:T(8,128)(2,1)S(1)} %get-tuple-element.48), channel_id=1, source_target_pairs={{0,1},{1,0},{2,3},{3,2},{4,5},{5,4},{6,7},{7,6},{8,9},{9,8},{10,11... | collective-permute-start | bytes 23592968 | tf_op jit(solution)/shard_map/ppermute | solution.py:124
  39.7 1.6 %collective-permute-start.6 = (bf16[128,5120]{1,0:T(8,128)(2,1)}, bf16[128,5120]{1,0:T(8,128)(2,1)}, u32[]{:S(2)}, u32[]{:S(2)}) collective-permute-start(bf16[128,5120]{1,0:T(8,128)(2,1)} %collective-permute-done.refs_1_), channel_id=1, source_target_pairs={{0,8},{1,9},{2,10},{3,11},{4,12},{5,13},{6,14},{7,15},{8,0},{9,1},... | collective-permute-start | bytes 3932168 | tf_op jit(solution)/shard_map/ppermute | solution.py:120
  41.4 1.9 %collective-permute-start.5 = (bf16[128,5120]{1,0:T(8,128)(2,1)}, bf16[128,5120]{1,0:T(8,128)(2,1)}, u32[]{:S(2)}, u32[]{:S(2)}) collective-permute-start(bf16[128,5120]{1,0:T(8,128)(2,1)} %collective-permute-done.2.refs_3_), channel_id=1, source_target_pairs={{0,6},{1,7},{2,0},{3,1},{4,2},{5,3},{6,4},{7,5},{8,14},{9,15},{10,... | collective-permute-start | bytes 3932168 | tf_op jit(solution)/shard_map/ppermute | solution.py:116
  43.3 8.1 %collective-permute-done.3 = bf16[3,5120,256]{2,1,0:T(8,128)(2,1)} collective-permute-done((bf16[3,5120,256]{2,1,0:T(8,128)(2,1)S(1)}, bf16[3,5120,256]{2,1,0:T(8,128)(2,1)}, u32[]{:S(2)}, u32[]{:S(2)}) %collective-permute-start.3) | collective-permute-done | bytes 7864352 | tf_op jit(solution)/shard_map/ppermute | solution.py:124
  51.3 3.7 %broadcast_multiply_fusion.refs_5_.refs_4_ = bf16[3,5120,256]{2,1,0:T(8,128)(2,1)S(1)} fusion(bf16[3,5120,256]{2,1,0:T(8,128)(2,1)} %collective-permute-done.3, bf16[]{:T(256)} %constant.77.clone.1), kind=kLoop, calls=%fused_computation.1 | loop fusion | flops 3932160 | bytes 15728642 | tf_op jit(solution)/shard_map/mul | solution.py:459
  55.1 3.2 %copy-done = bf16[3,5120,256]{2,1,0:T(8,128)(2,1)S(1)} copy-done((bf16[3,5120,256]{2,1,0:T(8,128)(2,1)S(1)}, bf16[3,5120,256]{2,1,0:T(8,128)(2,1)}, u32[]{:S(2)}) %copy-start) | copy-done | bytes 7864344
  58.3 1.3 copy-done.6
  59.6 1.3 copy-done.9
  60.9 11.6 %project.3 = (bf16[3,512,256]{2,1,0:T(8,128)(2,1)S(1)}, bf16[3,512,256]{2,1,0:T(8,128)(2,1)}, f32[3,4,128]{2,1,0:T(4,128)S(1)}) custom-call(bf16[128,5120]{1,0:T(8,128)(2,1)S(1)} %copy-done.6, bf16[128,5120]{1,0:T(8,128)(2,1)} %collective-permute-done.refs_1_, bf16[128,5120]{1,0:T(8,128)(2,1)S(1)} %copy-done.9, ...), custom_call_target="tpu_custom_call" | custom-call | flops 8053063680 | bytes 15728640 | tf_op jit(solution)/shard_map/project/pallas_call | solution.py:162
  72.6 1.4 cut_rows.1
  74.6 2.1 %collective-permute-start.9 = (bf16[48,5120]{1,0:T(8,128)(2,1)S(1)}, bf16[48,5120]{1,0:T(8,128)(2,1)S(1)}, u32[]{:S(2)}, u32[]{:S(2)}) collective-permute-start(bf16[48,5120]{1,0:T(8,128)(2,1)S(1)} %get-tuple-element.58), channel_id=1, source_target_pairs={{0,6},{1,7},{2,0},{3,1},{4,2},{5,3},{6,4},{7,5},{8,14},{9,15},{10,... | collective-permute-start | bytes 1474568 | tf_op jit(solution)/shard_map/ppermute | solution.py:116
  76.7 1.4 collective-permute-start.10
  79.4 9.8 %project.4 = (bf16[3,384,256]{2,1,0:T(8,128)(2,1)S(1)}, bf16[3,384,256]{2,1,0:T(8,128)(2,1)}, f32[3,3,128]{2,1,0:T(4,128)S(1)}) custom-call(bf16[128,5120]{1,0:T(8,128)(2,1)} %collective-permute-done.4.refs_2_.refs_0_, bf16[128,5120]{1,0:T(8,128)(2,1)} %collective-permute-done.6.refs_0_.refs_1_, bf16[128,5120]{1,0:T(8,128)(2,1)} %collective-permute-done.5.refs_1_.refs_2_, ...), custom_call_target="tpu_custom_call" | custom-call | flops 6039797760 | bytes 15728640 | tf_op jit(solution)/shard_map/project/pallas_call | solution.py:162
  89.5 3.9 %project.5 = (bf16[3,128,256]{2,1,0:T(8,128)(2,1)S(1)}, bf16[3,128,256]{2,1,0:T(8,128)(2,1)S(1)}, f32[3,1,128]{2,1,0:T(1,128)S(1)}) custom-call(bf16[48,5120]{1,0:T(8,128)(2,1)S(1)} %collective-permute-done.8.refs_0_, bf16[48,5120]{1,0:T(8,128)(2,1)S(1)} %collective-permute-done.9.refs_1_, bf16[32,5120]{1,0:T(8,128)(2,1)S(1)} %collective-permute-done.10.refs_2_, ...), custom_call_target="tpu_custom_call" | custom-call | flops 2013265920 | bytes 15728640 | tf_op jit(solution)/shard_map/project/pallas_call | solution.py:162
  94.8 4.8 %all-to-all-start = ((f32[16,16,128]{2,1,0:T(8,128)}), f32[16,16,128]{2,1,0:T(8,128)S(1)}, u32[]{:S(2)}, u32[]{:S(2)}) async-start(f32[16,16,128]{2,1,0:T(8,128)} %square_sums.1), calls=%async_computation | async-start | bytes 262144 | tf_op jit(solution)/shard_map/all_to_all | solution.py:474
  99.8 5.9 %all-to-all-done = f32[16,16,128]{2,1,0:T(8,128)S(1)} async-done(((f32[16,16,128]{2,1,0:T(8,128)}), f32[16,16,128]{2,1,0:T(8,128)S(1)}, u32[]{:S(2)}, u32[]{:S(2)}) %all-to-all-start) | async-done | bytes 131104 | tf_op jit(solution)/shard_map/all_to_all | solution.py:474
  108.1 1.9 %halo_keys.1 = (bf16[512,256]{1,0:T(8,128)(2,1)S(1)}, bf16[512,256]{1,0:T(8,128)(2,1)S(1)}) custom-call(bf16[3,512,256]{2,1,0:T(8,128)(2,1)S(1)} %get-tuple-element.52.fa, bf16[3,512,256]{2,1,0:T(8,128)(2,1)} %collective-permute-done.7.ga, bf16[3,384,256]{2,1,0:T(8,128)(2,1)S(1)} %copy-done.4, bf16[3,384,256]{2,1,0:T(8,128)(2,1)} %collective-permute-done.11.gb, ...), custom_call_target="tpu_custom_call" | custom-call | flops 1000000000 | bytes 10000 | tf_op jit(solution)/shard_map/halo_keys/pallas_call | solution.py:283
  110.0 3.4 %collective-permute-start.13 = (bf16[512,256]{1,0:T(8,128)(2,1)S(1)}, bf16[512,256]{1,0:T(8,128)(2,1)S(1)}, u32[]{:S(2)}, u32[]{:S(2)}) collective-permute-start(bf16[512,256]{1,0:T(8,128)(2,1)S(1)} %get-tuple-element.77), channel_id=1, source_target_pairs={{112,0},{0,16},{16,32},{32,48},{48,64},{64,80},{80,96},{96,112},{1... | collective-permute-start | bytes 786440 | tf_op jit(solution)/shard_map/ppermute | solution.py:408
  113.4 2.5 %collective-permute-start.14 = (bf16[512,256]{1,0:T(8,128)(2,1)S(1)}, bf16[512,256]{1,0:T(8,128)(2,1)S(1)}, u32[]{:S(2)}, u32[]{:S(2)}) collective-permute-start(bf16[512,256]{1,0:T(8,128)(2,1)S(1)} %get-tuple-element.78), channel_id=1, source_target_pairs={{16,0},{32,16},{48,32},{64,48},{80,64},{96,80},{112,96},{0,112},{1... | collective-permute-start | bytes 786440 | tf_op jit(solution)/shard_map/ppermute | solution.py:408
  115.9 10.7 %window_attention.1.rest_2_ = bf16[16,2,136,128]{3,2,1,0:T(8,128)(2,1)S(1)} custom-call(bf16[3,512,256]{2,1,0:T(8,128)(2,1)S(1)} %get-tuple-element.52.fa, bf16[3,512,256]{2,1,0:T(8,128)(2,1)} %collective-permute-done.7.ga, bf16[3,384,256]{2,1,0:T(8,128)(2,1)S(1)} %copy-done.5, bf16[3,384,256]{2,1,0:T(8,128)(2,1)} %collective-permute-done.11.gb, ...), custom_call_target="tpu_custom_call" | custom-call | flops 3000000000 | bytes 10000 | tf_op jit(solution)/shard_map/window_attention/pallas_call | solution.py:383
  126.6 1.6 %collective-permute-done.14.rest_1_ = bf16[512,256]{1,0:T(8,128)(2,1)S(1)} collective-permute-done((bf16[512,256]{1,0:T(8,128)(2,1)S(1)}, bf16[512,256]{1,0:T(8,128)(2,1)S(1)}, u32[]{:S(2)}, u32[]{:S(2)}) %collective-permute-start.14) | collective-permute-done | bytes 262176 | tf_op jit(solution)/shard_map/ppermute | solution.py:408
  128.2 4.3 %window_attention_halo.1 = bf16[16,2,136,128]{3,2,1,0:T(8,128)(2,1)S(1)} custom-call(bf16[3,512,256]{2,1,0:T(8,128)(2,1)S(1)} %get-tuple-element.52.fa, bf16[3,512,256]{2,1,0:T(8,128)(2,1)} %collective-permute-done.7.ga, bf16[3,384,256]{2,1,0:T(8,128)(2,1)S(1)} %copy-done.5, ...), custom_call_target="tpu_custom_call", output_to_operand_aliasing={{}: (14, {})} | custom-call | flops 1000000000 | bytes 10000 | tf_op jit(solution)/shard_map/window_attention_halo/pallas_call | solution.py:383
  132.5 19.9 %all_to_all.10.arrived_ref = bf16[16,2,136,128]{3,2,1,0:T(8,128)(2,1)S(1)} all-to-all(bf16[16,2,136,128]{3,2,1,0:T(8,128)(2,1)S(1)} %window_attention_halo.1), channel_id=1, replica_groups=mesh['sx'=8,'sy'=16] {'sy'}, dimensions={0} | all-to-all | bytes 2228224 | tf_op jit(solution)/shard_map/all_to_all | solution.py:481
  152.4 1.3 unpack.1
  (51 shorter events, 9.4 us)
Async XLA Ops:
  3.9 31.7 %collective-permute-start = (bf16[128,5120]{1,0:T(8,128)(2,1)}, bf16[128,5120]{1,0:T(8,128)(2,1)}, u32[]{:S(2)}, u32[]{:S(2)}) collective-permute-start(bf16[128,5120]{1,0:T(8,128)(2,1)} %layer_norm.1.refs_0_), channel_id=1, source_target_pairs={{0,2},{1,3},{2,4},{3,5},{4,6},{5,7},{6,0},{7,1},{8,10},{9,11},{10,... | collective-permute-start | bytes 3932168 | tf_op jit(solution)/shard_map/ppermute | solution.py:112
  6.0 29.6 %collective-permute-start.1 = (bf16[128,5120]{1,0:T(8,128)(2,1)}, bf16[128,5120]{1,0:T(8,128)(2,1)S(1)}, u32[]{:S(2)}, u32[]{:S(2)}) collective-permute-start(bf16[128,5120]{1,0:T(8,128)(2,1)} %layer_norm.1.refs_0_), channel_id=1, source_target_pairs={{0,6},{1,7},{2,0},{3,1},{4,2},{5,3},{6,4},{7,5},{8,14},{9,15},{10,... | collective-permute-start | bytes 3932168 | tf_op jit(solution)/shard_map/ppermute | solution.py:116
  7.3 30.0 %collective-permute-start.2 = (bf16[128,5120]{1,0:T(8,128)(2,1)}, bf16[128,5120]{1,0:T(8,128)(2,1)}, u32[]{:S(2)}, u32[]{:S(2)}) collective-permute-start(bf16[128,5120]{1,0:T(8,128)(2,1)} %layer_norm.1.refs_0_), channel_id=1, source_target_pairs={{0,8},{1,9},{2,10},{3,11},{4,12},{5,13},{6,14},{7,15},{8,0},{9,1},... | collective-permute-start | bytes 3932168 | tf_op jit(solution)/shard_map/ppermute | solution.py:120
  35.6 1.1 copy-start.8
  37.3 14.0 %collective-permute-start.3 = (bf16[3,5120,256]{2,1,0:T(8,128)(2,1)S(1)}, bf16[3,5120,256]{2,1,0:T(8,128)(2,1)}, u32[]{:S(2)}, u32[]{:S(2)}) collective-permute-start(bf16[3,5120,256]{2,1,0:T(8,128)(2,1)S(1)} %get-tuple-element.48), channel_id=1, source_target_pairs={{0,1},{1,0},{2,3},{3,2},{4,5},{5,4},{6,7},{7,6},{8,9},{9,8},{10,11... | collective-permute-start | bytes 23592968 | tf_op jit(solution)/shard_map/ppermute | solution.py:124
  39.2 33.4 %collective-permute-start.4 = (bf16[128,5120]{1,0:T(8,128)(2,1)}, bf16[128,5120]{1,0:T(8,128)(2,1)}, u32[]{:S(2)}, u32[]{:S(2)}) collective-permute-start(bf16[128,5120]{1,0:T(8,128)(2,1)} %collective-permute-done.refs_1_), channel_id=1, source_target_pairs={{0,2},{1,3},{2,4},{3,5},{4,6},{5,7},{6,0},{7,1},{8,10},{9,11},{10,... | collective-permute-start | bytes 3932168 | tf_op jit(solution)/shard_map/ppermute | solution.py:112
  39.7 32.9 %collective-permute-start.6 = (bf16[128,5120]{1,0:T(8,128)(2,1)}, bf16[128,5120]{1,0:T(8,128)(2,1)}, u32[]{:S(2)}, u32[]{:S(2)}) collective-permute-start(bf16[128,5120]{1,0:T(8,128)(2,1)} %collective-permute-done.refs_1_), channel_id=1, source_target_pairs={{0,8},{1,9},{2,10},{3,11},{4,12},{5,13},{6,14},{7,15},{8,0},{9,1},... | collective-permute-start | bytes 3932168 | tf_op jit(solution)/shard_map/ppermute | solution.py:120
  41.4 31.3 %collective-permute-start.5 = (bf16[128,5120]{1,0:T(8,128)(2,1)}, bf16[128,5120]{1,0:T(8,128)(2,1)}, u32[]{:S(2)}, u32[]{:S(2)}) collective-permute-start(bf16[128,5120]{1,0:T(8,128)(2,1)} %collective-permute-done.2.refs_3_), channel_id=1, source_target_pairs={{0,6},{1,7},{2,0},{3,1},{4,2},{5,3},{6,4},{7,5},{8,14},{9,15},{10,... | collective-permute-start | bytes 3932168 | tf_op jit(solution)/shard_map/ppermute | solution.py:116
  55.1 3.2 %copy-start = (bf16[3,5120,256]{2,1,0:T(8,128)(2,1)S(1)}, bf16[3,5120,256]{2,1,0:T(8,128)(2,1)}, u32[]{:S(2)}) copy-start(bf16[3,5120,256]{2,1,0:T(8,128)(2,1)} %get-tuple-element.47.refs_4_.refs_3_) | copy-start | bytes 23592964
  58.3 1.3 copy-start.6
  59.6 1.3 copy-start.9
  74.0 15.3 %collective-permute-start.8 = (bf16[48,5120]{1,0:T(8,128)(2,1)S(1)}, bf16[48,5120]{1,0:T(8,128)(2,1)S(1)}, u32[]{:S(2)}, u32[]{:S(2)}) collective-permute-start(bf16[48,5120]{1,0:T(8,128)(2,1)S(1)} %get-tuple-element.57), channel_id=1, source_target_pairs={{0,2},{1,3},{2,4},{3,5},{4,6},{5,7},{6,0},{7,1},{8,10},{9,11},{10,... | collective-permute-start | bytes 1474568 | tf_op jit(solution)/shard_map/ppermute | solution.py:112
  74.6 14.6 %collective-permute-start.9 = (bf16[48,5120]{1,0:T(8,128)(2,1)S(1)}, bf16[48,5120]{1,0:T(8,128)(2,1)S(1)}, u32[]{:S(2)}, u32[]{:S(2)}) collective-permute-start(bf16[48,5120]{1,0:T(8,128)(2,1)S(1)} %get-tuple-element.58), channel_id=1, source_target_pairs={{0,6},{1,7},{2,0},{3,1},{4,2},{5,3},{6,4},{7,5},{8,14},{9,15},{10,... | collective-permute-start | bytes 1474568 | tf_op jit(solution)/shard_map/ppermute | solution.py:116
  76.7 12.5 %collective-permute-start.10 = (bf16[32,5120]{1,0:T(8,128)(2,1)S(1)}, bf16[32,5120]{1,0:T(8,128)(2,1)S(1)}, u32[]{:S(2)}, u32[]{:S(2)}) collective-permute-start(bf16[32,5120]{1,0:T(8,128)(2,1)S(1)} %get-tuple-element.59), channel_id=1, source_target_pairs={{0,8},{1,9},{2,10},{3,11},{4,12},{5,13},{6,14},{7,15},{8,0},{9,1},... | collective-permute-start | bytes 983048 | tf_op jit(solution)/shard_map/ppermute | solution.py:120
  78.2 27.6 %collective-permute-start.7 = (bf16[3,512,256]{2,1,0:T(8,128)(2,1)}, bf16[3,512,256]{2,1,0:T(8,128)(2,1)}, u32[]{:S(2)}, u32[]{:S(2)}) collective-permute-start(bf16[3,512,256]{2,1,0:T(8,128)(2,1)} %get-tuple-element.53), channel_id=1, source_target_pairs={{0,1},{1,0},{2,3},{3,2},{4,5},{5,4},{6,7},{7,6},{8,9},{9,8},{10,11... | collective-permute-start | bytes 2359304 | tf_op jit(solution)/shard_map/ppermute | solution.py:124
  89.2 4.2 %copy-start.3 = (bf16[3,384,256]{2,1,0:T(8,128)(2,1)}, bf16[3,384,256]{2,1,0:T(8,128)(2,1)S(1)}, u32[]{:S(2)}) copy-start(bf16[3,384,256]{2,1,0:T(8,128)(2,1)S(1)} %get-tuple-element.63.fb) | copy-start | bytes 1769476
  89.3 16.5 %collective-permute-start.11 = (bf16[3,384,256]{2,1,0:T(8,128)(2,1)}, bf16[3,384,256]{2,1,0:T(8,128)(2,1)}, u32[]{:S(2)}, u32[]{:S(2)}) collective-permute-start(bf16[3,384,256]{2,1,0:T(8,128)(2,1)} %get-tuple-element.64), channel_id=1, source_target_pairs={{0,1},{1,0},{2,3},{3,2},{4,5},{5,4},{6,7},{7,6},{8,9},{9,8},{10,11... | collective-permute-start | bytes 1769480 | tf_op jit(solution)/shard_map/ppermute | solution.py:124
  93.5 0.7 copy-start.10
  94.8 10.9 %all-to-all-start = ((f32[16,16,128]{2,1,0:T(8,128)}), f32[16,16,128]{2,1,0:T(8,128)S(1)}, u32[]{:S(2)}, u32[]{:S(2)}) async-start(f32[16,16,128]{2,1,0:T(8,128)} %square_sums.1), calls=%async_computation | async-start | bytes 262144 | tf_op jit(solution)/shard_map/all_to_all | solution.py:474
  99.6 6.1 %collective-permute-start.12 = (bf16[3,128,256]{2,1,0:T(8,128)(2,1)}, bf16[3,128,256]{2,1,0:T(8,128)(2,1)S(1)}, u32[]{:S(2)}, u32[]{:S(2)}) collective-permute-start(bf16[3,128,256]{2,1,0:T(8,128)(2,1)} %copy-done.10), channel_id=1, source_target_pairs={{0,1},{1,0},{2,3},{3,2},{4,5},{5,4},{6,7},{7,6},{8,9},{9,8},{10,11... | collective-permute-start | bytes 589832 | tf_op jit(solution)/shard_map/ppermute | solution.py:124
  105.8 1.2 copy-start.1
  107.0 1.1 copy-start.4
  108.1 7.8 %copy-start.2 = (f32[2048,128]{1,0:T(8,128)S(1)}, f32[2048,128]{1,0:T(8,128)}, u32[]{:S(2)}) copy-start(f32[2048,128]{1,0:T(8,128)} %get-tuple-element.75.cos_lo.cos_hi.cos_ref) | copy-start | bytes 3145732
  108.1 7.8 %copy-start.5 = (bf16[3,384,256]{2,1,0:T(8,128)(2,1)S(1)}, bf16[3,384,256]{2,1,0:T(8,128)(2,1)}, u32[]{:S(2)}) copy-start(bf16[3,384,256]{2,1,0:T(8,128)(2,1)} %copy-done.3) | copy-start | bytes 1769476
  108.1 7.8 %copy-start.7 = (f32[256]{0:T(256)S(1)}, f32[256]{0:T(256)}, u32[]{:S(2)}) copy-start(f32[256]{0:T(256)} %dynamic_slice.6) | copy-start | bytes 3076
  110.0 16.6 %collective-permute-start.13 = (bf16[512,256]{1,0:T(8,128)(2,1)S(1)}, bf16[512,256]{1,0:T(8,128)(2,1)S(1)}, u32[]{:S(2)}, u32[]{:S(2)}) collective-permute-start(bf16[512,256]{1,0:T(8,128)(2,1)S(1)} %get-tuple-element.77), channel_id=1, source_target_pairs={{112,0},{0,16},{16,32},{32,48},{48,64},{64,80},{80,96},{96,112},{1... | collective-permute-start | bytes 786440 | tf_op jit(solution)/shard_map/ppermute | solution.py:408
  113.4 14.8 %collective-permute-start.14 = (bf16[512,256]{1,0:T(8,128)(2,1)S(1)}, bf16[512,256]{1,0:T(8,128)(2,1)S(1)}, u32[]{:S(2)}, u32[]{:S(2)}) collective-permute-start(bf16[512,256]{1,0:T(8,128)(2,1)S(1)} %get-tuple-element.78), channel_id=1, source_target_pairs={{16,0},{32,16},{48,32},{64,48},{80,64},{96,80},{112,96},{0,112},{1... | collective-permute-start | bytes 786440 | tf_op jit(solution)/shard_map/ppermute | solution.py:408

commit v10 on v8

--- a/solution.py
+++ b/solution.py
@@ -144,7 +144,7 @@
 
     total = None
     for weight, out in ((own_w, own_ref), (other_w, other_ref)):
-        made = jnp.dot(x_ref[...], weight[0], preferred_element_type=jnp.float32).astype(jnp.bfloat16)
+        made = jnp.dot(x_ref[...], weight[pl.program_id(0)], preferred_element_type=jnp.float32).astype(jnp.bfloat16)
         out[0] = made
         wide = made.astype(jnp.float32)
         part = jnp.sum(wide * wide, axis=-1, keepdims=True)
@@ -156,7 +156,7 @@
 def project(arrays, cuts, own_w, other_w):
     rows = sum(count for _, _, count in cuts)
     depth, wide = own_w.shape[1:]
-    w_spec = pl.BlockSpec((1, depth, wide), lambda i: (i, 0, 0))
+    w_spec = pl.BlockSpec(memory_space=pltpu.VMEM)
     o_spec = pl.BlockSpec((1, rows, wide), lambda i: (i, 0, 0))
     out = jax.ShapeDtypeStruct((3, rows, wide), jnp.bfloat16)
     return pl.pallas_call(
@@ -168,7 +168,7 @@
         scratch_shapes=[pltpu.VMEM((rows, depth), jnp.bfloat16), pltpu.SemaphoreType.DMA((len(cuts),))],
         compiler_params=pltpu.CompilerParams(
             dimension_semantics=("arbitrary",),
-            vmem_limit_bytes=2 * rows * depth + 8 * depth * wide + 4 * 1024 * 1024,
+            vmem_limit_bytes=2 * rows * depth + 6 * 1024 * 1024,
         ),
         cost_estimate=pl.CostEstimate(
             flops=12 * rows * depth * wide, bytes_accessed=12 * depth * wide, transcendentals=0

time: 154 us -> 154 us (level)
    unnamed x22 -> x26, local copies, waits for them, and re-layouts: 9.95 us -> 9.97 us
where the time goes in v10:
time: 154 us
  Pallas kernels  48.6 us (32%)
  starting transfers between devices  27.8 us (18%)
  waiting for transfers between devices  25.1 us (16%)
  blocking collectives  19.8 us (13%)
  other arithmetic  19 us (12%)
  local copies, waits for them, and re-layouts  12.3 us (8%)
    pallas_call x3, Pallas kernels, project(): pl.pallas_call(functools.partial(project_kernel, cuts), grid=(3,), in_spe...  25.1 us
    all_to_all x1, blocking collectives, body(): arrived = lax.all_to_all(out, 'sy', split_axis=0, concat_axis=0, tiled=True)  19.8 us
    pallas_call x2, Pallas kernels, attention(): pl.pallas_call(functools.partial(attention_kernel, part), grid=(steps, 2)...  15 us
    unnamed x26, local copies, waits for them, and re-layouts  9.97 us
    ppermute x3, waiting for transfers between devices, from_left(): return lax.ppermute(block, 'sy', chip_move(0, 1, 0))  8.94 us
    mul x1, other arithmetic, rope_tables(): return (jnp.cos(angles), jnp.sin(angles) * sign)  8.12 us
    ppermute x4, waiting for transfers between devices, from_core(): return lax.ppermute(block, 'sy', chip_move(0, 0, 1))  8.07 us
    another operation x1, other arithmetic, body(): sent_w = jnp.stack([key_w, query_w, value_w])  6.98 us
  transfers between devices with their start and end apart: 16, of which 5 were waited for; matrix products, arithmetic and copies ran while one was open for 14% of the time, Pallas kernels for 24%

profile of v10, /device:TPU:1, one launch (start us, length us, event | category | flops | bytes accessed | tf_op | source)
XLA Modules:
  0.0 153.5 jit_solution(6791646173564621281)
XLA Ops:
  0.6 3.3 %layer_norm.1.refs_0_ = bf16[128,5120]{1,0:T(8,128)(2,1)} custom-call(bf16[128,5120]{1,0:T(8,128)(2,1)} %tokens_ref.1, f32[1,5120]{1,0:T(1,128)} %bitcast.28, f32[1,5120]{1,0:T(1,128)} %bitcast.29), custom_call_target="tpu_custom_call" | custom-call | flops 6553600 | bytes 2621440 | tf_op jit(solution)/shard_map/layer_norm/pallas_call | solution.py:37
  3.9 2.0 %collective-permute-start = (bf16[128,5120]{1,0:T(8,128)(2,1)}, bf16[128,5120]{1,0:T(8,128)(2,1)}, u32[]{:S(2)}, u32[]{:S(2)}) collective-permute-start(bf16[128,5120]{1,0:T(8,128)(2,1)} %layer_norm.1.refs_0_), channel_id=1, source_target_pairs={{0,2},{1,3},{2,4},{3,5},{4,6},{5,7},{6,0},{7,1},{8,10},{9,11},{10,... | collective-permute-start | bytes 3932168 | tf_op jit(solution)/shard_map/ppermute | solution.py:112
  6.0 1.3 collective-permute-start.1
  7.2 1.8 %collective-permute-start.2 = (bf16[128,5120]{1,0:T(8,128)(2,1)}, bf16[128,5120]{1,0:T(8,128)(2,1)}, u32[]{:S(2)}, u32[]{:S(2)}) collective-permute-start(bf16[128,5120]{1,0:T(8,128)(2,1)} %layer_norm.1.refs_0_), channel_id=1, source_target_pairs={{0,8},{1,9},{2,10},{3,11},{4,12},{5,13},{6,14},{7,15},{8,0},{9,1},... | collective-permute-start | bytes 3932168 | tf_op jit(solution)/shard_map/ppermute | solution.py:120
  9.5 1.3 dynamic_slice.6
  11.6 8.1 %sine_multiply_fusion = (f32[2048,128]{1,0:T(8,128)S(1)}, f32[2048,128]{1,0:T(8,128)}) fusion(f32[128]{0:T(128)S(1)} %compare_select_fusion, f32[128]{0:T(128)S(1)} %mul.40, f32[2048]{0:T(1024)S(1)} %fusion.4, f32[2048]{0:T(1024)S(1)} %get-tuple-element.86, f32[2048]{0:T(1024)S(1)} %get-tuple-element.85, pred[128]{0:T(512)(128)(4,1)S(1)} %get-tuple-element.87, ...), kind=kLoop, calls=%fused_computation.3 | loop fusion | flops 1048576 | bytes 2123008 | tf_op jit(solution)/shard_map/mul | solution.py:66
  19.7 7.0 %pad_maximum_fusion = (bf16[3,5120,256]{2,1,0:T(8,128)(2,1)S(1)}, bf16[3,5120,256]{2,1,0:T(8,128)(2,1)}) fusion(bf16[1,5120,256]{2,1,0:T(8,128)(2,1)} %bitcast.23, bf16[1,5120,256]{2,1,0:T(8,128)(2,1)} %bitcast.24, bf16[1,5120,256]{2,1,0:T(8,128)(2,1)} %bitcast.25, bf16[]{:T(256)} %constant.77.clone.1), kind=kLoop, calls=%fused_computation | loop fusion | flops 11796480 | bytes 23592962 | tf_op jit(solution)/shard_map/stack | solution.py:449
  26.7 8.9 %collective-permute-done.refs_1_ = bf16[128,5120]{1,0:T(8,128)(2,1)} collective-permute-done((bf16[128,5120]{1,0:T(8,128)(2,1)}, bf16[128,5120]{1,0:T(8,128)(2,1)}, u32[]{:S(2)}, u32[]{:S(2)}) %collective-permute-start) | collective-permute-done | bytes 1310752 | tf_op jit(solution)/shard_map/ppermute | solution.py:112
  37.3 1.9 %collective-permute-start.3 = (bf16[3,5120,256]{2,1,0:T(8,128)(2,1)S(1)}, bf16[3,5120,256]{2,1,0:T(8,128)(2,1)}, u32[]{:S(2)}, u32[]{:S(2)}) collective-permute-start(bf16[3,5120,256]{2,1,0:T(8,128)(2,1)S(1)} %get-tuple-element.48), channel_id=1, source_target_pairs={{0,1},{1,0},{2,3},{3,2},{4,5},{5,4},{6,7},{7,6},{8,9},{9,8},{10,11... | collective-permute-start | bytes 23592968 | tf_op jit(solution)/shard_map/ppermute | solution.py:124
  39.7 1.6 %collective-permute-start.6 = (bf16[128,5120]{1,0:T(8,128)(2,1)}, bf16[128,5120]{1,0:T(8,128)(2,1)}, u32[]{:S(2)}, u32[]{:S(2)}) collective-permute-start(bf16[128,5120]{1,0:T(8,128)(2,1)} %collective-permute-done.refs_1_), channel_id=1, source_target_pairs={{0,8},{1,9},{2,10},{3,11},{4,12},{5,13},{6,14},{7,15},{8,0},{9,1},... | collective-permute-start | bytes 3932168 | tf_op jit(solution)/shard_map/ppermute | solution.py:120
  41.4 1.9 %collective-permute-start.5 = (bf16[128,5120]{1,0:T(8,128)(2,1)}, bf16[128,5120]{1,0:T(8,128)(2,1)}, u32[]{:S(2)}, u32[]{:S(2)}) collective-permute-start(bf16[128,5120]{1,0:T(8,128)(2,1)} %collective-permute-done.2.refs_3_), channel_id=1, source_target_pairs={{0,6},{1,7},{2,0},{3,1},{4,2},{5,3},{6,4},{7,5},{8,14},{9,15},{10,... | collective-permute-start | bytes 3932168 | tf_op jit(solution)/shard_map/ppermute | solution.py:116
  43.3 8.1 %collective-permute-done.3 = bf16[3,5120,256]{2,1,0:T(8,128)(2,1)} collective-permute-done((bf16[3,5120,256]{2,1,0:T(8,128)(2,1)S(1)}, bf16[3,5120,256]{2,1,0:T(8,128)(2,1)}, u32[]{:S(2)}, u32[]{:S(2)}) %collective-permute-start.3) | collective-permute-done | bytes 7864352 | tf_op jit(solution)/shard_map/ppermute | solution.py:124
  51.3 3.7 %broadcast_multiply_fusion.refs_5_.refs_4_ = bf16[3,5120,256]{2,1,0:T(8,128)(2,1)S(1)} fusion(bf16[3,5120,256]{2,1,0:T(8,128)(2,1)} %collective-permute-done.3, bf16[]{:T(256)} %constant.77.clone.1), kind=kLoop, calls=%fused_computation.1 | loop fusion | flops 3932160 | bytes 15728642 | tf_op jit(solution)/shard_map/mul | solution.py:459
  55.1 3.2 %copy-done = bf16[3,5120,256]{2,1,0:T(8,128)(2,1)S(1)} copy-done((bf16[3,5120,256]{2,1,0:T(8,128)(2,1)S(1)}, bf16[3,5120,256]{2,1,0:T(8,128)(2,1)}, u32[]{:S(2)}) %copy-start) | copy-done | bytes 7864344
  58.3 1.3 copy-done.6
  59.6 1.3 copy-done.9
  60.9 11.6 %project.3 = (bf16[3,512,256]{2,1,0:T(8,128)(2,1)S(1)}, bf16[3,512,256]{2,1,0:T(8,128)(2,1)}, f32[3,4,128]{2,1,0:T(4,128)S(1)}) custom-call(bf16[128,5120]{1,0:T(8,128)(2,1)S(1)} %copy-done.6, bf16[128,5120]{1,0:T(8,128)(2,1)} %collective-permute-done.refs_1_, bf16[128,5120]{1,0:T(8,128)(2,1)S(1)} %copy-done.9, ...), custom_call_target="tpu_custom_call" | custom-call | flops 8053063680 | bytes 15728640 | tf_op jit(solution)/shard_map/project/pallas_call | solution.py:162
  72.5 1.4 cut_rows.1
  74.6 2.1 %collective-permute-start.9 = (bf16[48,5120]{1,0:T(8,128)(2,1)S(1)}, bf16[48,5120]{1,0:T(8,128)(2,1)S(1)}, u32[]{:S(2)}, u32[]{:S(2)}) collective-permute-start(bf16[48,5120]{1,0:T(8,128)(2,1)S(1)} %get-tuple-element.58), channel_id=1, source_target_pairs={{0,6},{1,7},{2,0},{3,1},{4,2},{5,3},{6,4},{7,5},{8,14},{9,15},{10,... | collective-permute-start | bytes 1474568 | tf_op jit(solution)/shard_map/ppermute | solution.py:116
  76.7 1.4 collective-permute-start.10
  79.3 9.7 %project.4 = (bf16[3,384,256]{2,1,0:T(8,128)(2,1)S(1)}, bf16[3,384,256]{2,1,0:T(8,128)(2,1)}, f32[3,3,128]{2,1,0:T(4,128)S(1)}) custom-call(bf16[128,5120]{1,0:T(8,128)(2,1)} %collective-permute-done.4.refs_2_.refs_0_, bf16[128,5120]{1,0:T(8,128)(2,1)} %collective-permute-done.6.refs_0_.refs_1_, bf16[128,5120]{1,0:T(8,128)(2,1)} %collective-permute-done.5.refs_1_.refs_2_, ...), custom_call_target="tpu_custom_call" | custom-call | flops 6039797760 | bytes 15728640 | tf_op jit(solution)/shard_map/project/pallas_call | solution.py:162
  89.9 3.8 %project.5 = (bf16[3,128,256]{2,1,0:T(8,128)(2,1)S(1)}, bf16[3,128,256]{2,1,0:T(8,128)(2,1)S(1)}, f32[3,1,128]{2,1,0:T(1,128)S(1)}) custom-call(bf16[48,5120]{1,0:T(8,128)(2,1)S(1)} %collective-permute-done.8.refs_0_, bf16[48,5120]{1,0:T(8,128)(2,1)S(1)} %collective-permute-done.9.refs_1_, bf16[32,5120]{1,0:T(8,128)(2,1)S(1)} %collective-permute-done.10.refs_2_, ...), custom_call_target="tpu_custom_call" | custom-call | flops 2013265920 | bytes 15728640 | tf_op jit(solution)/shard_map/project/pallas_call | solution.py:162
  95.1 4.5 %all-to-all-start = ((f32[16,16,128]{2,1,0:T(8,128)}), f32[16,16,128]{2,1,0:T(8,128)S(1)}, u32[]{:S(2)}, u32[]{:S(2)}) async-start(f32[16,16,128]{2,1,0:T(8,128)} %square_sums.1), calls=%async_computation | async-start | bytes 262144 | tf_op jit(solution)/shard_map/all_to_all | solution.py:474
  99.7 5.9 %all-to-all-done = f32[16,16,128]{2,1,0:T(8,128)S(1)} async-done(((f32[16,16,128]{2,1,0:T(8,128)}), f32[16,16,128]{2,1,0:T(8,128)S(1)}, u32[]{:S(2)}, u32[]{:S(2)}) %all-to-all-start) | async-done | bytes 131104 | tf_op jit(solution)/shard_map/all_to_all | solution.py:474
  108.0 1.9 %halo_keys.1 = (bf16[512,256]{1,0:T(8,128)(2,1)S(1)}, bf16[512,256]{1,0:T(8,128)(2,1)S(1)}) custom-call(bf16[3,512,256]{2,1,0:T(8,128)(2,1)S(1)} %get-tuple-element.52.fa, bf16[3,512,256]{2,1,0:T(8,128)(2,1)} %collective-permute-done.7.ga, bf16[3,384,256]{2,1,0:T(8,128)(2,1)S(1)} %copy-done.4, bf16[3,384,256]{2,1,0:T(8,128)(2,1)} %collective-permute-done.11.gb, ...), custom_call_target="tpu_custom_call" | custom-call | flops 1000000000 | bytes 10000 | tf_op jit(solution)/shard_map/halo_keys/pallas_call | solution.py:283
  109.9 3.4 %collective-permute-start.13 = (bf16[512,256]{1,0:T(8,128)(2,1)S(1)}, bf16[512,256]{1,0:T(8,128)(2,1)S(1)}, u32[]{:S(2)}, u32[]{:S(2)}) collective-permute-start(bf16[512,256]{1,0:T(8,128)(2,1)S(1)} %get-tuple-element.77), channel_id=1, source_target_pairs={{112,0},{0,16},{16,32},{32,48},{48,64},{64,80},{80,96},{96,112},{1... | collective-permute-start | bytes 786440 | tf_op jit(solution)/shard_map/ppermute | solution.py:408
  113.3 2.5 %collective-permute-start.14 = (bf16[512,256]{1,0:T(8,128)(2,1)S(1)}, bf16[512,256]{1,0:T(8,128)(2,1)S(1)}, u32[]{:S(2)}, u32[]{:S(2)}) collective-permute-start(bf16[512,256]{1,0:T(8,128)(2,1)S(1)} %get-tuple-element.78), channel_id=1, source_target_pairs={{16,0},{32,16},{48,32},{64,48},{80,64},{96,80},{112,96},{0,112},{1... | collective-permute-start | bytes 786440 | tf_op jit(solution)/shard_map/ppermute | solution.py:408
  115.8 10.7 %window_attention.1.rest_2_ = bf16[16,2,136,128]{3,2,1,0:T(8,128)(2,1)S(1)} custom-call(bf16[3,512,256]{2,1,0:T(8,128)(2,1)S(1)} %get-tuple-element.52.fa, bf16[3,512,256]{2,1,0:T(8,128)(2,1)} %collective-permute-done.7.ga, bf16[3,384,256]{2,1,0:T(8,128)(2,1)S(1)} %copy-done.5, bf16[3,384,256]{2,1,0:T(8,128)(2,1)} %collective-permute-done.11.gb, ...), custom_call_target="tpu_custom_call" | custom-call | flops 3000000000 | bytes 10000 | tf_op jit(solution)/shard_map/window_attention/pallas_call | solution.py:383
  126.5 1.6 %collective-permute-done.14.rest_1_ = bf16[512,256]{1,0:T(8,128)(2,1)S(1)} collective-permute-done((bf16[512,256]{1,0:T(8,128)(2,1)S(1)}, bf16[512,256]{1,0:T(8,128)(2,1)S(1)}, u32[]{:S(2)}, u32[]{:S(2)}) %collective-permute-start.14) | collective-permute-done | bytes 262176 | tf_op jit(solution)/shard_map/ppermute | solution.py:408
  128.1 4.3 %window_attention_halo.1 = bf16[16,2,136,128]{3,2,1,0:T(8,128)(2,1)S(1)} custom-call(bf16[3,512,256]{2,1,0:T(8,128)(2,1)S(1)} %get-tuple-element.52.fa, bf16[3,512,256]{2,1,0:T(8,128)(2,1)} %collective-permute-done.7.ga, bf16[3,384,256]{2,1,0:T(8,128)(2,1)S(1)} %copy-done.5, ...), custom_call_target="tpu_custom_call", output_to_operand_aliasing={{}: (14, {})} | custom-call | flops 1000000000 | bytes 10000 | tf_op jit(solution)/shard_map/window_attention_halo/pallas_call | solution.py:383
  132.4 19.8 %all_to_all.10.arrived_ref = bf16[16,2,136,128]{3,2,1,0:T(8,128)(2,1)S(1)} all-to-all(bf16[16,2,136,128]{3,2,1,0:T(8,128)(2,1)S(1)} %window_attention_halo.1), channel_id=1, replica_groups=mesh['sx'=8,'sy'=16] {'sy'}, dimensions={0} | all-to-all | bytes 2228224 | tf_op jit(solution)/shard_map/all_to_all | solution.py:481
  152.3 1.3 unpack.1
  (56 shorter events, 9.9 us)
Async XLA Ops:
  3.9 31.7 %collective-permute-start = (bf16[128,5120]{1,0:T(8,128)(2,1)}, bf16[128,5120]{1,0:T(8,128)(2,1)}, u32[]{:S(2)}, u32[]{:S(2)}) collective-permute-start(bf16[128,5120]{1,0:T(8,128)(2,1)} %layer_norm.1.refs_0_), channel_id=1, source_target_pairs={{0,2},{1,3},{2,4},{3,5},{4,6},{5,7},{6,0},{7,1},{8,10},{9,11},{10,... | collective-permute-start | bytes 3932168 | tf_op jit(solution)/shard_map/ppermute | solution.py:112
  6.0 29.6 %collective-permute-start.1 = (bf16[128,5120]{1,0:T(8,128)(2,1)}, bf16[128,5120]{1,0:T(8,128)(2,1)S(1)}, u32[]{:S(2)}, u32[]{:S(2)}) collective-permute-start(bf16[128,5120]{1,0:T(8,128)(2,1)} %layer_norm.1.refs_0_), channel_id=1, source_target_pairs={{0,6},{1,7},{2,0},{3,1},{4,2},{5,3},{6,4},{7,5},{8,14},{9,15},{10,... | collective-permute-start | bytes 3932168 | tf_op jit(solution)/shard_map/ppermute | solution.py:116
  7.2 30.0 %collective-permute-start.2 = (bf16[128,5120]{1,0:T(8,128)(2,1)}, bf16[128,5120]{1,0:T(8,128)(2,1)}, u32[]{:S(2)}, u32[]{:S(2)}) collective-permute-start(bf16[128,5120]{1,0:T(8,128)(2,1)} %layer_norm.1.refs_0_), channel_id=1, source_target_pairs={{0,8},{1,9},{2,10},{3,11},{4,12},{5,13},{6,14},{7,15},{8,0},{9,1},... | collective-permute-start | bytes 3932168 | tf_op jit(solution)/shard_map/ppermute | solution.py:120
  35.6 1.1 copy-start.8
  37.3 14.0 %collective-permute-start.3 = (bf16[3,5120,256]{2,1,0:T(8,128)(2,1)S(1)}, bf16[3,5120,256]{2,1,0:T(8,128)(2,1)}, u32[]{:S(2)}, u32[]{:S(2)}) collective-permute-start(bf16[3,5120,256]{2,1,0:T(8,128)(2,1)S(1)} %get-tuple-element.48), channel_id=1, source_target_pairs={{0,1},{1,0},{2,3},{3,2},{4,5},{5,4},{6,7},{7,6},{8,9},{9,8},{10,11... | collective-permute-start | bytes 23592968 | tf_op jit(solution)/shard_map/ppermute | solution.py:124
  39.1 33.4 %collective-permute-start.4 = (bf16[128,5120]{1,0:T(8,128)(2,1)}, bf16[128,5120]{1,0:T(8,128)(2,1)}, u32[]{:S(2)}, u32[]{:S(2)}) collective-permute-start(bf16[128,5120]{1,0:T(8,128)(2,1)} %collective-permute-done.refs_1_), channel_id=1, source_target_pairs={{0,2},{1,3},{2,4},{3,5},{4,6},{5,7},{6,0},{7,1},{8,10},{9,11},{10,... | collective-permute-start | bytes 3932168 | tf_op jit(solution)/shard_map/ppermute | solution.py:112
  39.7 32.8 %collective-permute-start.6 = (bf16[128,5120]{1,0:T(8,128)(2,1)}, bf16[128,5120]{1,0:T(8,128)(2,1)}, u32[]{:S(2)}, u32[]{:S(2)}) collective-permute-start(bf16[128,5120]{1,0:T(8,128)(2,1)} %collective-permute-done.refs_1_), channel_id=1, source_target_pairs={{0,8},{1,9},{2,10},{3,11},{4,12},{5,13},{6,14},{7,15},{8,0},{9,1},... | collective-permute-start | bytes 3932168 | tf_op jit(solution)/shard_map/ppermute | solution.py:120
  41.4 31.2 %collective-permute-start.5 = (bf16[128,5120]{1,0:T(8,128)(2,1)}, bf16[128,5120]{1,0:T(8,128)(2,1)}, u32[]{:S(2)}, u32[]{:S(2)}) collective-permute-start(bf16[128,5120]{1,0:T(8,128)(2,1)} %collective-permute-done.2.refs_3_), channel_id=1, source_target_pairs={{0,6},{1,7},{2,0},{3,1},{4,2},{5,3},{6,4},{7,5},{8,14},{9,15},{10,... | collective-permute-start | bytes 3932168 | tf_op jit(solution)/shard_map/ppermute | solution.py:116
  55.1 3.2 %copy-start = (bf16[3,5120,256]{2,1,0:T(8,128)(2,1)S(1)}, bf16[3,5120,256]{2,1,0:T(8,128)(2,1)}, u32[]{:S(2)}) copy-start(bf16[3,5120,256]{2,1,0:T(8,128)(2,1)} %get-tuple-element.47.refs_4_.refs_3_) | copy-start | bytes 23592964
  58.3 1.3 copy-start.6
  59.6 1.3 copy-start.9
  73.9 15.2 %collective-permute-start.8 = (bf16[48,5120]{1,0:T(8,128)(2,1)S(1)}, bf16[48,5120]{1,0:T(8,128)(2,1)S(1)}, u32[]{:S(2)}, u32[]{:S(2)}) collective-permute-start(bf16[48,5120]{1,0:T(8,128)(2,1)S(1)} %get-tuple-element.57), channel_id=1, source_target_pairs={{0,2},{1,3},{2,4},{3,5},{4,6},{5,7},{6,0},{7,1},{8,10},{9,11},{10,... | collective-permute-start | bytes 1474568 | tf_op jit(solution)/shard_map/ppermute | solution.py:112
  74.6 14.5 %collective-permute-start.9 = (bf16[48,5120]{1,0:T(8,128)(2,1)S(1)}, bf16[48,5120]{1,0:T(8,128)(2,1)S(1)}, u32[]{:S(2)}, u32[]{:S(2)}) collective-permute-start(bf16[48,5120]{1,0:T(8,128)(2,1)S(1)} %get-tuple-element.58), channel_id=1, source_target_pairs={{0,6},{1,7},{2,0},{3,1},{4,2},{5,3},{6,4},{7,5},{8,14},{9,15},{10,... | collective-permute-start | bytes 1474568 | tf_op jit(solution)/shard_map/ppermute | solution.py:116
  76.7 13.2 %slice-start = ((s8[7864320]{0:T(1024)(128)(4,1)}), s8[4194304]{0:T(1024)(128)(4,1)S(1)}, s32[]{:S(2)}) async-start(s8[7864320]{0:T(1024)(128)(4,1)} %bitcast.11), calls=%async_computation.2 | async-start | bytes 8388608
  76.7 13.2 %slice-start.1 = ((s8[7864320]{0:T(1024)(128)(4,1)}), s8[3670016]{0:T(1024)(128)(4,1)S(1)}, s32[]{:S(2)}) async-start(s8[7864320]{0:T(1024)(128)(4,1)} %bitcast.11), calls=%async_computation.3 | async-start | bytes 7340032
  76.7 12.4 %collective-permute-start.10 = (bf16[32,5120]{1,0:T(8,128)(2,1)S(1)}, bf16[32,5120]{1,0:T(8,128)(2,1)S(1)}, u32[]{:S(2)}, u32[]{:S(2)}) collective-permute-start(bf16[32,5120]{1,0:T(8,128)(2,1)S(1)} %get-tuple-element.59), channel_id=1, source_target_pairs={{0,8},{1,9},{2,10},{3,11},{4,12},{5,13},{6,14},{7,15},{8,0},{9,1},... | collective-permute-start | bytes 983048 | tf_op jit(solution)/shard_map/ppermute | solution.py:120
  78.1 27.6 %collective-permute-start.7 = (bf16[3,512,256]{2,1,0:T(8,128)(2,1)}, bf16[3,512,256]{2,1,0:T(8,128)(2,1)}, u32[]{:S(2)}, u32[]{:S(2)}) collective-permute-start(bf16[3,512,256]{2,1,0:T(8,128)(2,1)} %get-tuple-element.53), channel_id=1, source_target_pairs={{0,1},{1,0},{2,3},{3,2},{4,5},{5,4},{6,7},{7,6},{8,9},{9,8},{10,11... | collective-permute-start | bytes 2359304 | tf_op jit(solution)/shard_map/ppermute | solution.py:124
  89.0 4.7 %copy-start.3 = (bf16[3,384,256]{2,1,0:T(8,128)(2,1)}, bf16[3,384,256]{2,1,0:T(8,128)(2,1)S(1)}, u32[]{:S(2)}) copy-start(bf16[3,384,256]{2,1,0:T(8,128)(2,1)S(1)} %get-tuple-element.63.fb) | copy-start | bytes 1769476
  89.1 16.6 %collective-permute-start.11 = (bf16[3,384,256]{2,1,0:T(8,128)(2,1)}, bf16[3,384,256]{2,1,0:T(8,128)(2,1)}, u32[]{:S(2)}, u32[]{:S(2)}) collective-permute-start(bf16[3,384,256]{2,1,0:T(8,128)(2,1)} %get-tuple-element.64), channel_id=1, source_target_pairs={{0,1},{1,0},{2,3},{3,2},{4,5},{5,4},{6,7},{7,6},{8,9},{9,8},{10,11... | collective-permute-start | bytes 1769480 | tf_op jit(solution)/shard_map/ppermute | solution.py:124
  93.7 0.7 copy-start.10
  95.1 10.5 %all-to-all-start = ((f32[16,16,128]{2,1,0:T(8,128)}), f32[16,16,128]{2,1,0:T(8,128)S(1)}, u32[]{:S(2)}, u32[]{:S(2)}) async-start(f32[16,16,128]{2,1,0:T(8,128)} %square_sums.1), calls=%async_computation | async-start | bytes 262144 | tf_op jit(solution)/shard_map/all_to_all | solution.py:474
  99.5 6.1 %collective-permute-start.12 = (bf16[3,128,256]{2,1,0:T(8,128)(2,1)}, bf16[3,128,256]{2,1,0:T(8,128)(2,1)S(1)}, u32[]{:S(2)}, u32[]{:S(2)}) collective-permute-start(bf16[3,128,256]{2,1,0:T(8,128)(2,1)} %copy-done.10), channel_id=1, source_target_pairs={{0,1},{1,0},{2,3},{3,2},{4,5},{5,4},{6,7},{7,6},{8,9},{9,8},{10,11... | collective-permute-start | bytes 589832 | tf_op jit(solution)/shard_map/ppermute | solution.py:124
  105.7 1.2 copy-start.1
  106.9 1.1 copy-start.4
  108.0 7.8 %copy-start.2 = (f32[2048,128]{1,0:T(8,128)S(1)}, f32[2048,128]{1,0:T(8,128)}, u32[]{:S(2)}) copy-start(f32[2048,128]{1,0:T(8,128)} %get-tuple-element.75.cos_lo.cos_hi.cos_ref) | copy-start | bytes 3145732
  108.0 7.8 %copy-start.5 = (bf16[3,384,256]{2,1,0:T(8,128)(2,1)S(1)}, bf16[3,384,256]{2,1,0:T(8,128)(2,1)}, u32[]{:S(2)}) copy-start(bf16[3,384,256]{2,1,0:T(8,128)(2,1)} %copy-done.3) | copy-start | bytes 1769476
  108.0 7.8 %copy-start.7 = (f32[256]{0:T(256)S(1)}, f32[256]{0:T(256)}, u32[]{:S(2)}) copy-start(f32[256]{0:T(256)} %dynamic_slice.6) | copy-start | bytes 3076
  109.9 16.6 %collective-permute-start.13 = (bf16[512,256]{1,0:T(8,128)(2,1)S(1)}, bf16[512,256]{1,0:T(8,128)(2,1)S(1)}, u32[]{:S(2)}, u32[]{:S(2)}) collective-permute-start(bf16[512,256]{1,0:T(8,128)(2,1)S(1)} %get-tuple-element.77), channel_id=1, source_target_pairs={{112,0},{0,16},{16,32},{32,48},{48,64},{64,80},{80,96},{96,112},{1... | collective-permute-start | bytes 786440 | tf_op jit(solution)/shard_map/ppermute | solution.py:408
  113.3 14.8 %collective-permute-start.14 = (bf16[512,256]{1,0:T(8,128)(2,1)S(1)}, bf16[512,256]{1,0:T(8,128)(2,1)S(1)}, u32[]{:S(2)}, u32[]{:S(2)}) collective-permute-start(bf16[512,256]{1,0:T(8,128)(2,1)S(1)} %get-tuple-element.78), channel_id=1, source_target_pairs={{16,0},{32,16},{48,32},{64,48},{80,64},{96,80},{112,96},{0,112},{1... | collective-permute-start | bytes 786440 | tf_op jit(solution)/shard_map/ppermute | solution.py:408
